TPU v7x, 32 devices: a whole 2x2x4 slice. The times are simulated.
32 devices in a mesh: grp: 2 (over y), exp: 8 (over z, x), hid: 2 (over core).
Axes of the slice: x: 2, y: 2, z: 4, core: 2. Of those that a mesh axis runs over, the one named last changes fastest.
Arguments:
- tokens: bfloat16 [64, 4096], P(('grp', 'exp')), parts along dimension 0, may hold values from -6 to 6
- w_gate: bfloat16 [4096, 32768], P(None, ('exp', 'hid')), may hold values from -0.09375 to 0.09375
- w_up: bfloat16 [4096, 32768], P(None, ('exp', 'hid')), may hold values from -0.09375 to 0.09375
- w_down: bfloat16 [32768, 4096], P(('exp', 'hid')), may hold values from -0.0625 to 0.0625
- block_counts: int32 [8], P('grp'), parts along dimension 0, may hold values from 1 to 1, as said below
- block_rows: int32 [8, 128], P('grp'), parts along dimension 0, may hold values from -1 to 31, as said below
- row_gates: float32 [8, 128], P('grp'), parts along dimension 0, may hold values from 0.1 to 1
Outputs:
- mixed: bfloat16 [64, 4096], P(('grp', 'exp'), 'hid'), parts along dimension 0
There are 2 independent parts, one for each index of `grp`. A program takes and returns all parts, laid end to end along the dimension named above; an argument that names none is the same for every part. Nothing has to cross between parts.
Inputs may be any that keep to these rules, and one draw needn't show every extreme that they name: `block_rows`: in the first block_counts[e] * 128 slots of expert e, the entries other than -1 fill its first slots and are distinct; the slots after them hold stale token indices, which are not live. Every token stands among the live entries of exactly 2 experts. Of one expert's live entries at most 3 name tokens of one aligned block of 4 tokens, and some expert has exactly 3 from every such block in every draw. block_counts[e] is the number of blocks of 128 slots of expert e that hold a live entry; some expert has 1 in every draw.
All inputs are finite; a program needn't handle non-finite values.
Results may differ from a plain program's by a relative error of at most 0.0058.
Values may be sent and summed in bfloat16 or wider, within the bound.
No kernel may reach another device: no remote copies, remote signals or barrier semaphores. Data moves between devices by JAX's collectives and lax.ppermute only.
A program may use at most 128 MiB of HBM per device.

v0:
```python
import jax
import jax.numpy as jnp
from jax import lax
from jax.sharding import PartitionSpec as P

BLOCK = 128
CAP = 3


def expert_block(segment, w_gate, w_up, w_down):
    gate_act = jnp.dot(segment, w_gate, preferred_element_type=jnp.float32)
    up_act = jnp.dot(segment, w_up, preferred_element_type=jnp.float32)
    hidden = (jax.nn.silu(gate_act) * up_act).astype(jnp.bfloat16)
    return jnp.dot(hidden, w_down, preferred_element_type=jnp.float32).astype(jnp.bfloat16)


def local(tokens, w_gate, w_up, w_down, block_counts, block_rows, row_gates):
    sources = lax.axis_size("exp")
    own_index = lax.axis_index("exp")
    token_count = tokens.shape[0]
    model_width = tokens.shape[1]
    experts = block_rows.shape[0]
    slot_count = block_rows.shape[1]
    per_expert = sources // experts
    my_expert = own_index // per_expert
    position = jnp.arange(slot_count, dtype=jnp.int32)
    is_live = (position[None, :] < block_counts[:, None] * BLOCK) & (block_rows >= 0)
    source = jnp.where(is_live, block_rows // token_count, sources)
    matches = (source[:, :, None] == jnp.arange(sources, dtype=jnp.int32)[None, None, :]).astype(
        jnp.int32
    )
    order_rank = jnp.sum(jnp.cumsum(matches, axis=1) * matches, axis=2) - 1
    is_mine = is_live & (source == own_index)
    slot_target = jnp.where(
        is_mine, jnp.arange(experts, dtype=jnp.int32)[:, None] * CAP + order_rank, experts * CAP
    )
    local_values = jnp.where(is_mine, block_rows - own_index * token_count, token_count)
    local_row = (
        jnp.full((experts * CAP + 1,), token_count, jnp.int32)
        .at[slot_target.ravel()]
        .set(local_values.ravel())[: experts * CAP]
    )
    gate_mine = (
        jnp.zeros((experts * CAP + 1,), jnp.float32)
        .at[slot_target.ravel()]
        .set(jnp.where(is_mine, row_gates, 0.0).ravel())[: experts * CAP]
    )
    live_mine = lax.dynamic_index_in_dim(is_live, my_expert, 0, keepdims=False)
    rows_mine = lax.dynamic_index_in_dim(block_rows, my_expert, 0, keepdims=False)
    source_mine = lax.dynamic_index_in_dim(source, my_expert, 0, keepdims=False)
    rank_mine = lax.dynamic_index_in_dim(order_rank, my_expert, 0, keepdims=False)
    back_index = jnp.where(live_mine, source_mine * CAP + rank_mine, sources * CAP)
    blank_row = jnp.zeros((1, model_width), jnp.bfloat16)
    everyone = lax.all_gather(tokens, "exp", axis=0, tiled=True)
    row_pool = jnp.concatenate([everyone, blank_row], axis=0)
    routed = row_pool[jnp.where(live_mine, rows_mine, sources * token_count)]
    partial_rows = expert_block(routed, w_gate, w_up, w_down)
    outbound = (
        jnp.zeros((sources * CAP + 1, model_width), jnp.bfloat16).at[back_index].set(partial_rows)
    )
    outbound = outbound[: sources * CAP].reshape(sources, CAP, model_width)
    returned = lax.all_to_all(outbound, "exp", split_axis=0, concat_axis=0, tiled=True)
    summed = jnp.sum(
        returned.reshape(experts, per_expert, CAP, model_width), axis=1, dtype=jnp.float32
    )
    weighted = (summed * gate_mine.reshape(experts, CAP, 1)).reshape(experts * CAP, model_width)
    selector = (local_row[:, None] == jnp.arange(token_count, dtype=jnp.int32)[None, :]).astype(
        jnp.float32
    )
    gathered_sum = jnp.einsum("st,sd->td", selector, weighted, precision=lax.Precision.HIGHEST)
    share = lax.psum_scatter(gathered_sum, "hid", scatter_dimension=1, tiled=True)
    return share.astype(jnp.bfloat16)


def solution(mesh):
    return jax.shard_map(
        local,
        mesh=mesh,
        in_specs=(
            P(("grp", "exp"), None),
            P(None, ("exp", "hid")),
            P(None, ("exp", "hid")),
            P(("exp", "hid"), None),
            P("grp"),
            P("grp", None),
            P("grp", None),
        ),
        out_specs=P(("grp", "exp"), "hid"),
        check_vma=False,
    )
```

profile of v0, /device:TPU:0, one launch (start us, length us, event | category | flops | bytes accessed | tf_op | source)
XLA Modules:
  0.0 104.3 jit_solution(967142043772491251)
XLA Ops:
  6.5 0.7 broadcast_multiply_fusion
  7.2 0.8 select_bitcast_fusion.1
  8.0 0.1 fusion.3
  8.1 0.3 reduce_window_sum.11
  8.4 0.2 select_reduce_fusion
  8.6 0.1 add_select_fusion.1
  8.7 0.7 fusion.18
  9.4 32.7 %all-gather = bf16[8,4,4096]{2,1,0:T(4,128)(2,1)S(1)} all-gather(bf16[1,4,4096]{2,1,0:T(4,128)(2,1)} %bitcast.36), channel_id=1, replica_groups=mesh['grp'=2,'exp'=8,'hid'=2] {'exp'}, dimensions={0}, use_global_device_ids=true | all-gather | bytes 294912 | tf_op jit(solution)/shard_map/all_gather | solution.py:54
  42.1 0.1 reshape.169
  42.2 1.2 %gather_fusion = bf16[128,4096]{1,0:T(8,128)(2,1)S(1)} fusion(bf16[33,4096]{1,0:T(8,128)(2,1)S(1)} %concatenate.3, s32[1024]{0:T(1024)S(1)} %pad_clamp_fusion), kind=kCustom, calls=%fused_computation | custom fusion | bytes 2097664 | tf_op jit(solution)/shard_map/gather | solution.py:56
  43.4 8.2 %fusion.26 = f32[128,2048]{1,0:T(8,128)S(1)} fusion(bf16[128,4096]{1,0:T(8,128)(2,1)S(1)} %gather_fusion, bf16[4096,2048]{1,0:T(8,128)(2,1)} %param.8), kind=kOutput, calls=%fused_computation.56 | convolution fusion | flops 2147483648 | bytes 18874368 | tf_op jit(solution)/shard_map/dot_general | solution.py:11
  51.6 0.0 copy-start
  51.6 15.4 %convolution_convert_fusion = bf16[128,4096]{1,0:T(8,128)(2,1)S(1)} fusion(bf16[2048,4096]{1,0:T(8,128)(2,1)} %param.10, bf16[128,4096]{1,0:T(8,128)(2,1)S(1)} %gather_fusion, bf16[4096,2048]{1,0:T(8,128)(2,1)} %param.9, f32[128,2048]{1,0:T(8,128)S(1)} %fusion.26), kind=kOutput, calls=%fused_computation.5 | convolution fusion | flops 4297064448 | bytes 36700160 | tf_op jit(solution)/shard_map/dot_general | solution.py:14
  67.1 2.0 %scatter_custom_fusion.1 = bf16[25,4096]{1,0:T(8,128)(2,1)S(1)} fusion(s32[128]{0:T(128)S(1)} %get-tuple-element.12, bf16[128,4096]{1,0:T(8,128)(2,1)S(1)} %convolution_convert_fusion, bf16[]{:T(256)} %constant.77.clone.1), kind=kCustom, calls=%fused_computation.15 | custom fusion | bytes 204802 | tf_op jit(solution)/shard_map/scatter | solution.py:59
  69.1 0.8 reshape.133
  69.9 5.5 %all-to-all-start = ((bf16[8,3,4096]{2,1,0:T(4,128)(2,1)}), bf16[8,3,4096]{2,1,0:T(4,128)(2,1)S(1)}, u32[]{:S(2)}, u32[]{:S(2)}) async-start(bf16[8,3,4096]{2,1,0:T(4,128)(2,1)} %reshape.133), calls=%async_computation | async-start | bytes 524288 | tf_op jit(solution)/shard_map/all_to_all | solution.py:62
  75.4 0.0 reduce-scatter.4.cloned.1.call-start
  75.5 2.6 %scatter_custom_fusion = s32[13]{0:T(128)S(1)} fusion(s32[512]{0:T(512)S(1)} %bitcast.38, s32[512]{0:T(512)S(1)} %get-tuple-element.5, s32[]{:T(128)} %constant.38.clone.1), kind=kCustom, calls=%fused_computation.53 | custom fusion | bytes 56 | tf_op jit(solution)/shard_map/scatter | solution.py:41
  78.1 0.0 copy-done
  78.1 2.4 %scatter_custom_fusion.2 = f32[13]{0:T(128)S(1)} fusion(s32[512]{0:T(512)S(1)} %bitcast.39, f32[512]{0:T(512)S(1)} %select_bitcast_fusion, f32[]{:T(128)} %constant.83.clone.1), kind=kCustom, calls=%fused_computation.50 | custom fusion | bytes 56 | tf_op jit(solution)/shard_map/scatter | solution.py:46
  80.6 3.1 %all-to-all-done = bf16[8,3,4096]{2,1,0:T(4,128)(2,1)S(1)} async-done(((bf16[8,3,4096]{2,1,0:T(4,128)(2,1)}), bf16[8,3,4096]{2,1,0:T(4,128)(2,1)S(1)}, u32[]{:S(2)}, u32[]{:S(2)}) %all-to-all-start) | async-done | bytes 196640 | tf_op jit(solution)/shard_map/all_to_all | solution.py:62
  83.6 0.1 convert_reduce_fusion
  83.8 0.1 reduce_sum.22
  83.9 3.2 %convolution_bitcast_fusion = f32[4096,4]{1,0:T(8,128)} fusion(f32[12,4096]{1,0:T(8,128)S(1)} %reduce_sum.22, f32[12]{0:T(128)S(1)} %bitcast.41, s32[12]{0:T(128)S(1)} %bitcast.40), kind=kOutput, calls=%fused_computation.4 | convolution fusion | flops 2408496 | bytes 262240
  87.1 0.0 reduce-scatter.4.cloned.1.call-update
  87.2 8.1 %reduce-scatter.4.cloned.1.call-done = f32[2048,4]{1,0:T(8,128)} async-done(((f32[4096,4]{1,0:T(8,128)}), f32[2048,4]{1,0:T(8,128)}) %reduce-scatter.4.cloned.1.call-update) | async-done | bytes 32784
  95.2 2.2 %copy.9 = bf16[4,2048]{1,0:T(4,128)(2,1)} copy(f32[4,2048]{0,1:T(8,128)} %bitcast.35) | data formatting | bytes 49152
  (6 shorter events, 0.1 us)
Async XLA Ops:
  51.6 26.5 %copy-start = (f32[4,128]{1,0:T(4,128)S(1)}, f32[4,128]{1,0:T(4,128)}, u32[]{:S(2)}) copy-start(f32[4,128]{1,0:T(4,128)} %param.13) | copy-start | bytes 6148
  69.9 13.7 %all-to-all-start = ((bf16[8,3,4096]{2,1,0:T(4,128)(2,1)}), bf16[8,3,4096]{2,1,0:T(4,128)(2,1)S(1)}, u32[]{:S(2)}, u32[]{:S(2)}) async-start(bf16[8,3,4096]{2,1,0:T(4,128)(2,1)} %reshape.133), calls=%async_computation | async-start | bytes 524288 | tf_op jit(solution)/shard_map/all_to_all | solution.py:62
  75.4 19.8 %reduce-scatter.4.cloned.1.call-start = ((), (), s32[]{:S(2)}) async-start(), calls=%async_computation.2 | async-start | bytes 3145728
Sparse Core Ops, SparseCore 0:
  87.3 7.9 reduce-scatter.3
where the time goes:
time: 105 us; the launch traced here: 104 us
  blocking collectives  32.7 us (31%)
  matrix products  26.8 us (26%)
  between operations  13.5 us (13%)
  local copies, waits for them, and re-layouts  11.4 us (11%)
  waiting for transfers between devices  11.2 us (11%)
  starting transfers between devices  5.56 us (5%)
  other arithmetic  2.98 us (3%)
    all_gather x1, blocking collectives, local(): everyone = lax.all_gather(tokens, 'exp', axis=0, tiled=True)  32.7 us
    dot_general x1, matrix products, expert_block(): jnp.dot(hidden, w_down, preferred_element_type=jnp.float32)  15.4 us
    dot_general x1, matrix products, expert_block(): gate_act = jnp.dot(segment, w_gate, preferred_element_type=jnp.float32)  8.17 us
    unnamed x2, waiting for transfers between devices  8.11 us
    all_to_all x1, starting transfers between devices, local(): lax.all_to_all(outbound, 'exp', split_axis=0, concat_axis=0, tiled=True)  5.52 us
    unnamed x1, matrix products  3.24 us
    all_to_all x1, waiting for transfers between devices, local(): lax.all_to_all(outbound, 'exp', split_axis=0, concat_axis=0, tiled=True)  3.07 us
    scatter x1, local copies, waits for them, and re-layouts, local(): local_row = jnp.full((experts * CAP + 1,), token_count, jnp.int32).at[slo...  2.62 us
  transfers between devices with their start and end apart: 2, of which 2 were waited for; matrix products, arithmetic and copies ran while one was open for 5% of the time, Pallas kernels for 0%

commit v1 on v0

--- a/solution.py
+++ b/solution.py
@@ -1,10 +1,205 @@
+import functools
+
 import jax
 import jax.numpy as jnp
 from jax import lax
+from jax.experimental import pallas as pl
+from jax.experimental.pallas import tpu as pltpu
 from jax.sharding import PartitionSpec as P
 
 BLOCK = 128
 CAP = 3
+TILE = 256
+CHUNKS = 8
+MIB = 1 << 20
+HBM = pl.BlockSpec(memory_space=pltpu.HBM)
+VMEM = pl.BlockSpec(memory_space=pltpu.VMEM)
+SMEM = pl.BlockSpec(memory_space=pltpu.SMEM)
+
+
+def chunk_copies(src, dst, sems):
+    step = src.shape[0] // CHUNKS
+    return [
+        pltpu.make_async_copy(
+            src.at[pl.ds(c * step, step)], dst.at[pl.ds(c * step, step)], sems.at[c]
+        )
+        for c in range(CHUNKS)
+    ]
+
+
+def fetch_kernel(wg_ref, wu_ref, wg_out, wu_out, sems):
+    copies = chunk_copies(wg_ref, wg_out, sems.at[0]) + chunk_copies(wu_ref, wu_out, sems.at[1])
+    for c in copies:
+        c.start()
+    for c in copies:
+        c.wait()
+
+
+def fetch(w_gate, w_up):
+    return pl.pallas_call(
+        fetch_kernel,
+        out_shape=(pltpu.VMEM(w_gate.shape, w_gate.dtype), pltpu.VMEM(w_up.shape, w_up.dtype)),
+        in_specs=[HBM, HBM],
+        out_specs=(VMEM, VMEM),
+        scratch_shapes=[pltpu.SemaphoreType.DMA((2, CHUNKS))],
+        compiler_params=pltpu.CompilerParams(vmem_limit_bytes=1 * MIB),
+        cost_estimate=pl.CostEstimate(
+            flops=0, bytes_accessed=2 * (w_gate.size + w_up.size), transcendentals=0
+        ),
+    )(in_hbm(w_gate), in_hbm(w_up))
+
+
+def token_gates(own, sources, per_expert, token_count, counts_ref, rows_ref, gates_ref):
+    experts, slots = rows_ref.shape
+    expert = own // per_expert
+    mine = lax.broadcasted_iota(jnp.int32, (experts, slots), 0) == expert
+    rows = jnp.sum(jnp.where(mine, rows_ref[...], 0), axis=0, keepdims=True)
+    gates = jnp.sum(jnp.where(mine, gates_ref[...], 0.0), axis=0, keepdims=True)
+    position = lax.broadcasted_iota(jnp.int32, (1, slots), 1)
+    live = (position < counts_ref[expert] * BLOCK) & (rows >= 0)
+    rows = jnp.where(live, rows, -1)
+    total = sources * token_count
+    line = lax.broadcasted_iota(jnp.int32, (total, slots), 0)
+    start = lax.rem(own - line // token_count + sources, sources) * token_count
+    token = start + lax.rem(line, token_count)
+    return jnp.sum(jnp.where(rows == token, gates, 0.0), axis=1, keepdims=True)
+
+
+def hidden_kernel(sources, per_expert, *refs):
+    pieces = refs[:sources]
+    (wg_ref, wu_ref, wd_ref, counts_ref, rows_ref, gates_ref, h_out, g_out, wd_out, wide, x_ref, sems) = refs[sources:]
+    copies = chunk_copies(wd_ref, wd_out, sems)
+    for c in copies:
+        c.start()
+    token_count = pieces[0].shape[0]
+    for k, piece in enumerate(pieces):
+        wide[pl.ds(k * token_count, token_count), :] = piece[...].astype(jnp.float32)
+    x_ref[...] = wide[...].astype(jnp.bfloat16)
+    own = lax.axis_index("exp")
+    g = token_gates(own, sources, per_expert, token_count, counts_ref, rows_ref, gates_ref)
+    g_out[...] = jnp.broadcast_to(g, g_out.shape)
+
+    @pl.loop(0, wg_ref.shape[1] // TILE)
+    def _(n):
+        cols = pl.ds(pl.multiple_of(n * TILE, TILE), TILE)
+        gate = jnp.dot(x_ref[...], wg_ref[:, cols], preferred_element_type=jnp.float32)
+        up = jnp.dot(x_ref[...], wu_ref[:, cols], preferred_element_type=jnp.float32)
+        h_out[:, cols] = (gate / (1.0 + jnp.exp(-gate)) * up).astype(jnp.bfloat16)
+
+    for c in copies:
+        c.wait()
+
+
+def hidden_rows(pieces, wg, wu, w_down, block_counts, block_rows, row_gates, per_expert):
+    sources = len(pieces)
+    total = sources * pieces[0].shape[0]
+    depth, width = wg.shape
+    return pl.pallas_call(
+        functools.partial(hidden_kernel, sources, per_expert),
+        out_shape=(
+            pltpu.VMEM((total, width), jnp.bfloat16),
+            pltpu.VMEM((total, 128), jnp.float32),
+            pltpu.VMEM(w_down.shape, w_down.dtype),
+        ),
+        in_specs=[VMEM] * sources + [VMEM, VMEM, HBM, SMEM, VMEM, VMEM],
+        out_specs=(VMEM, VMEM, VMEM),
+        scratch_shapes=[
+            pltpu.VMEM((total, depth), jnp.float32),
+            pltpu.VMEM((total, depth), jnp.bfloat16),
+            pltpu.SemaphoreType.DMA((CHUNKS,)),
+        ],
+        compiler_params=pltpu.CompilerParams(vmem_limit_bytes=2 * MIB),
+        cost_estimate=pl.CostEstimate(
+            flops=4 * total * depth * width, bytes_accessed=2 * w_down.size, transcendentals=total * width
+        ),
+    )(*pieces, in_vmem(wg), in_vmem(wu), in_hbm(w_down), block_counts, block_rows, row_gates)
+
+
+def in_hbm(x):
+    return pltpu.with_memory_space_constraint(x, pltpu.HBM)
+
+
+def in_vmem(x):
+    return pltpu.with_memory_space_constraint(x, pltpu.VMEM)
+
+
+def down_kernel(other, h_ref, g_ref, wd_ref, out_ref):
+    half = wd_ref.shape[1] // 2
+    side = lax.axis_index("hid")
+    base = (1 - side if other else side) * half
+    for n in range(half // TILE):
+        cols = pl.ds(pl.multiple_of(base + n * TILE, TILE), TILE)
+        part = jnp.dot(h_ref[...], wd_ref[:, cols], preferred_element_type=jnp.float32)
+        out_ref[:, pl.ds(n * TILE, TILE)] = (part * g_ref[:, :1]).astype(out_ref.dtype)
+
+
+def down_half(hidden, g, wd, other, dtype):
+    rows, depth = hidden.shape
+    half = wd.shape[1] // 2
+    return pl.pallas_call(
+        functools.partial(down_kernel, other),
+        out_shape=jax.ShapeDtypeStruct((rows, half), dtype),
+        in_specs=[VMEM, VMEM, VMEM],
+        out_specs=VMEM,
+        compiler_params=pltpu.CompilerParams(vmem_limit_bytes=2 * MIB),
+        cost_estimate=pl.CostEstimate(flops=2 * rows * depth * half, bytes_accessed=0, transcendentals=0),
+    )(in_vmem(hidden), in_vmem(g), in_vmem(wd))
+
+
+def merge_kernel(keep_ref, got_ref, own_ref, *out_refs):
+    both = keep_ref[...] + got_ref[...].astype(jnp.float32)
+    count = own_ref.shape[0]
+    own_ref[...] = both[:count]
+    for k, out_ref in enumerate(out_refs):
+        out_ref[...] = both[(k + 1) * count : (k + 2) * count].astype(out_ref.dtype)
+
+
+def merge(keep, got, sources):
+    rows, width = keep.shape
+    count = rows // sources
+    return pl.pallas_call(
+        merge_kernel,
+        out_shape=(jax.ShapeDtypeStruct((count, width), jnp.float32),)
+        + (jax.ShapeDtypeStruct((count, width), jnp.bfloat16),) * (sources - 1),
+        in_specs=[VMEM, VMEM],
+        out_specs=(VMEM,) * sources,
+        compiler_params=pltpu.CompilerParams(vmem_limit_bytes=2 * MIB),
+    )(keep, got)
+
+
+def sum_kernel(own_ref, *refs):
+    total = own_ref[...]
+    for ref in refs[:-1]:
+        total = total + ref[...].astype(jnp.float32)
+    refs[-1][...] = total.astype(jnp.bfloat16)
+
+
+def final_sum(own, got):
+    return pl.pallas_call(
+        sum_kernel,
+        out_shape=jax.ShapeDtypeStruct(own.shape, jnp.bfloat16),
+        in_specs=[VMEM] * (1 + len(got)),
+        out_specs=VMEM,
+        compiler_params=pltpu.CompilerParams(vmem_limit_bytes=2 * MIB),
+    )(own, *got)
+
+
+def shifted(x, k, sources):
+    return lax.ppermute(x, "exp", [(i, (i + k) % sources) for i in range(sources)])
+
+
+def local(tokens, w_gate, w_up, w_down, block_counts, block_rows, row_gates):
+    sources = lax.axis_size("exp")
+    per_expert = sources // block_rows.shape[0]
+    pieces = [tokens] + [shifted(tokens, k, sources) for k in range(1, sources)]
+    wg, wu = fetch(w_gate, w_up)
+    hidden, g, wd = hidden_rows(pieces, wg, wu, w_down, block_counts, block_rows, row_gates, per_expert)
+    send = down_half(hidden, g, wd, True, jnp.bfloat16)
+    keep = down_half(hidden, g, wd, False, jnp.float32)
+    got = lax.ppermute(send, "hid", [(0, 1), (1, 0)])
+    own, *outgoing = merge(keep, got, sources)
+    returned = [shifted(piece, -(k + 1), sources) for k, piece in enumerate(outgoing)]
+    return final_sum(own, returned)
 
 
 def expert_block(segment, w_gate, w_up, w_down):
@@ -14,7 +209,7 @@
     return jnp.dot(hidden, w_down, preferred_element_type=jnp.float32).astype(jnp.bfloat16)
 
 
-def local(tokens, w_gate, w_up, w_down, block_counts, block_rows, row_gates):
+def local_wide(tokens, w_gate, w_up, w_down, block_counts, block_rows, row_gates):
     sources = lax.axis_size("exp")
     own_index = lax.axis_index("exp")
     token_count = tokens.shape[0]
@@ -74,7 +269,7 @@
 
 def solution(mesh):
     return jax.shard_map(
-        local,
+        local if mesh.shape["exp"] <= 16 else local_wide,
         mesh=mesh,
         in_specs=(
             P(("grp", "exp"), None),

time: 105 us -> 63.2 us (0.60)
  blocking collectives: 32.7 us -> 0 us
  matrix products: 26.8 us -> 0 us
  Pallas kernels: 0 us -> 22.2 us
  starting transfers between devices: 5.56 us -> 22.8 us
  between operations: 13.5 us -> 0.12 us
  waiting for transfers between devices: 11.2 us -> 6.42 us
  other arithmetic: 2.98 us -> 0 us
    all_gather x1 -> x0, blocking collectives: 32.7 us -> none  [local(): everyone = lax.all_gather(tokens, 'exp', axis=0, tiled=True)]
    dot_general x2 -> x0, matrix products: 23.6 us -> none  [the longest x1 15.4 us: expert_block(): jnp.dot(hidden, w_down, preferred_element_type=jnp.float32)]
    ppermute x0 -> x15, starting transfers between devices: none -> 22.8 us  [the longest x14 22.8 us: shifted(): lax.ppermute(x, 'exp', [(i, (i + k) % sources) for i in range(sources)])]
    pallas_call x0 -> x6, Pallas kernels: none -> 22.2 us  [the longest x1 10.8 us: fetch(): pl.pallas_call(fetch_kernel, out_shape=(pltpu.VMEM(w_gate.shape, w_gate.d...]
    unnamed x4 -> x12, local copies, waits for them, and re-layouts: 2.24 us -> 11.5 us
    unnamed x2 -> x0, waiting for transfers between devices: 8.11 us -> none
    scatter x3 -> x0, local copies, waits for them, and re-layouts: 7.04 us -> none  [the longest x1 2.62 us: local(): local_row = jnp.full((experts * CAP + 1,), token_count, jnp.int32).at[slo...]
    ppermute x0 -> x15, waiting for transfers between devices: none -> 6.42 us  [the longest x14 6.4 us: shifted(): lax.ppermute(x, 'exp', [(i, (i + k) % sources) for i in range(sources)])]
  transfers between devices with their start and end apart: 2 -> 15, of which waited for: 2 -> 3; matrix products, arithmetic and copies ran while one was open for 5% -> 0% of each run, Pallas kernels for 0% -> 20%
where the time goes in v1:
time: 63.2 us; the launch traced here: 63.1 us
  starting transfers between devices  22.8 us (36%)
  Pallas kernels  22.2 us (35%)
  local copies, waits for them, and re-layouts  11.5 us (18%)
  waiting for transfers between devices  6.42 us (10%)
    ppermute x14, starting transfers between devices, shifted(): lax.ppermute(x, 'exp', [(i, (i + k) % sources) for i in range(sources)])  22.8 us
    unnamed x12, local copies, waits for them, and re-layouts  11.5 us
    pallas_call x1, Pallas kernels, fetch(): pl.pallas_call(fetch_kernel, out_shape=(pltpu.VMEM(w_gate.shape, w_gate.d...  10.8 us
    pallas_call x1, Pallas kernels, hidden_rows(): pl.pallas_call(functools.partial(hidden_kernel, sources, per_expert), out...  7.67 us
    ppermute x14, waiting for transfers between devices, shifted(): lax.ppermute(x, 'exp', [(i, (i + k) % sources) for i in range(sources)])  6.4 us
    pallas_call x2, Pallas kernels, down_half(): pl.pallas_call(functools.partial(down_kernel, other), out_shape=jax.Shape...  3.13 us
  transfers between devices with their start and end apart: 15, of which 3 were waited for; matrix products, arithmetic and copies ran while one was open for 0% of the time, Pallas kernels for 20%

profile of v1, /device:TPU:0, one launch (start us, length us, event | category | flops | bytes accessed | tf_op | source)
XLA Modules:
  0.0 63.1 jit_solution(730089285930241647)
XLA Ops:
  0.0 0.0 copy-start.2
  0.0 0.0 copy-start.4
  0.0 0.0 copy-start.3
  0.0 0.0 copy-start.5
  0.0 5.1 %collective-permute-start.5 = (bf16[4,4096]{1,0:T(4,128)(2,1)}, bf16[4,4096]{1,0:T(4,128)(2,1)S(1)}, u32[]{:S(2)}, u32[]{:S(2)}) collective-permute-start(bf16[4,4096]{1,0:T(4,128)(2,1)} %refs_0_.1), channel_id=1, source_target_pairs={{0,12},{2,14},{4,0},{6,2},{8,4},{10,6},{12,8},{14,10},{1,13},{3,15... | collective-permute-start | bytes 98312 | tf_op jit(solution)/shard_map/ppermute | solution.py:188
  5.1 0.4 collective-permute-start.4
  5.5 3.5 %collective-permute-start.3 = (bf16[4,4096]{1,0:T(4,128)(2,1)}, bf16[4,4096]{1,0:T(4,128)(2,1)S(1)}, u32[]{:S(2)}, u32[]{:S(2)}) collective-permute-start(bf16[4,4096]{1,0:T(4,128)(2,1)} %refs_0_.1), channel_id=1, source_target_pairs={{0,8},{2,10},{4,12},{6,14},{8,0},{10,2},{12,4},{14,6},{1,9},{3,11}... | collective-permute-start | bytes 98312 | tf_op jit(solution)/shard_map/ppermute | solution.py:188
  9.0 0.0 collective-permute-start.2
  9.0 1.0 %collective-permute-start.1 = (bf16[4,4096]{1,0:T(4,128)(2,1)}, bf16[4,4096]{1,0:T(4,128)(2,1)S(1)}, u32[]{:S(2)}, u32[]{:S(2)}) collective-permute-start(bf16[4,4096]{1,0:T(4,128)(2,1)} %refs_0_.1), channel_id=1, source_target_pairs={{0,4},{2,6},{4,8},{6,10},{8,12},{10,14},{12,0},{14,2},{1,5},{3,7},... | collective-permute-start | bytes 98312 | tf_op jit(solution)/shard_map/ppermute | solution.py:188
  10.0 0.0 collective-permute-done.5.refs_6_
  10.0 1.5 %collective-permute-start = (bf16[4,4096]{1,0:T(4,128)(2,1)}, bf16[4,4096]{1,0:T(4,128)(2,1)S(1)}, u32[]{:S(2)}, u32[]{:S(2)}) collective-permute-start(bf16[4,4096]{1,0:T(4,128)(2,1)} %refs_0_.1), channel_id=1, source_target_pairs={{0,2},{2,4},{4,6},{6,8},{8,10},{10,12},{12,14},{14,0},{1,3},{3,5},... | collective-permute-start | bytes 98312 | tf_op jit(solution)/shard_map/ppermute | solution.py:188
  11.5 0.0 collective-permute-done.4.refs_5_
  11.5 3.2 %collective-permute-start.6 = (bf16[4,4096]{1,0:T(4,128)(2,1)}, bf16[4,4096]{1,0:T(4,128)(2,1)S(1)}, u32[]{:S(2)}, u32[]{:S(2)}) collective-permute-start(bf16[4,4096]{1,0:T(4,128)(2,1)} %refs_0_.1), channel_id=1, source_target_pairs={{0,14},{2,0},{4,2},{6,4},{8,6},{10,8},{12,10},{14,12},{1,15},{3,1}... | collective-permute-start | bytes 98312 | tf_op jit(solution)/shard_map/ppermute | solution.py:188
  14.7 10.8 %shard_map.73 = (bf16[4096,2048]{1,0:T(8,128)(2,1)S(1)}, bf16[4096,2048]{1,0:T(8,128)(2,1)S(1)}) custom-call(bf16[4096,2048]{1,0:T(8,128)(2,1)} %wg_ref.1, bf16[4096,2048]{1,0:T(8,128)(2,1)} %wu_ref.1), custom_call_target="tpu_custom_call" | custom-call | bytes 33554432 | tf_op jit(solution)/shard_map/pallas_call | solution.py:39
  25.5 0.0 copy-start
  25.5 5.7 %copy-done = bf16[4096,2048]{1,0:T(8,128)(2,1)} copy-done((bf16[4096,2048]{1,0:T(8,128)(2,1)}, bf16[4096,2048]{1,0:T(8,128)(2,1)S(1)}, u32[]{:S(2)}) %copy-start) | copy-done | bytes 16777240
  31.2 0.0 collective-permute-done.3.refs_4_
  31.2 0.0 collective-permute-done.2.refs_3_
  31.2 0.0 collective-permute-done.1.refs_2_
  31.2 0.0 collective-permute-done.refs_1_
  31.2 0.0 collective-permute-done.6.refs_7_
  31.2 0.0 copy-done.2
  31.2 0.0 copy-done.4
  31.2 0.0 copy-done.3
  31.2 0.0 copy-done.5
  31.3 0.0 copy-start.1
  31.3 5.8 %copy-done.1 = bf16[4096,2048]{1,0:T(8,128)(2,1)S(1)} copy-done((bf16[4096,2048]{1,0:T(8,128)(2,1)S(1)}, bf16[4096,2048]{1,0:T(8,128)(2,1)}, u32[]{:S(2)}) %copy-start.1) | copy-done | bytes 16777240
  37.0 7.7 %shard_map.74 = (bf16[32,2048]{1,0:T(8,128)(2,1)S(1)}, f32[32,128]{1,0:T(8,128)S(1)}, bf16[2048,4096]{1,0:T(8,128)(2,1)S(1)}) custom-call(bf16[4,4096]{1,0:T(4,128)(2,1)S(1)} %copy-done.2, bf16[4,4096]{1,0:T(4,128)(2,1)S(1)} %collective-permute-done.refs_1_, bf16[4,4096]{1,0:T(4,128)(2,1)S(1)} %collective-permute-done.1.refs_2_, ...), custom_call_target="tpu_custom_call" | custom-call | flops 1073741824 | bytes 16777216 | tf_op jit(solution)/shard_map/pallas_call | solution.py:97
  44.7 1.6 %shard_map.76 = bf16[32,2048]{1,0:T(8,128)(2,1)S(1)} custom-call(bf16[32,2048]{1,0:T(8,128)(2,1)S(1)} %get-tuple-element.20.h_ref, f32[32,128]{1,0:T(8,128)S(1)} %get-tuple-element.21.g_ref, bf16[2048,4096]{1,0:T(8,128)(2,1)S(1)} %get-tuple-element.22.wd_ref), custom_call_target="tpu_custom_call" | custom-call | flops 268435456 | tf_op jit(solution)/shard_map/pallas_call | solution.py:139
  46.3 0.0 collective-permute-start.7
  46.3 1.6 %shard_map.75.keep_ref = f32[32,2048]{1,0:T(8,128)S(1)} custom-call(bf16[32,2048]{1,0:T(8,128)(2,1)S(1)} %get-tuple-element.20.h_ref, f32[32,128]{1,0:T(8,128)S(1)} %get-tuple-element.21.g_ref, bf16[2048,4096]{1,0:T(8,128)(2,1)S(1)} %get-tuple-element.22.wd_ref), custom_call_target="tpu_custom_call" | custom-call | flops 268435456 | tf_op jit(solution)/shard_map/pallas_call | solution.py:139
  47.9 0.0 collective-permute-done.7.got_ref
  48.0 1.1 %collective-permute-start.8 = (bf16[4,2048]{1,0:T(4,128)(2,1)S(1)}, bf16[4,2048]{1,0:T(4,128)(2,1)S(1)}, u32[]{:S(2)}, u32[]{:S(2)}) collective-permute-start(bf16[4,2048]{1,0:T(4,128)(2,1)S(1)} %get-tuple-element.24), channel_id=1, source_target_pairs={{0,14},{2,0},{4,2},{6,4},{8,6},{10,8},{12,10},{14,12},{1,15},{3,1}... | collective-permute-start | bytes 49160 | tf_op jit(solution)/shard_map/ppermute | solution.py:188
  49.0 0.6 collective-permute-start.9
  49.6 1.1 %collective-permute-start.10 = (bf16[4,2048]{1,0:T(4,128)(2,1)S(1)}, bf16[4,2048]{1,0:T(4,128)(2,1)S(1)}, u32[]{:S(2)}, u32[]{:S(2)}) collective-permute-start(bf16[4,2048]{1,0:T(4,128)(2,1)S(1)} %get-tuple-element.26), channel_id=1, source_target_pairs={{0,10},{2,12},{4,14},{6,0},{8,2},{10,4},{12,6},{14,8},{1,11},{3,13... | collective-permute-start | bytes 49160 | tf_op jit(solution)/shard_map/ppermute | solution.py:188
  50.7 2.7 %collective-permute-start.11 = (bf16[4,2048]{1,0:T(4,128)(2,1)S(1)}, bf16[4,2048]{1,0:T(4,128)(2,1)S(1)}, u32[]{:S(2)}, u32[]{:S(2)}) collective-permute-start(bf16[4,2048]{1,0:T(4,128)(2,1)S(1)} %get-tuple-element.27), channel_id=1, source_target_pairs={{0,8},{2,10},{4,12},{6,14},{8,0},{10,2},{12,4},{14,6},{1,9},{3,11}... | collective-permute-start | bytes 49160 | tf_op jit(solution)/shard_map/ppermute | solution.py:188
  53.4 0.0 collective-permute-start.12
  53.4 0.0 collective-permute-done.8.refs_0_
  53.4 2.6 %collective-permute-start.13 = (bf16[4,2048]{1,0:T(4,128)(2,1)S(1)}, bf16[4,2048]{1,0:T(4,128)(2,1)S(1)}, u32[]{:S(2)}, u32[]{:S(2)}) collective-permute-start(bf16[4,2048]{1,0:T(4,128)(2,1)S(1)} %get-tuple-element.29), channel_id=1, source_target_pairs={{0,4},{2,6},{4,8},{6,10},{8,12},{10,14},{12,0},{14,2},{1,5},{3,7},... | collective-permute-start | bytes 49160 | tf_op jit(solution)/shard_map/ppermute | solution.py:188
  56.0 0.0 collective-permute-done.9.refs_1_
  56.0 0.1 collective-permute-start.14
  56.1 0.0 collective-permute-done.10.refs_2_
  56.1 0.0 collective-permute-done.11.refs_3_
  56.1 2.9 %collective-permute-done.12.refs_4_ = bf16[4,2048]{1,0:T(4,128)(2,1)S(1)} collective-permute-done((bf16[4,2048]{1,0:T(4,128)(2,1)S(1)}, bf16[4,2048]{1,0:T(4,128)(2,1)S(1)}, u32[]{:S(2)}, u32[]{:S(2)}) %collective-permute-start.12) | collective-permute-done | bytes 16416 | tf_op jit(solution)/shard_map/ppermute | solution.py:188
  59.0 0.2 collective-permute-done.13.refs_5_
  59.2 3.3 %collective-permute-done.14.refs_6_ = bf16[4,2048]{1,0:T(4,128)(2,1)S(1)} collective-permute-done((bf16[4,2048]{1,0:T(4,128)(2,1)S(1)}, bf16[4,2048]{1,0:T(4,128)(2,1)S(1)}, u32[]{:S(2)}, u32[]{:S(2)}) %collective-permute-start.14) | collective-permute-done | bytes 16416 | tf_op jit(solution)/shard_map/ppermute | solution.py:188
  62.5 0.6 %shard_map.78 = bf16[4,2048]{1,0:T(4,128)(2,1)} custom-call(f32[4,2048]{1,0:T(4,128)S(1)} %get-tuple-element.23.own_ref, bf16[4,2048]{1,0:T(4,128)(2,1)S(1)} %collective-permute-done.8.refs_0_, bf16[4,2048]{1,0:T(4,128)(2,1)S(1)} %collective-permute-done.9.refs_1_, bf16[4,2048]{1,0:T(4,128)(2,1)S(1)} %collective-permute-done.10.refs_2_, ...), custom_call_target="tpu_custom_call" | custom-call | tf_op jit(solution)/shard_map/pallas_call | solution.py:178
  (1 shorter events, 0.0 us)
Async XLA Ops:
  0.0 31.2 %copy-start.2 = (bf16[4,4096]{1,0:T(4,128)(2,1)S(1)}, bf16[4,4096]{1,0:T(4,128)(2,1)}, u32[]{:S(2)}) copy-start(bf16[4,4096]{1,0:T(4,128)(2,1)} %refs_0_.1) | copy-start | bytes 98308
  0.0 31.2 %copy-start.4 = (f32[4,128]{1,0:T(4,128)S(1)}, f32[4,128]{1,0:T(4,128)}, u32[]{:S(2)}) copy-start(f32[4,128]{1,0:T(4,128)} %refs_13_.1) | copy-start | bytes 6148
  0.0 31.2 %copy-start.3 = (s32[4,128]{1,0:T(4,128)S(1)}, s32[4,128]{1,0:T(4,128)}, u32[]{:S(2)}) copy-start(s32[4,128]{1,0:T(4,128)} %refs_12_.1) | copy-start | bytes 6148
  0.0 31.2 %copy-start.5 = (s32[4]{0:T(128)S(1)}, s32[4]{0:T(128)}, u32[]{:S(2)}) copy-start(s32[4]{0:T(128)} %refs_11_.1) | copy-start | bytes 52
  0.0 10.0 %collective-permute-start.5 = (bf16[4,4096]{1,0:T(4,128)(2,1)}, bf16[4,4096]{1,0:T(4,128)(2,1)S(1)}, u32[]{:S(2)}, u32[]{:S(2)}) collective-permute-start(bf16[4,4096]{1,0:T(4,128)(2,1)} %refs_0_.1), channel_id=1, source_target_pairs={{0,12},{2,14},{4,0},{6,2},{8,4},{10,6},{12,8},{14,10},{1,13},{3,15... | collective-permute-start | bytes 98312 | tf_op jit(solution)/shard_map/ppermute | solution.py:188
  5.1 6.3 %collective-permute-start.4 = (bf16[4,4096]{1,0:T(4,128)(2,1)}, bf16[4,4096]{1,0:T(4,128)(2,1)S(1)}, u32[]{:S(2)}, u32[]{:S(2)}) collective-permute-start(bf16[4,4096]{1,0:T(4,128)(2,1)} %refs_0_.1), channel_id=1, source_target_pairs={{0,10},{2,12},{4,14},{6,0},{8,2},{10,4},{12,6},{14,8},{1,11},{3,13... | collective-permute-start | bytes 98312 | tf_op jit(solution)/shard_map/ppermute | solution.py:188
  5.5 25.7 %collective-permute-start.3 = (bf16[4,4096]{1,0:T(4,128)(2,1)}, bf16[4,4096]{1,0:T(4,128)(2,1)S(1)}, u32[]{:S(2)}, u32[]{:S(2)}) collective-permute-start(bf16[4,4096]{1,0:T(4,128)(2,1)} %refs_0_.1), channel_id=1, source_target_pairs={{0,8},{2,10},{4,12},{6,14},{8,0},{10,2},{12,4},{14,6},{1,9},{3,11}... | collective-permute-start | bytes 98312 | tf_op jit(solution)/shard_map/ppermute | solution.py:188
  9.0 22.2 %collective-permute-start.2 = (bf16[4,4096]{1,0:T(4,128)(2,1)}, bf16[4,4096]{1,0:T(4,128)(2,1)S(1)}, u32[]{:S(2)}, u32[]{:S(2)}) collective-permute-start(bf16[4,4096]{1,0:T(4,128)(2,1)} %refs_0_.1), channel_id=1, source_target_pairs={{0,6},{2,8},{4,10},{6,12},{8,14},{10,0},{12,2},{14,4},{1,7},{3,9},... | collective-permute-start | bytes 98312 | tf_op jit(solution)/shard_map/ppermute | solution.py:188
  9.0 22.2 %collective-permute-start.1 = (bf16[4,4096]{1,0:T(4,128)(2,1)}, bf16[4,4096]{1,0:T(4,128)(2,1)S(1)}, u32[]{:S(2)}, u32[]{:S(2)}) collective-permute-start(bf16[4,4096]{1,0:T(4,128)(2,1)} %refs_0_.1), channel_id=1, source_target_pairs={{0,4},{2,6},{4,8},{6,10},{8,12},{10,14},{12,0},{14,2},{1,5},{3,7},... | collective-permute-start | bytes 98312 | tf_op jit(solution)/shard_map/ppermute | solution.py:188
  10.0 21.2 %collective-permute-start = (bf16[4,4096]{1,0:T(4,128)(2,1)}, bf16[4,4096]{1,0:T(4,128)(2,1)S(1)}, u32[]{:S(2)}, u32[]{:S(2)}) collective-permute-start(bf16[4,4096]{1,0:T(4,128)(2,1)} %refs_0_.1), channel_id=1, source_target_pairs={{0,2},{2,4},{4,6},{6,8},{8,10},{10,12},{12,14},{14,0},{1,3},{3,5},... | collective-permute-start | bytes 98312 | tf_op jit(solution)/shard_map/ppermute | solution.py:188
  11.5 19.8 %collective-permute-start.6 = (bf16[4,4096]{1,0:T(4,128)(2,1)}, bf16[4,4096]{1,0:T(4,128)(2,1)S(1)}, u32[]{:S(2)}, u32[]{:S(2)}) collective-permute-start(bf16[4,4096]{1,0:T(4,128)(2,1)} %refs_0_.1), channel_id=1, source_target_pairs={{0,14},{2,0},{4,2},{6,4},{8,6},{10,8},{12,10},{14,12},{1,15},{3,1}... | collective-permute-start | bytes 98312 | tf_op jit(solution)/shard_map/ppermute | solution.py:188
  25.5 5.7 %copy-start = (bf16[4096,2048]{1,0:T(8,128)(2,1)}, bf16[4096,2048]{1,0:T(8,128)(2,1)S(1)}, u32[]{:S(2)}) copy-start(bf16[4096,2048]{1,0:T(8,128)(2,1)S(1)} %get-tuple-element.18.refs_8_) | copy-start | bytes 50331652
  31.3 5.8 %copy-start.1 = (bf16[4096,2048]{1,0:T(8,128)(2,1)S(1)}, bf16[4096,2048]{1,0:T(8,128)(2,1)}, u32[]{:S(2)}) copy-start(bf16[4096,2048]{1,0:T(8,128)(2,1)} %copy-done) | copy-start | bytes 50331652
  46.3 1.6 %collective-permute-start.7 = (bf16[32,2048]{1,0:T(8,128)(2,1)S(1)}, bf16[32,2048]{1,0:T(8,128)(2,1)S(1)}, u32[]{:S(2)}, u32[]{:S(2)}) collective-permute-start(bf16[32,2048]{1,0:T(8,128)(2,1)S(1)} %shard_map.76), channel_id=1, source_target_pairs={{0,1},{1,0},{2,3},{3,2},{4,5},{5,4},{6,7},{7,6},{8,9},{9,8},{10,11... | collective-permute-start | bytes 393224 | tf_op jit(solution)/shard_map/ppermute | solution.py:199
  48.0 5.5 %collective-permute-start.8 = (bf16[4,2048]{1,0:T(4,128)(2,1)S(1)}, bf16[4,2048]{1,0:T(4,128)(2,1)S(1)}, u32[]{:S(2)}, u32[]{:S(2)}) collective-permute-start(bf16[4,2048]{1,0:T(4,128)(2,1)S(1)} %get-tuple-element.24), channel_id=1, source_target_pairs={{0,14},{2,0},{4,2},{6,4},{8,6},{10,8},{12,10},{14,12},{1,15},{3,1}... | collective-permute-start | bytes 49160 | tf_op jit(solution)/shard_map/ppermute | solution.py:188
  49.0 7.0 %collective-permute-start.9 = (bf16[4,2048]{1,0:T(4,128)(2,1)S(1)}, bf16[4,2048]{1,0:T(4,128)(2,1)S(1)}, u32[]{:S(2)}, u32[]{:S(2)}) collective-permute-start(bf16[4,2048]{1,0:T(4,128)(2,1)S(1)} %get-tuple-element.25), channel_id=1, source_target_pairs={{0,12},{2,14},{4,0},{6,2},{8,4},{10,6},{12,8},{14,10},{1,13},{3,15... | collective-permute-start | bytes 49160 | tf_op jit(solution)/shard_map/ppermute | solution.py:188
  49.6 6.5 %collective-permute-start.10 = (bf16[4,2048]{1,0:T(4,128)(2,1)S(1)}, bf16[4,2048]{1,0:T(4,128)(2,1)S(1)}, u32[]{:S(2)}, u32[]{:S(2)}) collective-permute-start(bf16[4,2048]{1,0:T(4,128)(2,1)S(1)} %get-tuple-element.26), channel_id=1, source_target_pairs={{0,10},{2,12},{4,14},{6,0},{8,2},{10,4},{12,6},{14,8},{1,11},{3,13... | collective-permute-start | bytes 49160 | tf_op jit(solution)/shard_map/ppermute | solution.py:188
  50.7 5.4 %collective-permute-start.11 = (bf16[4,2048]{1,0:T(4,128)(2,1)S(1)}, bf16[4,2048]{1,0:T(4,128)(2,1)S(1)}, u32[]{:S(2)}, u32[]{:S(2)}) collective-permute-start(bf16[4,2048]{1,0:T(4,128)(2,1)S(1)} %get-tuple-element.27), channel_id=1, source_target_pairs={{0,8},{2,10},{4,12},{6,14},{8,0},{10,2},{12,4},{14,6},{1,9},{3,11}... | collective-permute-start | bytes 49160 | tf_op jit(solution)/shard_map/ppermute | solution.py:188
  53.4 5.5 %collective-permute-start.12 = (bf16[4,2048]{1,0:T(4,128)(2,1)S(1)}, bf16[4,2048]{1,0:T(4,128)(2,1)S(1)}, u32[]{:S(2)}, u32[]{:S(2)}) collective-permute-start(bf16[4,2048]{1,0:T(4,128)(2,1)S(1)} %get-tuple-element.28), channel_id=1, source_target_pairs={{0,6},{2,8},{4,10},{6,12},{8,14},{10,0},{12,2},{14,4},{1,7},{3,9},... | collective-permute-start | bytes 49160 | tf_op jit(solution)/shard_map/ppermute | solution.py:188
  53.4 5.7 %collective-permute-start.13 = (bf16[4,2048]{1,0:T(4,128)(2,1)S(1)}, bf16[4,2048]{1,0:T(4,128)(2,1)S(1)}, u32[]{:S(2)}, u32[]{:S(2)}) collective-permute-start(bf16[4,2048]{1,0:T(4,128)(2,1)S(1)} %get-tuple-element.29), channel_id=1, source_target_pairs={{0,4},{2,6},{4,8},{6,10},{8,12},{10,14},{12,0},{14,2},{1,5},{3,7},... | collective-permute-start | bytes 49160 | tf_op jit(solution)/shard_map/ppermute | solution.py:188
  56.0 6.4 %collective-permute-start.14 = (bf16[4,2048]{1,0:T(4,128)(2,1)S(1)}, bf16[4,2048]{1,0:T(4,128)(2,1)S(1)}, u32[]{:S(2)}, u32[]{:S(2)}) collective-permute-start(bf16[4,2048]{1,0:T(4,128)(2,1)S(1)} %get-tuple-element.30), channel_id=1, source_target_pairs={{0,2},{2,4},{4,6},{6,8},{8,10},{10,12},{12,14},{14,0},{1,3},{3,5},... | collective-permute-start | bytes 49160 | tf_op jit(solution)/shard_map/ppermute | solution.py:188

commit v2 on v1

--- a/solution.py
+++ b/solution.py
@@ -9,44 +9,11 @@
 
 BLOCK = 128
 CAP = 3
-TILE = 256
-CHUNKS = 8
+TILE = 512
 MIB = 1 << 20
-HBM = pl.BlockSpec(memory_space=pltpu.HBM)
+AHEAD = 20_000_000_000
 VMEM = pl.BlockSpec(memory_space=pltpu.VMEM)
 SMEM = pl.BlockSpec(memory_space=pltpu.SMEM)
-
-
-def chunk_copies(src, dst, sems):
-    step = src.shape[0] // CHUNKS
-    return [
-        pltpu.make_async_copy(
-            src.at[pl.ds(c * step, step)], dst.at[pl.ds(c * step, step)], sems.at[c]
-        )
-        for c in range(CHUNKS)
-    ]
-
-
-def fetch_kernel(wg_ref, wu_ref, wg_out, wu_out, sems):
-    copies = chunk_copies(wg_ref, wg_out, sems.at[0]) + chunk_copies(wu_ref, wu_out, sems.at[1])
-    for c in copies:
-        c.start()
-    for c in copies:
-        c.wait()
-
-
-def fetch(w_gate, w_up):
-    return pl.pallas_call(
-        fetch_kernel,
-        out_shape=(pltpu.VMEM(w_gate.shape, w_gate.dtype), pltpu.VMEM(w_up.shape, w_up.dtype)),
-        in_specs=[HBM, HBM],
-        out_specs=(VMEM, VMEM),
-        scratch_shapes=[pltpu.SemaphoreType.DMA((2, CHUNKS))],
-        compiler_params=pltpu.CompilerParams(vmem_limit_bytes=1 * MIB),
-        cost_estimate=pl.CostEstimate(
-            flops=0, bytes_accessed=2 * (w_gate.size + w_up.size), transcendentals=0
-        ),
-    )(in_hbm(w_gate), in_hbm(w_up))
 
 
 def token_gates(own, sources, per_expert, token_count, counts_ref, rows_ref, gates_ref):
@@ -65,19 +32,35 @@
     return jnp.sum(jnp.where(rows == token, gates, 0.0), axis=1, keepdims=True)
 
 
-def hidden_kernel(sources, per_expert, *refs):
+def route_kernel(sources, per_expert, tokens_ref, counts_ref, rows_ref, gates_ref, tokens_out, g_out):
+    tokens_out[...] = tokens_ref[...]
+    g = token_gates(
+        lax.axis_index("exp"), sources, per_expert, tokens_ref.shape[0], counts_ref, rows_ref, gates_ref
+    )
+    g_out[...] = jnp.broadcast_to(g, g_out.shape)
+
+
+def route(tokens, block_counts, block_rows, row_gates, sources, per_expert):
+    return pl.pallas_call(
+        functools.partial(route_kernel, sources, per_expert),
+        out_shape=(
+            jax.ShapeDtypeStruct(tokens.shape, tokens.dtype),
+            jax.ShapeDtypeStruct((sources * tokens.shape[0], 128), jnp.float32),
+        ),
+        in_specs=[VMEM, SMEM, VMEM, VMEM],
+        out_specs=(VMEM, VMEM),
+        compiler_params=pltpu.CompilerParams(vmem_limit_bytes=2 * MIB),
+        cost_estimate=pl.CostEstimate(flops=AHEAD, bytes_accessed=0, transcendentals=0),
+    )(tokens, block_counts, block_rows, row_gates)
+
+
+def hidden_kernel(sources, *refs):
     pieces = refs[:sources]
-    (wg_ref, wu_ref, wd_ref, counts_ref, rows_ref, gates_ref, h_out, g_out, wd_out, wide, x_ref, sems) = refs[sources:]
-    copies = chunk_copies(wd_ref, wd_out, sems)
-    for c in copies:
-        c.start()
+    wg_ref, wu_ref, h_out, wide, x_ref = refs[sources:]
     token_count = pieces[0].shape[0]
     for k, piece in enumerate(pieces):
         wide[pl.ds(k * token_count, token_count), :] = piece[...].astype(jnp.float32)
     x_ref[...] = wide[...].astype(jnp.bfloat16)
-    own = lax.axis_index("exp")
-    g = token_gates(own, sources, per_expert, token_count, counts_ref, rows_ref, gates_ref)
-    g_out[...] = jnp.broadcast_to(g, g_out.shape)
 
     @pl.loop(0, wg_ref.shape[1] // TILE)
     def _(n):
@@ -86,37 +69,25 @@
         up = jnp.dot(x_ref[...], wu_ref[:, cols], preferred_element_type=jnp.float32)
         h_out[:, cols] = (gate / (1.0 + jnp.exp(-gate)) * up).astype(jnp.bfloat16)
 
-    for c in copies:
-        c.wait()
-
-
-def hidden_rows(pieces, wg, wu, w_down, block_counts, block_rows, row_gates, per_expert):
+
+def hidden_rows(pieces, wg, wu):
     sources = len(pieces)
     total = sources * pieces[0].shape[0]
     depth, width = wg.shape
     return pl.pallas_call(
-        functools.partial(hidden_kernel, sources, per_expert),
-        out_shape=(
-            pltpu.VMEM((total, width), jnp.bfloat16),
-            pltpu.VMEM((total, 128), jnp.float32),
-            pltpu.VMEM(w_down.shape, w_down.dtype),
-        ),
-        in_specs=[VMEM] * sources + [VMEM, VMEM, HBM, SMEM, VMEM, VMEM],
-        out_specs=(VMEM, VMEM, VMEM),
+        functools.partial(hidden_kernel, sources),
+        out_shape=jax.ShapeDtypeStruct((total, width), jnp.bfloat16),
+        in_specs=[VMEM] * (sources + 2),
+        out_specs=VMEM,
         scratch_shapes=[
             pltpu.VMEM((total, depth), jnp.float32),
             pltpu.VMEM((total, depth), jnp.bfloat16),
-            pltpu.SemaphoreType.DMA((CHUNKS,)),
         ],
         compiler_params=pltpu.CompilerParams(vmem_limit_bytes=2 * MIB),
         cost_estimate=pl.CostEstimate(
-            flops=4 * total * depth * width, bytes_accessed=2 * w_down.size, transcendentals=total * width
+            flops=4 * total * depth * width, bytes_accessed=0, transcendentals=total * width
         ),
-    )(*pieces, in_vmem(wg), in_vmem(wu), in_hbm(w_down), block_counts, block_rows, row_gates)
-
-
-def in_hbm(x):
-    return pltpu.with_memory_space_constraint(x, pltpu.HBM)
+    )(*pieces, in_vmem(wg), in_vmem(wu))
 
 
 def in_vmem(x):
@@ -143,7 +114,7 @@
         out_specs=VMEM,
         compiler_params=pltpu.CompilerParams(vmem_limit_bytes=2 * MIB),
         cost_estimate=pl.CostEstimate(flops=2 * rows * depth * half, bytes_accessed=0, transcendentals=0),
-    )(in_vmem(hidden), in_vmem(g), in_vmem(wd))
+    )(hidden, g, in_vmem(wd))
 
 
 def merge_kernel(keep_ref, got_ref, own_ref, *out_refs):
@@ -191,11 +162,11 @@
 def local(tokens, w_gate, w_up, w_down, block_counts, block_rows, row_gates):
     sources = lax.axis_size("exp")
     per_expert = sources // block_rows.shape[0]
+    tokens, g = route(tokens, block_counts, block_rows, row_gates, sources, per_expert)
     pieces = [tokens] + [shifted(tokens, k, sources) for k in range(1, sources)]
-    wg, wu = fetch(w_gate, w_up)
-    hidden, g, wd = hidden_rows(pieces, wg, wu, w_down, block_counts, block_rows, row_gates, per_expert)
-    send = down_half(hidden, g, wd, True, jnp.bfloat16)
-    keep = down_half(hidden, g, wd, False, jnp.float32)
+    hidden = hidden_rows(pieces, w_gate, w_up)
+    send = down_half(hidden, g, w_down, True, jnp.bfloat16)
+    keep = down_half(hidden, g, w_down, False, jnp.float32)
     got = lax.ppermute(send, "hid", [(0, 1), (1, 0)])
     own, *outgoing = merge(keep, got, sources)
     returned = [shifted(piece, -(k + 1), sources) for k, piece in enumerate(outgoing)]

time: 63.2 us -> 47.9 us (0.76)
  Pallas kernels: 22.2 us -> 10.7 us
  local copies, waits for them, and re-layouts: 11.5 us -> 4.88 us
  waiting for transfers between devices: 6.42 us -> 9.98 us
  starting transfers between devices: 22.8 us -> 22.1 us
    pallas_call x2, Pallas kernels: 18.4 us -> 6.94 us  [the longest x1 6.3 us: hidden_rows(): pl.pallas_call(functools.partial(hidden_kernel, sources), out_shape=jax.S...]
    unnamed x12 -> x20, local copies, waits for them, and re-layouts: 11.5 us -> 4.88 us
    ppermute x14, waiting for transfers between devices: 6.4 us -> 9.96 us  [shifted(): lax.ppermute(x, 'exp', [(i, (i + k) % sources) for i in range(sources)])]
    ppermute x14, starting transfers between devices: 22.8 us -> 22.1 us  [shifted(): lax.ppermute(x, 'exp', [(i, (i + k) % sources) for i in range(sources)])]
  transfers between devices with their start and end apart: 15 -> 15, of which waited for: 3 -> 5; matrix products, arithmetic and copies ran while one was open for 0% -> 0% of each run, Pallas kernels for 20% -> 3%
where the time goes in v2:
time: 47.9 us; the launch traced here: 47.8 us
  starting transfers between devices  22.1 us (46%)
  Pallas kernels  10.7 us (22%)
  waiting for transfers between devices  9.98 us (21%)
  local copies, waits for them, and re-layouts  4.88 us (10%)
    ppermute x14, starting transfers between devices, shifted(): lax.ppermute(x, 'exp', [(i, (i + k) % sources) for i in range(sources)])  22.1 us
    ppermute x14, waiting for transfers between devices, shifted(): lax.ppermute(x, 'exp', [(i, (i + k) % sources) for i in range(sources)])  9.96 us
    pallas_call x1, Pallas kernels, hidden_rows(): pl.pallas_call(functools.partial(hidden_kernel, sources), out_shape=jax.S...  6.3 us
    unnamed x20, local copies, waits for them, and re-layouts  4.88 us
    pallas_call x2, Pallas kernels, down_half(): pl.pallas_call(functools.partial(down_kernel, other), out_shape=jax.Shape...  3.13 us
  transfers between devices with their start and end apart: 15, of which 5 were waited for; matrix products, arithmetic and copies ran while one was open for 0% of the time, Pallas kernels for 3%

profile of v2, /device:TPU:0, one launch (start us, length us, event | category | flops | bytes accessed | tf_op | source)
XLA Modules:
  0.0 47.8 jit_solution(6091129472403429508)
XLA Ops:
  0.0 0.0 copy-start.1
  0.0 0.0 copy-start
  0.0 0.0 copy-start.2
  0.0 0.9 %copy-done.2 = bf16[4,4096]{1,0:T(4,128)(2,1)S(1)} copy-done((bf16[4,4096]{1,0:T(4,128)(2,1)S(1)}, bf16[4,4096]{1,0:T(4,128)(2,1)}, u32[]{:S(2)}) %copy-start.2) | copy-done | bytes 32792
  0.9 0.0 copy-start.3
  0.9 1.1 %copy-done.3 = s32[4,128]{1,0:T(4,128)S(1)} copy-done((s32[4,128]{1,0:T(4,128)S(1)}, s32[4,128]{1,0:T(4,128)}, u32[]{:S(2)}) %copy-start.3) | copy-done | bytes 2072
  2.0 0.0 copy-start.4
  2.0 1.4 %copy-done.4 = f32[4,128]{1,0:T(4,128)S(1)} copy-done((f32[4,128]{1,0:T(4,128)S(1)}, f32[4,128]{1,0:T(4,128)}, u32[]{:S(2)}) %copy-start.4) | copy-done | bytes 2072
  3.4 0.0 copy-start.5
  3.4 1.4 %copy-done.5 = s32[4]{0:T(128)S(1)} copy-done((s32[4]{0:T(128)S(1)}, s32[4]{0:T(128)}, u32[]{:S(2)}) %copy-start.5) | copy-done | bytes 40
  4.9 0.6 %shard_map.73 = (bf16[4,4096]{1,0:T(4,128)(2,1)S(1)}, f32[32,128]{1,0:T(8,128)S(1)}) custom-call(bf16[4,4096]{1,0:T(4,128)(2,1)S(1)} %copy-done.2, s32[4]{0:T(128)S(1)} %copy-done.5, s32[4,128]{1,0:T(4,128)S(1)} %copy-done.3, f32[4,128]{1,0:T(4,128)S(1)} %copy-done.4), custom_call_target="tpu_custom_call" | custom-call | flops 20000000000 | tf_op jit(solution)/shard_map/pallas_call | solution.py:44
  5.5 0.0 slice-start
  5.5 0.0 slice-start.1
  5.5 0.0 slice-start.2
  5.5 0.0 slice-start.3
  5.5 6.0 %collective-permute-start.6 = (bf16[4,4096]{1,0:T(4,128)(2,1)S(1)}, bf16[4,4096]{1,0:T(4,128)(2,1)S(1)}, u32[]{:S(2)}, u32[]{:S(2)}) collective-permute-start(bf16[4,4096]{1,0:T(4,128)(2,1)S(1)} %get-tuple-element.15.refs_0_), channel_id=1, source_target_pairs={{0,14},{2,0},{4,2},{6,4},{8,6},{10,8},{12,10},{14,12},{1,15},{3,1}... | collective-permute-start | bytes 98312 | tf_op jit(solution)/shard_map/ppermute | solution.py:159
  11.6 0.4 collective-permute-start.5
  12.0 0.0 collective-permute-start.4
  12.0 3.0 %collective-permute-start.3 = (bf16[4,4096]{1,0:T(4,128)(2,1)S(1)}, bf16[4,4096]{1,0:T(4,128)(2,1)S(1)}, u32[]{:S(2)}, u32[]{:S(2)}) collective-permute-start(bf16[4,4096]{1,0:T(4,128)(2,1)S(1)} %get-tuple-element.15.refs_0_), channel_id=1, source_target_pairs={{0,8},{2,10},{4,12},{6,14},{8,0},{10,2},{12,4},{14,6},{1,9},{3,11}... | collective-permute-start | bytes 98312 | tf_op jit(solution)/shard_map/ppermute | solution.py:159
  15.0 0.0 collective-permute-start.2
  15.0 0.0 collective-permute-done.6.refs_7_
  15.0 1.8 %collective-permute-start.1 = (bf16[4,4096]{1,0:T(4,128)(2,1)S(1)}, bf16[4,4096]{1,0:T(4,128)(2,1)S(1)}, u32[]{:S(2)}, u32[]{:S(2)}) collective-permute-start(bf16[4,4096]{1,0:T(4,128)(2,1)S(1)} %get-tuple-element.15.refs_0_), channel_id=1, source_target_pairs={{0,4},{2,6},{4,8},{6,10},{8,12},{10,14},{12,0},{14,2},{1,5},{3,7},... | collective-permute-start | bytes 98312 | tf_op jit(solution)/shard_map/ppermute | solution.py:159
  16.8 0.0 collective-permute-done.5.refs_6_
  16.8 1.1 %collective-permute-start = (bf16[4,4096]{1,0:T(4,128)(2,1)S(1)}, bf16[4,4096]{1,0:T(4,128)(2,1)S(1)}, u32[]{:S(2)}, u32[]{:S(2)}) collective-permute-start(bf16[4,4096]{1,0:T(4,128)(2,1)S(1)} %get-tuple-element.15.refs_0_), channel_id=1, source_target_pairs={{0,2},{2,4},{4,6},{6,8},{8,10},{10,12},{12,14},{14,0},{1,3},{3,5},... | collective-permute-start | bytes 98312 | tf_op jit(solution)/shard_map/ppermute | solution.py:159
  18.0 0.0 collective-permute-done.4.refs_5_
  18.0 0.0 collective-permute-done.3.refs_4_
  18.0 3.0 %collective-permute-done.2.refs_3_ = bf16[4,4096]{1,0:T(4,128)(2,1)S(1)} collective-permute-done((bf16[4,4096]{1,0:T(4,128)(2,1)S(1)}, bf16[4,4096]{1,0:T(4,128)(2,1)S(1)}, u32[]{:S(2)}, u32[]{:S(2)}) %collective-permute-start.2) | collective-permute-done | bytes 32800 | tf_op jit(solution)/shard_map/ppermute | solution.py:159
  21.0 1.0 %collective-permute-done.1.refs_2_ = bf16[4,4096]{1,0:T(4,128)(2,1)S(1)} collective-permute-done((bf16[4,4096]{1,0:T(4,128)(2,1)S(1)}, bf16[4,4096]{1,0:T(4,128)(2,1)S(1)}, u32[]{:S(2)}, u32[]{:S(2)}) %collective-permute-start.1) | collective-permute-done | bytes 32800 | tf_op jit(solution)/shard_map/ppermute | solution.py:159
  22.0 1.5 %collective-permute-done.refs_1_ = bf16[4,4096]{1,0:T(4,128)(2,1)S(1)} collective-permute-done((bf16[4,4096]{1,0:T(4,128)(2,1)S(1)}, bf16[4,4096]{1,0:T(4,128)(2,1)S(1)}, u32[]{:S(2)}, u32[]{:S(2)}) %collective-permute-start) | collective-permute-done | bytes 32800 | tf_op jit(solution)/shard_map/ppermute | solution.py:159
  23.5 0.0 copy-done.1
  23.5 0.0 copy-done
  23.5 6.3 %shard_map.74.h_ref = bf16[32,2048]{1,0:T(8,128)(2,1)S(1)} custom-call(bf16[4,4096]{1,0:T(4,128)(2,1)S(1)} %get-tuple-element.15.refs_0_, bf16[4,4096]{1,0:T(4,128)(2,1)S(1)} %collective-permute-done.refs_1_, bf16[4,4096]{1,0:T(4,128)(2,1)S(1)} %collective-permute-done.1.refs_2_, bf16[4,4096]{1,0:T(4,128)(2,1)S(1)} %collective-permute-done.2.refs_3_, ...), custom_call_target="tpu_custom_call" | custom-call | flops 1073741824 | tf_op jit(solution)/shard_map/pallas_call | solution.py:77
  29.8 0.0 slice-done
  29.8 0.0 slice-done.1
  29.8 0.0 slice-done.2
  29.8 0.0 slice-done.3
  29.8 1.6 %shard_map.76 = bf16[32,2048]{1,0:T(8,128)(2,1)S(1)} custom-call(bf16[32,2048]{1,0:T(8,128)(2,1)S(1)} %shard_map.74.h_ref, f32[32,128]{1,0:T(8,128)S(1)} %get-tuple-element.16.g_ref, bf16[2048,4096]{1,0:T(8,128)(2,1)S(1)} %bitcast.1), custom_call_target="tpu_custom_call" | custom-call | flops 268435456 | tf_op jit(solution)/shard_map/pallas_call | solution.py:110
  31.4 0.0 collective-permute-start.7
  31.4 1.6 %shard_map.75.keep_ref = f32[32,2048]{1,0:T(8,128)S(1)} custom-call(bf16[32,2048]{1,0:T(8,128)(2,1)S(1)} %shard_map.74.h_ref, f32[32,128]{1,0:T(8,128)S(1)} %get-tuple-element.16.g_ref, bf16[2048,4096]{1,0:T(8,128)(2,1)S(1)} %bitcast.1), custom_call_target="tpu_custom_call" | custom-call | flops 268435456 | tf_op jit(solution)/shard_map/pallas_call | solution.py:110
  33.0 0.0 collective-permute-done.7.got_ref
  33.0 0.3 collective-permute-start.8
  33.3 1.5 %collective-permute-start.9 = (bf16[4,2048]{1,0:T(4,128)(2,1)S(1)}, bf16[4,2048]{1,0:T(4,128)(2,1)S(1)}, u32[]{:S(2)}, u32[]{:S(2)}) collective-permute-start(bf16[4,2048]{1,0:T(4,128)(2,1)S(1)} %get-tuple-element.19), channel_id=1, source_target_pairs={{0,12},{2,14},{4,0},{6,2},{8,4},{10,6},{12,8},{14,10},{1,13},{3,15... | collective-permute-start | bytes 49160 | tf_op jit(solution)/shard_map/ppermute | solution.py:159
  34.8 1.5 %collective-permute-start.10 = (bf16[4,2048]{1,0:T(4,128)(2,1)S(1)}, bf16[4,2048]{1,0:T(4,128)(2,1)S(1)}, u32[]{:S(2)}, u32[]{:S(2)}) collective-permute-start(bf16[4,2048]{1,0:T(4,128)(2,1)S(1)} %get-tuple-element.20), channel_id=1, source_target_pairs={{0,10},{2,12},{4,14},{6,0},{8,2},{10,4},{12,6},{14,8},{1,11},{3,13... | collective-permute-start | bytes 49160 | tf_op jit(solution)/shard_map/ppermute | solution.py:159
  36.2 2.4 %collective-permute-start.11 = (bf16[4,2048]{1,0:T(4,128)(2,1)S(1)}, bf16[4,2048]{1,0:T(4,128)(2,1)S(1)}, u32[]{:S(2)}, u32[]{:S(2)}) collective-permute-start(bf16[4,2048]{1,0:T(4,128)(2,1)S(1)} %get-tuple-element.21), channel_id=1, source_target_pairs={{0,8},{2,10},{4,12},{6,14},{8,0},{10,2},{12,4},{14,6},{1,9},{3,11}... | collective-permute-start | bytes 49160 | tf_op jit(solution)/shard_map/ppermute | solution.py:159
  38.6 0.0 collective-permute-start.12
  38.6 0.0 collective-permute-done.8.refs_0_
  38.7 2.0 %collective-permute-start.13 = (bf16[4,2048]{1,0:T(4,128)(2,1)S(1)}, bf16[4,2048]{1,0:T(4,128)(2,1)S(1)}, u32[]{:S(2)}, u32[]{:S(2)}) collective-permute-start(bf16[4,2048]{1,0:T(4,128)(2,1)S(1)} %get-tuple-element.23), channel_id=1, source_target_pairs={{0,4},{2,6},{4,8},{6,10},{8,12},{10,14},{12,0},{14,2},{1,5},{3,7},... | collective-permute-start | bytes 49160 | tf_op jit(solution)/shard_map/ppermute | solution.py:159
  40.7 0.0 collective-permute-done.9.refs_1_
  40.7 2.0 %collective-permute-start.14 = (bf16[4,2048]{1,0:T(4,128)(2,1)S(1)}, bf16[4,2048]{1,0:T(4,128)(2,1)S(1)}, u32[]{:S(2)}, u32[]{:S(2)}) collective-permute-start(bf16[4,2048]{1,0:T(4,128)(2,1)S(1)} %get-tuple-element.24), channel_id=1, source_target_pairs={{0,2},{2,4},{4,6},{6,8},{8,10},{10,12},{12,14},{14,0},{1,3},{3,5},... | collective-permute-start | bytes 49160 | tf_op jit(solution)/shard_map/ppermute | solution.py:159
  42.6 0.0 collective-permute-done.10.refs_2_
  42.7 0.0 collective-permute-done.11.refs_3_
  42.7 1.5 %collective-permute-done.12.refs_4_ = bf16[4,2048]{1,0:T(4,128)(2,1)S(1)} collective-permute-done((bf16[4,2048]{1,0:T(4,128)(2,1)S(1)}, bf16[4,2048]{1,0:T(4,128)(2,1)S(1)}, u32[]{:S(2)}, u32[]{:S(2)}) %collective-permute-start.12) | collective-permute-done | bytes 16416 | tf_op jit(solution)/shard_map/ppermute | solution.py:159
  44.2 0.0 collective-permute-done.13.refs_5_
  44.2 2.9 %collective-permute-done.14.refs_6_ = bf16[4,2048]{1,0:T(4,128)(2,1)S(1)} collective-permute-done((bf16[4,2048]{1,0:T(4,128)(2,1)S(1)}, bf16[4,2048]{1,0:T(4,128)(2,1)S(1)}, u32[]{:S(2)}, u32[]{:S(2)}) %collective-permute-start.14) | collective-permute-done | bytes 16416 | tf_op jit(solution)/shard_map/ppermute | solution.py:159
  47.1 0.6 %shard_map.78 = bf16[4,2048]{1,0:T(4,128)(2,1)} custom-call(f32[4,2048]{1,0:T(4,128)S(1)} %get-tuple-element.17.own_ref, bf16[4,2048]{1,0:T(4,128)(2,1)S(1)} %collective-permute-done.8.refs_0_, bf16[4,2048]{1,0:T(4,128)(2,1)S(1)} %collective-permute-done.9.refs_1_, bf16[4,2048]{1,0:T(4,128)(2,1)S(1)} %collective-permute-done.10.refs_2_, ...), custom_call_target="tpu_custom_call" | custom-call | tf_op jit(solution)/shard_map/pallas_call | solution.py:149
  (2 shorter events, 0.0 us)
Async XLA Ops:
  0.0 23.5 %copy-start.1 = (bf16[4096,2048]{1,0:T(8,128)(2,1)S(1)}, bf16[4096,2048]{1,0:T(8,128)(2,1)}, u32[]{:S(2)}) copy-start(bf16[4096,2048]{1,0:T(8,128)(2,1)} %refs_9_.1) | copy-start | bytes 50331652
  0.0 23.5 %copy-start = (bf16[4096,2048]{1,0:T(8,128)(2,1)S(1)}, bf16[4096,2048]{1,0:T(8,128)(2,1)}, u32[]{:S(2)}) copy-start(bf16[4096,2048]{1,0:T(8,128)(2,1)} %refs_8_.1) | copy-start | bytes 50331652
  0.0 0.9 %copy-start.2 = (bf16[4,4096]{1,0:T(4,128)(2,1)S(1)}, bf16[4,4096]{1,0:T(4,128)(2,1)}, u32[]{:S(2)}) copy-start(bf16[4,4096]{1,0:T(4,128)(2,1)} %tokens_ref.1) | copy-start | bytes 98308
  0.9 1.1 %copy-start.3 = (s32[4,128]{1,0:T(4,128)S(1)}, s32[4,128]{1,0:T(4,128)}, u32[]{:S(2)}) copy-start(s32[4,128]{1,0:T(4,128)} %rows_ref.1) | copy-start | bytes 6148
  2.0 1.5 %copy-start.4 = (f32[4,128]{1,0:T(4,128)S(1)}, f32[4,128]{1,0:T(4,128)}, u32[]{:S(2)}) copy-start(f32[4,128]{1,0:T(4,128)} %gates_ref.1) | copy-start | bytes 6148
  3.4 1.4 %copy-start.5 = (s32[4]{0:T(128)S(1)}, s32[4]{0:T(128)}, u32[]{:S(2)}) copy-start(s32[4]{0:T(128)} %counts_ref.1) | copy-start | bytes 52
  5.5 24.3 %slice-start = ((s8[16777216]{0:T(1024)(128)(4,1)}), s8[4194304]{0:T(1024)(128)(4,1)S(1)}, s32[]{:S(2)}) async-start(s8[16777216]{0:T(1024)(128)(4,1)} %bitcast), calls=%async_computation | async-start | bytes 8388608
  5.5 24.3 %slice-start.1 = ((s8[16777216]{0:T(1024)(128)(4,1)}), s8[4194304]{0:T(1024)(128)(4,1)S(1)}, s32[]{:S(2)}) async-start(s8[16777216]{0:T(1024)(128)(4,1)} %bitcast), calls=%async_computation.1 | async-start | bytes 8388608
  5.5 24.3 %slice-start.2 = ((s8[16777216]{0:T(1024)(128)(4,1)}), s8[4194304]{0:T(1024)(128)(4,1)S(1)}, s32[]{:S(2)}) async-start(s8[16777216]{0:T(1024)(128)(4,1)} %bitcast), calls=%async_computation.2 | async-start | bytes 8388608
  5.5 24.3 %slice-start.3 = ((s8[16777216]{0:T(1024)(128)(4,1)}), s8[4194304]{0:T(1024)(128)(4,1)S(1)}, s32[]{:S(2)}) async-start(s8[16777216]{0:T(1024)(128)(4,1)} %bitcast), calls=%async_computation.3 | async-start | bytes 8388608
  5.5 9.5 %collective-permute-start.6 = (bf16[4,4096]{1,0:T(4,128)(2,1)S(1)}, bf16[4,4096]{1,0:T(4,128)(2,1)S(1)}, u32[]{:S(2)}, u32[]{:S(2)}) collective-permute-start(bf16[4,4096]{1,0:T(4,128)(2,1)S(1)} %get-tuple-element.15.refs_0_), channel_id=1, source_target_pairs={{0,14},{2,0},{4,2},{6,4},{8,6},{10,8},{12,10},{14,12},{1,15},{3,1}... | collective-permute-start | bytes 98312 | tf_op jit(solution)/shard_map/ppermute | solution.py:159
  11.6 5.3 %collective-permute-start.5 = (bf16[4,4096]{1,0:T(4,128)(2,1)S(1)}, bf16[4,4096]{1,0:T(4,128)(2,1)S(1)}, u32[]{:S(2)}, u32[]{:S(2)}) collective-permute-start(bf16[4,4096]{1,0:T(4,128)(2,1)S(1)} %get-tuple-element.15.refs_0_), channel_id=1, source_target_pairs={{0,12},{2,14},{4,0},{6,2},{8,4},{10,6},{12,8},{14,10},{1,13},{3,15... | collective-permute-start | bytes 98312 | tf_op jit(solution)/shard_map/ppermute | solution.py:159
  12.0 6.0 %collective-permute-start.4 = (bf16[4,4096]{1,0:T(4,128)(2,1)S(1)}, bf16[4,4096]{1,0:T(4,128)(2,1)S(1)}, u32[]{:S(2)}, u32[]{:S(2)}) collective-permute-start(bf16[4,4096]{1,0:T(4,128)(2,1)S(1)} %get-tuple-element.15.refs_0_), channel_id=1, source_target_pairs={{0,10},{2,12},{4,14},{6,0},{8,2},{10,4},{12,6},{14,8},{1,11},{3,13... | collective-permute-start | bytes 98312 | tf_op jit(solution)/shard_map/ppermute | solution.py:159
  12.0 6.0 %collective-permute-start.3 = (bf16[4,4096]{1,0:T(4,128)(2,1)S(1)}, bf16[4,4096]{1,0:T(4,128)(2,1)S(1)}, u32[]{:S(2)}, u32[]{:S(2)}) collective-permute-start(bf16[4,4096]{1,0:T(4,128)(2,1)S(1)} %get-tuple-element.15.refs_0_), channel_id=1, source_target_pairs={{0,8},{2,10},{4,12},{6,14},{8,0},{10,2},{12,4},{14,6},{1,9},{3,11}... | collective-permute-start | bytes 98312 | tf_op jit(solution)/shard_map/ppermute | solution.py:159
  15.0 6.0 %collective-permute-start.2 = (bf16[4,4096]{1,0:T(4,128)(2,1)S(1)}, bf16[4,4096]{1,0:T(4,128)(2,1)S(1)}, u32[]{:S(2)}, u32[]{:S(2)}) collective-permute-start(bf16[4,4096]{1,0:T(4,128)(2,1)S(1)} %get-tuple-element.15.refs_0_), channel_id=1, source_target_pairs={{0,6},{2,8},{4,10},{6,12},{8,14},{10,0},{12,2},{14,4},{1,7},{3,9},... | collective-permute-start | bytes 98312 | tf_op jit(solution)/shard_map/ppermute | solution.py:159
  15.0 7.0 %collective-permute-start.1 = (bf16[4,4096]{1,0:T(4,128)(2,1)S(1)}, bf16[4,4096]{1,0:T(4,128)(2,1)S(1)}, u32[]{:S(2)}, u32[]{:S(2)}) collective-permute-start(bf16[4,4096]{1,0:T(4,128)(2,1)S(1)} %get-tuple-element.15.refs_0_), channel_id=1, source_target_pairs={{0,4},{2,6},{4,8},{6,10},{8,12},{10,14},{12,0},{14,2},{1,5},{3,7},... | collective-permute-start | bytes 98312 | tf_op jit(solution)/shard_map/ppermute | solution.py:159
  16.8 6.6 %collective-permute-start = (bf16[4,4096]{1,0:T(4,128)(2,1)S(1)}, bf16[4,4096]{1,0:T(4,128)(2,1)S(1)}, u32[]{:S(2)}, u32[]{:S(2)}) collective-permute-start(bf16[4,4096]{1,0:T(4,128)(2,1)S(1)} %get-tuple-element.15.refs_0_), channel_id=1, source_target_pairs={{0,2},{2,4},{4,6},{6,8},{8,10},{10,12},{12,14},{14,0},{1,3},{3,5},... | collective-permute-start | bytes 98312 | tf_op jit(solution)/shard_map/ppermute | solution.py:159
  31.4 1.6 %collective-permute-start.7 = (bf16[32,2048]{1,0:T(8,128)(2,1)S(1)}, bf16[32,2048]{1,0:T(8,128)(2,1)S(1)}, u32[]{:S(2)}, u32[]{:S(2)}) collective-permute-start(bf16[32,2048]{1,0:T(8,128)(2,1)S(1)} %shard_map.76), channel_id=1, source_target_pairs={{0,1},{1,0},{2,3},{3,2},{4,5},{5,4},{6,7},{7,6},{8,9},{9,8},{10,11... | collective-permute-start | bytes 393224 | tf_op jit(solution)/shard_map/ppermute | solution.py:170
  33.0 5.6 %collective-permute-start.8 = (bf16[4,2048]{1,0:T(4,128)(2,1)S(1)}, bf16[4,2048]{1,0:T(4,128)(2,1)S(1)}, u32[]{:S(2)}, u32[]{:S(2)}) collective-permute-start(bf16[4,2048]{1,0:T(4,128)(2,1)S(1)} %get-tuple-element.18), channel_id=1, source_target_pairs={{0,14},{2,0},{4,2},{6,4},{8,6},{10,8},{12,10},{14,12},{1,15},{3,1}... | collective-permute-start | bytes 49160 | tf_op jit(solution)/shard_map/ppermute | solution.py:159
  33.3 7.4 %collective-permute-start.9 = (bf16[4,2048]{1,0:T(4,128)(2,1)S(1)}, bf16[4,2048]{1,0:T(4,128)(2,1)S(1)}, u32[]{:S(2)}, u32[]{:S(2)}) collective-permute-start(bf16[4,2048]{1,0:T(4,128)(2,1)S(1)} %get-tuple-element.19), channel_id=1, source_target_pairs={{0,12},{2,14},{4,0},{6,2},{8,4},{10,6},{12,8},{14,10},{1,13},{3,15... | collective-permute-start | bytes 49160 | tf_op jit(solution)/shard_map/ppermute | solution.py:159
  34.8 7.9 %collective-permute-start.10 = (bf16[4,2048]{1,0:T(4,128)(2,1)S(1)}, bf16[4,2048]{1,0:T(4,128)(2,1)S(1)}, u32[]{:S(2)}, u32[]{:S(2)}) collective-permute-start(bf16[4,2048]{1,0:T(4,128)(2,1)S(1)} %get-tuple-element.20), channel_id=1, source_target_pairs={{0,10},{2,12},{4,14},{6,0},{8,2},{10,4},{12,6},{14,8},{1,11},{3,13... | collective-permute-start | bytes 49160 | tf_op jit(solution)/shard_map/ppermute | solution.py:159
  36.2 6.4 %collective-permute-start.11 = (bf16[4,2048]{1,0:T(4,128)(2,1)S(1)}, bf16[4,2048]{1,0:T(4,128)(2,1)S(1)}, u32[]{:S(2)}, u32[]{:S(2)}) collective-permute-start(bf16[4,2048]{1,0:T(4,128)(2,1)S(1)} %get-tuple-element.21), channel_id=1, source_target_pairs={{0,8},{2,10},{4,12},{6,14},{8,0},{10,2},{12,4},{14,6},{1,9},{3,11}... | collective-permute-start | bytes 49160 | tf_op jit(solution)/shard_map/ppermute | solution.py:159
  38.6 5.5 %collective-permute-start.12 = (bf16[4,2048]{1,0:T(4,128)(2,1)S(1)}, bf16[4,2048]{1,0:T(4,128)(2,1)S(1)}, u32[]{:S(2)}, u32[]{:S(2)}) collective-permute-start(bf16[4,2048]{1,0:T(4,128)(2,1)S(1)} %get-tuple-element.22), channel_id=1, source_target_pairs={{0,6},{2,8},{4,10},{6,12},{8,14},{10,0},{12,2},{14,4},{1,7},{3,9},... | collective-permute-start | bytes 49160 | tf_op jit(solution)/shard_map/ppermute | solution.py:159
  38.7 5.5 %collective-permute-start.13 = (bf16[4,2048]{1,0:T(4,128)(2,1)S(1)}, bf16[4,2048]{1,0:T(4,128)(2,1)S(1)}, u32[]{:S(2)}, u32[]{:S(2)}) collective-permute-start(bf16[4,2048]{1,0:T(4,128)(2,1)S(1)} %get-tuple-element.23), channel_id=1, source_target_pairs={{0,4},{2,6},{4,8},{6,10},{8,12},{10,14},{12,0},{14,2},{1,5},{3,7},... | collective-permute-start | bytes 49160 | tf_op jit(solution)/shard_map/ppermute | solution.py:159
  40.7 6.4 %collective-permute-start.14 = (bf16[4,2048]{1,0:T(4,128)(2,1)S(1)}, bf16[4,2048]{1,0:T(4,128)(2,1)S(1)}, u32[]{:S(2)}, u32[]{:S(2)}) collective-permute-start(bf16[4,2048]{1,0:T(4,128)(2,1)S(1)} %get-tuple-element.24), channel_id=1, source_target_pairs={{0,2},{2,4},{4,6},{6,8},{8,10},{10,12},{12,14},{14,0},{1,3},{3,5},... | collective-permute-start | bytes 49160 | tf_op jit(solution)/shard_map/ppermute | solution.py:159

commit v3 on v2

--- a/solution.py
+++ b/solution.py
@@ -12,46 +12,52 @@
 TILE = 512
 MIB = 1 << 20
 AHEAD = 20_000_000_000
+HBM = pl.BlockSpec(memory_space=pltpu.HBM)
 VMEM = pl.BlockSpec(memory_space=pltpu.VMEM)
 SMEM = pl.BlockSpec(memory_space=pltpu.SMEM)
 
 
-def token_gates(own, sources, per_expert, token_count, counts_ref, rows_ref, gates_ref):
+def pass_kernel(tokens_ref, out_ref, sem):
+    copy = pltpu.make_async_copy(tokens_ref, out_ref, sem)
+    copy.start()
+    copy.wait()
+
+
+def pass_on(tokens):
+    return pl.pallas_call(
+        pass_kernel,
+        out_shape=jax.ShapeDtypeStruct(tokens.shape, tokens.dtype),
+        in_specs=[HBM],
+        out_specs=VMEM,
+        scratch_shapes=[pltpu.SemaphoreType.DMA],
+        compiler_params=pltpu.CompilerParams(vmem_limit_bytes=2 * MIB),
+        cost_estimate=pl.CostEstimate(flops=AHEAD, bytes_accessed=0, transcendentals=0),
+    )(pltpu.with_memory_space_constraint(tokens, pltpu.HBM))
+
+
+def route_kernel(count, per_expert, counts_ref, rows_ref, gates_ref, out_ref):
     experts, slots = rows_ref.shape
-    expert = own // per_expert
-    mine = lax.broadcasted_iota(jnp.int32, (experts, slots), 0) == expert
-    rows = jnp.sum(jnp.where(mine, rows_ref[...], 0), axis=0, keepdims=True)
-    gates = jnp.sum(jnp.where(mine, gates_ref[...], 0.0), axis=0, keepdims=True)
-    position = lax.broadcasted_iota(jnp.int32, (1, slots), 1)
-    live = (position < counts_ref[expert] * BLOCK) & (rows >= 0)
-    rows = jnp.where(live, rows, -1)
-    total = sources * token_count
+    total = out_ref.shape[0]
     line = lax.broadcasted_iota(jnp.int32, (total, slots), 0)
-    start = lax.rem(own - line // token_count + sources, sources) * token_count
-    token = start + lax.rem(line, token_count)
-    return jnp.sum(jnp.where(rows == token, gates, 0.0), axis=1, keepdims=True)
-
-
-def route_kernel(sources, per_expert, tokens_ref, counts_ref, rows_ref, gates_ref, tokens_out, g_out):
-    tokens_out[...] = tokens_ref[...]
-    g = token_gates(
-        lax.axis_index("exp"), sources, per_expert, tokens_ref.shape[0], counts_ref, rows_ref, gates_ref
-    )
-    g_out[...] = jnp.broadcast_to(g, g_out.shape)
-
-
-def route(tokens, block_counts, block_rows, row_gates, sources, per_expert):
-    return pl.pallas_call(
-        functools.partial(route_kernel, sources, per_expert),
-        out_shape=(
-            jax.ShapeDtypeStruct(tokens.shape, tokens.dtype),
-            jax.ShapeDtypeStruct((sources * tokens.shape[0], 128), jnp.float32),
-        ),
-        in_specs=[VMEM, SMEM, VMEM, VMEM],
-        out_specs=(VMEM, VMEM),
-        compiler_params=pltpu.CompilerParams(vmem_limit_bytes=2 * MIB),
-        cost_estimate=pl.CostEstimate(flops=AHEAD, bytes_accessed=0, transcendentals=0),
-    )(tokens, block_counts, block_rows, row_gates)
+    position = lax.broadcasted_iota(jnp.int32, (total, slots), 1)
+    token = lax.axis_index("exp") * count + lax.rem(line, count)
+    expert = line // (count * per_expert)
+    found = jnp.zeros((total, slots), jnp.float32)
+    for e in range(experts):
+        rows = rows_ref[pl.ds(e, 1), :]
+        here = (expert == e) & (rows == token) & (position < counts_ref[e] * BLOCK)
+        found = jnp.where(here, gates_ref[pl.ds(e, 1), :], found)
+    out_ref[...] = jnp.broadcast_to(jnp.sum(found, axis=1, keepdims=True), out_ref.shape)
+
+
+def route(block_counts, block_rows, row_gates, sources, count):
+    return pl.pallas_call(
+        functools.partial(route_kernel, count, sources // block_rows.shape[0]),
+        out_shape=jax.ShapeDtypeStruct((sources * count, 128), jnp.float32),
+        in_specs=[SMEM, VMEM, VMEM],
+        out_specs=VMEM,
+        compiler_params=pltpu.CompilerParams(vmem_limit_bytes=2 * MIB),
+    )(block_counts, block_rows, row_gates)
 
 
 def hidden_kernel(sources, *refs):
@@ -94,65 +100,64 @@
     return pltpu.with_memory_space_constraint(x, pltpu.VMEM)
 
 
-def down_kernel(other, h_ref, g_ref, wd_ref, out_ref):
+def down_kernel(other, h_ref, wd_ref, out_ref):
     half = wd_ref.shape[1] // 2
     side = lax.axis_index("hid")
     base = (1 - side if other else side) * half
     for n in range(half // TILE):
         cols = pl.ds(pl.multiple_of(base + n * TILE, TILE), TILE)
         part = jnp.dot(h_ref[...], wd_ref[:, cols], preferred_element_type=jnp.float32)
-        out_ref[:, pl.ds(n * TILE, TILE)] = (part * g_ref[:, :1]).astype(out_ref.dtype)
-
-
-def down_half(hidden, g, wd, other, dtype):
+        out_ref[:, pl.ds(n * TILE, TILE)] = part.astype(out_ref.dtype)
+
+
+def down_half(hidden, wd, other, dtype):
     rows, depth = hidden.shape
     half = wd.shape[1] // 2
     return pl.pallas_call(
         functools.partial(down_kernel, other),
         out_shape=jax.ShapeDtypeStruct((rows, half), dtype),
-        in_specs=[VMEM, VMEM, VMEM],
+        in_specs=[VMEM, VMEM],
         out_specs=VMEM,
         compiler_params=pltpu.CompilerParams(vmem_limit_bytes=2 * MIB),
         cost_estimate=pl.CostEstimate(flops=2 * rows * depth * half, bytes_accessed=0, transcendentals=0),
-    )(hidden, g, in_vmem(wd))
-
-
-def merge_kernel(keep_ref, got_ref, own_ref, *out_refs):
-    both = keep_ref[...] + got_ref[...].astype(jnp.float32)
-    count = own_ref.shape[0]
-    own_ref[...] = both[:count]
-    for k, out_ref in enumerate(out_refs):
-        out_ref[...] = both[(k + 1) * count : (k + 2) * count].astype(out_ref.dtype)
+    )(hidden, in_vmem(wd))
+
+
+def merge_kernel(keep_ref, got_ref, out_ref):
+    sources, count, _ = out_ref.shape
+    own = lax.axis_index("exp")
+    both = (keep_ref[...] + got_ref[...].astype(jnp.float32)).astype(out_ref.dtype)
+    for k in range(sources):
+        out_ref[lax.rem(own - k + sources, sources)] = both[k * count : (k + 1) * count]
 
 
 def merge(keep, got, sources):
     rows, width = keep.shape
-    count = rows // sources
     return pl.pallas_call(
         merge_kernel,
-        out_shape=(jax.ShapeDtypeStruct((count, width), jnp.float32),)
-        + (jax.ShapeDtypeStruct((count, width), jnp.bfloat16),) * (sources - 1),
+        out_shape=jax.ShapeDtypeStruct((sources, rows // sources, width), jnp.bfloat16),
         in_specs=[VMEM, VMEM],
-        out_specs=(VMEM,) * sources,
+        out_specs=VMEM,
         compiler_params=pltpu.CompilerParams(vmem_limit_bytes=2 * MIB),
     )(keep, got)
 
 
-def sum_kernel(own_ref, *refs):
-    total = own_ref[...]
-    for ref in refs[:-1]:
-        total = total + ref[...].astype(jnp.float32)
-    refs[-1][...] = total.astype(jnp.bfloat16)
-
-
-def final_sum(own, got):
+def sum_kernel(got_ref, gates_ref, out_ref):
+    sources, count, _ = got_ref.shape
+    total = jnp.zeros(out_ref.shape, jnp.float32)
+    for s in range(sources):
+        total = total + got_ref[s].astype(jnp.float32) * gates_ref[pl.ds(s * count, count), :1]
+    out_ref[...] = total.astype(out_ref.dtype)
+
+
+def weighted_sum(got, gates):
     return pl.pallas_call(
         sum_kernel,
-        out_shape=jax.ShapeDtypeStruct(own.shape, jnp.bfloat16),
-        in_specs=[VMEM] * (1 + len(got)),
-        out_specs=VMEM,
-        compiler_params=pltpu.CompilerParams(vmem_limit_bytes=2 * MIB),
-    )(own, *got)
+        out_shape=jax.ShapeDtypeStruct(got.shape[1:], jnp.bfloat16),
+        in_specs=[VMEM, VMEM],
+        out_specs=VMEM,
+        compiler_params=pltpu.CompilerParams(vmem_limit_bytes=2 * MIB),
+    )(got, gates)
 
 
 def shifted(x, k, sources):
@@ -161,16 +166,16 @@
 
 def local(tokens, w_gate, w_up, w_down, block_counts, block_rows, row_gates):
     sources = lax.axis_size("exp")
-    per_expert = sources // block_rows.shape[0]
-    tokens, g = route(tokens, block_counts, block_rows, row_gates, sources, per_expert)
+    tokens = pass_on(tokens)
     pieces = [tokens] + [shifted(tokens, k, sources) for k in range(1, sources)]
     hidden = hidden_rows(pieces, w_gate, w_up)
-    send = down_half(hidden, g, w_down, True, jnp.bfloat16)
-    keep = down_half(hidden, g, w_down, False, jnp.float32)
+    send = down_half(hidden, w_down, True, jnp.bfloat16)
+    keep = down_half(hidden, w_down, False, jnp.float32)
     got = lax.ppermute(send, "hid", [(0, 1), (1, 0)])
-    own, *outgoing = merge(keep, got, sources)
-    returned = [shifted(piece, -(k + 1), sources) for k, piece in enumerate(outgoing)]
-    return final_sum(own, returned)
+    outgoing = merge(keep, got, sources)
+    returned = lax.all_to_all(outgoing, "exp", split_axis=0, concat_axis=0, tiled=True)
+    gates = route(block_counts, block_rows, row_gates, sources, tokens.shape[0])
+    return weighted_sum(returned, gates)
 
 
 def expert_block(segment, w_gate, w_up, w_down):

time: 47.9 us -> 41.5 us (0.87)
  local copies, waits for them, and re-layouts: 4.88 us -> 0.05 us
  starting transfers between devices: 22.1 us -> 19.2 us
  Pallas kernels: 10.7 us -> 12.4 us
  waiting for transfers between devices: 9.98 us -> 9.47 us
    ppermute x14 -> x7, starting transfers between devices: 22.1 us -> 13.8 us  [shifted(): lax.ppermute(x, 'exp', [(i, (i + k) % sources) for i in range(sources)])]
    ppermute x14 -> x7, waiting for transfers between devices: 9.96 us -> 2.48 us  [shifted(): lax.ppermute(x, 'exp', [(i, (i + k) % sources) for i in range(sources)])]
    all_to_all x0 -> x1, waiting for transfers between devices: none -> 6.99 us  [local(): lax.all_to_all(outgoing, 'exp', split_axis=0, concat_axis=0, tiled=True)]
    all_to_all x0 -> x1, starting transfers between devices: none -> 5.41 us  [local(): lax.all_to_all(outgoing, 'exp', split_axis=0, concat_axis=0, tiled=True)]
    unnamed x20 -> x18, local copies, waits for them, and re-layouts: 4.88 us -> 0.05 us
    pallas_call x3 -> x4, Pallas kernels: 1.31 us -> 2.96 us  [the longest x1 0.92 us: pass_on(): pl.pallas_call(pass_kernel, out_shape=jax.ShapeDtypeStruct(tokens.shape,...]
  transfers between devices with their start and end apart: 15 -> 9, of which waited for: 5 -> 3; matrix products, arithmetic and copies ran while one was open for 0% -> 0% of each run, Pallas kernels for 3% -> 5%
where the time goes in v3:
time: 41.5 us; the launch traced here: 41.2 us
  starting transfers between devices  19.2 us (46%)
  Pallas kernels  12.4 us (30%)
  waiting for transfers between devices  9.47 us (23%)
    ppermute x7, starting transfers between devices, shifted(): lax.ppermute(x, 'exp', [(i, (i + k) % sources) for i in range(sources)])  13.8 us
    all_to_all x1, waiting for transfers between devices, local(): lax.all_to_all(outgoing, 'exp', split_axis=0, concat_axis=0, tiled=True)  6.99 us
    pallas_call x1, Pallas kernels, hidden_rows(): pl.pallas_call(functools.partial(hidden_kernel, sources), out_shape=jax.S...  6.3 us
    all_to_all x1, starting transfers between devices, local(): lax.all_to_all(outgoing, 'exp', split_axis=0, concat_axis=0, tiled=True)  5.41 us
    pallas_call x2, Pallas kernels, down_half(): pl.pallas_call(functools.partial(down_kernel, other), out_shape=jax.Shape...  3.13 us
    ppermute x7, waiting for transfers between devices, shifted(): lax.ppermute(x, 'exp', [(i, (i + k) % sources) for i in range(sources)])  2.48 us
    pallas_call x1, Pallas kernels, pass_on(): pl.pallas_call(pass_kernel, out_shape=jax.ShapeDtypeStruct(tokens.shape,...  0.92 us
  transfers between devices with their start and end apart: 9, of which 3 were waited for; matrix products, arithmetic and copies ran while one was open for 0% of the time, Pallas kernels for 5%

profile of v3, /device:TPU:0, one launch (start us, length us, event | category | flops | bytes accessed | tf_op | source)
XLA Modules:
  0.0 41.2 jit_solution(9972615689512741927)
XLA Ops:
  0.0 0.0 copy-start
  0.0 0.0 copy-start.1
  0.0 0.0 slice-start
  0.0 0.0 slice-start.1
  0.0 0.0 slice-start.2
  0.0 0.9 %shard_map.73.refs_0_ = bf16[4,4096]{1,0:T(4,128)(2,1)S(1)} custom-call(bf16[4,4096]{1,0:T(4,128)(2,1)} %tokens_ref.1), custom_call_target="tpu_custom_call" | custom-call | flops 20000000000 | tf_op jit(solution)/shard_map/pallas_call | solution.py:27
  0.9 0.0 slice-start.3
  1.0 3.0 %collective-permute-start = (bf16[4,4096]{1,0:T(4,128)(2,1)S(1)}, bf16[4,4096]{1,0:T(4,128)(2,1)S(1)}, u32[]{:S(2)}, u32[]{:S(2)}) collective-permute-start(bf16[4,4096]{1,0:T(4,128)(2,1)S(1)} %shard_map.73.refs_0_), channel_id=1, source_target_pairs={{0,2},{2,4},{4,6},{6,8},{8,10},{10,12},{12,14},{14,0},{1,3},{3,5},... | collective-permute-start | bytes 98312 | tf_op jit(solution)/shard_map/ppermute | solution.py:164
  4.0 1.6 %collective-permute-start.1 = (bf16[4,4096]{1,0:T(4,128)(2,1)S(1)}, bf16[4,4096]{1,0:T(4,128)(2,1)S(1)}, u32[]{:S(2)}, u32[]{:S(2)}) collective-permute-start(bf16[4,4096]{1,0:T(4,128)(2,1)S(1)} %shard_map.73.refs_0_), channel_id=1, source_target_pairs={{0,4},{2,6},{4,8},{6,10},{8,12},{10,14},{12,0},{14,2},{1,5},{3,7},... | collective-permute-start | bytes 98312 | tf_op jit(solution)/shard_map/ppermute | solution.py:164
  5.5 2.6 %collective-permute-start.2 = (bf16[4,4096]{1,0:T(4,128)(2,1)S(1)}, bf16[4,4096]{1,0:T(4,128)(2,1)S(1)}, u32[]{:S(2)}, u32[]{:S(2)}) collective-permute-start(bf16[4,4096]{1,0:T(4,128)(2,1)S(1)} %shard_map.73.refs_0_), channel_id=1, source_target_pairs={{0,6},{2,8},{4,10},{6,12},{8,14},{10,0},{12,2},{14,4},{1,7},{3,9},... | collective-permute-start | bytes 98312 | tf_op jit(solution)/shard_map/ppermute | solution.py:164
  8.1 1.2 %collective-permute-start.3 = (bf16[4,4096]{1,0:T(4,128)(2,1)S(1)}, bf16[4,4096]{1,0:T(4,128)(2,1)S(1)}, u32[]{:S(2)}, u32[]{:S(2)}) collective-permute-start(bf16[4,4096]{1,0:T(4,128)(2,1)S(1)} %shard_map.73.refs_0_), channel_id=1, source_target_pairs={{0,8},{2,10},{4,12},{6,14},{8,0},{10,2},{12,4},{14,6},{1,9},{3,11}... | collective-permute-start | bytes 98312 | tf_op jit(solution)/shard_map/ppermute | solution.py:164
  9.3 2.6 %collective-permute-start.4 = (bf16[4,4096]{1,0:T(4,128)(2,1)S(1)}, bf16[4,4096]{1,0:T(4,128)(2,1)S(1)}, u32[]{:S(2)}, u32[]{:S(2)}) collective-permute-start(bf16[4,4096]{1,0:T(4,128)(2,1)S(1)} %shard_map.73.refs_0_), channel_id=1, source_target_pairs={{0,10},{2,12},{4,14},{6,0},{8,2},{10,4},{12,6},{14,8},{1,11},{3,13... | collective-permute-start | bytes 98312 | tf_op jit(solution)/shard_map/ppermute | solution.py:164
  12.0 0.0 collective-permute-done.refs_1_
  12.0 1.3 %collective-permute-start.5 = (bf16[4,4096]{1,0:T(4,128)(2,1)S(1)}, bf16[4,4096]{1,0:T(4,128)(2,1)S(1)}, u32[]{:S(2)}, u32[]{:S(2)}) collective-permute-start(bf16[4,4096]{1,0:T(4,128)(2,1)S(1)} %shard_map.73.refs_0_), channel_id=1, source_target_pairs={{0,12},{2,14},{4,0},{6,2},{8,4},{10,6},{12,8},{14,10},{1,13},{3,15... | collective-permute-start | bytes 98312 | tf_op jit(solution)/shard_map/ppermute | solution.py:164
  13.3 0.0 collective-permute-done.1.refs_2_
  13.3 1.4 %collective-permute-start.6 = (bf16[4,4096]{1,0:T(4,128)(2,1)S(1)}, bf16[4,4096]{1,0:T(4,128)(2,1)S(1)}, u32[]{:S(2)}, u32[]{:S(2)}) collective-permute-start(bf16[4,4096]{1,0:T(4,128)(2,1)S(1)} %shard_map.73.refs_0_), channel_id=1, source_target_pairs={{0,14},{2,0},{4,2},{6,4},{8,6},{10,8},{12,10},{14,12},{1,15},{3,1}... | collective-permute-start | bytes 98312 | tf_op jit(solution)/shard_map/ppermute | solution.py:164
  14.7 0.0 collective-permute-done.2.refs_3_
  14.7 0.0 collective-permute-done.3.refs_4_
  14.8 0.0 collective-permute-done.4.refs_5_
  14.8 1.1 %collective-permute-done.5.refs_6_ = bf16[4,4096]{1,0:T(4,128)(2,1)S(1)} collective-permute-done((bf16[4,4096]{1,0:T(4,128)(2,1)S(1)}, bf16[4,4096]{1,0:T(4,128)(2,1)S(1)}, u32[]{:S(2)}, u32[]{:S(2)}) %collective-permute-start.5) | collective-permute-done | bytes 32800 | tf_op jit(solution)/shard_map/ppermute | solution.py:164
  15.9 1.4 %collective-permute-done.6.refs_7_ = bf16[4,4096]{1,0:T(4,128)(2,1)S(1)} collective-permute-done((bf16[4,4096]{1,0:T(4,128)(2,1)S(1)}, bf16[4,4096]{1,0:T(4,128)(2,1)S(1)}, u32[]{:S(2)}, u32[]{:S(2)}) %collective-permute-start.6) | collective-permute-done | bytes 32800 | tf_op jit(solution)/shard_map/ppermute | solution.py:164
  17.2 0.0 copy-done
  17.2 0.0 copy-done.1
  17.2 6.3 %shard_map.74.h_ref = bf16[32,2048]{1,0:T(8,128)(2,1)S(1)} custom-call(bf16[4,4096]{1,0:T(4,128)(2,1)S(1)} %shard_map.73.refs_0_, bf16[4,4096]{1,0:T(4,128)(2,1)S(1)} %collective-permute-done.refs_1_, bf16[4,4096]{1,0:T(4,128)(2,1)S(1)} %collective-permute-done.1.refs_2_, bf16[4,4096]{1,0:T(4,128)(2,1)S(1)} %collective-permute-done.2.refs_3_, ...), custom_call_target="tpu_custom_call" | custom-call | flops 1073741824 | tf_op jit(solution)/shard_map/pallas_call | solution.py:83
  23.5 0.0 slice-done
  23.5 0.0 slice-done.1
  23.5 0.0 slice-done.2
  23.6 0.0 slice-done.3
  23.6 0.0 copy-start.2
  23.6 0.0 copy-start.3
  23.6 0.0 copy-start.4
  23.6 1.6 %shard_map.76 = bf16[32,2048]{1,0:T(8,128)(2,1)S(1)} custom-call(bf16[32,2048]{1,0:T(8,128)(2,1)S(1)} %shard_map.74.h_ref, bf16[2048,4096]{1,0:T(8,128)(2,1)S(1)} %bitcast.1), custom_call_target="tpu_custom_call" | custom-call | flops 268435456 | tf_op jit(solution)/shard_map/pallas_call | solution.py:116
  25.2 0.0 collective-permute-start.7
  25.2 1.6 %shard_map.75.keep_ref = f32[32,2048]{1,0:T(8,128)S(1)} custom-call(bf16[32,2048]{1,0:T(8,128)(2,1)S(1)} %shard_map.74.h_ref, bf16[2048,4096]{1,0:T(8,128)(2,1)S(1)} %bitcast.1), custom_call_target="tpu_custom_call" | custom-call | flops 268435456 | tf_op jit(solution)/shard_map/pallas_call | solution.py:116
  26.8 0.0 collective-permute-done.7.got_ref
  26.8 0.7 %shard_map.77 = bf16[8,4,2048]{2,1,0:T(4,128)(2,1)} custom-call(f32[32,2048]{1,0:T(8,128)S(1)} %shard_map.75.keep_ref, bf16[32,2048]{1,0:T(8,128)(2,1)S(1)} %collective-permute-done.7.got_ref), custom_call_target="tpu_custom_call" | custom-call | tf_op jit(solution)/shard_map/pallas_call | solution.py:136
  27.5 5.4 %all-to-all-start = ((bf16[8,4,2048]{2,1,0:T(4,128)(2,1)}), bf16[8,4,2048]{2,1,0:T(4,128)(2,1)S(1)}, u32[]{:S(2)}, u32[]{:S(2)}) async-start(bf16[8,4,2048]{2,1,0:T(4,128)(2,1)} %shard_map.77), calls=%async_computation | async-start | bytes 262144 | tf_op jit(solution)/shard_map/all_to_all | solution.py:176
  32.9 0.0 copy-done.2
  32.9 0.0 copy-done.3
  32.9 0.0 copy-done.4
  32.9 0.6 %shard_map.78.gates_ref = f32[32,128]{1,0:T(8,128)S(1)} custom-call(s32[4]{0:T(128)S(1)} %copy-done.4, s32[4,128]{1,0:T(4,128)S(1)} %copy-done.2, f32[4,128]{1,0:T(4,128)S(1)} %copy-done.3), custom_call_target="tpu_custom_call" | custom-call | tf_op jit(solution)/shard_map/pallas_call | solution.py:54
  33.5 7.0 %all-to-all-done.got_ref = bf16[8,4,2048]{2,1,0:T(4,128)(2,1)S(1)} async-done(((bf16[8,4,2048]{2,1,0:T(4,128)(2,1)}), bf16[8,4,2048]{2,1,0:T(4,128)(2,1)S(1)}, u32[]{:S(2)}, u32[]{:S(2)}) %all-to-all-start) | async-done | bytes 131104 | tf_op jit(solution)/shard_map/all_to_all | solution.py:176
  40.5 0.7 %shard_map.79 = bf16[4,2048]{1,0:T(4,128)(2,1)} custom-call(bf16[8,4,2048]{2,1,0:T(4,128)(2,1)S(1)} %all-to-all-done.got_ref, f32[32,128]{1,0:T(8,128)S(1)} %shard_map.78.gates_ref), custom_call_target="tpu_custom_call" | custom-call | tf_op jit(solution)/shard_map/pallas_call | solution.py:154
  (1 shorter events, 0.0 us)
Async XLA Ops:
  0.0 17.2 %copy-start = (bf16[4096,2048]{1,0:T(8,128)(2,1)S(1)}, bf16[4096,2048]{1,0:T(8,128)(2,1)}, u32[]{:S(2)}) copy-start(bf16[4096,2048]{1,0:T(8,128)(2,1)} %refs_8_.1) | copy-start | bytes 50331652
  0.0 17.2 %copy-start.1 = (bf16[4096,2048]{1,0:T(8,128)(2,1)S(1)}, bf16[4096,2048]{1,0:T(8,128)(2,1)}, u32[]{:S(2)}) copy-start(bf16[4096,2048]{1,0:T(8,128)(2,1)} %refs_9_.1) | copy-start | bytes 50331652
  0.0 23.5 %slice-start = ((s8[16777216]{0:T(1024)(128)(4,1)}), s8[4194304]{0:T(1024)(128)(4,1)S(1)}, s32[]{:S(2)}) async-start(s8[16777216]{0:T(1024)(128)(4,1)} %bitcast), calls=%async_computation.1 | async-start | bytes 8388608
  0.0 23.5 %slice-start.1 = ((s8[16777216]{0:T(1024)(128)(4,1)}), s8[4194304]{0:T(1024)(128)(4,1)S(1)}, s32[]{:S(2)}) async-start(s8[16777216]{0:T(1024)(128)(4,1)} %bitcast), calls=%async_computation.2 | async-start | bytes 8388608
  0.0 23.5 %slice-start.2 = ((s8[16777216]{0:T(1024)(128)(4,1)}), s8[4194304]{0:T(1024)(128)(4,1)S(1)}, s32[]{:S(2)}) async-start(s8[16777216]{0:T(1024)(128)(4,1)} %bitcast), calls=%async_computation.3 | async-start | bytes 8388608
  0.9 22.6 %slice-start.3 = ((s8[16777216]{0:T(1024)(128)(4,1)}), s8[4194304]{0:T(1024)(128)(4,1)S(1)}, s32[]{:S(2)}) async-start(s8[16777216]{0:T(1024)(128)(4,1)} %bitcast), calls=%async_computation.4 | async-start | bytes 8388608
  1.0 11.0 %collective-permute-start = (bf16[4,4096]{1,0:T(4,128)(2,1)S(1)}, bf16[4,4096]{1,0:T(4,128)(2,1)S(1)}, u32[]{:S(2)}, u32[]{:S(2)}) collective-permute-start(bf16[4,4096]{1,0:T(4,128)(2,1)S(1)} %shard_map.73.refs_0_), channel_id=1, source_target_pairs={{0,2},{2,4},{4,6},{6,8},{8,10},{10,12},{12,14},{14,0},{1,3},{3,5},... | collective-permute-start | bytes 98312 | tf_op jit(solution)/shard_map/ppermute | solution.py:164
  4.0 9.3 %collective-permute-start.1 = (bf16[4,4096]{1,0:T(4,128)(2,1)S(1)}, bf16[4,4096]{1,0:T(4,128)(2,1)S(1)}, u32[]{:S(2)}, u32[]{:S(2)}) collective-permute-start(bf16[4,4096]{1,0:T(4,128)(2,1)S(1)} %shard_map.73.refs_0_), channel_id=1, source_target_pairs={{0,4},{2,6},{4,8},{6,10},{8,12},{10,14},{12,0},{14,2},{1,5},{3,7},... | collective-permute-start | bytes 98312 | tf_op jit(solution)/shard_map/ppermute | solution.py:164
  5.5 9.2 %collective-permute-start.2 = (bf16[4,4096]{1,0:T(4,128)(2,1)S(1)}, bf16[4,4096]{1,0:T(4,128)(2,1)S(1)}, u32[]{:S(2)}, u32[]{:S(2)}) collective-permute-start(bf16[4,4096]{1,0:T(4,128)(2,1)S(1)} %shard_map.73.refs_0_), channel_id=1, source_target_pairs={{0,6},{2,8},{4,10},{6,12},{8,14},{10,0},{12,2},{14,4},{1,7},{3,9},... | collective-permute-start | bytes 98312 | tf_op jit(solution)/shard_map/ppermute | solution.py:164
  8.1 6.6 %collective-permute-start.3 = (bf16[4,4096]{1,0:T(4,128)(2,1)S(1)}, bf16[4,4096]{1,0:T(4,128)(2,1)S(1)}, u32[]{:S(2)}, u32[]{:S(2)}) collective-permute-start(bf16[4,4096]{1,0:T(4,128)(2,1)S(1)} %shard_map.73.refs_0_), channel_id=1, source_target_pairs={{0,8},{2,10},{4,12},{6,14},{8,0},{10,2},{12,4},{14,6},{1,9},{3,11}... | collective-permute-start | bytes 98312 | tf_op jit(solution)/shard_map/ppermute | solution.py:164
  9.3 5.4 %collective-permute-start.4 = (bf16[4,4096]{1,0:T(4,128)(2,1)S(1)}, bf16[4,4096]{1,0:T(4,128)(2,1)S(1)}, u32[]{:S(2)}, u32[]{:S(2)}) collective-permute-start(bf16[4,4096]{1,0:T(4,128)(2,1)S(1)} %shard_map.73.refs_0_), channel_id=1, source_target_pairs={{0,10},{2,12},{4,14},{6,0},{8,2},{10,4},{12,6},{14,8},{1,11},{3,13... | collective-permute-start | bytes 98312 | tf_op jit(solution)/shard_map/ppermute | solution.py:164
  12.0 3.9 %collective-permute-start.5 = (bf16[4,4096]{1,0:T(4,128)(2,1)S(1)}, bf16[4,4096]{1,0:T(4,128)(2,1)S(1)}, u32[]{:S(2)}, u32[]{:S(2)}) collective-permute-start(bf16[4,4096]{1,0:T(4,128)(2,1)S(1)} %shard_map.73.refs_0_), channel_id=1, source_target_pairs={{0,12},{2,14},{4,0},{6,2},{8,4},{10,6},{12,8},{14,10},{1,13},{3,15... | collective-permute-start | bytes 98312 | tf_op jit(solution)/shard_map/ppermute | solution.py:164
  13.3 3.9 %collective-permute-start.6 = (bf16[4,4096]{1,0:T(4,128)(2,1)S(1)}, bf16[4,4096]{1,0:T(4,128)(2,1)S(1)}, u32[]{:S(2)}, u32[]{:S(2)}) collective-permute-start(bf16[4,4096]{1,0:T(4,128)(2,1)S(1)} %shard_map.73.refs_0_), channel_id=1, source_target_pairs={{0,14},{2,0},{4,2},{6,4},{8,6},{10,8},{12,10},{14,12},{1,15},{3,1}... | collective-permute-start | bytes 98312 | tf_op jit(solution)/shard_map/ppermute | solution.py:164
  23.6 9.3 %copy-start.2 = (s32[4,128]{1,0:T(4,128)S(1)}, s32[4,128]{1,0:T(4,128)}, u32[]{:S(2)}) copy-start(s32[4,128]{1,0:T(4,128)} %rows_ref.1) | copy-start | bytes 6148
  23.6 9.3 %copy-start.3 = (f32[4,128]{1,0:T(4,128)S(1)}, f32[4,128]{1,0:T(4,128)}, u32[]{:S(2)}) copy-start(f32[4,128]{1,0:T(4,128)} %gates_ref.1) | copy-start | bytes 6148
  23.6 9.3 %copy-start.4 = (s32[4]{0:T(128)S(1)}, s32[4]{0:T(128)}, u32[]{:S(2)}) copy-start(s32[4]{0:T(128)} %counts_ref.1) | copy-start | bytes 52
  25.2 1.6 %collective-permute-start.7 = (bf16[32,2048]{1,0:T(8,128)(2,1)S(1)}, bf16[32,2048]{1,0:T(8,128)(2,1)S(1)}, u32[]{:S(2)}, u32[]{:S(2)}) collective-permute-start(bf16[32,2048]{1,0:T(8,128)(2,1)S(1)} %shard_map.76), channel_id=1, source_target_pairs={{0,1},{1,0},{2,3},{3,2},{4,5},{5,4},{6,7},{7,6},{8,9},{9,8},{10,11... | collective-permute-start | bytes 393224 | tf_op jit(solution)/shard_map/ppermute | solution.py:174
  27.5 13.1 %all-to-all-start = ((bf16[8,4,2048]{2,1,0:T(4,128)(2,1)}), bf16[8,4,2048]{2,1,0:T(4,128)(2,1)S(1)}, u32[]{:S(2)}, u32[]{:S(2)}) async-start(bf16[8,4,2048]{2,1,0:T(4,128)(2,1)} %shard_map.77), calls=%async_computation | async-start | bytes 262144 | tf_op jit(solution)/shard_map/all_to_all | solution.py:176

commit v4 on v3

--- a/solution.py
+++ b/solution.py
@@ -17,18 +17,19 @@
 SMEM = pl.BlockSpec(memory_space=pltpu.SMEM)
 
 
-def pass_kernel(tokens_ref, out_ref, sem):
+def pass_kernel(tokens_ref, out_ref, side_ref, sem):
     copy = pltpu.make_async_copy(tokens_ref, out_ref, sem)
     copy.start()
+    side_ref[0] = lax.axis_index("hid")
     copy.wait()
 
 
 def pass_on(tokens):
     return pl.pallas_call(
         pass_kernel,
-        out_shape=jax.ShapeDtypeStruct(tokens.shape, tokens.dtype),
+        out_shape=(jax.ShapeDtypeStruct(tokens.shape, tokens.dtype), pltpu.SMEM((1,), jnp.int32)),
         in_specs=[HBM],
-        out_specs=VMEM,
+        out_specs=(VMEM, SMEM),
         scratch_shapes=[pltpu.SemaphoreType.DMA],
         compiler_params=pltpu.CompilerParams(vmem_limit_bytes=2 * MIB),
         cost_estimate=pl.CostEstimate(flops=AHEAD, bytes_accessed=0, transcendentals=0),
@@ -40,8 +41,9 @@
     total = out_ref.shape[0]
     line = lax.broadcasted_iota(jnp.int32, (total, slots), 0)
     position = lax.broadcasted_iota(jnp.int32, (total, slots), 1)
-    token = lax.axis_index("exp") * count + lax.rem(line, count)
-    expert = line // (count * per_expert)
+    own = lax.axis_index("exp")
+    token = own * count + lax.rem(line, count)
+    expert = (own ^ (line // count)) // per_expert
     found = jnp.zeros((total, slots), jnp.float32)
     for e in range(experts):
         rows = rows_ref[pl.ds(e, 1), :]
@@ -100,9 +102,9 @@
     return pltpu.with_memory_space_constraint(x, pltpu.VMEM)
 
 
-def down_kernel(other, h_ref, wd_ref, out_ref):
+def down_kernel(other, side_ref, h_ref, wd_ref, out_ref):
     half = wd_ref.shape[1] // 2
-    side = lax.axis_index("hid")
+    side = side_ref[0]
     base = (1 - side if other else side) * half
     for n in range(half // TILE):
         cols = pl.ds(pl.multiple_of(base + n * TILE, TILE), TILE)
@@ -110,72 +112,74 @@
         out_ref[:, pl.ds(n * TILE, TILE)] = part.astype(out_ref.dtype)
 
 
-def down_half(hidden, wd, other, dtype):
+def down_half(side, hidden, wd, other, dtype):
     rows, depth = hidden.shape
     half = wd.shape[1] // 2
     return pl.pallas_call(
         functools.partial(down_kernel, other),
         out_shape=jax.ShapeDtypeStruct((rows, half), dtype),
-        in_specs=[VMEM, VMEM],
+        in_specs=[SMEM, VMEM, VMEM],
         out_specs=VMEM,
         compiler_params=pltpu.CompilerParams(vmem_limit_bytes=2 * MIB),
         cost_estimate=pl.CostEstimate(flops=2 * rows * depth * half, bytes_accessed=0, transcendentals=0),
-    )(hidden, in_vmem(wd))
-
-
-def merge_kernel(keep_ref, got_ref, out_ref):
-    sources, count, _ = out_ref.shape
-    own = lax.axis_index("exp")
-    both = (keep_ref[...] + got_ref[...].astype(jnp.float32)).astype(out_ref.dtype)
-    for k in range(sources):
-        out_ref[lax.rem(own - k + sources, sources)] = both[k * count : (k + 1) * count]
+    )(pltpu.with_memory_space_constraint(side, pltpu.SMEM), hidden, in_vmem(wd))
+
+
+def merge_kernel(keep_ref, got_ref, own_ref, *out_refs):
+    both = keep_ref[...] + got_ref[...].astype(jnp.float32)
+    count = own_ref.shape[0]
+    own_ref[...] = both[:count]
+    for k, out_ref in enumerate(out_refs):
+        out_ref[...] = both[(k + 1) * count : (k + 2) * count].astype(out_ref.dtype)
 
 
 def merge(keep, got, sources):
     rows, width = keep.shape
+    count = rows // sources
     return pl.pallas_call(
         merge_kernel,
-        out_shape=jax.ShapeDtypeStruct((sources, rows // sources, width), jnp.bfloat16),
+        out_shape=(jax.ShapeDtypeStruct((count, width), jnp.float32),)
+        + (jax.ShapeDtypeStruct((count, width), jnp.bfloat16),) * (sources - 1),
         in_specs=[VMEM, VMEM],
-        out_specs=VMEM,
+        out_specs=(VMEM,) * sources,
         compiler_params=pltpu.CompilerParams(vmem_limit_bytes=2 * MIB),
     )(keep, got)
 
 
-def sum_kernel(got_ref, gates_ref, out_ref):
-    sources, count, _ = got_ref.shape
-    total = jnp.zeros(out_ref.shape, jnp.float32)
-    for s in range(sources):
-        total = total + got_ref[s].astype(jnp.float32) * gates_ref[pl.ds(s * count, count), :1]
-    out_ref[...] = total.astype(out_ref.dtype)
-
-
-def weighted_sum(got, gates):
+def sum_kernel(gates_ref, *refs):
+    total = jnp.zeros(refs[-1].shape, jnp.float32)
+    count = total.shape[0]
+    for k, ref in enumerate(refs[:-1]):
+        total = total + ref[...].astype(jnp.float32) * gates_ref[pl.ds(k * count, count), :1]
+    refs[-1][...] = total.astype(jnp.bfloat16)
+
+
+def weighted_sum(gates, own, got):
     return pl.pallas_call(
         sum_kernel,
-        out_shape=jax.ShapeDtypeStruct(got.shape[1:], jnp.bfloat16),
-        in_specs=[VMEM, VMEM],
-        out_specs=VMEM,
-        compiler_params=pltpu.CompilerParams(vmem_limit_bytes=2 * MIB),
-    )(got, gates)
-
-
-def shifted(x, k, sources):
-    return lax.ppermute(x, "exp", [(i, (i + k) % sources) for i in range(sources)])
+        out_shape=jax.ShapeDtypeStruct(own.shape, jnp.bfloat16),
+        in_specs=[VMEM] * (2 + len(got)),
+        out_specs=VMEM,
+        compiler_params=pltpu.CompilerParams(vmem_limit_bytes=2 * MIB),
+    )(gates, own, *got)
+
+
+def swapped(x, k, sources):
+    return lax.ppermute(x, "exp", [(i, i ^ k) for i in range(sources)])
 
 
 def local(tokens, w_gate, w_up, w_down, block_counts, block_rows, row_gates):
     sources = lax.axis_size("exp")
-    tokens = pass_on(tokens)
-    pieces = [tokens] + [shifted(tokens, k, sources) for k in range(1, sources)]
+    tokens, side = pass_on(tokens)
+    pieces = [tokens] + [swapped(tokens, k, sources) for k in range(1, sources)]
     hidden = hidden_rows(pieces, w_gate, w_up)
-    send = down_half(hidden, w_down, True, jnp.bfloat16)
-    keep = down_half(hidden, w_down, False, jnp.float32)
+    send = down_half(side, hidden, w_down, True, jnp.bfloat16)
+    keep = down_half(side, hidden, w_down, False, jnp.float32)
     got = lax.ppermute(send, "hid", [(0, 1), (1, 0)])
-    outgoing = merge(keep, got, sources)
-    returned = lax.all_to_all(outgoing, "exp", split_axis=0, concat_axis=0, tiled=True)
+    own, *outgoing = merge(keep, got, sources)
+    returned = [swapped(piece, k + 1, sources) for k, piece in enumerate(outgoing)]
     gates = route(block_counts, block_rows, row_gates, sources, tokens.shape[0])
-    return weighted_sum(returned, gates)
+    return weighted_sum(gates, own, returned)
 
 
 def expert_block(segment, w_gate, w_up, w_down):
@@ -244,8 +248,9 @@
 
 
 def solution(mesh):
+    sources = mesh.shape["exp"]
     return jax.shard_map(
-        local if mesh.shape["exp"] <= 16 else local_wide,
+        local if sources in (4, 8, 16) and mesh.shape["hid"] == 2 else local_wide,
         mesh=mesh,
         in_specs=(
             P(("grp", "exp"), None),

time: 41.5 us -> 42.6 us (1.027)
  starting transfers between devices: 19.2 us -> 21.9 us
  waiting for transfers between devices: 9.47 us -> 8.58 us
  Pallas kernels: 12.4 us -> 11.8 us
    ppermute x7 -> x14, starting transfers between devices: 13.8 us -> 21.9 us  [swapped(): return lax.ppermute(x, 'exp', [(i, i ^ k) for i in range(sources)])]
    all_to_all x1 -> x0, waiting for transfers between devices: 6.99 us -> none  [local(): lax.all_to_all(outgoing, 'exp', split_axis=0, concat_axis=0, tiled=True)]
    ppermute x7 -> x14, waiting for transfers between devices: 2.48 us -> 8.58 us  [swapped(): return lax.ppermute(x, 'exp', [(i, i ^ k) for i in range(sources)])]
    all_to_all x1 -> x0, starting transfers between devices: 5.41 us -> none  [local(): lax.all_to_all(outgoing, 'exp', split_axis=0, concat_axis=0, tiled=True)]
    pallas_call x3, Pallas kernels: 2.32 us -> 1.67 us  [the longest x1 0.92 us: pass_on(): pl.pallas_call(pass_kernel, out_shape=(jax.ShapeDtypeStruct(tokens.shape,...]
  transfers between devices with their start and end apart: 9 -> 15, of which waited for: 3 -> 5; matrix products, arithmetic and copies ran while one was open for 0% -> 0% of each run, Pallas kernels for 5% -> 5%
where the time goes in v4:
time: 42.6 us; the launch traced here: 42.4 us
  starting transfers between devices  21.9 us (51%)
  Pallas kernels  11.8 us (28%)
  waiting for transfers between devices  8.58 us (20%)
    ppermute x14, starting transfers between devices, swapped(): return lax.ppermute(x, 'exp', [(i, i ^ k) for i in range(sources)])  21.9 us
    ppermute x14, waiting for transfers between devices, swapped(): return lax.ppermute(x, 'exp', [(i, i ^ k) for i in range(sources)])  8.58 us
    pallas_call x1, Pallas kernels, hidden_rows(): pl.pallas_call(functools.partial(hidden_kernel, sources), out_shape=jax.S...  6.3 us
    pallas_call x2, Pallas kernels, down_half(): pl.pallas_call(functools.partial(down_kernel, other), out_shape=jax.Shape...  3.13 us
    pallas_call x1, Pallas kernels, pass_on(): pl.pallas_call(pass_kernel, out_shape=(jax.ShapeDtypeStruct(tokens.shape,...  0.92 us
  transfers between devices with their start and end apart: 15, of which 5 were waited for; matrix products, arithmetic and copies ran while one was open for 0% of the time, Pallas kernels for 5%

profile of v4, /device:TPU:0, one launch (start us, length us, event | category | flops | bytes accessed | tf_op | source)
XLA Modules:
  0.0 42.4 jit_solution(10204996949813119274)
XLA Ops:
  0.0 0.0 copy-start
  0.0 0.0 copy-start.1
  0.0 0.9 %shard_map.74 = (bf16[4,4096]{1,0:T(4,128)(2,1)S(1)}, s32[1]{0:T(128)S(4)}) custom-call(bf16[4,4096]{1,0:T(4,128)(2,1)} %tokens_ref.1), custom_call_target="tpu_custom_call" | custom-call | flops 20000000000 | tf_op jit(solution)/shard_map/pallas_call | solution.py:28
  0.9 0.0 slice-start
  0.9 0.0 slice-start.1
  1.0 0.0 slice-start.2
  1.0 0.0 slice-start.3
  1.0 3.0 %collective-permute-start = (bf16[4,4096]{1,0:T(4,128)(2,1)S(1)}, bf16[4,4096]{1,0:T(4,128)(2,1)S(1)}, u32[]{:S(2)}, u32[]{:S(2)}) collective-permute-start(bf16[4,4096]{1,0:T(4,128)(2,1)S(1)} %get-tuple-element.16.refs_0_), channel_id=1, source_target_pairs={{0,2},{2,0},{4,6},{6,4},{8,10},{10,8},{12,14},{14,12},{1,3},{3,1},... | collective-permute-start | bytes 98312 | tf_op jit(solution)/shard_map/ppermute | solution.py:168
  4.0 1.6 %collective-permute-start.1 = (bf16[4,4096]{1,0:T(4,128)(2,1)S(1)}, bf16[4,4096]{1,0:T(4,128)(2,1)S(1)}, u32[]{:S(2)}, u32[]{:S(2)}) collective-permute-start(bf16[4,4096]{1,0:T(4,128)(2,1)S(1)} %get-tuple-element.16.refs_0_), channel_id=1, source_target_pairs={{0,4},{2,6},{4,0},{6,2},{8,12},{10,14},{12,8},{14,10},{1,5},{3,7},... | collective-permute-start | bytes 98312 | tf_op jit(solution)/shard_map/ppermute | solution.py:168
  5.6 0.0 collective-permute-start.2
  5.6 3.0 %collective-permute-start.3 = (bf16[4,4096]{1,0:T(4,128)(2,1)S(1)}, bf16[4,4096]{1,0:T(4,128)(2,1)S(1)}, u32[]{:S(2)}, u32[]{:S(2)}) collective-permute-start(bf16[4,4096]{1,0:T(4,128)(2,1)S(1)} %get-tuple-element.16.refs_0_), channel_id=1, source_target_pairs={{0,8},{2,10},{4,12},{6,14},{8,0},{10,2},{12,4},{14,6},{1,9},{3,11}... | collective-permute-start | bytes 98312 | tf_op jit(solution)/shard_map/ppermute | solution.py:168
  8.6 1.3 %collective-permute-start.4 = (bf16[4,4096]{1,0:T(4,128)(2,1)S(1)}, bf16[4,4096]{1,0:T(4,128)(2,1)S(1)}, u32[]{:S(2)}, u32[]{:S(2)}) collective-permute-start(bf16[4,4096]{1,0:T(4,128)(2,1)S(1)} %get-tuple-element.16.refs_0_), channel_id=1, source_target_pairs={{0,10},{2,8},{4,14},{6,12},{8,2},{10,0},{12,6},{14,4},{1,11},{3,9}... | collective-permute-start | bytes 98312 | tf_op jit(solution)/shard_map/ppermute | solution.py:168
  9.8 0.0 collective-permute-done.refs_1_
  9.8 3.6 %collective-permute-start.5 = (bf16[4,4096]{1,0:T(4,128)(2,1)S(1)}, bf16[4,4096]{1,0:T(4,128)(2,1)S(1)}, u32[]{:S(2)}, u32[]{:S(2)}) collective-permute-start(bf16[4,4096]{1,0:T(4,128)(2,1)S(1)} %get-tuple-element.16.refs_0_), channel_id=1, source_target_pairs={{0,12},{2,14},{4,8},{6,10},{8,4},{10,6},{12,0},{14,2},{1,13},{3,15... | collective-permute-start | bytes 98312 | tf_op jit(solution)/shard_map/ppermute | solution.py:168
  13.4 0.0 collective-permute-done.1.refs_2_
  13.4 0.0 collective-permute-start.6
  13.5 0.0 collective-permute-done.2.refs_3_
  13.5 0.0 collective-permute-done.3.refs_4_
  13.5 1.0 %collective-permute-done.4.refs_5_ = bf16[4,4096]{1,0:T(4,128)(2,1)S(1)} collective-permute-done((bf16[4,4096]{1,0:T(4,128)(2,1)S(1)}, bf16[4,4096]{1,0:T(4,128)(2,1)S(1)}, u32[]{:S(2)}, u32[]{:S(2)}) %collective-permute-start.4) | collective-permute-done | bytes 32800 | tf_op jit(solution)/shard_map/ppermute | solution.py:168
  14.5 1.2 %collective-permute-done.5.refs_6_ = bf16[4,4096]{1,0:T(4,128)(2,1)S(1)} collective-permute-done((bf16[4,4096]{1,0:T(4,128)(2,1)S(1)}, bf16[4,4096]{1,0:T(4,128)(2,1)S(1)}, u32[]{:S(2)}, u32[]{:S(2)}) %collective-permute-start.5) | collective-permute-done | bytes 32800 | tf_op jit(solution)/shard_map/ppermute | solution.py:168
  15.7 4.4 %collective-permute-done.6.refs_7_ = bf16[4,4096]{1,0:T(4,128)(2,1)S(1)} collective-permute-done((bf16[4,4096]{1,0:T(4,128)(2,1)S(1)}, bf16[4,4096]{1,0:T(4,128)(2,1)S(1)}, u32[]{:S(2)}, u32[]{:S(2)}) %collective-permute-start.6) | collective-permute-done | bytes 32800 | tf_op jit(solution)/shard_map/ppermute | solution.py:168
  20.1 0.0 copy-done
  20.1 0.0 copy-done.1
  20.1 6.3 %shard_map.75.h_ref = bf16[32,2048]{1,0:T(8,128)(2,1)S(1)} custom-call(bf16[4,4096]{1,0:T(4,128)(2,1)S(1)} %get-tuple-element.16.refs_0_, bf16[4,4096]{1,0:T(4,128)(2,1)S(1)} %collective-permute-done.refs_1_, bf16[4,4096]{1,0:T(4,128)(2,1)S(1)} %collective-permute-done.1.refs_2_, bf16[4,4096]{1,0:T(4,128)(2,1)S(1)} %collective-permute-done.2.refs_3_, ...), custom_call_target="tpu_custom_call" | custom-call | flops 1073741824 | tf_op jit(solution)/shard_map/pallas_call | solution.py:85
  26.4 0.0 slice-done
  26.4 0.0 slice-done.1
  26.4 0.0 slice-done.2
  26.4 0.0 slice-done.3
  26.4 0.0 copy-start.2
  26.4 0.0 copy-start.3
  26.4 0.0 copy-start.4
  26.4 1.6 %shard_map.77 = bf16[32,2048]{1,0:T(8,128)(2,1)S(1)} custom-call(s32[1]{0:T(128)S(4)} %get-tuple-element.15.side_ref, bf16[32,2048]{1,0:T(8,128)(2,1)S(1)} %shard_map.75.h_ref, bf16[2048,4096]{1,0:T(8,128)(2,1)S(1)} %bitcast.1), custom_call_target="tpu_custom_call" | custom-call | flops 268435456 | tf_op jit(solution)/shard_map/pallas_call | solution.py:118
  28.0 0.0 collective-permute-start.7
  28.0 1.6 %shard_map.76.keep_ref = f32[32,2048]{1,0:T(8,128)S(1)} custom-call(s32[1]{0:T(128)S(4)} %get-tuple-element.15.side_ref, bf16[32,2048]{1,0:T(8,128)(2,1)S(1)} %shard_map.75.h_ref, bf16[2048,4096]{1,0:T(8,128)(2,1)S(1)} %bitcast.1), custom_call_target="tpu_custom_call" | custom-call | flops 268435456 | tf_op jit(solution)/shard_map/pallas_call | solution.py:118
  29.6 0.0 collective-permute-done.7.got_ref
  29.6 0.1 collective-permute-start.10
  29.7 0.9 %collective-permute-start.11 = (bf16[4,2048]{1,0:T(4,128)(2,1)S(1)}, bf16[4,2048]{1,0:T(4,128)(2,1)S(1)}, u32[]{:S(2)}, u32[]{:S(2)}) collective-permute-start(bf16[4,2048]{1,0:T(4,128)(2,1)S(1)} %get-tuple-element.21), channel_id=1, source_target_pairs={{0,8},{2,10},{4,12},{6,14},{8,0},{10,2},{12,4},{14,6},{1,9},{3,11}... | collective-permute-start | bytes 49160 | tf_op jit(solution)/shard_map/ppermute | solution.py:168
  30.6 2.1 %collective-permute-start.12 = (bf16[4,2048]{1,0:T(4,128)(2,1)S(1)}, bf16[4,2048]{1,0:T(4,128)(2,1)S(1)}, u32[]{:S(2)}, u32[]{:S(2)}) collective-permute-start(bf16[4,2048]{1,0:T(4,128)(2,1)S(1)} %get-tuple-element.22), channel_id=1, source_target_pairs={{0,10},{2,8},{4,14},{6,12},{8,2},{10,0},{12,6},{14,4},{1,11},{3,9}... | collective-permute-start | bytes 49160 | tf_op jit(solution)/shard_map/ppermute | solution.py:168
  32.7 2.3 %collective-permute-start.13 = (bf16[4,2048]{1,0:T(4,128)(2,1)S(1)}, bf16[4,2048]{1,0:T(4,128)(2,1)S(1)}, u32[]{:S(2)}, u32[]{:S(2)}) collective-permute-start(bf16[4,2048]{1,0:T(4,128)(2,1)S(1)} %get-tuple-element.23), channel_id=1, source_target_pairs={{0,12},{2,14},{4,8},{6,10},{8,4},{10,6},{12,0},{14,2},{1,13},{3,15... | collective-permute-start | bytes 49160 | tf_op jit(solution)/shard_map/ppermute | solution.py:168
  35.0 2.4 %collective-permute-start.14 = (bf16[4,2048]{1,0:T(4,128)(2,1)S(1)}, bf16[4,2048]{1,0:T(4,128)(2,1)S(1)}, u32[]{:S(2)}, u32[]{:S(2)}) collective-permute-start(bf16[4,2048]{1,0:T(4,128)(2,1)S(1)} %get-tuple-element.24), channel_id=1, source_target_pairs={{0,14},{2,12},{4,10},{6,8},{8,6},{10,4},{12,2},{14,0},{1,15},{3,13... | collective-permute-start | bytes 49160 | tf_op jit(solution)/shard_map/ppermute | solution.py:168
  37.4 0.0 collective-permute-done.10.refs_3_
  37.4 0.5 %collective-permute-start.8 = (bf16[4,2048]{1,0:T(4,128)(2,1)S(1)}, bf16[4,2048]{1,0:T(4,128)(2,1)S(1)}, u32[]{:S(2)}, u32[]{:S(2)}) collective-permute-start(bf16[4,2048]{1,0:T(4,128)(2,1)S(1)} %get-tuple-element.18), channel_id=1, source_target_pairs={{0,2},{2,0},{4,6},{6,4},{8,10},{10,8},{12,14},{14,12},{1,3},{3,1},... | collective-permute-start | bytes 49160 | tf_op jit(solution)/shard_map/ppermute | solution.py:168
  38.0 0.0 collective-permute-done.11.refs_4_
  38.0 1.1 %collective-permute-start.9 = (bf16[4,2048]{1,0:T(4,128)(2,1)S(1)}, bf16[4,2048]{1,0:T(4,128)(2,1)S(1)}, u32[]{:S(2)}, u32[]{:S(2)}) collective-permute-start(bf16[4,2048]{1,0:T(4,128)(2,1)S(1)} %get-tuple-element.19), channel_id=1, source_target_pairs={{0,4},{2,6},{4,0},{6,2},{8,12},{10,14},{12,8},{14,10},{1,5},{3,7},... | collective-permute-start | bytes 49160 | tf_op jit(solution)/shard_map/ppermute | solution.py:168
  39.0 0.0 copy-done.2
  39.0 0.0 copy-done.3
  39.1 0.0 copy-done.4
  39.1 0.7 %shard_map.73.gates_ref = f32[32,128]{1,0:T(8,128)S(1)} custom-call(s32[4]{0:T(128)S(1)} %copy-done.4, s32[4,128]{1,0:T(4,128)S(1)} %copy-done.2, f32[4,128]{1,0:T(4,128)S(1)} %copy-done.3), custom_call_target="tpu_custom_call" | custom-call | tf_op jit(solution)/shard_map/pallas_call | solution.py:56
  39.7 0.0 collective-permute-done.12.refs_5_
  39.7 0.0 collective-permute-done.13.refs_6_
  39.7 1.7 %collective-permute-done.14.refs_7_ = bf16[4,2048]{1,0:T(4,128)(2,1)S(1)} collective-permute-done((bf16[4,2048]{1,0:T(4,128)(2,1)S(1)}, bf16[4,2048]{1,0:T(4,128)(2,1)S(1)}, u32[]{:S(2)}, u32[]{:S(2)}) %collective-permute-start.14) | collective-permute-done | bytes 16416 | tf_op jit(solution)/shard_map/ppermute | solution.py:168
  41.4 0.0 collective-permute-done.8.refs_1_
  41.4 0.3 collective-permute-done.9.refs_2_
  41.7 0.7 %shard_map.79 = bf16[4,2048]{1,0:T(4,128)(2,1)} custom-call(f32[32,128]{1,0:T(8,128)S(1)} %shard_map.73.gates_ref, f32[4,2048]{1,0:T(4,128)S(1)} %get-tuple-element.17.refs_0_, bf16[4,2048]{1,0:T(4,128)(2,1)S(1)} %collective-permute-done.8.refs_1_, bf16[4,2048]{1,0:T(4,128)(2,1)S(1)} %collective-permute-done.9.refs_2_, ...), custom_call_target="tpu_custom_call" | custom-call | tf_op jit(solution)/shard_map/pallas_call | solution.py:158
  (2 shorter events, 0.0 us)
Async XLA Ops:
  0.0 20.1 %copy-start = (bf16[4096,2048]{1,0:T(8,128)(2,1)S(1)}, bf16[4096,2048]{1,0:T(8,128)(2,1)}, u32[]{:S(2)}) copy-start(bf16[4096,2048]{1,0:T(8,128)(2,1)} %refs_8_.1) | copy-start | bytes 50331652
  0.0 20.1 %copy-start.1 = (bf16[4096,2048]{1,0:T(8,128)(2,1)S(1)}, bf16[4096,2048]{1,0:T(8,128)(2,1)}, u32[]{:S(2)}) copy-start(bf16[4096,2048]{1,0:T(8,128)(2,1)} %refs_9_.1) | copy-start | bytes 50331652
  0.9 25.4 %slice-start = ((s8[16777216]{0:T(1024)(128)(4,1)}), s8[4194304]{0:T(1024)(128)(4,1)S(1)}, s32[]{:S(2)}) async-start(s8[16777216]{0:T(1024)(128)(4,1)} %bitcast), calls=%async_computation | async-start | bytes 8388608
  0.9 25.4 %slice-start.1 = ((s8[16777216]{0:T(1024)(128)(4,1)}), s8[4194304]{0:T(1024)(128)(4,1)S(1)}, s32[]{:S(2)}) async-start(s8[16777216]{0:T(1024)(128)(4,1)} %bitcast), calls=%async_computation.1 | async-start | bytes 8388608
  1.0 25.4 %slice-start.2 = ((s8[16777216]{0:T(1024)(128)(4,1)}), s8[4194304]{0:T(1024)(128)(4,1)S(1)}, s32[]{:S(2)}) async-start(s8[16777216]{0:T(1024)(128)(4,1)} %bitcast), calls=%async_computation.2 | async-start | bytes 8388608
  1.0 25.4 %slice-start.3 = ((s8[16777216]{0:T(1024)(128)(4,1)}), s8[4194304]{0:T(1024)(128)(4,1)S(1)}, s32[]{:S(2)}) async-start(s8[16777216]{0:T(1024)(128)(4,1)} %bitcast), calls=%async_computation.3 | async-start | bytes 8388608
  1.0 8.9 %collective-permute-start = (bf16[4,4096]{1,0:T(4,128)(2,1)S(1)}, bf16[4,4096]{1,0:T(4,128)(2,1)S(1)}, u32[]{:S(2)}, u32[]{:S(2)}) collective-permute-start(bf16[4,4096]{1,0:T(4,128)(2,1)S(1)} %get-tuple-element.16.refs_0_), channel_id=1, source_target_pairs={{0,2},{2,0},{4,6},{6,4},{8,10},{10,8},{12,14},{14,12},{1,3},{3,1},... | collective-permute-start | bytes 98312 | tf_op jit(solution)/shard_map/ppermute | solution.py:168
  4.0 9.5 %collective-permute-start.1 = (bf16[4,4096]{1,0:T(4,128)(2,1)S(1)}, bf16[4,4096]{1,0:T(4,128)(2,1)S(1)}, u32[]{:S(2)}, u32[]{:S(2)}) collective-permute-start(bf16[4,4096]{1,0:T(4,128)(2,1)S(1)} %get-tuple-element.16.refs_0_), channel_id=1, source_target_pairs={{0,4},{2,6},{4,0},{6,2},{8,12},{10,14},{12,8},{14,10},{1,5},{3,7},... | collective-permute-start | bytes 98312 | tf_op jit(solution)/shard_map/ppermute | solution.py:168
  5.6 7.9 %collective-permute-start.2 = (bf16[4,4096]{1,0:T(4,128)(2,1)S(1)}, bf16[4,4096]{1,0:T(4,128)(2,1)S(1)}, u32[]{:S(2)}, u32[]{:S(2)}) collective-permute-start(bf16[4,4096]{1,0:T(4,128)(2,1)S(1)} %get-tuple-element.16.refs_0_), channel_id=1, source_target_pairs={{0,6},{2,4},{4,2},{6,0},{8,14},{10,12},{12,10},{14,8},{1,7},{3,5},... | collective-permute-start | bytes 98312 | tf_op jit(solution)/shard_map/ppermute | solution.py:168
  5.6 7.9 %collective-permute-start.3 = (bf16[4,4096]{1,0:T(4,128)(2,1)S(1)}, bf16[4,4096]{1,0:T(4,128)(2,1)S(1)}, u32[]{:S(2)}, u32[]{:S(2)}) collective-permute-start(bf16[4,4096]{1,0:T(4,128)(2,1)S(1)} %get-tuple-element.16.refs_0_), channel_id=1, source_target_pairs={{0,8},{2,10},{4,12},{6,14},{8,0},{10,2},{12,4},{14,6},{1,9},{3,11}... | collective-permute-start | bytes 98312 | tf_op jit(solution)/shard_map/ppermute | solution.py:168
  8.6 5.9 %collective-permute-start.4 = (bf16[4,4096]{1,0:T(4,128)(2,1)S(1)}, bf16[4,4096]{1,0:T(4,128)(2,1)S(1)}, u32[]{:S(2)}, u32[]{:S(2)}) collective-permute-start(bf16[4,4096]{1,0:T(4,128)(2,1)S(1)} %get-tuple-element.16.refs_0_), channel_id=1, source_target_pairs={{0,10},{2,8},{4,14},{6,12},{8,2},{10,0},{12,6},{14,4},{1,11},{3,9}... | collective-permute-start | bytes 98312 | tf_op jit(solution)/shard_map/ppermute | solution.py:168
  9.8 5.8 %collective-permute-start.5 = (bf16[4,4096]{1,0:T(4,128)(2,1)S(1)}, bf16[4,4096]{1,0:T(4,128)(2,1)S(1)}, u32[]{:S(2)}, u32[]{:S(2)}) collective-permute-start(bf16[4,4096]{1,0:T(4,128)(2,1)S(1)} %get-tuple-element.16.refs_0_), channel_id=1, source_target_pairs={{0,12},{2,14},{4,8},{6,10},{8,4},{10,6},{12,0},{14,2},{1,13},{3,15... | collective-permute-start | bytes 98312 | tf_op jit(solution)/shard_map/ppermute | solution.py:168
  13.4 6.6 %collective-permute-start.6 = (bf16[4,4096]{1,0:T(4,128)(2,1)S(1)}, bf16[4,4096]{1,0:T(4,128)(2,1)S(1)}, u32[]{:S(2)}, u32[]{:S(2)}) collective-permute-start(bf16[4,4096]{1,0:T(4,128)(2,1)S(1)} %get-tuple-element.16.refs_0_), channel_id=1, source_target_pairs={{0,14},{2,12},{4,10},{6,8},{8,6},{10,4},{12,2},{14,0},{1,15},{3,13... | collective-permute-start | bytes 98312 | tf_op jit(solution)/shard_map/ppermute | solution.py:168
  26.4 12.7 %copy-start.2 = (s32[4,128]{1,0:T(4,128)S(1)}, s32[4,128]{1,0:T(4,128)}, u32[]{:S(2)}) copy-start(s32[4,128]{1,0:T(4,128)} %rows_ref.1) | copy-start | bytes 6148
  26.4 12.6 %copy-start.3 = (f32[4,128]{1,0:T(4,128)S(1)}, f32[4,128]{1,0:T(4,128)}, u32[]{:S(2)}) copy-start(f32[4,128]{1,0:T(4,128)} %gates_ref.1) | copy-start | bytes 6148
  26.4 12.6 %copy-start.4 = (s32[4]{0:T(128)S(1)}, s32[4]{0:T(128)}, u32[]{:S(2)}) copy-start(s32[4]{0:T(128)} %counts_ref.1) | copy-start | bytes 52
  28.0 1.6 %collective-permute-start.7 = (bf16[32,2048]{1,0:T(8,128)(2,1)S(1)}, bf16[32,2048]{1,0:T(8,128)(2,1)S(1)}, u32[]{:S(2)}, u32[]{:S(2)}) collective-permute-start(bf16[32,2048]{1,0:T(8,128)(2,1)S(1)} %shard_map.77), channel_id=1, source_target_pairs={{0,1},{1,0},{2,3},{3,2},{4,5},{5,4},{6,7},{7,6},{8,9},{9,8},{10,11... | collective-permute-start | bytes 393224 | tf_op jit(solution)/shard_map/ppermute | solution.py:178
  29.6 7.8 %collective-permute-start.10 = (bf16[4,2048]{1,0:T(4,128)(2,1)S(1)}, bf16[4,2048]{1,0:T(4,128)(2,1)S(1)}, u32[]{:S(2)}, u32[]{:S(2)}) collective-permute-start(bf16[4,2048]{1,0:T(4,128)(2,1)S(1)} %get-tuple-element.20), channel_id=1, source_target_pairs={{0,6},{2,4},{4,2},{6,0},{8,14},{10,12},{12,10},{14,8},{1,7},{3,5},... | collective-permute-start | bytes 49160 | tf_op jit(solution)/shard_map/ppermute | solution.py:168
  29.7 8.3 %collective-permute-start.11 = (bf16[4,2048]{1,0:T(4,128)(2,1)S(1)}, bf16[4,2048]{1,0:T(4,128)(2,1)S(1)}, u32[]{:S(2)}, u32[]{:S(2)}) collective-permute-start(bf16[4,2048]{1,0:T(4,128)(2,1)S(1)} %get-tuple-element.21), channel_id=1, source_target_pairs={{0,8},{2,10},{4,12},{6,14},{8,0},{10,2},{12,4},{14,6},{1,9},{3,11}... | collective-permute-start | bytes 49160 | tf_op jit(solution)/shard_map/ppermute | solution.py:168
  30.6 9.1 %collective-permute-start.12 = (bf16[4,2048]{1,0:T(4,128)(2,1)S(1)}, bf16[4,2048]{1,0:T(4,128)(2,1)S(1)}, u32[]{:S(2)}, u32[]{:S(2)}) collective-permute-start(bf16[4,2048]{1,0:T(4,128)(2,1)S(1)} %get-tuple-element.22), channel_id=1, source_target_pairs={{0,10},{2,8},{4,14},{6,12},{8,2},{10,0},{12,6},{14,4},{1,11},{3,9}... | collective-permute-start | bytes 49160 | tf_op jit(solution)/shard_map/ppermute | solution.py:168
  32.7 7.0 %collective-permute-start.13 = (bf16[4,2048]{1,0:T(4,128)(2,1)S(1)}, bf16[4,2048]{1,0:T(4,128)(2,1)S(1)}, u32[]{:S(2)}, u32[]{:S(2)}) collective-permute-start(bf16[4,2048]{1,0:T(4,128)(2,1)S(1)} %get-tuple-element.23), channel_id=1, source_target_pairs={{0,12},{2,14},{4,8},{6,10},{8,4},{10,6},{12,0},{14,2},{1,13},{3,15... | collective-permute-start | bytes 49160 | tf_op jit(solution)/shard_map/ppermute | solution.py:168
  35.0 6.4 %collective-permute-start.14 = (bf16[4,2048]{1,0:T(4,128)(2,1)S(1)}, bf16[4,2048]{1,0:T(4,128)(2,1)S(1)}, u32[]{:S(2)}, u32[]{:S(2)}) collective-permute-start(bf16[4,2048]{1,0:T(4,128)(2,1)S(1)} %get-tuple-element.24), channel_id=1, source_target_pairs={{0,14},{2,12},{4,10},{6,8},{8,6},{10,4},{12,2},{14,0},{1,15},{3,13... | collective-permute-start | bytes 49160 | tf_op jit(solution)/shard_map/ppermute | solution.py:168
  37.4 4.0 %collective-permute-start.8 = (bf16[4,2048]{1,0:T(4,128)(2,1)S(1)}, bf16[4,2048]{1,0:T(4,128)(2,1)S(1)}, u32[]{:S(2)}, u32[]{:S(2)}) collective-permute-start(bf16[4,2048]{1,0:T(4,128)(2,1)S(1)} %get-tuple-element.18), channel_id=1, source_target_pairs={{0,2},{2,0},{4,6},{6,4},{8,10},{10,8},{12,14},{14,12},{1,3},{3,1},... | collective-permute-start | bytes 49160 | tf_op jit(solution)/shard_map/ppermute | solution.py:168
  38.0 3.7 %collective-permute-start.9 = (bf16[4,2048]{1,0:T(4,128)(2,1)S(1)}, bf16[4,2048]{1,0:T(4,128)(2,1)S(1)}, u32[]{:S(2)}, u32[]{:S(2)}) collective-permute-start(bf16[4,2048]{1,0:T(4,128)(2,1)S(1)} %get-tuple-element.19), channel_id=1, source_target_pairs={{0,4},{2,6},{4,0},{6,2},{8,12},{10,14},{12,8},{14,10},{1,5},{3,7},... | collective-permute-start | bytes 49160 | tf_op jit(solution)/shard_map/ppermute | solution.py:168

commit v5 on v4

--- a/solution.py
+++ b/solution.py
@@ -11,6 +11,7 @@
 CAP = 3
 TILE = 512
 MIB = 1 << 20
+ORDER = (0, 1, 2, 3, 7, 4, 5, 6)
 AHEAD = 20_000_000_000
 HBM = pl.BlockSpec(memory_space=pltpu.HBM)
 VMEM = pl.BlockSpec(memory_space=pltpu.VMEM)
@@ -43,7 +44,7 @@
     position = lax.broadcasted_iota(jnp.int32, (total, slots), 1)
     own = lax.axis_index("exp")
     token = own * count + lax.rem(line, count)
-    expert = (own ^ (line // count)) // per_expert
+    expert = (own // per_expert) ^ (line // count)
     found = jnp.zeros((total, slots), jnp.float32)
     for e in range(experts):
         rows = rows_ref[pl.ds(e, 1), :]
@@ -55,19 +56,38 @@
 def route(block_counts, block_rows, row_gates, sources, count):
     return pl.pallas_call(
         functools.partial(route_kernel, count, sources // block_rows.shape[0]),
-        out_shape=jax.ShapeDtypeStruct((sources * count, 128), jnp.float32),
+        out_shape=jax.ShapeDtypeStruct((block_rows.shape[0] * count, 128), jnp.float32),
         in_specs=[SMEM, VMEM, VMEM],
         out_specs=VMEM,
         compiler_params=pltpu.CompilerParams(vmem_limit_bytes=2 * MIB),
     )(block_counts, block_rows, row_gates)
 
 
-def hidden_kernel(sources, *refs):
-    pieces = refs[:sources]
-    wg_ref, wu_ref, h_out, wide, x_ref = refs[sources:]
-    token_count = pieces[0].shape[0]
-    for k, piece in enumerate(pieces):
-        wide[pl.ds(k * token_count, token_count), :] = piece[...].astype(jnp.float32)
+def pack_kernel(side_ref, tokens_ref, last_ref, *refs):
+    out_ref = refs[-1]
+    out_ref[0] = jnp.where(side_ref[0] == 0, tokens_ref[...], last_ref[...])
+    for r, ref in enumerate(refs[:-1]):
+        out_ref[r + 1] = ref[...]
+
+
+def pack(side, tokens, last, pieces):
+    return pl.pallas_call(
+        pack_kernel,
+        out_shape=jax.ShapeDtypeStruct((1 + len(pieces), *tokens.shape), tokens.dtype),
+        in_specs=[SMEM] + [VMEM] * (2 + len(pieces)),
+        out_specs=VMEM,
+        compiler_params=pltpu.CompilerParams(vmem_limit_bytes=2 * MIB),
+    )(in_smem(side), tokens, last, *pieces)
+
+
+def hidden_kernel(side_ref, mine_ref, got_ref, wg_ref, wu_ref, h_out, wide, x_ref):
+    sets, count, _ = mine_ref.shape
+    first = side_ref[0] == 0
+    for j in range(sets):
+        mine = mine_ref[j].astype(jnp.float32)
+        got = got_ref[j].astype(jnp.float32)
+        wide[pl.ds(j * count, count), :] = jnp.where(first, mine, got)
+        wide[pl.ds((sets + j) * count, count), :] = jnp.where(first, got, mine)
     x_ref[...] = wide[...].astype(jnp.bfloat16)
 
     @pl.loop(0, wg_ref.shape[1] // TILE)
@@ -78,14 +98,13 @@
         h_out[:, cols] = (gate / (1.0 + jnp.exp(-gate)) * up).astype(jnp.bfloat16)
 
 
-def hidden_rows(pieces, wg, wu):
-    sources = len(pieces)
-    total = sources * pieces[0].shape[0]
+def hidden_rows(side, mine, got, wg, wu):
+    total = 2 * mine.shape[0] * mine.shape[1]
     depth, width = wg.shape
     return pl.pallas_call(
-        functools.partial(hidden_kernel, sources),
+        hidden_kernel,
         out_shape=jax.ShapeDtypeStruct((total, width), jnp.bfloat16),
-        in_specs=[VMEM] * (sources + 2),
+        in_specs=[SMEM] + [VMEM] * 4,
         out_specs=VMEM,
         scratch_shapes=[
             pltpu.VMEM((total, depth), jnp.float32),
@@ -93,9 +112,13 @@
         ],
         compiler_params=pltpu.CompilerParams(vmem_limit_bytes=2 * MIB),
         cost_estimate=pl.CostEstimate(
-            flops=4 * total * depth * width, bytes_accessed=0, transcendentals=total * width
+            flops=AHEAD, bytes_accessed=0, transcendentals=total * width
         ),
-    )(*pieces, in_vmem(wg), in_vmem(wu))
+    )(in_smem(side), mine, got, in_vmem(wg), in_vmem(wu))
+
+
+def in_smem(x):
+    return pltpu.with_memory_space_constraint(x, pltpu.SMEM)
 
 
 def in_vmem(x):
@@ -122,28 +145,47 @@
         out_specs=VMEM,
         compiler_params=pltpu.CompilerParams(vmem_limit_bytes=2 * MIB),
         cost_estimate=pl.CostEstimate(flops=2 * rows * depth * half, bytes_accessed=0, transcendentals=0),
-    )(pltpu.with_memory_space_constraint(side, pltpu.SMEM), hidden, in_vmem(wd))
-
-
-def merge_kernel(keep_ref, got_ref, own_ref, *out_refs):
+    )(in_smem(side), hidden, in_vmem(wd))
+
+
+def near_kernel(keep_ref, got_ref, even_ref, odd_ref):
     both = keep_ref[...] + got_ref[...].astype(jnp.float32)
-    count = own_ref.shape[0]
-    own_ref[...] = both[:count]
-    for k, out_ref in enumerate(out_refs):
-        out_ref[...] = both[(k + 1) * count : (k + 2) * count].astype(out_ref.dtype)
-
-
-def merge(keep, got, sources):
+    pairs, count, _ = odd_ref.shape
+    for at, k in enumerate(ORDER):
+        rows = both[at * count : (at + 1) * count]
+        if k % 2:
+            odd_ref[k // 2] = rows.astype(odd_ref.dtype)
+        else:
+            even_ref[k // 2] = rows
+
+
+def near(keep, got):
     rows, width = keep.shape
-    count = rows // sources
-    return pl.pallas_call(
-        merge_kernel,
+    shape = (len(ORDER) // 2, rows // len(ORDER), width)
+    return pl.pallas_call(
+        near_kernel,
+        out_shape=(jax.ShapeDtypeStruct(shape, jnp.float32), jax.ShapeDtypeStruct(shape, jnp.bfloat16)),
+        in_specs=[VMEM, VMEM],
+        out_specs=(VMEM, VMEM),
+        compiler_params=pltpu.CompilerParams(vmem_limit_bytes=2 * MIB),
+    )(keep, got)
+
+
+def far_kernel(even_ref, got_ref, own_ref, *out_refs):
+    for j, out_ref in enumerate((own_ref, *out_refs)):
+        out_ref[...] = (even_ref[j] + got_ref[j].astype(jnp.float32)).astype(out_ref.dtype)
+
+
+def far(even, got):
+    sets, count, width = even.shape
+    return pl.pallas_call(
+        far_kernel,
         out_shape=(jax.ShapeDtypeStruct((count, width), jnp.float32),)
-        + (jax.ShapeDtypeStruct((count, width), jnp.bfloat16),) * (sources - 1),
+        + (jax.ShapeDtypeStruct((count, width), jnp.bfloat16),) * (sets - 1),
         in_specs=[VMEM, VMEM],
-        out_specs=(VMEM,) * sources,
-        compiler_params=pltpu.CompilerParams(vmem_limit_bytes=2 * MIB),
-    )(keep, got)
+        out_specs=(VMEM,) * sets,
+        compiler_params=pltpu.CompilerParams(vmem_limit_bytes=2 * MIB),
+    )(even, got)
 
 
 def sum_kernel(gates_ref, *refs):
@@ -168,16 +210,31 @@
     return lax.ppermute(x, "exp", [(i, i ^ k) for i in range(sources)])
 
 
+def fetched(x, first, second, sources):
+    pairs = []
+    for side, k in enumerate((first, second)):
+        if k is not None:
+            pairs += [(2 * i + side, 2 * (i ^ k) + side) for i in range(sources)]
+    return lax.ppermute(x, ("exp", "hid"), pairs)
+
+
+def swap_cores(x):
+    return lax.ppermute(x, "hid", [(0, 1), (1, 0)])
+
+
 def local(tokens, w_gate, w_up, w_down, block_counts, block_rows, row_gates):
     sources = lax.axis_size("exp")
     tokens, side = pass_on(tokens)
-    pieces = [tokens] + [swapped(tokens, k, sources) for k in range(1, sources)]
-    hidden = hidden_rows(pieces, w_gate, w_up)
+    half = len(ORDER) // 2
+    pieces = [fetched(tokens, ORDER[b], ORDER[half + b], sources) for b in range(1, half)]
+    last = fetched(tokens, None, ORDER[half], sources)
+    mine = pack(side, tokens, last, pieces)
+    hidden = hidden_rows(side, mine, swap_cores(mine), w_gate, w_up)
     send = down_half(side, hidden, w_down, True, jnp.bfloat16)
     keep = down_half(side, hidden, w_down, False, jnp.float32)
-    got = lax.ppermute(send, "hid", [(0, 1), (1, 0)])
-    own, *outgoing = merge(keep, got, sources)
-    returned = [swapped(piece, k + 1, sources) for k, piece in enumerate(outgoing)]
+    even, odd = near(keep, swap_cores(send))
+    own, *outgoing = far(even, swapped(odd, 1, sources))
+    returned = [swapped(piece, 2 * (j + 1), sources) for j, piece in enumerate(outgoing)]
     gates = route(block_counts, block_rows, row_gates, sources, tokens.shape[0])
     return weighted_sum(gates, own, returned)
 
@@ -248,9 +305,13 @@
 
 
 def solution(mesh):
-    sources = mesh.shape["exp"]
+    small = mesh.shape["exp"] == len(ORDER) and mesh.shape["hid"] == 2
+
+    def chosen(*args):
+        return (local if small and args[5].shape[0] * 2 == len(ORDER) else local_wide)(*args)
+
     return jax.shard_map(
-        local if sources in (4, 8, 16) and mesh.shape["hid"] == 2 else local_wide,
+        chosen,
         mesh=mesh,
         in_specs=(
             P(("grp", "exp"), None),

time: 42.6 us -> 38.8 us (0.911)
  starting transfers between devices: 21.9 us -> 16.4 us
  waiting for transfers between devices: 8.58 us -> 10.3 us
    ppermute x14 -> x4, starting transfers between devices: 21.9 us -> 6 us  [swapped(): return lax.ppermute(x, 'exp', [(i, i ^ k) for i in range(sources)])]
    ppermute x1 -> x6, starting transfers between devices: 0.01 us -> 10.4 us  [the longest x4 5.38 us: fetched(): return lax.ppermute(x, ('exp', 'hid'), pairs)]
    ppermute x1 -> x6, waiting for transfers between devices: 0.01 us -> 5.8 us  [the longest x4 4.81 us: fetched(): return lax.ppermute(x, ('exp', 'hid'), pairs)]
    ppermute x14 -> x4, waiting for transfers between devices: 8.58 us -> 4.47 us  [swapped(): return lax.ppermute(x, 'exp', [(i, i ^ k) for i in range(sources)])]
    pallas_call x2 -> x4, Pallas kernels: 6.35 us -> 6.4 us  [the longest x1 6.31 us: hidden_rows(): pl.pallas_call(hidden_kernel, out_shape=jax.ShapeDtypeStruct((total, widt...]
  transfers between devices with their start and end apart: 15 -> 10, of which waited for: 5 -> 6; matrix products, arithmetic and copies ran while one was open for 0% -> 0% of each run, Pallas kernels for 5% -> 6%
where the time goes in v5:
time: 38.8 us; the launch traced here: 38.6 us
  starting transfers between devices  16.4 us (42%)
  Pallas kernels  11.8 us (30%)
  waiting for transfers between devices  10.3 us (27%)
    pallas_call x1, Pallas kernels, hidden_rows(): pl.pallas_call(hidden_kernel, out_shape=jax.ShapeDtypeStruct((total, widt...  6.31 us
    ppermute x4, starting transfers between devices, swapped(): return lax.ppermute(x, 'exp', [(i, i ^ k) for i in range(sources)])  6 us
    ppermute x4, starting transfers between devices, fetched(): return lax.ppermute(x, ('exp', 'hid'), pairs)  5.38 us
    ppermute x2, starting transfers between devices, swap_cores(): return lax.ppermute(x, 'hid', [(0, 1), (1, 0)])  5.06 us
    ppermute x4, waiting for transfers between devices, fetched(): return lax.ppermute(x, ('exp', 'hid'), pairs)  4.81 us
    ppermute x4, waiting for transfers between devices, swapped(): return lax.ppermute(x, 'exp', [(i, i ^ k) for i in range(sources)])  4.47 us
    pallas_call x2, Pallas kernels, down_half(): pl.pallas_call(functools.partial(down_kernel, other), out_shape=jax.Shape...  3.12 us
    ppermute x2, waiting for transfers between devices, swap_cores(): return lax.ppermute(x, 'hid', [(0, 1), (1, 0)])  0.99 us
  transfers between devices with their start and end apart: 10, of which 6 were waited for; matrix products, arithmetic and copies ran while one was open for 0% of the time, Pallas kernels for 6%

profile of v5, /device:TPU:0, one launch (start us, length us, event | category | flops | bytes accessed | tf_op | source)
XLA Modules:
  0.0 38.6 jit_solution(4258059752335616787)
XLA Ops:
  0.0 0.0 copy-start.3
  0.0 0.0 copy-start.4
  0.0 0.9 %shard_map.74 = (bf16[4,4096]{1,0:T(4,128)(2,1)S(1)}, s32[1]{0:T(128)S(4)}) custom-call(bf16[4,4096]{1,0:T(4,128)(2,1)} %tokens_ref.1), custom_call_target="tpu_custom_call" | custom-call | flops 20000000000 | tf_op jit(solution)/shard_map/pallas_call | solution.py:29
  0.9 0.8 %collective-permute-start = (bf16[4,4096]{1,0:T(4,128)(2,1)S(1)}, bf16[4,4096]{1,0:T(4,128)(2,1)S(1)}, u32[]{:S(2)}, u32[]{:S(2)}) collective-permute-start(bf16[4,4096]{1,0:T(4,128)(2,1)S(1)} %get-tuple-element.14.tokens_ref), channel_id=1, source_target_pairs={{1,15},{3,13},{5,11},{7,9},{9,7},{11,5},{13,3},{15,1},{17,31},{19,... | collective-permute-start | bytes 98312 | tf_op jit(solution)/shard_map/ppermute | solution.py:218
  1.7 3.0 %collective-permute-start.1 = (bf16[4,4096]{1,0:T(4,128)(2,1)S(1)}, bf16[4,4096]{1,0:T(4,128)(2,1)S(1)}, u32[]{:S(2)}, u32[]{:S(2)}) collective-permute-start(bf16[4,4096]{1,0:T(4,128)(2,1)S(1)} %get-tuple-element.14.tokens_ref), channel_id=1, source_target_pairs={{0,2},{2,0},{4,6},{6,4},{8,10},{10,8},{12,14},{14,12},{1,9},{3,11}... | collective-permute-start | bytes 98312 | tf_op jit(solution)/shard_map/ppermute | solution.py:218
  4.7 1.6 %collective-permute-start.2 = (bf16[4,4096]{1,0:T(4,128)(2,1)S(1)}, bf16[4,4096]{1,0:T(4,128)(2,1)S(1)}, u32[]{:S(2)}, u32[]{:S(2)}) collective-permute-start(bf16[4,4096]{1,0:T(4,128)(2,1)S(1)} %get-tuple-element.14.tokens_ref), channel_id=1, source_target_pairs={{0,4},{2,6},{4,0},{6,2},{8,12},{10,14},{12,8},{14,10},{1,11},{3,9}... | collective-permute-start | bytes 98312 | tf_op jit(solution)/shard_map/ppermute | solution.py:218
  6.3 0.0 collective-permute-start.3
  6.3 0.0 collective-permute-done.last_ref
  6.3 0.3 collective-permute-done.1.refs_0_
  6.6 2.0 %collective-permute-done.2.refs_1_ = bf16[4,4096]{1,0:T(4,128)(2,1)S(1)} collective-permute-done((bf16[4,4096]{1,0:T(4,128)(2,1)S(1)}, bf16[4,4096]{1,0:T(4,128)(2,1)S(1)}, u32[]{:S(2)}, u32[]{:S(2)}) %collective-permute-start.2) | collective-permute-done | bytes 32800 | tf_op jit(solution)/shard_map/ppermute | solution.py:218
  8.7 2.5 %collective-permute-done.3.refs_2_ = bf16[4,4096]{1,0:T(4,128)(2,1)S(1)} collective-permute-done((bf16[4,4096]{1,0:T(4,128)(2,1)S(1)}, bf16[4,4096]{1,0:T(4,128)(2,1)S(1)}, u32[]{:S(2)}, u32[]{:S(2)}) %collective-permute-start.3) | collective-permute-done | bytes 32800 | tf_op jit(solution)/shard_map/ppermute | solution.py:218
  11.1 0.0 slice-start
  11.1 0.0 slice-start.1
  11.2 0.0 slice-start.2
  11.2 0.0 slice-start.3
  11.2 4.7 %collective-permute-start.4 = (bf16[4,4,4096]{2,1,0:T(4,128)(2,1)S(1)}, bf16[4,4,4096]{2,1,0:T(4,128)(2,1)S(1)}, u32[]{:S(2)}, u32[]{:S(2)}) collective-permute-start(bf16[4,4,4096]{2,1,0:T(4,128)(2,1)S(1)} %shard_map.75.mine_ref), channel_id=1, source_target_pairs={{0,1},{1,0},{2,3},{3,2},{4,5},{5,4},{6,7},{7,6},{8,9},{9,8},{10,11... | collective-permute-start | bytes 393224 | tf_op jit(solution)/shard_map/ppermute | solution.py:222
  15.9 1.0 %collective-permute-done.4.got_ref = bf16[4,4,4096]{2,1,0:T(4,128)(2,1)S(1)} collective-permute-done((bf16[4,4,4096]{2,1,0:T(4,128)(2,1)S(1)}, bf16[4,4,4096]{2,1,0:T(4,128)(2,1)S(1)}, u32[]{:S(2)}, u32[]{:S(2)}) %collective-permute-start.4) | collective-permute-done | bytes 131104 | tf_op jit(solution)/shard_map/ppermute | solution.py:222
  16.8 0.0 copy-done.3
  16.8 0.0 copy-done.4
  16.8 6.3 %shard_map.76.h_ref = bf16[32,2048]{1,0:T(8,128)(2,1)S(1)} custom-call(s32[1]{0:T(128)S(4)} %get-tuple-element.13.side_ref, bf16[4,4,4096]{2,1,0:T(4,128)(2,1)S(1)} %shard_map.75.mine_ref, bf16[4,4,4096]{2,1,0:T(4,128)(2,1)S(1)} %collective-permute-done.4.got_ref, bf16[4096,2048]{1,0:T(8,128)(2,1)S(1)} %copy-done.3, bf16[4096,2048]{1,0:T(8,128)(2,1)S(1)} %copy-done.4), custom_call_target="tpu_custom_call" | custom-call | flops 20000000000 | tf_op jit(solution)/shard_map/pallas_call | solution.py:104
  23.2 0.0 slice-done
  23.2 0.0 slice-done.1
  23.2 0.0 slice-done.2
  23.2 0.0 slice-done.3
  23.2 0.0 copy-start
  23.2 0.0 copy-start.1
  23.2 0.0 copy-start.2
  23.2 1.6 %shard_map.78 = bf16[32,2048]{1,0:T(8,128)(2,1)S(1)} custom-call(s32[1]{0:T(128)S(4)} %get-tuple-element.13.side_ref, bf16[32,2048]{1,0:T(8,128)(2,1)S(1)} %shard_map.76.h_ref, bf16[2048,4096]{1,0:T(8,128)(2,1)S(1)} %bitcast.1), custom_call_target="tpu_custom_call" | custom-call | flops 268435456 | tf_op jit(solution)/shard_map/pallas_call | solution.py:141
  24.8 0.4 collective-permute-start.5
  25.2 1.6 %shard_map.77.keep_ref = f32[32,2048]{1,0:T(8,128)S(1)} custom-call(s32[1]{0:T(128)S(4)} %get-tuple-element.13.side_ref, bf16[32,2048]{1,0:T(8,128)(2,1)S(1)} %shard_map.76.h_ref, bf16[2048,4096]{1,0:T(8,128)(2,1)S(1)} %bitcast.1), custom_call_target="tpu_custom_call" | custom-call | flops 268435456 | tf_op jit(solution)/shard_map/pallas_call | solution.py:141
  26.7 0.0 collective-permute-done.5.got_ref
  26.7 0.1 shard_map.79
  26.8 1.6 %collective-permute-start.6 = (bf16[4,4,2048]{2,1,0:T(4,128)(2,1)S(1)}, bf16[4,4,2048]{2,1,0:T(4,128)(2,1)S(1)}, u32[]{:S(2)}, u32[]{:S(2)}) collective-permute-start(bf16[4,4,2048]{2,1,0:T(4,128)(2,1)S(1)} %get-tuple-element.16), channel_id=1, source_target_pairs={{0,2},{2,0},{4,6},{6,4},{8,10},{10,8},{12,14},{14,12},{1,3},{3,1},... | collective-permute-start | bytes 196616 | tf_op jit(solution)/shard_map/ppermute | solution.py:210
  28.4 2.8 %collective-permute-done.6.got_ref = bf16[4,4,2048]{2,1,0:T(4,128)(2,1)S(1)} collective-permute-done((bf16[4,4,2048]{2,1,0:T(4,128)(2,1)S(1)}, bf16[4,4,2048]{2,1,0:T(4,128)(2,1)S(1)}, u32[]{:S(2)}, u32[]{:S(2)}) %collective-permute-start.6) | collective-permute-done | bytes 65568 | tf_op jit(solution)/shard_map/ppermute | solution.py:210
  31.2 0.1 collective-permute-start.7
  31.2 1.2 %collective-permute-start.8 = (bf16[4,2048]{1,0:T(4,128)(2,1)S(1)}, bf16[4,2048]{1,0:T(4,128)(2,1)S(1)}, u32[]{:S(2)}, u32[]{:S(2)}) collective-permute-start(bf16[4,2048]{1,0:T(4,128)(2,1)S(1)} %get-tuple-element.19), channel_id=1, source_target_pairs={{0,8},{2,10},{4,12},{6,14},{8,0},{10,2},{12,4},{14,6},{1,9},{3,11}... | collective-permute-start | bytes 49160 | tf_op jit(solution)/shard_map/ppermute | solution.py:210
  32.4 3.2 %collective-permute-start.9 = (bf16[4,2048]{1,0:T(4,128)(2,1)S(1)}, bf16[4,2048]{1,0:T(4,128)(2,1)S(1)}, u32[]{:S(2)}, u32[]{:S(2)}) collective-permute-start(bf16[4,2048]{1,0:T(4,128)(2,1)S(1)} %get-tuple-element.20), channel_id=1, source_target_pairs={{0,12},{2,14},{4,8},{6,10},{8,4},{10,6},{12,0},{14,2},{1,13},{3,15... | collective-permute-start | bytes 49160 | tf_op jit(solution)/shard_map/ppermute | solution.py:210
  35.6 0.0 copy-done
  35.6 0.0 copy-done.1
  35.6 0.0 copy-done.2
  35.6 0.6 %shard_map.73.gates_ref = f32[16,128]{1,0:T(8,128)S(1)} custom-call(s32[4]{0:T(128)S(1)} %copy-done.2, s32[4,128]{1,0:T(4,128)S(1)} %copy-done, f32[4,128]{1,0:T(4,128)S(1)} %copy-done.1), custom_call_target="tpu_custom_call" | custom-call | tf_op jit(solution)/shard_map/pallas_call | solution.py:57
  36.3 0.0 collective-permute-done.7.refs_1_
  36.3 0.0 collective-permute-done.8.refs_2_
  36.3 1.7 %collective-permute-done.9.refs_3_ = bf16[4,2048]{1,0:T(4,128)(2,1)S(1)} collective-permute-done((bf16[4,2048]{1,0:T(4,128)(2,1)S(1)}, bf16[4,2048]{1,0:T(4,128)(2,1)S(1)}, u32[]{:S(2)}, u32[]{:S(2)}) %collective-permute-start.9) | collective-permute-done | bytes 16416 | tf_op jit(solution)/shard_map/ppermute | solution.py:210
  38.0 0.7 %shard_map.81 = bf16[4,2048]{1,0:T(4,128)(2,1)} custom-call(f32[16,128]{1,0:T(8,128)S(1)} %shard_map.73.gates_ref, f32[4,2048]{1,0:T(4,128)S(1)} %get-tuple-element.17.refs_0_, bf16[4,2048]{1,0:T(4,128)(2,1)S(1)} %collective-permute-done.7.refs_1_, bf16[4,2048]{1,0:T(4,128)(2,1)S(1)} %collective-permute-done.8.refs_2_, ...), custom_call_target="tpu_custom_call" | custom-call | tf_op jit(solution)/shard_map/pallas_call | solution.py:200
  (3 shorter events, 0.0 us)
Async XLA Ops:
  0.0 16.8 %copy-start.3 = (bf16[4096,2048]{1,0:T(8,128)(2,1)S(1)}, bf16[4096,2048]{1,0:T(8,128)(2,1)}, u32[]{:S(2)}) copy-start(bf16[4096,2048]{1,0:T(8,128)(2,1)} %wg_ref.1) | copy-start | bytes 50331652
  0.0 16.8 %copy-start.4 = (bf16[4096,2048]{1,0:T(8,128)(2,1)S(1)}, bf16[4096,2048]{1,0:T(8,128)(2,1)}, u32[]{:S(2)}) copy-start(bf16[4096,2048]{1,0:T(8,128)(2,1)} %wu_ref.1) | copy-start | bytes 50331652
  0.9 5.4 %collective-permute-start = (bf16[4,4096]{1,0:T(4,128)(2,1)S(1)}, bf16[4,4096]{1,0:T(4,128)(2,1)S(1)}, u32[]{:S(2)}, u32[]{:S(2)}) collective-permute-start(bf16[4,4096]{1,0:T(4,128)(2,1)S(1)} %get-tuple-element.14.tokens_ref), channel_id=1, source_target_pairs={{1,15},{3,13},{5,11},{7,9},{9,7},{11,5},{13,3},{15,1},{17,31},{19,... | collective-permute-start | bytes 98312 | tf_op jit(solution)/shard_map/ppermute | solution.py:218
  1.7 4.9 %collective-permute-start.1 = (bf16[4,4096]{1,0:T(4,128)(2,1)S(1)}, bf16[4,4096]{1,0:T(4,128)(2,1)S(1)}, u32[]{:S(2)}, u32[]{:S(2)}) collective-permute-start(bf16[4,4096]{1,0:T(4,128)(2,1)S(1)} %get-tuple-element.14.tokens_ref), channel_id=1, source_target_pairs={{0,2},{2,0},{4,6},{6,4},{8,10},{10,8},{12,14},{14,12},{1,9},{3,11}... | collective-permute-start | bytes 98312 | tf_op jit(solution)/shard_map/ppermute | solution.py:218
  4.7 3.9 %collective-permute-start.2 = (bf16[4,4096]{1,0:T(4,128)(2,1)S(1)}, bf16[4,4096]{1,0:T(4,128)(2,1)S(1)}, u32[]{:S(2)}, u32[]{:S(2)}) collective-permute-start(bf16[4,4096]{1,0:T(4,128)(2,1)S(1)} %get-tuple-element.14.tokens_ref), channel_id=1, source_target_pairs={{0,4},{2,6},{4,0},{6,2},{8,12},{10,14},{12,8},{14,10},{1,11},{3,9}... | collective-permute-start | bytes 98312 | tf_op jit(solution)/shard_map/ppermute | solution.py:218
  6.3 4.8 %collective-permute-start.3 = (bf16[4,4096]{1,0:T(4,128)(2,1)S(1)}, bf16[4,4096]{1,0:T(4,128)(2,1)S(1)}, u32[]{:S(2)}, u32[]{:S(2)}) collective-permute-start(bf16[4,4096]{1,0:T(4,128)(2,1)S(1)} %get-tuple-element.14.tokens_ref), channel_id=1, source_target_pairs={{0,6},{2,4},{4,2},{6,0},{8,14},{10,12},{12,10},{14,8},{1,13},{3,15... | collective-permute-start | bytes 98312 | tf_op jit(solution)/shard_map/ppermute | solution.py:218
  11.1 12.0 %slice-start = ((s8[16777216]{0:T(1024)(128)(4,1)}), s8[4194304]{0:T(1024)(128)(4,1)S(1)}, s32[]{:S(2)}) async-start(s8[16777216]{0:T(1024)(128)(4,1)} %bitcast), calls=%async_computation | async-start | bytes 8388608
  11.1 12.0 %slice-start.1 = ((s8[16777216]{0:T(1024)(128)(4,1)}), s8[4194304]{0:T(1024)(128)(4,1)S(1)}, s32[]{:S(2)}) async-start(s8[16777216]{0:T(1024)(128)(4,1)} %bitcast), calls=%async_computation.1 | async-start | bytes 8388608
  11.2 12.0 %slice-start.2 = ((s8[16777216]{0:T(1024)(128)(4,1)}), s8[4194304]{0:T(1024)(128)(4,1)S(1)}, s32[]{:S(2)}) async-start(s8[16777216]{0:T(1024)(128)(4,1)} %bitcast), calls=%async_computation.2 | async-start | bytes 8388608
  11.2 12.0 %slice-start.3 = ((s8[16777216]{0:T(1024)(128)(4,1)}), s8[4194304]{0:T(1024)(128)(4,1)S(1)}, s32[]{:S(2)}) async-start(s8[16777216]{0:T(1024)(128)(4,1)} %bitcast), calls=%async_computation.3 | async-start | bytes 8388608
  11.2 5.7 %collective-permute-start.4 = (bf16[4,4,4096]{2,1,0:T(4,128)(2,1)S(1)}, bf16[4,4,4096]{2,1,0:T(4,128)(2,1)S(1)}, u32[]{:S(2)}, u32[]{:S(2)}) collective-permute-start(bf16[4,4,4096]{2,1,0:T(4,128)(2,1)S(1)} %shard_map.75.mine_ref), channel_id=1, source_target_pairs={{0,1},{1,0},{2,3},{3,2},{4,5},{5,4},{6,7},{7,6},{8,9},{9,8},{10,11... | collective-permute-start | bytes 393224 | tf_op jit(solution)/shard_map/ppermute | solution.py:222
  23.2 12.4 %copy-start = (s32[4,128]{1,0:T(4,128)S(1)}, s32[4,128]{1,0:T(4,128)}, u32[]{:S(2)}) copy-start(s32[4,128]{1,0:T(4,128)} %rows_ref.1) | copy-start | bytes 6148
  23.2 12.4 %copy-start.1 = (f32[4,128]{1,0:T(4,128)S(1)}, f32[4,128]{1,0:T(4,128)}, u32[]{:S(2)}) copy-start(f32[4,128]{1,0:T(4,128)} %gates_ref.1) | copy-start | bytes 6148
  23.2 12.4 %copy-start.2 = (s32[4]{0:T(128)S(1)}, s32[4]{0:T(128)}, u32[]{:S(2)}) copy-start(s32[4]{0:T(128)} %counts_ref.1) | copy-start | bytes 52
  24.8 1.9 %collective-permute-start.5 = (bf16[32,2048]{1,0:T(8,128)(2,1)S(1)}, bf16[32,2048]{1,0:T(8,128)(2,1)S(1)}, u32[]{:S(2)}, u32[]{:S(2)}) collective-permute-start(bf16[32,2048]{1,0:T(8,128)(2,1)S(1)} %shard_map.78), channel_id=1, source_target_pairs={{0,1},{1,0},{2,3},{3,2},{4,5},{5,4},{6,7},{7,6},{8,9},{9,8},{10,11... | collective-permute-start | bytes 393224 | tf_op jit(solution)/shard_map/ppermute | solution.py:222
  26.8 4.3 %collective-permute-start.6 = (bf16[4,4,2048]{2,1,0:T(4,128)(2,1)S(1)}, bf16[4,4,2048]{2,1,0:T(4,128)(2,1)S(1)}, u32[]{:S(2)}, u32[]{:S(2)}) collective-permute-start(bf16[4,4,2048]{2,1,0:T(4,128)(2,1)S(1)} %get-tuple-element.16), channel_id=1, source_target_pairs={{0,2},{2,0},{4,6},{6,4},{8,10},{10,8},{12,14},{14,12},{1,3},{3,1},... | collective-permute-start | bytes 196616 | tf_op jit(solution)/shard_map/ppermute | solution.py:210
  31.2 5.1 %collective-permute-start.7 = (bf16[4,2048]{1,0:T(4,128)(2,1)S(1)}, bf16[4,2048]{1,0:T(4,128)(2,1)S(1)}, u32[]{:S(2)}, u32[]{:S(2)}) collective-permute-start(bf16[4,2048]{1,0:T(4,128)(2,1)S(1)} %get-tuple-element.18), channel_id=1, source_target_pairs={{0,4},{2,6},{4,0},{6,2},{8,12},{10,14},{12,8},{14,10},{1,5},{3,7},... | collective-permute-start | bytes 49160 | tf_op jit(solution)/shard_map/ppermute | solution.py:210
  31.2 5.0 %collective-permute-start.8 = (bf16[4,2048]{1,0:T(4,128)(2,1)S(1)}, bf16[4,2048]{1,0:T(4,128)(2,1)S(1)}, u32[]{:S(2)}, u32[]{:S(2)}) collective-permute-start(bf16[4,2048]{1,0:T(4,128)(2,1)S(1)} %get-tuple-element.19), channel_id=1, source_target_pairs={{0,8},{2,10},{4,12},{6,14},{8,0},{10,2},{12,4},{14,6},{1,9},{3,11}... | collective-permute-start | bytes 49160 | tf_op jit(solution)/shard_map/ppermute | solution.py:210
  32.4 5.5 %collective-permute-start.9 = (bf16[4,2048]{1,0:T(4,128)(2,1)S(1)}, bf16[4,2048]{1,0:T(4,128)(2,1)S(1)}, u32[]{:S(2)}, u32[]{:S(2)}) collective-permute-start(bf16[4,2048]{1,0:T(4,128)(2,1)S(1)} %get-tuple-element.20), channel_id=1, source_target_pairs={{0,12},{2,14},{4,8},{6,10},{8,4},{10,6},{12,0},{14,2},{1,13},{3,15... | collective-permute-start | bytes 49160 | tf_op jit(solution)/shard_map/ppermute | solution.py:210

commit v6 on v5

--- a/solution.py
+++ b/solution.py
@@ -11,30 +11,48 @@
 CAP = 3
 TILE = 512
 MIB = 1 << 20
-ORDER = (0, 1, 2, 3, 7, 4, 5, 6)
+SOURCES = 8
+GATE = 2_000_000_000
+UP = 2_000_000_000
 AHEAD = 20_000_000_000
 HBM = pl.BlockSpec(memory_space=pltpu.HBM)
 VMEM = pl.BlockSpec(memory_space=pltpu.VMEM)
 SMEM = pl.BlockSpec(memory_space=pltpu.SMEM)
 
 
-def pass_kernel(tokens_ref, out_ref, side_ref, sem):
-    copy = pltpu.make_async_copy(tokens_ref, out_ref, sem)
+def in_hbm(x):
+    return pltpu.with_memory_space_constraint(x, pltpu.HBM)
+
+
+def in_smem(x):
+    return pltpu.with_memory_space_constraint(x, pltpu.SMEM)
+
+
+def in_vmem(x):
+    return pltpu.with_memory_space_constraint(x, pltpu.VMEM)
+
+
+def take_kernel(tokens_ref, half_ref, side_ref, sem):
+    side = lax.axis_index("hid")
+    width = half_ref.shape[1]
+    columns = pl.ds(pl.multiple_of(side * width, width), width)
+    copy = pltpu.make_async_copy(tokens_ref.at[:, columns], half_ref, sem)
     copy.start()
-    side_ref[0] = lax.axis_index("hid")
+    side_ref[0] = side
     copy.wait()
 
 
-def pass_on(tokens):
-    return pl.pallas_call(
-        pass_kernel,
-        out_shape=(jax.ShapeDtypeStruct(tokens.shape, tokens.dtype), pltpu.SMEM((1,), jnp.int32)),
+def take_half(tokens):
+    count, width = tokens.shape
+    return pl.pallas_call(
+        take_kernel,
+        out_shape=(jax.ShapeDtypeStruct((count, width // 2), tokens.dtype), pltpu.SMEM((1,), jnp.int32)),
         in_specs=[HBM],
         out_specs=(VMEM, SMEM),
         scratch_shapes=[pltpu.SemaphoreType.DMA],
         compiler_params=pltpu.CompilerParams(vmem_limit_bytes=2 * MIB),
         cost_estimate=pl.CostEstimate(flops=AHEAD, bytes_accessed=0, transcendentals=0),
-    )(pltpu.with_memory_space_constraint(tokens, pltpu.HBM))
+    )(in_hbm(tokens))
 
 
 def route_kernel(count, per_expert, counts_ref, rows_ref, gates_ref, out_ref):
@@ -63,66 +81,75 @@
     )(block_counts, block_rows, row_gates)
 
 
-def pack_kernel(side_ref, tokens_ref, last_ref, *refs):
+def stack_kernel(*refs):
     out_ref = refs[-1]
-    out_ref[0] = jnp.where(side_ref[0] == 0, tokens_ref[...], last_ref[...])
-    for r, ref in enumerate(refs[:-1]):
-        out_ref[r + 1] = ref[...]
-
-
-def pack(side, tokens, last, pieces):
-    return pl.pallas_call(
-        pack_kernel,
-        out_shape=jax.ShapeDtypeStruct((1 + len(pieces), *tokens.shape), tokens.dtype),
-        in_specs=[SMEM] + [VMEM] * (2 + len(pieces)),
-        out_specs=VMEM,
-        compiler_params=pltpu.CompilerParams(vmem_limit_bytes=2 * MIB),
-    )(in_smem(side), tokens, last, *pieces)
-
-
-def hidden_kernel(side_ref, mine_ref, got_ref, wg_ref, wu_ref, h_out, wide, x_ref):
-    sets, count, _ = mine_ref.shape
+    for i, ref in enumerate(refs[:-1]):
+        out_ref[i] = ref[...]
+
+
+def stack(*parts):
+    return pl.pallas_call(
+        stack_kernel,
+        out_shape=jax.ShapeDtypeStruct((len(parts), *parts[0].shape), parts[0].dtype),
+        in_specs=[VMEM] * len(parts),
+        out_specs=VMEM,
+        compiler_params=pltpu.CompilerParams(vmem_limit_bytes=2 * MIB),
+    )(*parts)
+
+
+def gate_kernel(side_ref, mine_ref, got_ref, wg_ref, x_ref, act_ref, wide):
+    far, near, count, width = mine_ref.shape
     first = side_ref[0] == 0
-    for j in range(sets):
-        mine = mine_ref[j].astype(jnp.float32)
-        got = got_ref[j].astype(jnp.float32)
-        wide[pl.ds(j * count, count), :] = jnp.where(first, mine, got)
-        wide[pl.ds((sets + j) * count, count), :] = jnp.where(first, got, mine)
+    for j in range(far):
+        for i in range(near):
+            rows = pl.ds((j * near + i) * count, count)
+            mine = mine_ref[j, i].astype(jnp.float32)
+            got = got_ref[j, i].astype(jnp.float32)
+            wide[rows, :width] = jnp.where(first, mine, got)
+            wide[rows, width:] = jnp.where(first, got, mine)
     x_ref[...] = wide[...].astype(jnp.bfloat16)
 
     @pl.loop(0, wg_ref.shape[1] // TILE)
     def _(n):
         cols = pl.ds(pl.multiple_of(n * TILE, TILE), TILE)
         gate = jnp.dot(x_ref[...], wg_ref[:, cols], preferred_element_type=jnp.float32)
+        act_ref[:, cols] = gate / (1.0 + jnp.exp(-gate))
+
+
+def gate_rows(side, mine, got, wg):
+    total = mine.shape[0] * mine.shape[1] * mine.shape[2]
+    depth, width = wg.shape
+    return pl.pallas_call(
+        gate_kernel,
+        out_shape=(
+            jax.ShapeDtypeStruct((total, depth), jnp.bfloat16),
+            jax.ShapeDtypeStruct((total, width), jnp.float32),
+        ),
+        in_specs=[SMEM] + [VMEM] * 3,
+        out_specs=(VMEM, VMEM),
+        scratch_shapes=[pltpu.VMEM((total, depth), jnp.float32)],
+        compiler_params=pltpu.CompilerParams(vmem_limit_bytes=2 * MIB),
+        cost_estimate=pl.CostEstimate(flops=GATE, bytes_accessed=0, transcendentals=total * width),
+    )(in_smem(side), mine, got, in_vmem(wg))
+
+
+def up_kernel(x_ref, act_ref, wu_ref, h_out):
+    @pl.loop(0, wu_ref.shape[1] // TILE)
+    def _(n):
+        cols = pl.ds(pl.multiple_of(n * TILE, TILE), TILE)
         up = jnp.dot(x_ref[...], wu_ref[:, cols], preferred_element_type=jnp.float32)
-        h_out[:, cols] = (gate / (1.0 + jnp.exp(-gate)) * up).astype(jnp.bfloat16)
-
-
-def hidden_rows(side, mine, got, wg, wu):
-    total = 2 * mine.shape[0] * mine.shape[1]
-    depth, width = wg.shape
-    return pl.pallas_call(
-        hidden_kernel,
-        out_shape=jax.ShapeDtypeStruct((total, width), jnp.bfloat16),
-        in_specs=[SMEM] + [VMEM] * 4,
-        out_specs=VMEM,
-        scratch_shapes=[
-            pltpu.VMEM((total, depth), jnp.float32),
-            pltpu.VMEM((total, depth), jnp.bfloat16),
-        ],
-        compiler_params=pltpu.CompilerParams(vmem_limit_bytes=2 * MIB),
-        cost_estimate=pl.CostEstimate(
-            flops=AHEAD, bytes_accessed=0, transcendentals=total * width
-        ),
-    )(in_smem(side), mine, got, in_vmem(wg), in_vmem(wu))
-
-
-def in_smem(x):
-    return pltpu.with_memory_space_constraint(x, pltpu.SMEM)
-
-
-def in_vmem(x):
-    return pltpu.with_memory_space_constraint(x, pltpu.VMEM)
+        h_out[:, cols] = (act_ref[:, cols] * up).astype(jnp.bfloat16)
+
+
+def hidden_rows(x, act, wu):
+    return pl.pallas_call(
+        up_kernel,
+        out_shape=jax.ShapeDtypeStruct(act.shape, jnp.bfloat16),
+        in_specs=[VMEM] * 3,
+        out_specs=VMEM,
+        compiler_params=pltpu.CompilerParams(vmem_limit_bytes=2 * MIB),
+        cost_estimate=pl.CostEstimate(flops=UP, bytes_accessed=0, transcendentals=0),
+    )(x, act, in_vmem(wu))
 
 
 def down_kernel(other, side_ref, h_ref, wd_ref, out_ref):
@@ -150,18 +177,15 @@
 
 def near_kernel(keep_ref, got_ref, even_ref, odd_ref):
     both = keep_ref[...] + got_ref[...].astype(jnp.float32)
-    pairs, count, _ = odd_ref.shape
-    for at, k in enumerate(ORDER):
-        rows = both[at * count : (at + 1) * count]
-        if k % 2:
-            odd_ref[k // 2] = rows.astype(odd_ref.dtype)
-        else:
-            even_ref[k // 2] = rows
+    sets, count, _ = odd_ref.shape
+    for j in range(sets):
+        even_ref[j] = both[2 * j * count : (2 * j + 1) * count]
+        odd_ref[j] = both[(2 * j + 1) * count : (2 * j + 2) * count].astype(odd_ref.dtype)
 
 
 def near(keep, got):
     rows, width = keep.shape
-    shape = (len(ORDER) // 2, rows // len(ORDER), width)
+    shape = (SOURCES // 2, rows // SOURCES, width)
     return pl.pallas_call(
         near_kernel,
         out_shape=(jax.ShapeDtypeStruct(shape, jnp.float32), jax.ShapeDtypeStruct(shape, jnp.bfloat16)),
@@ -206,16 +230,8 @@
     )(gates, own, *got)
 
 
-def swapped(x, k, sources):
-    return lax.ppermute(x, "exp", [(i, i ^ k) for i in range(sources)])
-
-
-def fetched(x, first, second, sources):
-    pairs = []
-    for side, k in enumerate((first, second)):
-        if k is not None:
-            pairs += [(2 * i + side, 2 * (i ^ k) + side) for i in range(sources)]
-    return lax.ppermute(x, ("exp", "hid"), pairs)
+def swapped(x, k):
+    return lax.ppermute(x, "exp", [(i, i ^ k) for i in range(SOURCES)])
 
 
 def swap_cores(x):
@@ -223,19 +239,17 @@
 
 
 def local(tokens, w_gate, w_up, w_down, block_counts, block_rows, row_gates):
-    sources = lax.axis_size("exp")
-    tokens, side = pass_on(tokens)
-    half = len(ORDER) // 2
-    pieces = [fetched(tokens, ORDER[b], ORDER[half + b], sources) for b in range(1, half)]
-    last = fetched(tokens, None, ORDER[half], sources)
-    mine = pack(side, tokens, last, pieces)
-    hidden = hidden_rows(side, mine, swap_cores(mine), w_gate, w_up)
+    half, side = take_half(tokens)
+    pair = stack(half, swapped(half, 1))
+    mine = stack(pair, *[swapped(pair, 2 * j) for j in range(1, SOURCES // 2)])
+    x, act = gate_rows(side, mine, swap_cores(mine), w_gate)
+    hidden = hidden_rows(x, act, w_up)
     send = down_half(side, hidden, w_down, True, jnp.bfloat16)
     keep = down_half(side, hidden, w_down, False, jnp.float32)
     even, odd = near(keep, swap_cores(send))
-    own, *outgoing = far(even, swapped(odd, 1, sources))
-    returned = [swapped(piece, 2 * (j + 1), sources) for j, piece in enumerate(outgoing)]
-    gates = route(block_counts, block_rows, row_gates, sources, tokens.shape[0])
+    own, *outgoing = far(even, swapped(odd, 1))
+    returned = [swapped(piece, 2 * (j + 1)) for j, piece in enumerate(outgoing)]
+    gates = route(block_counts, block_rows, row_gates, SOURCES, tokens.shape[0])
     return weighted_sum(gates, own, returned)
 
 
@@ -305,10 +319,10 @@
 
 
 def solution(mesh):
-    small = mesh.shape["exp"] == len(ORDER) and mesh.shape["hid"] == 2
+    small = mesh.shape["exp"] == SOURCES and mesh.shape["hid"] == 2
 
     def chosen(*args):
-        return (local if small and args[5].shape[0] * 2 == len(ORDER) else local_wide)(*args)
+        return (local if small and args[5].shape[0] * 2 == SOURCES else local_wide)(*args)
 
     return jax.shard_map(
         chosen,

time: 38.8 us -> 39.8 us (1.026)
  waiting for transfers between devices: 10.3 us -> 13 us
  starting transfers between devices: 16.4 us -> 14 us
  Pallas kernels: 11.8 us -> 12.3 us
    ppermute x2, starting transfers between devices: 5.06 us -> 0.24 us  [swap_cores(): return lax.ppermute(x, 'hid', [(0, 1), (1, 0)])]
    ppermute x8, waiting for transfers between devices: 9.28 us -> 11.7 us  [swapped(): return lax.ppermute(x, 'exp', [(i, i ^ k) for i in range(SOURCES)])]
    ppermute x8, starting transfers between devices: 11.4 us -> 13.7 us  [swapped(): return lax.ppermute(x, 'exp', [(i, i ^ k) for i in range(SOURCES)])]
    pallas_call x3 -> x5, Pallas kernels: 7.24 us -> 7.81 us  [the longest x1 3.56 us: gate_rows(): pl.pallas_call(gate_kernel, out_shape=(jax.ShapeDtypeStruct((total, depth...]
where the time goes in v6:
time: 39.8 us; the launch traced here: 39.5 us
  starting transfers between devices  14 us (35%)
  waiting for transfers between devices  13 us (33%)
  Pallas kernels  12.3 us (31%)
    ppermute x8, starting transfers between devices, swapped(): return lax.ppermute(x, 'exp', [(i, i ^ k) for i in range(SOURCES)])  13.7 us
    ppermute x8, waiting for transfers between devices, swapped(): return lax.ppermute(x, 'exp', [(i, i ^ k) for i in range(SOURCES)])  11.7 us
    pallas_call x1, Pallas kernels, gate_rows(): pl.pallas_call(gate_kernel, out_shape=(jax.ShapeDtypeStruct((total, depth...  3.56 us
    pallas_call x1, Pallas kernels, hidden_rows(): pl.pallas_call(up_kernel, out_shape=jax.ShapeDtypeStruct(act.shape, jnp.b...  3.37 us
    pallas_call x2, Pallas kernels, down_half(): pl.pallas_call(functools.partial(down_kernel, other), out_shape=jax.Shape...  3.12 us
    ppermute x2, waiting for transfers between devices, swap_cores(): return lax.ppermute(x, 'hid', [(0, 1), (1, 0)])  1.34 us
    pallas_call x1, Pallas kernels, take_half(): pl.pallas_call(take_kernel, out_shape=(jax.ShapeDtypeStruct((count, width...  0.87 us
  transfers between devices with their start and end apart: 10, of which 6 were waited for; matrix products, arithmetic and copies ran while one was open for 0% of the time, Pallas kernels for 6%

profile of v6, /device:TPU:0, one launch (start us, length us, event | category | flops | bytes accessed | tf_op | source)
XLA Modules:
  0.0 39.5 jit_solution(10308886751061377757)
XLA Ops:
  0.0 0.0 copy-start
  0.0 0.9 %shard_map.74 = (bf16[4,2048]{1,0:T(4,128)(2,1)S(1)}, s32[1]{0:T(128)S(4)}) custom-call(bf16[4,4096]{1,0:T(4,128)(2,1)} %tokens_ref.1), custom_call_target="tpu_custom_call" | custom-call | flops 20000000000 | tf_op jit(solution)/shard_map/pallas_call | solution.py:47
  0.9 0.0 copy-start.1
  0.9 3.0 %collective-permute-start = (bf16[4,2048]{1,0:T(4,128)(2,1)S(1)}, bf16[4,2048]{1,0:T(4,128)(2,1)S(1)}, u32[]{:S(2)}, u32[]{:S(2)}) collective-permute-start(bf16[4,2048]{1,0:T(4,128)(2,1)S(1)} %get-tuple-element.16.refs_0_), channel_id=1, source_target_pairs={{0,2},{2,0},{4,6},{6,4},{8,10},{10,8},{12,14},{14,12},{1,3},{3,1},... | collective-permute-start | bytes 49160 | tf_op jit(solution)/shard_map/ppermute | solution.py:234
  3.9 1.7 %collective-permute-done.refs_1_ = bf16[4,2048]{1,0:T(4,128)(2,1)S(1)} collective-permute-done((bf16[4,2048]{1,0:T(4,128)(2,1)S(1)}, bf16[4,2048]{1,0:T(4,128)(2,1)S(1)}, u32[]{:S(2)}, u32[]{:S(2)}) %collective-permute-start) | collective-permute-done | bytes 16416 | tf_op jit(solution)/shard_map/ppermute | solution.py:234
  5.6 2.1 %collective-permute-start.1 = (bf16[2,4,2048]{2,1,0:T(4,128)(2,1)S(1)}, bf16[2,4,2048]{2,1,0:T(4,128)(2,1)S(1)}, u32[]{:S(2)}, u32[]{:S(2)}) collective-permute-start(bf16[2,4,2048]{2,1,0:T(4,128)(2,1)S(1)} %shard_map.75.refs_0_), channel_id=1, source_target_pairs={{0,4},{2,6},{4,0},{6,2},{8,12},{10,14},{12,8},{14,10},{1,5},{3,7},... | collective-permute-start | bytes 98312 | tf_op jit(solution)/shard_map/ppermute | solution.py:234
  7.7 2.6 %collective-permute-start.2 = (bf16[2,4,2048]{2,1,0:T(4,128)(2,1)S(1)}, bf16[2,4,2048]{2,1,0:T(4,128)(2,1)S(1)}, u32[]{:S(2)}, u32[]{:S(2)}) collective-permute-start(bf16[2,4,2048]{2,1,0:T(4,128)(2,1)S(1)} %shard_map.75.refs_0_), channel_id=1, source_target_pairs={{0,8},{2,10},{4,12},{6,14},{8,0},{10,2},{12,4},{14,6},{1,9},{3,11}... | collective-permute-start | bytes 98312 | tf_op jit(solution)/shard_map/ppermute | solution.py:234
  10.3 0.0 collective-permute-start.3
  10.3 0.0 collective-permute-done.1.refs_1_
  10.3 2.5 %collective-permute-done.2.refs_2_ = bf16[2,4,2048]{2,1,0:T(4,128)(2,1)S(1)} collective-permute-done((bf16[2,4,2048]{2,1,0:T(4,128)(2,1)S(1)}, bf16[2,4,2048]{2,1,0:T(4,128)(2,1)S(1)}, u32[]{:S(2)}, u32[]{:S(2)}) %collective-permute-start.2) | collective-permute-done | bytes 32800 | tf_op jit(solution)/shard_map/ppermute | solution.py:234
  12.8 3.2 %collective-permute-done.3.refs_3_ = bf16[2,4,2048]{2,1,0:T(4,128)(2,1)S(1)} collective-permute-done((bf16[2,4,2048]{2,1,0:T(4,128)(2,1)S(1)}, bf16[2,4,2048]{2,1,0:T(4,128)(2,1)S(1)}, u32[]{:S(2)}, u32[]{:S(2)}) %collective-permute-start.3) | collective-permute-done | bytes 32800 | tf_op jit(solution)/shard_map/ppermute | solution.py:234
  16.0 0.1 collective-permute-start.4
  16.1 1.3 %collective-permute-done.4.got_ref = bf16[4,2,4,2048]{3,2,1,0:T(4,128)(2,1)S(1)} collective-permute-done((bf16[4,2,4,2048]{3,2,1,0:T(4,128)(2,1)S(1)}, bf16[4,2,4,2048]{3,2,1,0:T(4,128)(2,1)S(1)}, u32[]{:S(2)}, u32[]{:S(2)}) %collective-permute-start.4) | collective-permute-done | bytes 131104 | tf_op jit(solution)/shard_map/ppermute | solution.py:238
  17.5 0.0 copy-done
  17.5 0.0 slice-start
  17.5 0.0 slice-start.1
  17.5 3.6 %shard_map.77 = (bf16[32,4096]{1,0:T(8,128)(2,1)S(1)}, f32[32,2048]{1,0:T(8,128)S(1)}) custom-call(s32[1]{0:T(128)S(4)} %get-tuple-element.15.side_ref, bf16[4,2,4,2048]{3,2,1,0:T(4,128)(2,1)S(1)} %shard_map.76.mine_ref, bf16[4,2,4,2048]{3,2,1,0:T(4,128)(2,1)S(1)} %collective-permute-done.4.got_ref, bf16[4096,2048]{1,0:T(8,128)(2,1)S(1)} %copy-done), custom_call_target="tpu_custom_call" | custom-call | flops 2000000000 | tf_op jit(solution)/shard_map/pallas_call | solution.py:122
  21.0 0.0 copy-done.1
  21.0 0.0 slice-start.2
  21.1 0.0 slice-start.3
  21.1 3.4 %shard_map.78.h_ref = bf16[32,2048]{1,0:T(8,128)(2,1)S(1)} custom-call(bf16[32,4096]{1,0:T(8,128)(2,1)S(1)} %get-tuple-element.17.x_ref, f32[32,2048]{1,0:T(8,128)S(1)} %get-tuple-element.18.act_ref, bf16[4096,2048]{1,0:T(8,128)(2,1)S(1)} %copy-done.1), custom_call_target="tpu_custom_call" | custom-call | flops 2000000000 | tf_op jit(solution)/shard_map/pallas_call | solution.py:145
  24.4 0.0 slice-done
  24.4 0.0 slice-done.1
  24.5 0.0 slice-done.2
  24.5 0.1 slice-done.3
  24.5 0.0 copy-start.2
  24.5 0.0 copy-start.3
  24.5 0.0 copy-start.4
  24.5 1.6 %shard_map.80 = bf16[32,2048]{1,0:T(8,128)(2,1)S(1)} custom-call(s32[1]{0:T(128)S(4)} %get-tuple-element.15.side_ref, bf16[32,2048]{1,0:T(8,128)(2,1)S(1)} %shard_map.78.h_ref, bf16[2048,4096]{1,0:T(8,128)(2,1)S(1)} %bitcast.1), custom_call_target="tpu_custom_call" | custom-call | flops 268435456 | tf_op jit(solution)/shard_map/pallas_call | solution.py:168
  26.1 0.2 collective-permute-start.5
  26.2 1.6 %shard_map.79.keep_ref = f32[32,2048]{1,0:T(8,128)S(1)} custom-call(s32[1]{0:T(128)S(4)} %get-tuple-element.15.side_ref, bf16[32,2048]{1,0:T(8,128)(2,1)S(1)} %shard_map.78.h_ref, bf16[2048,4096]{1,0:T(8,128)(2,1)S(1)} %bitcast.1), custom_call_target="tpu_custom_call" | custom-call | flops 268435456 | tf_op jit(solution)/shard_map/pallas_call | solution.py:168
  27.8 0.0 collective-permute-done.5.got_ref
  27.9 1.6 %collective-permute-start.6 = (bf16[4,4,2048]{2,1,0:T(4,128)(2,1)S(1)}, bf16[4,4,2048]{2,1,0:T(4,128)(2,1)S(1)}, u32[]{:S(2)}, u32[]{:S(2)}) collective-permute-start(bf16[4,4,2048]{2,1,0:T(4,128)(2,1)S(1)} %get-tuple-element.20), channel_id=1, source_target_pairs={{0,2},{2,0},{4,6},{6,4},{8,10},{10,8},{12,14},{14,12},{1,3},{3,1},... | collective-permute-start | bytes 196616 | tf_op jit(solution)/shard_map/ppermute | solution.py:234
  29.4 2.9 %collective-permute-done.6.got_ref = bf16[4,4,2048]{2,1,0:T(4,128)(2,1)S(1)} collective-permute-done((bf16[4,4,2048]{2,1,0:T(4,128)(2,1)S(1)}, bf16[4,4,2048]{2,1,0:T(4,128)(2,1)S(1)}, u32[]{:S(2)}, u32[]{:S(2)}) %collective-permute-start.6) | collective-permute-done | bytes 65568 | tf_op jit(solution)/shard_map/ppermute | solution.py:234
  32.3 0.1 collective-permute-start.7
  32.4 0.9 %collective-permute-start.8 = (bf16[4,2048]{1,0:T(4,128)(2,1)S(1)}, bf16[4,2048]{1,0:T(4,128)(2,1)S(1)}, u32[]{:S(2)}, u32[]{:S(2)}) collective-permute-start(bf16[4,2048]{1,0:T(4,128)(2,1)S(1)} %get-tuple-element.23), channel_id=1, source_target_pairs={{0,8},{2,10},{4,12},{6,14},{8,0},{10,2},{12,4},{14,6},{1,9},{3,11}... | collective-permute-start | bytes 49160 | tf_op jit(solution)/shard_map/ppermute | solution.py:234
  33.3 3.5 %collective-permute-start.9 = (bf16[4,2048]{1,0:T(4,128)(2,1)S(1)}, bf16[4,2048]{1,0:T(4,128)(2,1)S(1)}, u32[]{:S(2)}, u32[]{:S(2)}) collective-permute-start(bf16[4,2048]{1,0:T(4,128)(2,1)S(1)} %get-tuple-element.24), channel_id=1, source_target_pairs={{0,12},{2,14},{4,8},{6,10},{8,4},{10,6},{12,0},{14,2},{1,13},{3,15... | collective-permute-start | bytes 49160 | tf_op jit(solution)/shard_map/ppermute | solution.py:234
  36.8 0.0 copy-done.2
  36.8 0.0 copy-done.3
  36.8 0.0 copy-done.4
  36.8 0.6 %shard_map.73.gates_ref = f32[16,128]{1,0:T(8,128)S(1)} custom-call(s32[4]{0:T(128)S(1)} %copy-done.4, s32[4,128]{1,0:T(4,128)S(1)} %copy-done.2, f32[4,128]{1,0:T(4,128)S(1)} %copy-done.3), custom_call_target="tpu_custom_call" | custom-call | tf_op jit(solution)/shard_map/pallas_call | solution.py:75
  37.4 0.0 collective-permute-done.7.refs_1_
  37.4 0.0 collective-permute-done.8.refs_2_
  37.4 1.4 %collective-permute-done.9.refs_3_ = bf16[4,2048]{1,0:T(4,128)(2,1)S(1)} collective-permute-done((bf16[4,2048]{1,0:T(4,128)(2,1)S(1)}, bf16[4,2048]{1,0:T(4,128)(2,1)S(1)}, u32[]{:S(2)}, u32[]{:S(2)}) %collective-permute-start.9) | collective-permute-done | bytes 16416 | tf_op jit(solution)/shard_map/ppermute | solution.py:234
  38.8 0.7 %shard_map.83 = bf16[4,2048]{1,0:T(4,128)(2,1)} custom-call(f32[16,128]{1,0:T(8,128)S(1)} %shard_map.73.gates_ref, f32[4,2048]{1,0:T(4,128)S(1)} %get-tuple-element.21.refs_0_, bf16[4,2048]{1,0:T(4,128)(2,1)S(1)} %collective-permute-done.7.refs_1_, bf16[4,2048]{1,0:T(4,128)(2,1)S(1)} %collective-permute-done.8.refs_2_, ...), custom_call_target="tpu_custom_call" | custom-call | tf_op jit(solution)/shard_map/pallas_call | solution.py:224
  (5 shorter events, 0.1 us)
Async XLA Ops:
  0.0 17.5 %copy-start = (bf16[4096,2048]{1,0:T(8,128)(2,1)S(1)}, bf16[4096,2048]{1,0:T(8,128)(2,1)}, u32[]{:S(2)}) copy-start(bf16[4096,2048]{1,0:T(8,128)(2,1)} %wg_ref.1) | copy-start | bytes 50331652
  0.9 20.2 %copy-start.1 = (bf16[4096,2048]{1,0:T(8,128)(2,1)S(1)}, bf16[4096,2048]{1,0:T(8,128)(2,1)}, u32[]{:S(2)}) copy-start(bf16[4096,2048]{1,0:T(8,128)(2,1)} %wu_ref.1) | copy-start | bytes 50331652
  0.9 4.7 %collective-permute-start = (bf16[4,2048]{1,0:T(4,128)(2,1)S(1)}, bf16[4,2048]{1,0:T(4,128)(2,1)S(1)}, u32[]{:S(2)}, u32[]{:S(2)}) collective-permute-start(bf16[4,2048]{1,0:T(4,128)(2,1)S(1)} %get-tuple-element.16.refs_0_), channel_id=1, source_target_pairs={{0,2},{2,0},{4,6},{6,4},{8,10},{10,8},{12,14},{14,12},{1,3},{3,1},... | collective-permute-start | bytes 49160 | tf_op jit(solution)/shard_map/ppermute | solution.py:234
  5.6 4.7 %collective-permute-start.1 = (bf16[2,4,2048]{2,1,0:T(4,128)(2,1)S(1)}, bf16[2,4,2048]{2,1,0:T(4,128)(2,1)S(1)}, u32[]{:S(2)}, u32[]{:S(2)}) collective-permute-start(bf16[2,4,2048]{2,1,0:T(4,128)(2,1)S(1)} %shard_map.75.refs_0_), channel_id=1, source_target_pairs={{0,4},{2,6},{4,0},{6,2},{8,12},{10,14},{12,8},{14,10},{1,5},{3,7},... | collective-permute-start | bytes 98312 | tf_op jit(solution)/shard_map/ppermute | solution.py:234
  7.7 5.1 %collective-permute-start.2 = (bf16[2,4,2048]{2,1,0:T(4,128)(2,1)S(1)}, bf16[2,4,2048]{2,1,0:T(4,128)(2,1)S(1)}, u32[]{:S(2)}, u32[]{:S(2)}) collective-permute-start(bf16[2,4,2048]{2,1,0:T(4,128)(2,1)S(1)} %shard_map.75.refs_0_), channel_id=1, source_target_pairs={{0,8},{2,10},{4,12},{6,14},{8,0},{10,2},{12,4},{14,6},{1,9},{3,11}... | collective-permute-start | bytes 98312 | tf_op jit(solution)/shard_map/ppermute | solution.py:234
  10.3 5.7 %collective-permute-start.3 = (bf16[2,4,2048]{2,1,0:T(4,128)(2,1)S(1)}, bf16[2,4,2048]{2,1,0:T(4,128)(2,1)S(1)}, u32[]{:S(2)}, u32[]{:S(2)}) collective-permute-start(bf16[2,4,2048]{2,1,0:T(4,128)(2,1)S(1)} %shard_map.75.refs_0_), channel_id=1, source_target_pairs={{0,12},{2,14},{4,8},{6,10},{8,4},{10,6},{12,0},{14,2},{1,13},{3,15... | collective-permute-start | bytes 98312 | tf_op jit(solution)/shard_map/ppermute | solution.py:234
  16.0 1.4 %collective-permute-start.4 = (bf16[4,2,4,2048]{3,2,1,0:T(4,128)(2,1)S(1)}, bf16[4,2,4,2048]{3,2,1,0:T(4,128)(2,1)S(1)}, u32[]{:S(2)}, u32[]{:S(2)}) collective-permute-start(bf16[4,2,4,2048]{3,2,1,0:T(4,128)(2,1)S(1)} %shard_map.76.mine_ref), channel_id=1, source_target_pairs={{0,1},{1,0},{2,3},{3,2},{4,5},{5,4},{6,7},{7,6},{8,9},{9,8},{10,11... | collective-permute-start | bytes 393224 | tf_op jit(solution)/shard_map/ppermute | solution.py:238
  17.5 7.0 %slice-start = ((s8[16777216]{0:T(1024)(128)(4,1)}), s8[4194304]{0:T(1024)(128)(4,1)S(1)}, s32[]{:S(2)}) async-start(s8[16777216]{0:T(1024)(128)(4,1)} %bitcast), calls=%async_computation | async-start | bytes 8388608
  17.5 7.0 %slice-start.1 = ((s8[16777216]{0:T(1024)(128)(4,1)}), s8[4194304]{0:T(1024)(128)(4,1)S(1)}, s32[]{:S(2)}) async-start(s8[16777216]{0:T(1024)(128)(4,1)} %bitcast), calls=%async_computation.1 | async-start | bytes 8388608
  21.0 3.4 %slice-start.2 = ((s8[16777216]{0:T(1024)(128)(4,1)}), s8[4194304]{0:T(1024)(128)(4,1)S(1)}, s32[]{:S(2)}) async-start(s8[16777216]{0:T(1024)(128)(4,1)} %bitcast), calls=%async_computation.2 | async-start | bytes 8388608
  21.1 3.5 %slice-start.3 = ((s8[16777216]{0:T(1024)(128)(4,1)}), s8[4194304]{0:T(1024)(128)(4,1)S(1)}, s32[]{:S(2)}) async-start(s8[16777216]{0:T(1024)(128)(4,1)} %bitcast), calls=%async_computation.3 | async-start | bytes 8388608
  24.5 12.3 %copy-start.2 = (s32[4,128]{1,0:T(4,128)S(1)}, s32[4,128]{1,0:T(4,128)}, u32[]{:S(2)}) copy-start(s32[4,128]{1,0:T(4,128)} %rows_ref.1) | copy-start | bytes 6148
  24.5 12.3 %copy-start.3 = (f32[4,128]{1,0:T(4,128)S(1)}, f32[4,128]{1,0:T(4,128)}, u32[]{:S(2)}) copy-start(f32[4,128]{1,0:T(4,128)} %gates_ref.1) | copy-start | bytes 6148
  24.5 12.3 %copy-start.4 = (s32[4]{0:T(128)S(1)}, s32[4]{0:T(128)}, u32[]{:S(2)}) copy-start(s32[4]{0:T(128)} %counts_ref.1) | copy-start | bytes 52
  26.1 1.7 %collective-permute-start.5 = (bf16[32,2048]{1,0:T(8,128)(2,1)S(1)}, bf16[32,2048]{1,0:T(8,128)(2,1)S(1)}, u32[]{:S(2)}, u32[]{:S(2)}) collective-permute-start(bf16[32,2048]{1,0:T(8,128)(2,1)S(1)} %shard_map.80), channel_id=1, source_target_pairs={{0,1},{1,0},{2,3},{3,2},{4,5},{5,4},{6,7},{7,6},{8,9},{9,8},{10,11... | collective-permute-start | bytes 393224 | tf_op jit(solution)/shard_map/ppermute | solution.py:238
  27.9 4.4 %collective-permute-start.6 = (bf16[4,4,2048]{2,1,0:T(4,128)(2,1)S(1)}, bf16[4,4,2048]{2,1,0:T(4,128)(2,1)S(1)}, u32[]{:S(2)}, u32[]{:S(2)}) collective-permute-start(bf16[4,4,2048]{2,1,0:T(4,128)(2,1)S(1)} %get-tuple-element.20), channel_id=1, source_target_pairs={{0,2},{2,0},{4,6},{6,4},{8,10},{10,8},{12,14},{14,12},{1,3},{3,1},... | collective-permute-start | bytes 196616 | tf_op jit(solution)/shard_map/ppermute | solution.py:234
  32.3 5.1 %collective-permute-start.7 = (bf16[4,2048]{1,0:T(4,128)(2,1)S(1)}, bf16[4,2048]{1,0:T(4,128)(2,1)S(1)}, u32[]{:S(2)}, u32[]{:S(2)}) collective-permute-start(bf16[4,2048]{1,0:T(4,128)(2,1)S(1)} %get-tuple-element.22), channel_id=1, source_target_pairs={{0,4},{2,6},{4,0},{6,2},{8,12},{10,14},{12,8},{14,10},{1,5},{3,7},... | collective-permute-start | bytes 49160 | tf_op jit(solution)/shard_map/ppermute | solution.py:234
  32.4 5.0 %collective-permute-start.8 = (bf16[4,2048]{1,0:T(4,128)(2,1)S(1)}, bf16[4,2048]{1,0:T(4,128)(2,1)S(1)}, u32[]{:S(2)}, u32[]{:S(2)}) collective-permute-start(bf16[4,2048]{1,0:T(4,128)(2,1)S(1)} %get-tuple-element.23), channel_id=1, source_target_pairs={{0,8},{2,10},{4,12},{6,14},{8,0},{10,2},{12,4},{14,6},{1,9},{3,11}... | collective-permute-start | bytes 49160 | tf_op jit(solution)/shard_map/ppermute | solution.py:234
  33.3 5.5 %collective-permute-start.9 = (bf16[4,2048]{1,0:T(4,128)(2,1)S(1)}, bf16[4,2048]{1,0:T(4,128)(2,1)S(1)}, u32[]{:S(2)}, u32[]{:S(2)}) collective-permute-start(bf16[4,2048]{1,0:T(4,128)(2,1)S(1)} %get-tuple-element.24), channel_id=1, source_target_pairs={{0,12},{2,14},{4,8},{6,10},{8,4},{10,6},{12,0},{14,2},{1,13},{3,15... | collective-permute-start | bytes 49160 | tf_op jit(solution)/shard_map/ppermute | solution.py:234

commit v7 on v6

--- a/solution.py
+++ b/solution.py
@@ -11,8 +11,9 @@
 CAP = 3
 TILE = 512
 MIB = 1 << 20
-SOURCES = 8
-GATE = 2_000_000_000
+ORDER = (0, 7, 6, 1, 2, 5, 4, 3)
+SOURCES = len(ORDER)
+GATE = 5_000_000_000
 UP = 2_000_000_000
 AHEAD = 20_000_000_000
 HBM = pl.BlockSpec(memory_space=pltpu.HBM)
@@ -32,21 +33,17 @@
     return pltpu.with_memory_space_constraint(x, pltpu.VMEM)
 
 
-def take_kernel(tokens_ref, half_ref, side_ref, sem):
-    side = lax.axis_index("hid")
-    width = half_ref.shape[1]
-    columns = pl.ds(pl.multiple_of(side * width, width), width)
-    copy = pltpu.make_async_copy(tokens_ref.at[:, columns], half_ref, sem)
+def pass_kernel(tokens_ref, out_ref, side_ref, sem):
+    copy = pltpu.make_async_copy(tokens_ref, out_ref, sem)
     copy.start()
-    side_ref[0] = side
+    side_ref[0] = lax.axis_index("hid")
     copy.wait()
 
 
-def take_half(tokens):
-    count, width = tokens.shape
-    return pl.pallas_call(
-        take_kernel,
-        out_shape=(jax.ShapeDtypeStruct((count, width // 2), tokens.dtype), pltpu.SMEM((1,), jnp.int32)),
+def pass_on(tokens):
+    return pl.pallas_call(
+        pass_kernel,
+        out_shape=(jax.ShapeDtypeStruct(tokens.shape, tokens.dtype), pltpu.SMEM((1,), jnp.int32)),
         in_specs=[HBM],
         out_specs=(VMEM, SMEM),
         scratch_shapes=[pltpu.SemaphoreType.DMA],
@@ -61,8 +58,9 @@
     line = lax.broadcasted_iota(jnp.int32, (total, slots), 0)
     position = lax.broadcasted_iota(jnp.int32, (total, slots), 1)
     own = lax.axis_index("exp")
-    token = own * count + lax.rem(line, count)
-    expert = (own // per_expert) ^ (line // count)
+    block = line // count
+    token = (own ^ lax.rem(block, per_expert)) * count + lax.rem(line, count)
+    expert = (own // per_expert) ^ (block // per_expert)
     found = jnp.zeros((total, slots), jnp.float32)
     for e in range(experts):
         rows = rows_ref[pl.ds(e, 1), :]
@@ -71,42 +69,41 @@
     out_ref[...] = jnp.broadcast_to(jnp.sum(found, axis=1, keepdims=True), out_ref.shape)
 
 
-def route(block_counts, block_rows, row_gates, sources, count):
-    return pl.pallas_call(
-        functools.partial(route_kernel, count, sources // block_rows.shape[0]),
-        out_shape=jax.ShapeDtypeStruct((block_rows.shape[0] * count, 128), jnp.float32),
+def route(block_counts, block_rows, row_gates, count):
+    return pl.pallas_call(
+        functools.partial(route_kernel, count, SOURCES // block_rows.shape[0]),
+        out_shape=jax.ShapeDtypeStruct((SOURCES * count, 128), jnp.float32),
         in_specs=[SMEM, VMEM, VMEM],
         out_specs=VMEM,
         compiler_params=pltpu.CompilerParams(vmem_limit_bytes=2 * MIB),
     )(block_counts, block_rows, row_gates)
 
 
-def stack_kernel(*refs):
-    out_ref = refs[-1]
-    for i, ref in enumerate(refs[:-1]):
-        out_ref[i] = ref[...]
-
-
-def stack(*parts):
-    return pl.pallas_call(
-        stack_kernel,
-        out_shape=jax.ShapeDtypeStruct((len(parts), *parts[0].shape), parts[0].dtype),
-        in_specs=[VMEM] * len(parts),
-        out_specs=VMEM,
-        compiler_params=pltpu.CompilerParams(vmem_limit_bytes=2 * MIB),
-    )(*parts)
+def pack_kernel(side_ref, tokens_ref, *refs):
+    *pieces, last_ref, out_ref = refs
+    for r, ref in enumerate(pieces):
+        out_ref[r + 1] = ref[...]
+    out_ref[0] = jnp.where(side_ref[0] == 0, tokens_ref[...], last_ref[...])
+
+
+def pack(side, tokens, pieces):
+    return pl.pallas_call(
+        pack_kernel,
+        out_shape=jax.ShapeDtypeStruct((len(pieces), *tokens.shape), tokens.dtype),
+        in_specs=[SMEM] + [VMEM] * (1 + len(pieces)),
+        out_specs=VMEM,
+        compiler_params=pltpu.CompilerParams(vmem_limit_bytes=2 * MIB),
+    )(in_smem(side), tokens, *pieces)
 
 
 def gate_kernel(side_ref, mine_ref, got_ref, wg_ref, x_ref, act_ref, wide):
-    far, near, count, width = mine_ref.shape
+    sets, count, _ = mine_ref.shape
     first = side_ref[0] == 0
-    for j in range(far):
-        for i in range(near):
-            rows = pl.ds((j * near + i) * count, count)
-            mine = mine_ref[j, i].astype(jnp.float32)
-            got = got_ref[j, i].astype(jnp.float32)
-            wide[rows, :width] = jnp.where(first, mine, got)
-            wide[rows, width:] = jnp.where(first, got, mine)
+    for j in range(sets):
+        mine = mine_ref[j].astype(jnp.float32)
+        got = got_ref[j].astype(jnp.float32)
+        wide[pl.ds(j * count, count), :] = jnp.where(first, mine, got)
+        wide[pl.ds((sets + j) * count, count), :] = jnp.where(first, got, mine)
     x_ref[...] = wide[...].astype(jnp.bfloat16)
 
     @pl.loop(0, wg_ref.shape[1] // TILE)
@@ -117,7 +114,7 @@
 
 
 def gate_rows(side, mine, got, wg):
-    total = mine.shape[0] * mine.shape[1] * mine.shape[2]
+    total = 2 * mine.shape[0] * mine.shape[1]
     depth, width = wg.shape
     return pl.pallas_call(
         gate_kernel,
@@ -175,82 +172,97 @@
     )(in_smem(side), hidden, in_vmem(wd))
 
 
-def near_kernel(keep_ref, got_ref, even_ref, odd_ref):
+def near_kernel(keep_ref, got_ref, own_ref, *out_refs):
+    near, count, _ = own_ref.shape
     both = keep_ref[...] + got_ref[...].astype(jnp.float32)
-    sets, count, _ = odd_ref.shape
-    for j in range(sets):
-        even_ref[j] = both[2 * j * count : (2 * j + 1) * count]
-        odd_ref[j] = both[(2 * j + 1) * count : (2 * j + 2) * count].astype(odd_ref.dtype)
-
-
-def near(keep, got):
+    for at, k in enumerate(ORDER):
+        out_ref = (own_ref, *out_refs)[k // near]
+        out_ref[k % near] = both[at * count : (at + 1) * count].astype(out_ref.dtype)
+
+
+def near(keep, got, per_expert):
     rows, width = keep.shape
-    shape = (SOURCES // 2, rows // SOURCES, width)
+    shape = (per_expert, rows // SOURCES, width)
+    others = SOURCES // per_expert - 1
     return pl.pallas_call(
         near_kernel,
+        out_shape=(jax.ShapeDtypeStruct(shape, jnp.float32),)
+        + (jax.ShapeDtypeStruct(shape, jnp.bfloat16),) * others,
+        in_specs=[VMEM, VMEM],
+        out_specs=(VMEM,) * (1 + others),
+        compiler_params=pltpu.CompilerParams(vmem_limit_bytes=2 * MIB),
+    )(keep, got)
+
+
+def weigh_kernel(gates_ref, *refs):
+    *parts, own_ref, next_ref = refs
+    near, count, _ = parts[0].shape
+    for i, out_ref in enumerate((own_ref, next_ref)):
+        total = jnp.zeros(out_ref.shape, jnp.float32)
+        for at, part_ref in enumerate(parts):
+            j = (len(parts) - at) % len(parts)
+            gates = gates_ref[pl.ds((j * near + i) * count, count), :1]
+            total = total + part_ref[i].astype(jnp.float32) * gates
+        out_ref[...] = total.astype(out_ref.dtype)
+
+
+def weigh(gates, parts):
+    shape = parts[0].shape[1:]
+    return pl.pallas_call(
+        weigh_kernel,
         out_shape=(jax.ShapeDtypeStruct(shape, jnp.float32), jax.ShapeDtypeStruct(shape, jnp.bfloat16)),
-        in_specs=[VMEM, VMEM],
+        in_specs=[VMEM] * (1 + len(parts)),
         out_specs=(VMEM, VMEM),
         compiler_params=pltpu.CompilerParams(vmem_limit_bytes=2 * MIB),
-    )(keep, got)
-
-
-def far_kernel(even_ref, got_ref, own_ref, *out_refs):
-    for j, out_ref in enumerate((own_ref, *out_refs)):
-        out_ref[...] = (even_ref[j] + got_ref[j].astype(jnp.float32)).astype(out_ref.dtype)
-
-
-def far(even, got):
-    sets, count, width = even.shape
-    return pl.pallas_call(
-        far_kernel,
-        out_shape=(jax.ShapeDtypeStruct((count, width), jnp.float32),)
-        + (jax.ShapeDtypeStruct((count, width), jnp.bfloat16),) * (sets - 1),
-        in_specs=[VMEM, VMEM],
-        out_specs=(VMEM,) * sets,
-        compiler_params=pltpu.CompilerParams(vmem_limit_bytes=2 * MIB),
-    )(even, got)
-
-
-def sum_kernel(gates_ref, *refs):
-    total = jnp.zeros(refs[-1].shape, jnp.float32)
-    count = total.shape[0]
-    for k, ref in enumerate(refs[:-1]):
-        total = total + ref[...].astype(jnp.float32) * gates_ref[pl.ds(k * count, count), :1]
-    refs[-1][...] = total.astype(jnp.bfloat16)
-
-
-def weighted_sum(gates, own, got):
+    )(gates, *parts)
+
+
+def sum_kernel(own_ref, got_ref, out_ref):
+    out_ref[...] = (own_ref[...] + got_ref[...].astype(jnp.float32)).astype(out_ref.dtype)
+
+
+def final_sum(own, got):
     return pl.pallas_call(
         sum_kernel,
         out_shape=jax.ShapeDtypeStruct(own.shape, jnp.bfloat16),
-        in_specs=[VMEM] * (2 + len(got)),
-        out_specs=VMEM,
-        compiler_params=pltpu.CompilerParams(vmem_limit_bytes=2 * MIB),
-    )(gates, own, *got)
+        in_specs=[VMEM, VMEM],
+        out_specs=VMEM,
+        compiler_params=pltpu.CompilerParams(vmem_limit_bytes=2 * MIB),
+    )(own, got)
 
 
 def swapped(x, k):
     return lax.ppermute(x, "exp", [(i, i ^ k) for i in range(SOURCES)])
 
 
+def fetched(x, first, second):
+    pairs = []
+    for side, k in enumerate((first, second)):
+        if k is not None:
+            pairs += [(2 * i + side, 2 * (i ^ k) + side) for i in range(SOURCES)]
+    return lax.ppermute(x, ("exp", "hid"), pairs)
+
+
 def swap_cores(x):
     return lax.ppermute(x, "hid", [(0, 1), (1, 0)])
 
 
 def local(tokens, w_gate, w_up, w_down, block_counts, block_rows, row_gates):
-    half, side = take_half(tokens)
-    pair = stack(half, swapped(half, 1))
-    mine = stack(pair, *[swapped(pair, 2 * j) for j in range(1, SOURCES // 2)])
+    per_expert = SOURCES // block_rows.shape[0]
+    tokens, side = pass_on(tokens)
+    half = SOURCES // 2
+    pieces = [fetched(tokens, ORDER[b], ORDER[half + b]) for b in range(1, half)]
+    pieces += [fetched(tokens, None, ORDER[half])]
+    mine = pack(side, tokens, pieces)
     x, act = gate_rows(side, mine, swap_cores(mine), w_gate)
     hidden = hidden_rows(x, act, w_up)
     send = down_half(side, hidden, w_down, True, jnp.bfloat16)
     keep = down_half(side, hidden, w_down, False, jnp.float32)
-    even, odd = near(keep, swap_cores(send))
-    own, *outgoing = far(even, swapped(odd, 1))
-    returned = [swapped(piece, 2 * (j + 1)) for j, piece in enumerate(outgoing)]
-    gates = route(block_counts, block_rows, row_gates, SOURCES, tokens.shape[0])
-    return weighted_sum(gates, own, returned)
+    parts = near(keep, swap_cores(send), per_expert)
+    returned = [swapped(parts[j], per_expert * j) for j in range(len(parts) - 1, 0, -1)]
+    gates = route(block_counts, block_rows, row_gates, tokens.shape[0])
+    own, other = weigh(gates, [parts[0], *returned])
+    return final_sum(own, swapped(other, 1))
 
 
 def expert_block(segment, w_gate, w_up, w_down):

time: 39.8 us -> 36.2 us (0.910)
  waiting for transfers between devices: 13 us -> 9.97 us
  starting transfers between devices: 14 us -> 13.4 us
    ppermute x8 -> x4, starting transfers between devices: 13.7 us -> 5.73 us  [swapped(): return lax.ppermute(x, 'exp', [(i, i ^ k) for i in range(SOURCES)])]
    ppermute x0 -> x4, starting transfers between devices: none -> 7.47 us  [fetched(): return lax.ppermute(x, ('exp', 'hid'), pairs)]
    ppermute x8 -> x4, waiting for transfers between devices: 11.7 us -> 4.35 us  [swapped(): return lax.ppermute(x, 'exp', [(i, i ^ k) for i in range(SOURCES)])]
    ppermute x0 -> x4, waiting for transfers between devices: none -> 4.28 us  [fetched(): return lax.ppermute(x, ('exp', 'hid'), pairs)]
    pallas_call x6 -> x5, Pallas kernels: 2.24 us -> 2.28 us  [the longest x1 0.92 us: pass_on(): pl.pallas_call(pass_kernel, out_shape=(jax.ShapeDtypeStruct(tokens.shape,...]
where the time goes in v7:
time: 36.2 us; the launch traced here: 36 us
  starting transfers between devices  13.4 us (37%)
  Pallas kernels  12.4 us (34%)
  waiting for transfers between devices  9.97 us (28%)
    ppermute x4, starting transfers between devices, fetched(): return lax.ppermute(x, ('exp', 'hid'), pairs)  7.47 us
    ppermute x4, starting transfers between devices, swapped(): return lax.ppermute(x, 'exp', [(i, i ^ k) for i in range(SOURCES)])  5.73 us
    ppermute x4, waiting for transfers between devices, swapped(): return lax.ppermute(x, 'exp', [(i, i ^ k) for i in range(SOURCES)])  4.35 us
    ppermute x4, waiting for transfers between devices, fetched(): return lax.ppermute(x, ('exp', 'hid'), pairs)  4.28 us
    pallas_call x1, Pallas kernels, gate_rows(): pl.pallas_call(gate_kernel, out_shape=(jax.ShapeDtypeStruct((total, depth...  3.56 us
    pallas_call x1, Pallas kernels, hidden_rows(): pl.pallas_call(up_kernel, out_shape=jax.ShapeDtypeStruct(act.shape, jnp.b...  3.36 us
    pallas_call x2, Pallas kernels, down_half(): pl.pallas_call(functools.partial(down_kernel, other), out_shape=jax.Shape...  3.12 us
    ppermute x2, waiting for transfers between devices, swap_cores(): return lax.ppermute(x, 'hid', [(0, 1), (1, 0)])  1.34 us
  transfers between devices with their start and end apart: 10, of which 6 were waited for; matrix products, arithmetic and copies ran while one was open for 0% of the time, Pallas kernels for 6%

profile of v7, /device:TPU:0, one launch (start us, length us, event | category | flops | bytes accessed | tf_op | source)
XLA Modules:
  0.0 36.0 jit_solution(739582520731130882)
XLA Ops:
  0.0 0.0 copy-start.4
  0.0 0.9 %shard_map.74 = (bf16[4,4096]{1,0:T(4,128)(2,1)S(1)}, s32[1]{0:T(128)S(4)}) custom-call(bf16[4,4096]{1,0:T(4,128)(2,1)} %tokens_ref.1), custom_call_target="tpu_custom_call" | custom-call | flops 20000000000 | tf_op jit(solution)/shard_map/pallas_call | solution.py:44
  0.9 0.0 copy-start
  0.9 6.0 %collective-permute-start = (bf16[4,4096]{1,0:T(4,128)(2,1)S(1)}, bf16[4,4096]{1,0:T(4,128)(2,1)S(1)}, u32[]{:S(2)}, u32[]{:S(2)}) collective-permute-start(bf16[4,4096]{1,0:T(4,128)(2,1)S(1)} %get-tuple-element.16.tokens_ref), channel_id=1, source_target_pairs={{0,14},{2,12},{4,10},{6,8},{8,6},{10,4},{12,2},{14,0},{1,11},{3,9}... | collective-permute-start | bytes 98312 | tf_op jit(solution)/shard_map/ppermute | solution.py:243
  7.0 0.2 collective-permute-start.1
  7.2 0.4 %collective-permute-start.2 = (bf16[4,4096]{1,0:T(4,128)(2,1)S(1)}, bf16[4,4096]{1,0:T(4,128)(2,1)S(1)}, u32[]{:S(2)}, u32[]{:S(2)}) collective-permute-start(bf16[4,4096]{1,0:T(4,128)(2,1)S(1)} %get-tuple-element.16.tokens_ref), channel_id=1, source_target_pairs={{0,2},{2,0},{4,6},{6,4},{8,10},{10,8},{12,14},{14,12},{1,7},{3,5},... | collective-permute-start | bytes 98312 | tf_op jit(solution)/shard_map/ppermute | solution.py:243
  7.6 0.8 %collective-permute-start.3 = (bf16[4,4096]{1,0:T(4,128)(2,1)S(1)}, bf16[4,4096]{1,0:T(4,128)(2,1)S(1)}, u32[]{:S(2)}, u32[]{:S(2)}) collective-permute-start(bf16[4,4096]{1,0:T(4,128)(2,1)S(1)} %get-tuple-element.16.tokens_ref), channel_id=1, source_target_pairs={{1,5},{3,7},{5,1},{7,3},{9,13},{11,15},{13,9},{15,11},{17,21},{19,... | collective-permute-start | bytes 98312 | tf_op jit(solution)/shard_map/ppermute | solution.py:243
  8.4 0.5 %collective-permute-done.refs_0_ = bf16[4,4096]{1,0:T(4,128)(2,1)S(1)} collective-permute-done((bf16[4,4096]{1,0:T(4,128)(2,1)S(1)}, bf16[4,4096]{1,0:T(4,128)(2,1)S(1)}, u32[]{:S(2)}, u32[]{:S(2)}) %collective-permute-start) | collective-permute-done | bytes 32800 | tf_op jit(solution)/shard_map/ppermute | solution.py:243
  8.9 3.8 %collective-permute-done.1.refs_1_ = bf16[4,4096]{1,0:T(4,128)(2,1)S(1)} collective-permute-done((bf16[4,4096]{1,0:T(4,128)(2,1)S(1)}, bf16[4,4096]{1,0:T(4,128)(2,1)S(1)}, u32[]{:S(2)}, u32[]{:S(2)}) %collective-permute-start.1) | collective-permute-done | bytes 32800 | tf_op jit(solution)/shard_map/ppermute | solution.py:243
  12.7 0.0 collective-permute-done.2.refs_2_
  12.7 0.0 collective-permute-done.3.refs_3_
  12.7 0.0 slice-start
  12.7 0.0 slice-start.1
  12.7 0.0 slice-start.2
  12.8 0.1 collective-permute-start.4
  12.8 1.3 %collective-permute-done.4.got_ref = bf16[4,4,4096]{2,1,0:T(4,128)(2,1)S(1)} collective-permute-done((bf16[4,4,4096]{2,1,0:T(4,128)(2,1)S(1)}, bf16[4,4,4096]{2,1,0:T(4,128)(2,1)S(1)}, u32[]{:S(2)}, u32[]{:S(2)}) %collective-permute-start.4) | collective-permute-done | bytes 131104 | tf_op jit(solution)/shard_map/ppermute | solution.py:247
  14.2 0.0 copy-done.4
  14.2 3.6 %shard_map.76 = (bf16[32,4096]{1,0:T(8,128)(2,1)S(1)}, f32[32,2048]{1,0:T(8,128)S(1)}) custom-call(s32[1]{0:T(128)S(4)} %get-tuple-element.15.side_ref, bf16[4,4,4096]{2,1,0:T(4,128)(2,1)S(1)} %shard_map.75.mine_ref, bf16[4,4,4096]{2,1,0:T(4,128)(2,1)S(1)} %collective-permute-done.4.got_ref, bf16[4096,2048]{1,0:T(8,128)(2,1)S(1)} %copy-done.4), custom_call_target="tpu_custom_call" | custom-call | flops 5000000000 | tf_op jit(solution)/shard_map/pallas_call | solution.py:119
  17.7 0.0 copy-done
  17.7 0.0 slice-start.3
  17.8 3.4 %shard_map.77.h_ref = bf16[32,2048]{1,0:T(8,128)(2,1)S(1)} custom-call(bf16[32,4096]{1,0:T(8,128)(2,1)S(1)} %get-tuple-element.17.x_ref, f32[32,2048]{1,0:T(8,128)S(1)} %get-tuple-element.18.act_ref, bf16[4096,2048]{1,0:T(8,128)(2,1)S(1)} %copy-done), custom_call_target="tpu_custom_call" | custom-call | flops 2000000000 | tf_op jit(solution)/shard_map/pallas_call | solution.py:142
  21.1 0.0 slice-done
  21.1 0.0 slice-done.1
  21.1 0.0 slice-done.2
  21.2 0.0 slice-done.3
  21.2 0.0 copy-start.1
  21.2 0.0 copy-start.2
  21.2 0.0 copy-start.3
  21.2 1.6 %shard_map.79 = bf16[32,2048]{1,0:T(8,128)(2,1)S(1)} custom-call(s32[1]{0:T(128)S(4)} %get-tuple-element.15.side_ref, bf16[32,2048]{1,0:T(8,128)(2,1)S(1)} %shard_map.77.h_ref, bf16[2048,4096]{1,0:T(8,128)(2,1)S(1)} %bitcast.1), custom_call_target="tpu_custom_call" | custom-call | flops 268435456 | tf_op jit(solution)/shard_map/pallas_call | solution.py:165
  22.8 0.2 collective-permute-start.5
  22.9 1.6 %shard_map.78.keep_ref = f32[32,2048]{1,0:T(8,128)S(1)} custom-call(s32[1]{0:T(128)S(4)} %get-tuple-element.15.side_ref, bf16[32,2048]{1,0:T(8,128)(2,1)S(1)} %shard_map.77.h_ref, bf16[2048,4096]{1,0:T(8,128)(2,1)S(1)} %bitcast.1), custom_call_target="tpu_custom_call" | custom-call | flops 268435456 | tf_op jit(solution)/shard_map/pallas_call | solution.py:165
  24.5 0.0 collective-permute-done.5.got_ref
  24.6 2.1 %collective-permute-start.6 = (bf16[2,4,2048]{2,1,0:T(4,128)(2,1)S(1)}, bf16[2,4,2048]{2,1,0:T(4,128)(2,1)S(1)}, u32[]{:S(2)}, u32[]{:S(2)}) collective-permute-start(bf16[2,4,2048]{2,1,0:T(4,128)(2,1)S(1)} %get-tuple-element.20), channel_id=1, source_target_pairs={{0,12},{2,14},{4,8},{6,10},{8,4},{10,6},{12,0},{14,2},{1,13},{3,15... | collective-permute-start | bytes 98312 | tf_op jit(solution)/shard_map/ppermute | solution.py:235
  26.7 0.0 collective-permute-start.7
  26.7 2.4 %collective-permute-start.8 = (bf16[2,4,2048]{2,1,0:T(4,128)(2,1)S(1)}, bf16[2,4,2048]{2,1,0:T(4,128)(2,1)S(1)}, u32[]{:S(2)}, u32[]{:S(2)}) collective-permute-start(bf16[2,4,2048]{2,1,0:T(4,128)(2,1)S(1)} %get-tuple-element.22), channel_id=1, source_target_pairs={{0,4},{2,6},{4,0},{6,2},{8,12},{10,14},{12,8},{14,10},{1,5},{3,7},... | collective-permute-start | bytes 98312 | tf_op jit(solution)/shard_map/ppermute | solution.py:235
  29.0 0.0 copy-done.1
  29.0 0.0 copy-done.2
  29.0 0.0 copy-done.3
  29.0 0.6 %shard_map.73.gates_ref = f32[32,128]{1,0:T(8,128)S(1)} custom-call(s32[4]{0:T(128)S(1)} %copy-done.3, s32[4,128]{1,0:T(4,128)S(1)} %copy-done.1, f32[4,128]{1,0:T(4,128)S(1)} %copy-done.2), custom_call_target="tpu_custom_call" | custom-call | tf_op jit(solution)/shard_map/pallas_call | solution.py:73
  29.7 0.8 %collective-permute-done.6.refs_1_ = bf16[2,4,2048]{2,1,0:T(4,128)(2,1)S(1)} collective-permute-done((bf16[2,4,2048]{2,1,0:T(4,128)(2,1)S(1)}, bf16[2,4,2048]{2,1,0:T(4,128)(2,1)S(1)}, u32[]{:S(2)}, u32[]{:S(2)}) %collective-permute-start.6) | collective-permute-done | bytes 32800 | tf_op jit(solution)/shard_map/ppermute | solution.py:235
  30.5 1.0 %collective-permute-done.7.refs_2_ = bf16[2,4,2048]{2,1,0:T(4,128)(2,1)S(1)} collective-permute-done((bf16[2,4,2048]{2,1,0:T(4,128)(2,1)S(1)}, bf16[2,4,2048]{2,1,0:T(4,128)(2,1)S(1)}, u32[]{:S(2)}, u32[]{:S(2)}) %collective-permute-start.7) | collective-permute-done | bytes 32800 | tf_op jit(solution)/shard_map/ppermute | solution.py:235
  31.5 0.0 collective-permute-done.8.refs_3_
  31.5 0.1 shard_map.81
  31.6 1.3 %collective-permute-start.9 = (bf16[4,2048]{1,0:T(4,128)(2,1)S(1)}, bf16[4,2048]{1,0:T(4,128)(2,1)S(1)}, u32[]{:S(2)}, u32[]{:S(2)}) collective-permute-start(bf16[4,2048]{1,0:T(4,128)(2,1)S(1)} %get-tuple-element.24), channel_id=1, source_target_pairs={{0,2},{2,0},{4,6},{6,4},{8,10},{10,8},{12,14},{14,12},{1,3},{3,1},... | collective-permute-start | bytes 49160 | tf_op jit(solution)/shard_map/ppermute | solution.py:235
  32.9 2.5 %collective-permute-done.9.got_ref = bf16[4,2048]{1,0:T(4,128)(2,1)S(1)} collective-permute-done((bf16[4,2048]{1,0:T(4,128)(2,1)S(1)}, bf16[4,2048]{1,0:T(4,128)(2,1)S(1)}, u32[]{:S(2)}, u32[]{:S(2)}) %collective-permute-start.9) | collective-permute-done | bytes 16416 | tf_op jit(solution)/shard_map/ppermute | solution.py:235
  35.4 0.6 %shard_map.82 = bf16[4,2048]{1,0:T(4,128)(2,1)} custom-call(f32[4,2048]{1,0:T(4,128)S(1)} %get-tuple-element.23.own_ref, bf16[4,2048]{1,0:T(4,128)(2,1)S(1)} %collective-permute-done.9.got_ref), custom_call_target="tpu_custom_call" | custom-call | tf_op jit(solution)/shard_map/pallas_call | solution.py:225
  (3 shorter events, 0.1 us)
Async XLA Ops:
  0.0 14.2 %copy-start.4 = (bf16[4096,2048]{1,0:T(8,128)(2,1)S(1)}, bf16[4096,2048]{1,0:T(8,128)(2,1)}, u32[]{:S(2)}) copy-start(bf16[4096,2048]{1,0:T(8,128)(2,1)} %wg_ref.1) | copy-start | bytes 50331652
  0.9 16.8 %copy-start = (bf16[4096,2048]{1,0:T(8,128)(2,1)S(1)}, bf16[4096,2048]{1,0:T(8,128)(2,1)}, u32[]{:S(2)}) copy-start(bf16[4096,2048]{1,0:T(8,128)(2,1)} %wu_ref.1) | copy-start | bytes 50331652
  0.9 7.9 %collective-permute-start = (bf16[4,4096]{1,0:T(4,128)(2,1)S(1)}, bf16[4,4096]{1,0:T(4,128)(2,1)S(1)}, u32[]{:S(2)}, u32[]{:S(2)}) collective-permute-start(bf16[4,4096]{1,0:T(4,128)(2,1)S(1)} %get-tuple-element.16.tokens_ref), channel_id=1, source_target_pairs={{0,14},{2,12},{4,10},{6,8},{8,6},{10,4},{12,2},{14,0},{1,11},{3,9}... | collective-permute-start | bytes 98312 | tf_op jit(solution)/shard_map/ppermute | solution.py:243
  7.0 5.7 %collective-permute-start.1 = (bf16[4,4096]{1,0:T(4,128)(2,1)S(1)}, bf16[4,4096]{1,0:T(4,128)(2,1)S(1)}, u32[]{:S(2)}, u32[]{:S(2)}) collective-permute-start(bf16[4,4096]{1,0:T(4,128)(2,1)S(1)} %get-tuple-element.16.tokens_ref), channel_id=1, source_target_pairs={{0,12},{2,14},{4,8},{6,10},{8,4},{10,6},{12,0},{14,2},{1,9},{3,11}... | collective-permute-start | bytes 98312 | tf_op jit(solution)/shard_map/ppermute | solution.py:243
  7.2 5.5 %collective-permute-start.2 = (bf16[4,4096]{1,0:T(4,128)(2,1)S(1)}, bf16[4,4096]{1,0:T(4,128)(2,1)S(1)}, u32[]{:S(2)}, u32[]{:S(2)}) collective-permute-start(bf16[4,4096]{1,0:T(4,128)(2,1)S(1)} %get-tuple-element.16.tokens_ref), channel_id=1, source_target_pairs={{0,2},{2,0},{4,6},{6,4},{8,10},{10,8},{12,14},{14,12},{1,7},{3,5},... | collective-permute-start | bytes 98312 | tf_op jit(solution)/shard_map/ppermute | solution.py:243
  7.6 5.1 %collective-permute-start.3 = (bf16[4,4096]{1,0:T(4,128)(2,1)S(1)}, bf16[4,4096]{1,0:T(4,128)(2,1)S(1)}, u32[]{:S(2)}, u32[]{:S(2)}) collective-permute-start(bf16[4,4096]{1,0:T(4,128)(2,1)S(1)} %get-tuple-element.16.tokens_ref), channel_id=1, source_target_pairs={{1,5},{3,7},{5,1},{7,3},{9,13},{11,15},{13,9},{15,11},{17,21},{19,... | collective-permute-start | bytes 98312 | tf_op jit(solution)/shard_map/ppermute | solution.py:243
  12.7 8.4 %slice-start = ((s8[16777216]{0:T(1024)(128)(4,1)}), s8[4194304]{0:T(1024)(128)(4,1)S(1)}, s32[]{:S(2)}) async-start(s8[16777216]{0:T(1024)(128)(4,1)} %bitcast), calls=%async_computation | async-start | bytes 8388608
  12.7 8.4 %slice-start.1 = ((s8[16777216]{0:T(1024)(128)(4,1)}), s8[4194304]{0:T(1024)(128)(4,1)S(1)}, s32[]{:S(2)}) async-start(s8[16777216]{0:T(1024)(128)(4,1)} %bitcast), calls=%async_computation.1 | async-start | bytes 8388608
  12.7 8.4 %slice-start.2 = ((s8[16777216]{0:T(1024)(128)(4,1)}), s8[4194304]{0:T(1024)(128)(4,1)S(1)}, s32[]{:S(2)}) async-start(s8[16777216]{0:T(1024)(128)(4,1)} %bitcast), calls=%async_computation.2 | async-start | bytes 8388608
  12.8 1.4 %collective-permute-start.4 = (bf16[4,4,4096]{2,1,0:T(4,128)(2,1)S(1)}, bf16[4,4,4096]{2,1,0:T(4,128)(2,1)S(1)}, u32[]{:S(2)}, u32[]{:S(2)}) collective-permute-start(bf16[4,4,4096]{2,1,0:T(4,128)(2,1)S(1)} %shard_map.75.mine_ref), channel_id=1, source_target_pairs={{0,1},{1,0},{2,3},{3,2},{4,5},{5,4},{6,7},{7,6},{8,9},{9,8},{10,11... | collective-permute-start | bytes 393224 | tf_op jit(solution)/shard_map/ppermute | solution.py:247
  17.7 3.4 %slice-start.3 = ((s8[16777216]{0:T(1024)(128)(4,1)}), s8[4194304]{0:T(1024)(128)(4,1)S(1)}, s32[]{:S(2)}) async-start(s8[16777216]{0:T(1024)(128)(4,1)} %bitcast), calls=%async_computation.3 | async-start | bytes 8388608
  21.2 7.9 %copy-start.1 = (s32[4,128]{1,0:T(4,128)S(1)}, s32[4,128]{1,0:T(4,128)}, u32[]{:S(2)}) copy-start(s32[4,128]{1,0:T(4,128)} %rows_ref.1) | copy-start | bytes 6148
  21.2 7.8 %copy-start.2 = (f32[4,128]{1,0:T(4,128)S(1)}, f32[4,128]{1,0:T(4,128)}, u32[]{:S(2)}) copy-start(f32[4,128]{1,0:T(4,128)} %gates_ref.1) | copy-start | bytes 6148
  21.2 7.8 %copy-start.3 = (s32[4]{0:T(128)S(1)}, s32[4]{0:T(128)}, u32[]{:S(2)}) copy-start(s32[4]{0:T(128)} %counts_ref.1) | copy-start | bytes 52
  22.8 1.7 %collective-permute-start.5 = (bf16[32,2048]{1,0:T(8,128)(2,1)S(1)}, bf16[32,2048]{1,0:T(8,128)(2,1)S(1)}, u32[]{:S(2)}, u32[]{:S(2)}) collective-permute-start(bf16[32,2048]{1,0:T(8,128)(2,1)S(1)} %shard_map.79), channel_id=1, source_target_pairs={{0,1},{1,0},{2,3},{3,2},{4,5},{5,4},{6,7},{7,6},{8,9},{9,8},{10,11... | collective-permute-start | bytes 393224 | tf_op jit(solution)/shard_map/ppermute | solution.py:247
  24.6 5.9 %collective-permute-start.6 = (bf16[2,4,2048]{2,1,0:T(4,128)(2,1)S(1)}, bf16[2,4,2048]{2,1,0:T(4,128)(2,1)S(1)}, u32[]{:S(2)}, u32[]{:S(2)}) collective-permute-start(bf16[2,4,2048]{2,1,0:T(4,128)(2,1)S(1)} %get-tuple-element.20), channel_id=1, source_target_pairs={{0,12},{2,14},{4,8},{6,10},{8,4},{10,6},{12,0},{14,2},{1,13},{3,15... | collective-permute-start | bytes 98312 | tf_op jit(solution)/shard_map/ppermute | solution.py:235
  26.7 4.8 %collective-permute-start.7 = (bf16[2,4,2048]{2,1,0:T(4,128)(2,1)S(1)}, bf16[2,4,2048]{2,1,0:T(4,128)(2,1)S(1)}, u32[]{:S(2)}, u32[]{:S(2)}) collective-permute-start(bf16[2,4,2048]{2,1,0:T(4,128)(2,1)S(1)} %get-tuple-element.21), channel_id=1, source_target_pairs={{0,8},{2,10},{4,12},{6,14},{8,0},{10,2},{12,4},{14,6},{1,9},{3,11}... | collective-permute-start | bytes 98312 | tf_op jit(solution)/shard_map/ppermute | solution.py:235
  26.7 4.8 %collective-permute-start.8 = (bf16[2,4,2048]{2,1,0:T(4,128)(2,1)S(1)}, bf16[2,4,2048]{2,1,0:T(4,128)(2,1)S(1)}, u32[]{:S(2)}, u32[]{:S(2)}) collective-permute-start(bf16[2,4,2048]{2,1,0:T(4,128)(2,1)S(1)} %get-tuple-element.22), channel_id=1, source_target_pairs={{0,4},{2,6},{4,0},{6,2},{8,12},{10,14},{12,8},{14,10},{1,5},{3,7},... | collective-permute-start | bytes 98312 | tf_op jit(solution)/shard_map/ppermute | solution.py:235
  31.6 3.8 %collective-permute-start.9 = (bf16[4,2048]{1,0:T(4,128)(2,1)S(1)}, bf16[4,2048]{1,0:T(4,128)(2,1)S(1)}, u32[]{:S(2)}, u32[]{:S(2)}) collective-permute-start(bf16[4,2048]{1,0:T(4,128)(2,1)S(1)} %get-tuple-element.24), channel_id=1, source_target_pairs={{0,2},{2,0},{4,6},{6,4},{8,10},{10,8},{12,14},{14,12},{1,3},{3,1},... | collective-permute-start | bytes 49160 | tf_op jit(solution)/shard_map/ppermute | solution.py:235

commit v8 on v7

--- a/solution.py
+++ b/solution.py
@@ -33,17 +33,18 @@
     return pltpu.with_memory_space_constraint(x, pltpu.VMEM)
 
 
-def pass_kernel(tokens_ref, out_ref, side_ref, sem):
+def pass_kernel(tokens_ref, out_ref, place_ref, sem):
     copy = pltpu.make_async_copy(tokens_ref, out_ref, sem)
     copy.start()
-    side_ref[0] = lax.axis_index("hid")
+    place_ref[0] = lax.axis_index("hid")
+    place_ref[1] = lax.axis_index("exp")
     copy.wait()
 
 
 def pass_on(tokens):
     return pl.pallas_call(
         pass_kernel,
-        out_shape=(jax.ShapeDtypeStruct(tokens.shape, tokens.dtype), pltpu.SMEM((1,), jnp.int32)),
+        out_shape=(jax.ShapeDtypeStruct(tokens.shape, tokens.dtype), pltpu.SMEM((2,), jnp.int32)),
         in_specs=[HBM],
         out_specs=(VMEM, SMEM),
         scratch_shapes=[pltpu.SemaphoreType.DMA],
@@ -60,7 +61,7 @@
     own = lax.axis_index("exp")
     block = line // count
     token = (own ^ lax.rem(block, per_expert)) * count + lax.rem(line, count)
-    expert = (own // per_expert) ^ (block // per_expert)
+    expert = block // per_expert
     found = jnp.zeros((total, slots), jnp.float32)
     for e in range(experts):
         rows = rows_ref[pl.ds(e, 1), :]
@@ -79,41 +80,38 @@
     )(block_counts, block_rows, row_gates)
 
 
-def pack_kernel(side_ref, tokens_ref, *refs):
+def pack_kernel(place_ref, tokens_ref, *refs):
     *pieces, last_ref, out_ref = refs
     for r, ref in enumerate(pieces):
         out_ref[r + 1] = ref[...]
-    out_ref[0] = jnp.where(side_ref[0] == 0, tokens_ref[...], last_ref[...])
-
-
-def pack(side, tokens, pieces):
+    out_ref[0] = jnp.where(place_ref[0] == 0, tokens_ref[...], last_ref[...])
+
+
+def pack(place, tokens, pieces):
     return pl.pallas_call(
         pack_kernel,
         out_shape=jax.ShapeDtypeStruct((len(pieces), *tokens.shape), tokens.dtype),
         in_specs=[SMEM] + [VMEM] * (1 + len(pieces)),
         out_specs=VMEM,
         compiler_params=pltpu.CompilerParams(vmem_limit_bytes=2 * MIB),
-    )(in_smem(side), tokens, *pieces)
-
-
-def gate_kernel(side_ref, mine_ref, got_ref, wg_ref, x_ref, act_ref, wide):
+    )(in_smem(place), tokens, *pieces)
+
+
+def gate_kernel(place_ref, mine_ref, got_ref, wg_ref, x_ref, act_ref, wide):
     sets, count, _ = mine_ref.shape
-    first = side_ref[0] == 0
     for j in range(sets):
-        mine = mine_ref[j].astype(jnp.float32)
-        got = got_ref[j].astype(jnp.float32)
-        wide[pl.ds(j * count, count), :] = jnp.where(first, mine, got)
-        wide[pl.ds((sets + j) * count, count), :] = jnp.where(first, got, mine)
-    x_ref[...] = wide[...].astype(jnp.bfloat16)
-
-    @pl.loop(0, wg_ref.shape[1] // TILE)
-    def _(n):
-        cols = pl.ds(pl.multiple_of(n * TILE, TILE), TILE)
+        rows = pl.ds(j * count, count)
+        wide[place_ref[0], rows, :] = mine_ref[j].astype(jnp.float32)
+        wide[1 - place_ref[0], rows, :] = got_ref[j].astype(jnp.float32)
+    x_ref[...] = wide[...].reshape(x_ref.shape).astype(jnp.bfloat16)
+
+    for n in range(wg_ref.shape[1] // TILE):
+        cols = pl.ds(n * TILE, TILE)
         gate = jnp.dot(x_ref[...], wg_ref[:, cols], preferred_element_type=jnp.float32)
         act_ref[:, cols] = gate / (1.0 + jnp.exp(-gate))
 
 
-def gate_rows(side, mine, got, wg):
+def gate_rows(place, mine, got, wg):
     total = 2 * mine.shape[0] * mine.shape[1]
     depth, width = wg.shape
     return pl.pallas_call(
@@ -124,16 +122,15 @@
         ),
         in_specs=[SMEM] + [VMEM] * 3,
         out_specs=(VMEM, VMEM),
-        scratch_shapes=[pltpu.VMEM((total, depth), jnp.float32)],
+        scratch_shapes=[pltpu.VMEM((2, total // 2, depth), jnp.float32)],
         compiler_params=pltpu.CompilerParams(vmem_limit_bytes=2 * MIB),
         cost_estimate=pl.CostEstimate(flops=GATE, bytes_accessed=0, transcendentals=total * width),
-    )(in_smem(side), mine, got, in_vmem(wg))
+    )(in_smem(place), mine, got, in_vmem(wg))
 
 
 def up_kernel(x_ref, act_ref, wu_ref, h_out):
-    @pl.loop(0, wu_ref.shape[1] // TILE)
-    def _(n):
-        cols = pl.ds(pl.multiple_of(n * TILE, TILE), TILE)
+    for n in range(wu_ref.shape[1] // TILE):
+        cols = pl.ds(n * TILE, TILE)
         up = jnp.dot(x_ref[...], wu_ref[:, cols], preferred_element_type=jnp.float32)
         h_out[:, cols] = (act_ref[:, cols] * up).astype(jnp.bfloat16)
 
@@ -149,9 +146,9 @@
     )(x, act, in_vmem(wu))
 
 
-def down_kernel(other, side_ref, h_ref, wd_ref, out_ref):
+def down_kernel(other, place_ref, h_ref, wd_ref, out_ref):
     half = wd_ref.shape[1] // 2
-    side = side_ref[0]
+    side = place_ref[0]
     base = (1 - side if other else side) * half
     for n in range(half // TILE):
         cols = pl.ds(pl.multiple_of(base + n * TILE, TILE), TILE)
@@ -159,7 +156,7 @@
         out_ref[:, pl.ds(n * TILE, TILE)] = part.astype(out_ref.dtype)
 
 
-def down_half(side, hidden, wd, other, dtype):
+def down_half(place, hidden, wd, other, dtype):
     rows, depth = hidden.shape
     half = wd.shape[1] // 2
     return pl.pallas_call(
@@ -169,52 +166,49 @@
         out_specs=VMEM,
         compiler_params=pltpu.CompilerParams(vmem_limit_bytes=2 * MIB),
         cost_estimate=pl.CostEstimate(flops=2 * rows * depth * half, bytes_accessed=0, transcendentals=0),
-    )(in_smem(side), hidden, in_vmem(wd))
-
-
-def near_kernel(keep_ref, got_ref, own_ref, *out_refs):
-    near, count, _ = own_ref.shape
+    )(in_smem(place), hidden, in_vmem(wd))
+
+
+def near_kernel(place_ref, keep_ref, got_ref, out_ref):
+    _, near, count, _ = out_ref.shape
     both = keep_ref[...] + got_ref[...].astype(jnp.float32)
+    expert = place_ref[1] // near
     for at, k in enumerate(ORDER):
-        out_ref = (own_ref, *out_refs)[k // near]
-        out_ref[k % near] = both[at * count : (at + 1) * count].astype(out_ref.dtype)
-
-
-def near(keep, got, per_expert):
+        out_ref[expert ^ (k // near), k % near] = both[at * count : (at + 1) * count].astype(out_ref.dtype)
+
+
+def near(place, keep, got, per_expert):
     rows, width = keep.shape
-    shape = (per_expert, rows // SOURCES, width)
-    others = SOURCES // per_expert - 1
     return pl.pallas_call(
         near_kernel,
-        out_shape=(jax.ShapeDtypeStruct(shape, jnp.float32),)
-        + (jax.ShapeDtypeStruct(shape, jnp.bfloat16),) * others,
-        in_specs=[VMEM, VMEM],
-        out_specs=(VMEM,) * (1 + others),
-        compiler_params=pltpu.CompilerParams(vmem_limit_bytes=2 * MIB),
-    )(keep, got)
-
-
-def weigh_kernel(gates_ref, *refs):
-    *parts, own_ref, next_ref = refs
-    near, count, _ = parts[0].shape
+        out_shape=jax.ShapeDtypeStruct(
+            (SOURCES // per_expert, per_expert, rows // SOURCES, width), jnp.bfloat16
+        ),
+        in_specs=[SMEM, VMEM, VMEM],
+        out_specs=VMEM,
+        compiler_params=pltpu.CompilerParams(vmem_limit_bytes=2 * MIB),
+    )(in_smem(place), keep, got)
+
+
+def weigh_kernel(gates_ref, parts_ref, own_ref, next_ref):
+    experts, near, count, _ = parts_ref.shape
     for i, out_ref in enumerate((own_ref, next_ref)):
         total = jnp.zeros(out_ref.shape, jnp.float32)
-        for at, part_ref in enumerate(parts):
-            j = (len(parts) - at) % len(parts)
-            gates = gates_ref[pl.ds((j * near + i) * count, count), :1]
-            total = total + part_ref[i].astype(jnp.float32) * gates
+        for e in range(experts):
+            gates = gates_ref[pl.ds((e * near + i) * count, count), :1]
+            total = total + parts_ref[e, i].astype(jnp.float32) * gates
         out_ref[...] = total.astype(out_ref.dtype)
 
 
 def weigh(gates, parts):
-    shape = parts[0].shape[1:]
+    shape = parts.shape[2:]
     return pl.pallas_call(
         weigh_kernel,
         out_shape=(jax.ShapeDtypeStruct(shape, jnp.float32), jax.ShapeDtypeStruct(shape, jnp.bfloat16)),
-        in_specs=[VMEM] * (1 + len(parts)),
+        in_specs=[VMEM, VMEM],
         out_specs=(VMEM, VMEM),
         compiler_params=pltpu.CompilerParams(vmem_limit_bytes=2 * MIB),
-    )(gates, *parts)
+    )(gates, parts)
 
 
 def sum_kernel(own_ref, got_ref, out_ref):
@@ -249,19 +243,22 @@
 
 def local(tokens, w_gate, w_up, w_down, block_counts, block_rows, row_gates):
     per_expert = SOURCES // block_rows.shape[0]
-    tokens, side = pass_on(tokens)
+    tokens, place = pass_on(tokens)
     half = SOURCES // 2
     pieces = [fetched(tokens, ORDER[b], ORDER[half + b]) for b in range(1, half)]
     pieces += [fetched(tokens, None, ORDER[half])]
-    mine = pack(side, tokens, pieces)
-    x, act = gate_rows(side, mine, swap_cores(mine), w_gate)
+    mine = pack(place, tokens, pieces)
+    x, act = gate_rows(place, mine, swap_cores(mine), w_gate)
     hidden = hidden_rows(x, act, w_up)
-    send = down_half(side, hidden, w_down, True, jnp.bfloat16)
-    keep = down_half(side, hidden, w_down, False, jnp.float32)
-    parts = near(keep, swap_cores(send), per_expert)
-    returned = [swapped(parts[j], per_expert * j) for j in range(len(parts) - 1, 0, -1)]
+    send = down_half(place, hidden, w_down, True, jnp.bfloat16)
+    keep = down_half(place, hidden, w_down, False, jnp.float32)
+    parts = near(place, keep, swap_cores(send), per_expert)
+    lines = [[i + per_expert * e for e in range(SOURCES // per_expert)] for i in range(per_expert)]
+    returned = lax.all_to_all(
+        parts, "exp", split_axis=0, concat_axis=0, tiled=True, axis_index_groups=lines
+    )
     gates = route(block_counts, block_rows, row_gates, tokens.shape[0])
-    own, other = weigh(gates, [parts[0], *returned])
+    own, other = weigh(gates, returned)
     return final_sum(own, swapped(other, 1))
 
 

time: 36.2 us -> 38.9 us (1.075)
  waiting for transfers between devices: 9.97 us -> 14.4 us
  starting transfers between devices: 13.4 us -> 11.9 us
    all_to_all x0 -> x1, waiting for transfers between devices: none -> 5.82 us  [local(): lax.all_to_all(parts, 'exp', split_axis=0, concat_axis=0, tiled=True, axi...]
    ppermute x4 -> x1, starting transfers between devices: 5.73 us -> 0.86 us  [swapped(): return lax.ppermute(x, 'exp', [(i, i ^ k) for i in range(SOURCES)])]
    all_to_all x0 -> x1, starting transfers between devices: none -> 3.32 us  [local(): lax.all_to_all(parts, 'exp', split_axis=0, concat_axis=0, tiled=True, axi...]
    ppermute x4 -> x1, waiting for transfers between devices: 4.35 us -> 2.94 us  [swapped(): return lax.ppermute(x, 'exp', [(i, i ^ k) for i in range(SOURCES)])]
    pallas_call x1, Pallas kernels: 0.05 us -> 0.69 us  [near(): pl.pallas_call(near_kernel, out_shape=jax.ShapeDtypeStruct((SOURCES // pe...]
    pallas_call x1, Pallas kernels: 3.56 us -> 3.08 us  [gate_rows(): pl.pallas_call(gate_kernel, out_shape=(jax.ShapeDtypeStruct((total, depth...]
  transfers between devices with their start and end apart: 10 -> 8, of which waited for: 6 -> 5; matrix products, arithmetic and copies ran while one was open for 0% -> 0% of each run, Pallas kernels for 6% -> 6%
where the time goes in v8:
time: 38.9 us; the launch traced here: 38.7 us
  waiting for transfers between devices  14.4 us (37%)
  Pallas kernels  12.2 us (31%)
  starting transfers between devices  11.9 us (31%)
    ppermute x4, starting transfers between devices, fetched(): return lax.ppermute(x, ('exp', 'hid'), pairs)  7.47 us
    all_to_all x1, waiting for transfers between devices, local(): lax.all_to_all(parts, 'exp', split_axis=0, concat_axis=0, tiled=True, axi...  5.82 us
    ppermute x4, waiting for transfers between devices, fetched(): return lax.ppermute(x, ('exp', 'hid'), pairs)  4.28 us
    all_to_all x1, starting transfers between devices, local(): lax.all_to_all(parts, 'exp', split_axis=0, concat_axis=0, tiled=True, axi...  3.32 us
    pallas_call x2, Pallas kernels, down_half(): pl.pallas_call(functools.partial(down_kernel, other), out_shape=jax.Shape...  3.12 us
    pallas_call x1, Pallas kernels, gate_rows(): pl.pallas_call(gate_kernel, out_shape=(jax.ShapeDtypeStruct((total, depth...  3.08 us
    pallas_call x1, Pallas kernels, hidden_rows(): pl.pallas_call(up_kernel, out_shape=jax.ShapeDtypeStruct(act.shape, jnp.b...  3.01 us
    ppermute x1, waiting for transfers between devices, swapped(): return lax.ppermute(x, 'exp', [(i, i ^ k) for i in range(SOURCES)])  2.94 us
  transfers between devices with their start and end apart: 8, of which 5 were waited for; matrix products, arithmetic and copies ran while one was open for 0% of the time, Pallas kernels for 6%

profile of v8, /device:TPU:0, one launch (start us, length us, event | category | flops | bytes accessed | tf_op | source)
XLA Modules:
  0.0 38.7 jit_solution(8410641885898180662)
XLA Ops:
  0.0 0.0 copy-start.4
  0.0 0.9 %shard_map.74 = (bf16[4,4096]{1,0:T(4,128)(2,1)S(1)}, s32[2]{0:T(128)S(4)}) custom-call(bf16[4,4096]{1,0:T(4,128)(2,1)} %tokens_ref.1), custom_call_target="tpu_custom_call" | custom-call | flops 20000000000 | tf_op jit(solution)/shard_map/pallas_call | solution.py:45
  0.9 0.0 copy-start
  0.9 6.0 %collective-permute-start = (bf16[4,4096]{1,0:T(4,128)(2,1)S(1)}, bf16[4,4096]{1,0:T(4,128)(2,1)S(1)}, u32[]{:S(2)}, u32[]{:S(2)}) collective-permute-start(bf16[4,4096]{1,0:T(4,128)(2,1)S(1)} %get-tuple-element.12.tokens_ref), channel_id=1, source_target_pairs={{0,14},{2,12},{4,10},{6,8},{8,6},{10,4},{12,2},{14,0},{1,11},{3,9}... | collective-permute-start | bytes 98312 | tf_op jit(solution)/shard_map/ppermute | solution.py:237
  7.0 0.2 collective-permute-start.1
  7.2 0.4 %collective-permute-start.2 = (bf16[4,4096]{1,0:T(4,128)(2,1)S(1)}, bf16[4,4096]{1,0:T(4,128)(2,1)S(1)}, u32[]{:S(2)}, u32[]{:S(2)}) collective-permute-start(bf16[4,4096]{1,0:T(4,128)(2,1)S(1)} %get-tuple-element.12.tokens_ref), channel_id=1, source_target_pairs={{0,2},{2,0},{4,6},{6,4},{8,10},{10,8},{12,14},{14,12},{1,7},{3,5},... | collective-permute-start | bytes 98312 | tf_op jit(solution)/shard_map/ppermute | solution.py:237
  7.6 0.8 %collective-permute-start.3 = (bf16[4,4096]{1,0:T(4,128)(2,1)S(1)}, bf16[4,4096]{1,0:T(4,128)(2,1)S(1)}, u32[]{:S(2)}, u32[]{:S(2)}) collective-permute-start(bf16[4,4096]{1,0:T(4,128)(2,1)S(1)} %get-tuple-element.12.tokens_ref), channel_id=1, source_target_pairs={{1,5},{3,7},{5,1},{7,3},{9,13},{11,15},{13,9},{15,11},{17,21},{19,... | collective-permute-start | bytes 98312 | tf_op jit(solution)/shard_map/ppermute | solution.py:237
  8.4 0.5 %collective-permute-done.refs_0_ = bf16[4,4096]{1,0:T(4,128)(2,1)S(1)} collective-permute-done((bf16[4,4096]{1,0:T(4,128)(2,1)S(1)}, bf16[4,4096]{1,0:T(4,128)(2,1)S(1)}, u32[]{:S(2)}, u32[]{:S(2)}) %collective-permute-start) | collective-permute-done | bytes 32800 | tf_op jit(solution)/shard_map/ppermute | solution.py:237
  8.9 3.8 %collective-permute-done.1.refs_1_ = bf16[4,4096]{1,0:T(4,128)(2,1)S(1)} collective-permute-done((bf16[4,4096]{1,0:T(4,128)(2,1)S(1)}, bf16[4,4096]{1,0:T(4,128)(2,1)S(1)}, u32[]{:S(2)}, u32[]{:S(2)}) %collective-permute-start.1) | collective-permute-done | bytes 32800 | tf_op jit(solution)/shard_map/ppermute | solution.py:237
  12.7 0.0 collective-permute-done.2.refs_2_
  12.7 0.0 collective-permute-done.3.refs_3_
  12.7 0.0 slice-start
  12.7 0.0 slice-start.1
  12.7 0.0 slice-start.2
  12.8 0.1 collective-permute-start.4
  12.8 1.3 %collective-permute-done.4.got_ref = bf16[4,4,4096]{2,1,0:T(4,128)(2,1)S(1)} collective-permute-done((bf16[4,4,4096]{2,1,0:T(4,128)(2,1)S(1)}, bf16[4,4,4096]{2,1,0:T(4,128)(2,1)S(1)}, u32[]{:S(2)}, u32[]{:S(2)}) %collective-permute-start.4) | collective-permute-done | bytes 131104 | tf_op jit(solution)/shard_map/ppermute | solution.py:241
  14.2 0.0 copy-done.4
  14.2 3.1 %shard_map.76 = (bf16[32,4096]{1,0:T(8,128)(2,1)S(1)}, f32[32,2048]{1,0:T(8,128)S(1)}) custom-call(s32[2]{0:T(128)S(4)} %get-tuple-element.11.place_ref, bf16[4,4,4096]{2,1,0:T(4,128)(2,1)S(1)} %shard_map.75.mine_ref, bf16[4,4,4096]{2,1,0:T(4,128)(2,1)S(1)} %collective-permute-done.4.got_ref, bf16[4096,2048]{1,0:T(8,128)(2,1)S(1)} %copy-done.4), custom_call_target="tpu_custom_call" | custom-call | flops 5000000000 | tf_op jit(solution)/shard_map/pallas_call | solution.py:117
  17.3 0.0 copy-done
  17.3 0.0 slice-start.3
  17.3 3.0 %shard_map.77.h_ref = bf16[32,2048]{1,0:T(8,128)(2,1)S(1)} custom-call(bf16[32,4096]{1,0:T(8,128)(2,1)S(1)} %get-tuple-element.13.x_ref, f32[32,2048]{1,0:T(8,128)S(1)} %get-tuple-element.14.act_ref, bf16[4096,2048]{1,0:T(8,128)(2,1)S(1)} %copy-done), custom_call_target="tpu_custom_call" | custom-call | flops 2000000000 | tf_op jit(solution)/shard_map/pallas_call | solution.py:139
  20.3 0.0 slice-done
  20.3 0.0 slice-done.1
  20.3 0.0 slice-done.2
  20.3 0.0 slice-done.3
  20.3 0.0 copy-start.1
  20.4 0.0 copy-start.2
  20.4 0.0 copy-start.3
  20.4 1.6 %shard_map.79 = bf16[32,2048]{1,0:T(8,128)(2,1)S(1)} custom-call(s32[2]{0:T(128)S(4)} %get-tuple-element.11.place_ref, bf16[32,2048]{1,0:T(8,128)(2,1)S(1)} %shard_map.77.h_ref, bf16[2048,4096]{1,0:T(8,128)(2,1)S(1)} %bitcast.1), custom_call_target="tpu_custom_call" | custom-call | flops 268435456 | tf_op jit(solution)/shard_map/pallas_call | solution.py:162
  21.9 0.2 collective-permute-start.5
  22.1 1.6 %shard_map.78.keep_ref = f32[32,2048]{1,0:T(8,128)S(1)} custom-call(s32[2]{0:T(128)S(4)} %get-tuple-element.11.place_ref, bf16[32,2048]{1,0:T(8,128)(2,1)S(1)} %shard_map.77.h_ref, bf16[2048,4096]{1,0:T(8,128)(2,1)S(1)} %bitcast.1), custom_call_target="tpu_custom_call" | custom-call | flops 268435456 | tf_op jit(solution)/shard_map/pallas_call | solution.py:162
  23.7 0.0 collective-permute-done.5.got_ref
  23.7 0.7 %shard_map.80 = bf16[4,2,4,2048]{3,2,1,0:T(4,128)(2,1)} custom-call(s32[2]{0:T(128)S(4)} %get-tuple-element.11.place_ref, f32[32,2048]{1,0:T(8,128)S(1)} %shard_map.78.keep_ref, bf16[32,2048]{1,0:T(8,128)(2,1)S(1)} %collective-permute-done.5.got_ref), custom_call_target="tpu_custom_call" | custom-call | tf_op jit(solution)/shard_map/pallas_call | solution.py:182
  24.4 3.3 %all-to-all-start = ((bf16[4,2,4,2048]{3,2,1,0:T(4,128)(2,1)}), bf16[4,2,4,2048]{3,2,1,0:T(4,128)(2,1)S(1)}, u32[]{:S(2)}, u32[]{:S(2)}) async-start(bf16[4,2,4,2048]{3,2,1,0:T(4,128)(2,1)} %shard_map.80), calls=%async_computation | async-start | bytes 262144 | tf_op jit(solution)/shard_map/all_to_all | solution.py:257
  27.7 0.0 copy-done.1
  27.7 0.0 copy-done.2
  27.7 0.0 copy-done.3
  27.7 0.6 %shard_map.73.gates_ref = f32[32,128]{1,0:T(8,128)S(1)} custom-call(s32[4]{0:T(128)S(1)} %copy-done.3, s32[4,128]{1,0:T(4,128)S(1)} %copy-done.1, f32[4,128]{1,0:T(4,128)S(1)} %copy-done.2), custom_call_target="tpu_custom_call" | custom-call | tf_op jit(solution)/shard_map/pallas_call | solution.py:74
  28.4 5.8 %all-to-all-done.parts_ref = bf16[4,2,4,2048]{3,2,1,0:T(4,128)(2,1)S(1)} async-done(((bf16[4,2,4,2048]{3,2,1,0:T(4,128)(2,1)}), bf16[4,2,4,2048]{3,2,1,0:T(4,128)(2,1)S(1)}, u32[]{:S(2)}, u32[]{:S(2)}) %all-to-all-start) | async-done | bytes 131104 | tf_op jit(solution)/shard_map/all_to_all | solution.py:257
  34.2 0.1 shard_map.81
  34.3 0.9 %collective-permute-start.6 = (bf16[4,2048]{1,0:T(4,128)(2,1)S(1)}, bf16[4,2048]{1,0:T(4,128)(2,1)S(1)}, u32[]{:S(2)}, u32[]{:S(2)}) collective-permute-start(bf16[4,2048]{1,0:T(4,128)(2,1)S(1)} %get-tuple-element.16), channel_id=1, source_target_pairs={{0,2},{2,0},{4,6},{6,4},{8,10},{10,8},{12,14},{14,12},{1,3},{3,1},... | collective-permute-start | bytes 49160 | tf_op jit(solution)/shard_map/ppermute | solution.py:229
  35.1 2.9 %collective-permute-done.6.got_ref = bf16[4,2048]{1,0:T(4,128)(2,1)S(1)} collective-permute-done((bf16[4,2048]{1,0:T(4,128)(2,1)S(1)}, bf16[4,2048]{1,0:T(4,128)(2,1)S(1)}, u32[]{:S(2)}, u32[]{:S(2)}) %collective-permute-start.6) | collective-permute-done | bytes 16416 | tf_op jit(solution)/shard_map/ppermute | solution.py:229
  38.1 0.6 %shard_map.82 = bf16[4,2048]{1,0:T(4,128)(2,1)} custom-call(f32[4,2048]{1,0:T(4,128)S(1)} %get-tuple-element.15.own_ref, bf16[4,2048]{1,0:T(4,128)(2,1)S(1)} %collective-permute-done.6.got_ref), custom_call_target="tpu_custom_call" | custom-call | tf_op jit(solution)/shard_map/pallas_call | solution.py:219
  (2 shorter events, 0.0 us)
Async XLA Ops:
  0.0 14.2 %copy-start.4 = (bf16[4096,2048]{1,0:T(8,128)(2,1)S(1)}, bf16[4096,2048]{1,0:T(8,128)(2,1)}, u32[]{:S(2)}) copy-start(bf16[4096,2048]{1,0:T(8,128)(2,1)} %wg_ref.1) | copy-start | bytes 50331652
  0.9 16.3 %copy-start = (bf16[4096,2048]{1,0:T(8,128)(2,1)S(1)}, bf16[4096,2048]{1,0:T(8,128)(2,1)}, u32[]{:S(2)}) copy-start(bf16[4096,2048]{1,0:T(8,128)(2,1)} %wu_ref.1) | copy-start | bytes 50331652
  0.9 7.9 %collective-permute-start = (bf16[4,4096]{1,0:T(4,128)(2,1)S(1)}, bf16[4,4096]{1,0:T(4,128)(2,1)S(1)}, u32[]{:S(2)}, u32[]{:S(2)}) collective-permute-start(bf16[4,4096]{1,0:T(4,128)(2,1)S(1)} %get-tuple-element.12.tokens_ref), channel_id=1, source_target_pairs={{0,14},{2,12},{4,10},{6,8},{8,6},{10,4},{12,2},{14,0},{1,11},{3,9}... | collective-permute-start | bytes 98312 | tf_op jit(solution)/shard_map/ppermute | solution.py:237
  7.0 5.7 %collective-permute-start.1 = (bf16[4,4096]{1,0:T(4,128)(2,1)S(1)}, bf16[4,4096]{1,0:T(4,128)(2,1)S(1)}, u32[]{:S(2)}, u32[]{:S(2)}) collective-permute-start(bf16[4,4096]{1,0:T(4,128)(2,1)S(1)} %get-tuple-element.12.tokens_ref), channel_id=1, source_target_pairs={{0,12},{2,14},{4,8},{6,10},{8,4},{10,6},{12,0},{14,2},{1,9},{3,11}... | collective-permute-start | bytes 98312 | tf_op jit(solution)/shard_map/ppermute | solution.py:237
  7.2 5.5 %collective-permute-start.2 = (bf16[4,4096]{1,0:T(4,128)(2,1)S(1)}, bf16[4,4096]{1,0:T(4,128)(2,1)S(1)}, u32[]{:S(2)}, u32[]{:S(2)}) collective-permute-start(bf16[4,4096]{1,0:T(4,128)(2,1)S(1)} %get-tuple-element.12.tokens_ref), channel_id=1, source_target_pairs={{0,2},{2,0},{4,6},{6,4},{8,10},{10,8},{12,14},{14,12},{1,7},{3,5},... | collective-permute-start | bytes 98312 | tf_op jit(solution)/shard_map/ppermute | solution.py:237
  7.6 5.1 %collective-permute-start.3 = (bf16[4,4096]{1,0:T(4,128)(2,1)S(1)}, bf16[4,4096]{1,0:T(4,128)(2,1)S(1)}, u32[]{:S(2)}, u32[]{:S(2)}) collective-permute-start(bf16[4,4096]{1,0:T(4,128)(2,1)S(1)} %get-tuple-element.12.tokens_ref), channel_id=1, source_target_pairs={{1,5},{3,7},{5,1},{7,3},{9,13},{11,15},{13,9},{15,11},{17,21},{19,... | collective-permute-start | bytes 98312 | tf_op jit(solution)/shard_map/ppermute | solution.py:237
  12.7 7.6 %slice-start = ((s8[16777216]{0:T(1024)(128)(4,1)}), s8[4194304]{0:T(1024)(128)(4,1)S(1)}, s32[]{:S(2)}) async-start(s8[16777216]{0:T(1024)(128)(4,1)} %bitcast), calls=%async_computation.1 | async-start | bytes 8388608
  12.7 7.6 %slice-start.1 = ((s8[16777216]{0:T(1024)(128)(4,1)}), s8[4194304]{0:T(1024)(128)(4,1)S(1)}, s32[]{:S(2)}) async-start(s8[16777216]{0:T(1024)(128)(4,1)} %bitcast), calls=%async_computation.2 | async-start | bytes 8388608
  12.7 7.6 %slice-start.2 = ((s8[16777216]{0:T(1024)(128)(4,1)}), s8[4194304]{0:T(1024)(128)(4,1)S(1)}, s32[]{:S(2)}) async-start(s8[16777216]{0:T(1024)(128)(4,1)} %bitcast), calls=%async_computation.3 | async-start | bytes 8388608
  12.8 1.4 %collective-permute-start.4 = (bf16[4,4,4096]{2,1,0:T(4,128)(2,1)S(1)}, bf16[4,4,4096]{2,1,0:T(4,128)(2,1)S(1)}, u32[]{:S(2)}, u32[]{:S(2)}) collective-permute-start(bf16[4,4,4096]{2,1,0:T(4,128)(2,1)S(1)} %shard_map.75.mine_ref), channel_id=1, source_target_pairs={{0,1},{1,0},{2,3},{3,2},{4,5},{5,4},{6,7},{7,6},{8,9},{9,8},{10,11... | collective-permute-start | bytes 393224 | tf_op jit(solution)/shard_map/ppermute | solution.py:241
  17.3 3.1 %slice-start.3 = ((s8[16777216]{0:T(1024)(128)(4,1)}), s8[4194304]{0:T(1024)(128)(4,1)S(1)}, s32[]{:S(2)}) async-start(s8[16777216]{0:T(1024)(128)(4,1)} %bitcast), calls=%async_computation.4 | async-start | bytes 8388608
  20.3 7.4 %copy-start.1 = (s32[4,128]{1,0:T(4,128)S(1)}, s32[4,128]{1,0:T(4,128)}, u32[]{:S(2)}) copy-start(s32[4,128]{1,0:T(4,128)} %rows_ref.1) | copy-start | bytes 6148
  20.4 7.4 %copy-start.2 = (f32[4,128]{1,0:T(4,128)S(1)}, f32[4,128]{1,0:T(4,128)}, u32[]{:S(2)}) copy-start(f32[4,128]{1,0:T(4,128)} %gates_ref.1) | copy-start | bytes 6148
  20.4 7.4 %copy-start.3 = (s32[4]{0:T(128)S(1)}, s32[4]{0:T(128)}, u32[]{:S(2)}) copy-start(s32[4]{0:T(128)} %counts_ref.1) | copy-start | bytes 52
  21.9 1.7 %collective-permute-start.5 = (bf16[32,2048]{1,0:T(8,128)(2,1)S(1)}, bf16[32,2048]{1,0:T(8,128)(2,1)S(1)}, u32[]{:S(2)}, u32[]{:S(2)}) collective-permute-start(bf16[32,2048]{1,0:T(8,128)(2,1)S(1)} %shard_map.79), channel_id=1, source_target_pairs={{0,1},{1,0},{2,3},{3,2},{4,5},{5,4},{6,7},{7,6},{8,9},{9,8},{10,11... | collective-permute-start | bytes 393224 | tf_op jit(solution)/shard_map/ppermute | solution.py:241
  24.4 9.8 %all-to-all-start = ((bf16[4,2,4,2048]{3,2,1,0:T(4,128)(2,1)}), bf16[4,2,4,2048]{3,2,1,0:T(4,128)(2,1)S(1)}, u32[]{:S(2)}, u32[]{:S(2)}) async-start(bf16[4,2,4,2048]{3,2,1,0:T(4,128)(2,1)} %shard_map.80), calls=%async_computation | async-start | bytes 262144 | tf_op jit(solution)/shard_map/all_to_all | solution.py:257
  34.3 3.8 %collective-permute-start.6 = (bf16[4,2048]{1,0:T(4,128)(2,1)S(1)}, bf16[4,2048]{1,0:T(4,128)(2,1)S(1)}, u32[]{:S(2)}, u32[]{:S(2)}) collective-permute-start(bf16[4,2048]{1,0:T(4,128)(2,1)S(1)} %get-tuple-element.16), channel_id=1, source_target_pairs={{0,2},{2,0},{4,6},{6,4},{8,10},{10,8},{12,14},{14,12},{1,3},{3,1},... | collective-permute-start | bytes 49160 | tf_op jit(solution)/shard_map/ppermute | solution.py:229

commit v9 on v8

--- a/solution.py
+++ b/solution.py
@@ -33,56 +33,53 @@
     return pltpu.with_memory_space_constraint(x, pltpu.VMEM)
 
 
-def pass_kernel(tokens_ref, out_ref, place_ref, sem):
-    copy = pltpu.make_async_copy(tokens_ref, out_ref, sem)
+def pass_kernel(tokens_ref, counts_ref, out_ref, counts_out, place_ref, sems):
+    copy = pltpu.make_async_copy(tokens_ref, out_ref, sems.at[0])
     copy.start()
+    small = pltpu.make_async_copy(counts_ref, counts_out, sems.at[1])
+    small.start()
     place_ref[0] = lax.axis_index("hid")
     place_ref[1] = lax.axis_index("exp")
     copy.wait()
-
-
-def pass_on(tokens):
+    small.wait()
+
+
+def pass_on(tokens, counts):
     return pl.pallas_call(
         pass_kernel,
-        out_shape=(jax.ShapeDtypeStruct(tokens.shape, tokens.dtype), pltpu.SMEM((2,), jnp.int32)),
-        in_specs=[HBM],
-        out_specs=(VMEM, SMEM),
-        scratch_shapes=[pltpu.SemaphoreType.DMA],
+        out_shape=(
+            jax.ShapeDtypeStruct(tokens.shape, tokens.dtype),
+            pltpu.SMEM(counts.shape, counts.dtype),
+            pltpu.SMEM((2,), jnp.int32),
+        ),
+        in_specs=[HBM, HBM],
+        out_specs=(VMEM, SMEM, SMEM),
+        scratch_shapes=[pltpu.SemaphoreType.DMA((2,))],
         compiler_params=pltpu.CompilerParams(vmem_limit_bytes=2 * MIB),
         cost_estimate=pl.CostEstimate(flops=AHEAD, bytes_accessed=0, transcendentals=0),
-    )(in_hbm(tokens))
-
-
-def route_kernel(count, per_expert, counts_ref, rows_ref, gates_ref, out_ref):
+    )(in_hbm(tokens), in_hbm(counts))
+
+
+def routed_gates(own, per_expert, count, counts_ref, rows_ref, gates_ref):
     experts, slots = rows_ref.shape
-    total = out_ref.shape[0]
-    line = lax.broadcasted_iota(jnp.int32, (total, slots), 0)
-    position = lax.broadcasted_iota(jnp.int32, (total, slots), 1)
-    own = lax.axis_index("exp")
+    expert = own // per_expert
+    mine = lax.broadcasted_iota(jnp.int32, (experts, slots), 0) == expert
+    rows = jnp.sum(jnp.where(mine, rows_ref[...], 0), axis=0, keepdims=True)
+    gates = jnp.sum(jnp.where(mine, gates_ref[...], 0.0), axis=0, keepdims=True)
+    position = lax.broadcasted_iota(jnp.int32, (1, slots), 1)
+    rows = jnp.where(position < counts_ref[expert] * BLOCK, rows, -1)
+    line = lax.broadcasted_iota(jnp.int32, (SOURCES * count, slots), 0)
     block = line // count
-    token = (own ^ lax.rem(block, per_expert)) * count + lax.rem(line, count)
-    expert = block // per_expert
-    found = jnp.zeros((total, slots), jnp.float32)
-    for e in range(experts):
-        rows = rows_ref[pl.ds(e, 1), :]
-        here = (expert == e) & (rows == token) & (position < counts_ref[e] * BLOCK)
-        found = jnp.where(here, gates_ref[pl.ds(e, 1), :], found)
-    out_ref[...] = jnp.broadcast_to(jnp.sum(found, axis=1, keepdims=True), out_ref.shape)
-
-
-def route(block_counts, block_rows, row_gates, count):
-    return pl.pallas_call(
-        functools.partial(route_kernel, count, SOURCES // block_rows.shape[0]),
-        out_shape=jax.ShapeDtypeStruct((SOURCES * count, 128), jnp.float32),
-        in_specs=[SMEM, VMEM, VMEM],
-        out_specs=VMEM,
-        compiler_params=pltpu.CompilerParams(vmem_limit_bytes=2 * MIB),
-    )(block_counts, block_rows, row_gates)
-
-
-def pack_kernel(place_ref, tokens_ref, *refs):
-    *pieces, last_ref, out_ref = refs
-    for r, ref in enumerate(pieces):
+    source = jnp.zeros_like(line)
+    for at, k in enumerate(ORDER):
+        source = jnp.where(block == at, own ^ k, source)
+    token = source * count + lax.rem(line, count)
+    return jnp.sum(jnp.where(rows == token, gates, 0.0), axis=1, keepdims=True)
+
+
+def pack_kernel(place_ref, tokens_ref, last_ref, *refs):
+    *pieces, out_ref = refs
+    for r, ref in enumerate(pieces[::-1]):
         out_ref[r + 1] = ref[...]
     out_ref[0] = jnp.where(place_ref[0] == 0, tokens_ref[...], last_ref[...])
 
@@ -97,8 +94,12 @@
     )(in_smem(place), tokens, *pieces)
 
 
-def gate_kernel(place_ref, mine_ref, got_ref, wg_ref, x_ref, act_ref, wide):
+def gate_kernel(
+    per_expert, place_ref, counts_ref, mine_ref, got_ref, rows_ref, gates_ref, wg_ref, x_ref, act_ref, g_ref, wide
+):
     sets, count, _ = mine_ref.shape
+    g = routed_gates(place_ref[1], per_expert, count, counts_ref, rows_ref, gates_ref)
+    g_ref[...] = jnp.broadcast_to(g, g_ref.shape)
     for j in range(sets):
         rows = pl.ds(j * count, count)
         wide[place_ref[0], rows, :] = mine_ref[j].astype(jnp.float32)
@@ -111,21 +112,22 @@
         act_ref[:, cols] = gate / (1.0 + jnp.exp(-gate))
 
 
-def gate_rows(place, mine, got, wg):
+def gate_rows(place, counts, mine, got, block_rows, row_gates, wg):
     total = 2 * mine.shape[0] * mine.shape[1]
     depth, width = wg.shape
     return pl.pallas_call(
-        gate_kernel,
+        functools.partial(gate_kernel, SOURCES // block_rows.shape[0]),
         out_shape=(
             jax.ShapeDtypeStruct((total, depth), jnp.bfloat16),
             jax.ShapeDtypeStruct((total, width), jnp.float32),
+            jax.ShapeDtypeStruct((total, 128), jnp.float32),
         ),
-        in_specs=[SMEM] + [VMEM] * 3,
-        out_specs=(VMEM, VMEM),
+        in_specs=[SMEM] * 2 + [VMEM] * 5,
+        out_specs=(VMEM,) * 3,
         scratch_shapes=[pltpu.VMEM((2, total // 2, depth), jnp.float32)],
         compiler_params=pltpu.CompilerParams(vmem_limit_bytes=2 * MIB),
         cost_estimate=pl.CostEstimate(flops=GATE, bytes_accessed=0, transcendentals=total * width),
-    )(in_smem(place), mine, got, in_vmem(wg))
+    )(in_smem(place), in_smem(counts), mine, got, block_rows, row_gates, in_vmem(wg))
 
 
 def up_kernel(x_ref, act_ref, wu_ref, h_out):
@@ -169,46 +171,47 @@
     )(in_smem(place), hidden, in_vmem(wd))
 
 
-def near_kernel(place_ref, keep_ref, got_ref, out_ref):
-    _, near, count, _ = out_ref.shape
-    both = keep_ref[...] + got_ref[...].astype(jnp.float32)
-    expert = place_ref[1] // near
+def near_kernel(g_ref, keep_ref, got_ref, own_ref, *out_refs):
+    both = (keep_ref[...] + got_ref[...].astype(jnp.float32)) * g_ref[:, :1]
+    pair, count, _ = own_ref.shape
+    group = SOURCES // pair
     for at, k in enumerate(ORDER):
-        out_ref[expert ^ (k // near), k % near] = both[at * count : (at + 1) * count].astype(out_ref.dtype)
-
-
-def near(place, keep, got, per_expert):
+        out_ref = (own_ref, *out_refs)[k % group]
+        out_ref[k // group] = both[at * count : (at + 1) * count].astype(out_ref.dtype)
+
+
+def near(g, keep, got):
     rows, width = keep.shape
+    group = SOURCES // 2
+    shape = (2, rows // SOURCES, width)
     return pl.pallas_call(
         near_kernel,
-        out_shape=jax.ShapeDtypeStruct(
-            (SOURCES // per_expert, per_expert, rows // SOURCES, width), jnp.bfloat16
-        ),
-        in_specs=[SMEM, VMEM, VMEM],
-        out_specs=VMEM,
-        compiler_params=pltpu.CompilerParams(vmem_limit_bytes=2 * MIB),
-    )(in_smem(place), keep, got)
-
-
-def weigh_kernel(gates_ref, parts_ref, own_ref, next_ref):
-    experts, near, count, _ = parts_ref.shape
+        out_shape=(jax.ShapeDtypeStruct(shape, jnp.float32),)
+        + (jax.ShapeDtypeStruct(shape, jnp.bfloat16),) * (group - 1),
+        in_specs=[VMEM] * 3,
+        out_specs=(VMEM,) * group,
+        compiler_params=pltpu.CompilerParams(vmem_limit_bytes=2 * MIB),
+    )(g, keep, got)
+
+
+def far_kernel(*refs):
+    *part_refs, own_ref, next_ref = refs
     for i, out_ref in enumerate((own_ref, next_ref)):
-        total = jnp.zeros(out_ref.shape, jnp.float32)
-        for e in range(experts):
-            gates = gates_ref[pl.ds((e * near + i) * count, count), :1]
-            total = total + parts_ref[e, i].astype(jnp.float32) * gates
+        total = part_refs[0][i]
+        for part_ref in part_refs[1:]:
+            total = total + part_ref[i].astype(jnp.float32)
         out_ref[...] = total.astype(out_ref.dtype)
 
 
-def weigh(gates, parts):
-    shape = parts.shape[2:]
-    return pl.pallas_call(
-        weigh_kernel,
+def far(parts):
+    shape = parts[0].shape[1:]
+    return pl.pallas_call(
+        far_kernel,
         out_shape=(jax.ShapeDtypeStruct(shape, jnp.float32), jax.ShapeDtypeStruct(shape, jnp.bfloat16)),
-        in_specs=[VMEM, VMEM],
+        in_specs=[VMEM] * len(parts),
         out_specs=(VMEM, VMEM),
         compiler_params=pltpu.CompilerParams(vmem_limit_bytes=2 * MIB),
-    )(gates, parts)
+    )(*parts)
 
 
 def sum_kernel(own_ref, got_ref, out_ref):
@@ -242,24 +245,19 @@
 
 
 def local(tokens, w_gate, w_up, w_down, block_counts, block_rows, row_gates):
-    per_expert = SOURCES // block_rows.shape[0]
-    tokens, place = pass_on(tokens)
+    tokens, counts, place = pass_on(tokens, block_counts)
     half = SOURCES // 2
     pieces = [fetched(tokens, ORDER[b], ORDER[half + b]) for b in range(1, half)]
     pieces += [fetched(tokens, None, ORDER[half])]
-    mine = pack(place, tokens, pieces)
-    x, act = gate_rows(place, mine, swap_cores(mine), w_gate)
+    mine = pack(place, tokens, pieces[::-1])
+    x, act, g = gate_rows(place, counts, mine, swap_cores(mine), block_rows, row_gates, w_gate)
     hidden = hidden_rows(x, act, w_up)
     send = down_half(place, hidden, w_down, True, jnp.bfloat16)
     keep = down_half(place, hidden, w_down, False, jnp.float32)
-    parts = near(place, keep, swap_cores(send), per_expert)
-    lines = [[i + per_expert * e for e in range(SOURCES // per_expert)] for i in range(per_expert)]
-    returned = lax.all_to_all(
-        parts, "exp", split_axis=0, concat_axis=0, tiled=True, axis_index_groups=lines
-    )
-    gates = route(block_counts, block_rows, row_gates, tokens.shape[0])
-    own, other = weigh(gates, returned)
-    return final_sum(own, swapped(other, 1))
+    own, *parts = near(g, keep, swap_cores(send))
+    returned = [swapped(parts[j - 1], j) for j in range(half - 1, 0, -1)]
+    own, other = far([own, *returned])
+    return final_sum(own, swapped(other, half))
 
 
 def expert_block(segment, w_gate, w_up, w_down):

time: 38.9 us -> 35.3 us (0.907)
  waiting for transfers between devices: 14.4 us -> 10.2 us
  starting transfers between devices: 11.9 us -> 13.9 us
  Pallas kernels: 12.2 us -> 10.9 us
    all_to_all x1 -> x0, waiting for transfers between devices: 5.82 us -> none  [local(): lax.all_to_all(parts, 'exp', split_axis=0, concat_axis=0, tiled=True, axi...]
    ppermute x1 -> x4, starting transfers between devices: 0.86 us -> 6.2 us  [swapped(): return lax.ppermute(x, 'exp', [(i, i ^ k) for i in range(SOURCES)])]
    all_to_all x1 -> x0, starting transfers between devices: 3.32 us -> none  [local(): lax.all_to_all(parts, 'exp', split_axis=0, concat_axis=0, tiled=True, axi...]
    ppermute x1 -> x4, waiting for transfers between devices: 2.94 us -> 4.54 us  [swapped(): return lax.ppermute(x, 'exp', [(i, i ^ k) for i in range(SOURCES)])]
    pallas_call x4 -> x3, Pallas kernels: 4.51 us -> 3.24 us  [the longest x1 3.1 us: gate_rows(): pl.pallas_call(functools.partial(gate_kernel, SOURCES // block_rows.shape...]
  transfers between devices with their start and end apart: 8 -> 10, of which waited for: 5 -> 6; matrix products, arithmetic and copies ran while one was open for 0% -> 0% of each run, Pallas kernels for 6% -> 4%
where the time goes in v9:
time: 35.3 us; the launch traced here: 35.2 us
  starting transfers between devices  13.9 us (39%)
  Pallas kernels  10.9 us (31%)
  waiting for transfers between devices  10.2 us (29%)
    ppermute x4, starting transfers between devices, fetched(): return lax.ppermute(x, ('exp', 'hid'), pairs)  7.47 us
    ppermute x4, starting transfers between devices, swapped(): return lax.ppermute(x, 'exp', [(i, i ^ k) for i in range(SOURCES)])  6.2 us
    ppermute x4, waiting for transfers between devices, swapped(): return lax.ppermute(x, 'exp', [(i, i ^ k) for i in range(SOURCES)])  4.54 us
    ppermute x4, waiting for transfers between devices, fetched(): return lax.ppermute(x, ('exp', 'hid'), pairs)  4.28 us
    pallas_call x2, Pallas kernels, down_half(): pl.pallas_call(functools.partial(down_kernel, other), out_shape=jax.Shape...  3.12 us
    pallas_call x1, Pallas kernels, gate_rows(): pl.pallas_call(functools.partial(gate_kernel, SOURCES // block_rows.shape...  3.1 us
    pallas_call x1, Pallas kernels, hidden_rows(): pl.pallas_call(up_kernel, out_shape=jax.ShapeDtypeStruct(act.shape, jnp.b...  3.01 us
    ppermute x2, waiting for transfers between devices, swap_cores(): return lax.ppermute(x, 'hid', [(0, 1), (1, 0)])  1.34 us
  transfers between devices with their start and end apart: 10, of which 6 were waited for; matrix products, arithmetic and copies ran while one was open for 0% of the time, Pallas kernels for 4%

profile of v9, /device:TPU:0, one launch (start us, length us, event | category | flops | bytes accessed | tf_op | source)
XLA Modules:
  0.0 35.2 jit_solution(334793220389257711)
XLA Ops:
  0.0 0.0 copy-start.3
  0.0 0.0 copy-start.2
  0.0 0.0 copy-start.1
  0.0 0.9 %shard_map.73 = (bf16[4,4096]{1,0:T(4,128)(2,1)S(1)}, s32[4]{0:T(128)S(4)}, s32[2]{0:T(128)S(4)}) custom-call(bf16[4,4096]{1,0:T(4,128)(2,1)} %tokens_ref.1, s32[4]{0:T(128)} %counts_ref.1), custom_call_target="tpu_custom_call" | custom-call | flops 20000000000 | tf_op jit(solution)/shard_map/pallas_call | solution.py:48
  0.9 0.0 copy-start
  1.0 6.0 %collective-permute-start.3 = (bf16[4,4096]{1,0:T(4,128)(2,1)S(1)}, bf16[4,4096]{1,0:T(4,128)(2,1)S(1)}, u32[]{:S(2)}, u32[]{:S(2)}) collective-permute-start(bf16[4,4096]{1,0:T(4,128)(2,1)S(1)} %get-tuple-element.19.tokens_ref), channel_id=1, source_target_pairs={{0,14},{2,12},{4,10},{6,8},{8,6},{10,4},{12,2},{14,0},{1,11},{3,9}... | collective-permute-start | bytes 98312 | tf_op jit(solution)/shard_map/ppermute | solution.py:240
  7.0 0.2 collective-permute-start.2
  7.2 0.4 %collective-permute-start.1 = (bf16[4,4096]{1,0:T(4,128)(2,1)S(1)}, bf16[4,4096]{1,0:T(4,128)(2,1)S(1)}, u32[]{:S(2)}, u32[]{:S(2)}) collective-permute-start(bf16[4,4096]{1,0:T(4,128)(2,1)S(1)} %get-tuple-element.19.tokens_ref), channel_id=1, source_target_pairs={{0,2},{2,0},{4,6},{6,4},{8,10},{10,8},{12,14},{14,12},{1,7},{3,5},... | collective-permute-start | bytes 98312 | tf_op jit(solution)/shard_map/ppermute | solution.py:240
  7.7 0.8 %collective-permute-start = (bf16[4,4096]{1,0:T(4,128)(2,1)S(1)}, bf16[4,4096]{1,0:T(4,128)(2,1)S(1)}, u32[]{:S(2)}, u32[]{:S(2)}) collective-permute-start(bf16[4,4096]{1,0:T(4,128)(2,1)S(1)} %get-tuple-element.19.tokens_ref), channel_id=1, source_target_pairs={{1,5},{3,7},{5,1},{7,3},{9,13},{11,15},{13,9},{15,11},{17,21},{19,... | collective-permute-start | bytes 98312 | tf_op jit(solution)/shard_map/ppermute | solution.py:240
  8.4 0.5 %collective-permute-done.3.refs_2_ = bf16[4,4096]{1,0:T(4,128)(2,1)S(1)} collective-permute-done((bf16[4,4096]{1,0:T(4,128)(2,1)S(1)}, bf16[4,4096]{1,0:T(4,128)(2,1)S(1)}, u32[]{:S(2)}, u32[]{:S(2)}) %collective-permute-start.3) | collective-permute-done | bytes 32800 | tf_op jit(solution)/shard_map/ppermute | solution.py:240
  8.9 3.8 %collective-permute-done.2.refs_1_ = bf16[4,4096]{1,0:T(4,128)(2,1)S(1)} collective-permute-done((bf16[4,4096]{1,0:T(4,128)(2,1)S(1)}, bf16[4,4096]{1,0:T(4,128)(2,1)S(1)}, u32[]{:S(2)}, u32[]{:S(2)}) %collective-permute-start.2) | collective-permute-done | bytes 32800 | tf_op jit(solution)/shard_map/ppermute | solution.py:240
  12.7 0.0 collective-permute-done.1.refs_0_
  12.7 0.0 collective-permute-done.last_ref
  12.7 0.1 collective-permute-start.4
  12.8 1.3 %collective-permute-done.4.got_ref = bf16[4,4,4096]{2,1,0:T(4,128)(2,1)S(1)} collective-permute-done((bf16[4,4,4096]{2,1,0:T(4,128)(2,1)S(1)}, bf16[4,4,4096]{2,1,0:T(4,128)(2,1)S(1)}, u32[]{:S(2)}, u32[]{:S(2)}) %collective-permute-start.4) | collective-permute-done | bytes 131104 | tf_op jit(solution)/shard_map/ppermute | solution.py:244
  14.2 0.0 copy-done.3
  14.2 0.0 copy-done.2
  14.2 0.0 copy-done.1
  14.2 0.0 slice-start
  14.2 0.0 slice-start.1
  14.2 0.0 slice-start.2
  14.2 3.1 %shard_map.75 = (bf16[32,4096]{1,0:T(8,128)(2,1)S(1)}, f32[32,2048]{1,0:T(8,128)S(1)}, f32[32,128]{1,0:T(8,128)S(1)}) custom-call(s32[2]{0:T(128)S(4)} %get-tuple-element.17.place_ref, s32[4]{0:T(128)S(4)} %get-tuple-element.18.counts_ref, bf16[4,4,4096]{2,1,0:T(4,128)(2,1)S(1)} %shard_map.74.mine_ref, ...), custom_call_target="tpu_custom_call" | custom-call | flops 5000000000 | tf_op jit(solution)/shard_map/pallas_call | solution.py:118
  17.3 0.0 copy-done
  17.3 0.0 slice-start.3
  17.3 3.0 %shard_map.76.h_ref = bf16[32,2048]{1,0:T(8,128)(2,1)S(1)} custom-call(bf16[32,4096]{1,0:T(8,128)(2,1)S(1)} %get-tuple-element.21.x_ref, f32[32,2048]{1,0:T(8,128)S(1)} %get-tuple-element.22.act_ref, bf16[4096,2048]{1,0:T(8,128)(2,1)S(1)} %copy-done), custom_call_target="tpu_custom_call" | custom-call | flops 2000000000 | tf_op jit(solution)/shard_map/pallas_call | solution.py:141
  20.3 0.0 slice-done
  20.4 0.0 slice-done.1
  20.4 0.0 slice-done.2
  20.4 0.0 slice-done.3
  20.4 1.6 %shard_map.78 = bf16[32,2048]{1,0:T(8,128)(2,1)S(1)} custom-call(s32[2]{0:T(128)S(4)} %get-tuple-element.17.place_ref, bf16[32,2048]{1,0:T(8,128)(2,1)S(1)} %shard_map.76.h_ref, bf16[2048,4096]{1,0:T(8,128)(2,1)S(1)} %bitcast.1), custom_call_target="tpu_custom_call" | custom-call | flops 268435456 | tf_op jit(solution)/shard_map/pallas_call | solution.py:164
  22.0 0.2 collective-permute-start.5
  22.1 1.6 %shard_map.77.keep_ref = f32[32,2048]{1,0:T(8,128)S(1)} custom-call(s32[2]{0:T(128)S(4)} %get-tuple-element.17.place_ref, bf16[32,2048]{1,0:T(8,128)(2,1)S(1)} %shard_map.76.h_ref, bf16[2048,4096]{1,0:T(8,128)(2,1)S(1)} %bitcast.1), custom_call_target="tpu_custom_call" | custom-call | flops 268435456 | tf_op jit(solution)/shard_map/pallas_call | solution.py:164
  23.7 0.0 collective-permute-done.5.got_ref
  23.7 0.1 shard_map.79
  23.8 0.5 %collective-permute-start.6 = (bf16[2,4,2048]{2,1,0:T(4,128)(2,1)S(1)}, bf16[2,4,2048]{2,1,0:T(4,128)(2,1)S(1)}, u32[]{:S(2)}, u32[]{:S(2)}) collective-permute-start(bf16[2,4,2048]{2,1,0:T(4,128)(2,1)S(1)} %get-tuple-element.24), channel_id=1, source_target_pairs={{0,6},{2,4},{4,2},{6,0},{8,14},{10,12},{12,10},{14,8},{1,7},{3,5},... | collective-permute-start | bytes 98312 | tf_op jit(solution)/shard_map/ppermute | solution.py:232
  24.3 1.6 %collective-permute-start.7 = (bf16[2,4,2048]{2,1,0:T(4,128)(2,1)S(1)}, bf16[2,4,2048]{2,1,0:T(4,128)(2,1)S(1)}, u32[]{:S(2)}, u32[]{:S(2)}) collective-permute-start(bf16[2,4,2048]{2,1,0:T(4,128)(2,1)S(1)} %get-tuple-element.25), channel_id=1, source_target_pairs={{0,4},{2,6},{4,0},{6,2},{8,12},{10,14},{12,8},{14,10},{1,5},{3,7},... | collective-permute-start | bytes 98312 | tf_op jit(solution)/shard_map/ppermute | solution.py:232
  25.9 1.5 %collective-permute-start.8 = (bf16[2,4,2048]{2,1,0:T(4,128)(2,1)S(1)}, bf16[2,4,2048]{2,1,0:T(4,128)(2,1)S(1)}, u32[]{:S(2)}, u32[]{:S(2)}) collective-permute-start(bf16[2,4,2048]{2,1,0:T(4,128)(2,1)S(1)} %get-tuple-element.26), channel_id=1, source_target_pairs={{0,2},{2,0},{4,6},{6,4},{8,10},{10,8},{12,14},{14,12},{1,3},{3,1},... | collective-permute-start | bytes 98312 | tf_op jit(solution)/shard_map/ppermute | solution.py:232
  27.4 1.5 %collective-permute-done.6.refs_1_ = bf16[2,4,2048]{2,1,0:T(4,128)(2,1)S(1)} collective-permute-done((bf16[2,4,2048]{2,1,0:T(4,128)(2,1)S(1)}, bf16[2,4,2048]{2,1,0:T(4,128)(2,1)S(1)}, u32[]{:S(2)}, u32[]{:S(2)}) %collective-permute-start.6) | collective-permute-done | bytes 32800 | tf_op jit(solution)/shard_map/ppermute | solution.py:232
  28.8 0.0 collective-permute-done.7.refs_2_
  28.8 1.0 %collective-permute-done.8.refs_3_ = bf16[2,4,2048]{2,1,0:T(4,128)(2,1)S(1)} collective-permute-done((bf16[2,4,2048]{2,1,0:T(4,128)(2,1)S(1)}, bf16[2,4,2048]{2,1,0:T(4,128)(2,1)S(1)}, u32[]{:S(2)}, u32[]{:S(2)}) %collective-permute-start.8) | collective-permute-done | bytes 32800 | tf_op jit(solution)/shard_map/ppermute | solution.py:232
  29.8 2.6 %collective-permute-start.9 = (bf16[4,2048]{1,0:T(4,128)(2,1)S(1)}, bf16[4,2048]{1,0:T(4,128)(2,1)S(1)}, u32[]{:S(2)}, u32[]{:S(2)}) collective-permute-start(bf16[4,2048]{1,0:T(4,128)(2,1)S(1)} %get-tuple-element.28), channel_id=1, source_target_pairs={{0,8},{2,10},{4,12},{6,14},{8,0},{10,2},{12,4},{14,6},{1,9},{3,11}... | collective-permute-start | bytes 49160 | tf_op jit(solution)/shard_map/ppermute | solution.py:232
  32.5 2.1 %collective-permute-done.9.got_ref = bf16[4,2048]{1,0:T(4,128)(2,1)S(1)} collective-permute-done((bf16[4,2048]{1,0:T(4,128)(2,1)S(1)}, bf16[4,2048]{1,0:T(4,128)(2,1)S(1)}, u32[]{:S(2)}, u32[]{:S(2)}) %collective-permute-start.9) | collective-permute-done | bytes 16416 | tf_op jit(solution)/shard_map/ppermute | solution.py:232
  34.6 0.6 %shard_map.81 = bf16[4,2048]{1,0:T(4,128)(2,1)} custom-call(f32[4,2048]{1,0:T(4,128)S(1)} %get-tuple-element.27.own_ref, bf16[4,2048]{1,0:T(4,128)(2,1)S(1)} %collective-permute-done.9.got_ref), custom_call_target="tpu_custom_call" | custom-call | tf_op jit(solution)/shard_map/pallas_call | solution.py:222
  (3 shorter events, 0.0 us)
Async XLA Ops:
  0.0 14.2 %copy-start.3 = (f32[4,128]{1,0:T(4,128)S(1)}, f32[4,128]{1,0:T(4,128)}, u32[]{:S(2)}) copy-start(f32[4,128]{1,0:T(4,128)} %gates_ref.1) | copy-start | bytes 6148
  0.0 14.2 %copy-start.2 = (s32[4,128]{1,0:T(4,128)S(1)}, s32[4,128]{1,0:T(4,128)}, u32[]{:S(2)}) copy-start(s32[4,128]{1,0:T(4,128)} %rows_ref.1) | copy-start | bytes 6148
  0.0 14.2 %copy-start.1 = (bf16[4096,2048]{1,0:T(8,128)(2,1)S(1)}, bf16[4096,2048]{1,0:T(8,128)(2,1)}, u32[]{:S(2)}) copy-start(bf16[4096,2048]{1,0:T(8,128)(2,1)} %wg_ref.1) | copy-start | bytes 50331652
  0.9 16.4 %copy-start = (bf16[4096,2048]{1,0:T(8,128)(2,1)S(1)}, bf16[4096,2048]{1,0:T(8,128)(2,1)}, u32[]{:S(2)}) copy-start(bf16[4096,2048]{1,0:T(8,128)(2,1)} %wu_ref.1) | copy-start | bytes 50331652
  1.0 7.9 %collective-permute-start.3 = (bf16[4,4096]{1,0:T(4,128)(2,1)S(1)}, bf16[4,4096]{1,0:T(4,128)(2,1)S(1)}, u32[]{:S(2)}, u32[]{:S(2)}) collective-permute-start(bf16[4,4096]{1,0:T(4,128)(2,1)S(1)} %get-tuple-element.19.tokens_ref), channel_id=1, source_target_pairs={{0,14},{2,12},{4,10},{6,8},{8,6},{10,4},{12,2},{14,0},{1,11},{3,9}... | collective-permute-start | bytes 98312 | tf_op jit(solution)/shard_map/ppermute | solution.py:240
  7.0 5.7 %collective-permute-start.2 = (bf16[4,4096]{1,0:T(4,128)(2,1)S(1)}, bf16[4,4096]{1,0:T(4,128)(2,1)S(1)}, u32[]{:S(2)}, u32[]{:S(2)}) collective-permute-start(bf16[4,4096]{1,0:T(4,128)(2,1)S(1)} %get-tuple-element.19.tokens_ref), channel_id=1, source_target_pairs={{0,12},{2,14},{4,8},{6,10},{8,4},{10,6},{12,0},{14,2},{1,9},{3,11}... | collective-permute-start | bytes 98312 | tf_op jit(solution)/shard_map/ppermute | solution.py:240
  7.2 5.5 %collective-permute-start.1 = (bf16[4,4096]{1,0:T(4,128)(2,1)S(1)}, bf16[4,4096]{1,0:T(4,128)(2,1)S(1)}, u32[]{:S(2)}, u32[]{:S(2)}) collective-permute-start(bf16[4,4096]{1,0:T(4,128)(2,1)S(1)} %get-tuple-element.19.tokens_ref), channel_id=1, source_target_pairs={{0,2},{2,0},{4,6},{6,4},{8,10},{10,8},{12,14},{14,12},{1,7},{3,5},... | collective-permute-start | bytes 98312 | tf_op jit(solution)/shard_map/ppermute | solution.py:240
  7.7 5.1 %collective-permute-start = (bf16[4,4096]{1,0:T(4,128)(2,1)S(1)}, bf16[4,4096]{1,0:T(4,128)(2,1)S(1)}, u32[]{:S(2)}, u32[]{:S(2)}) collective-permute-start(bf16[4,4096]{1,0:T(4,128)(2,1)S(1)} %get-tuple-element.19.tokens_ref), channel_id=1, source_target_pairs={{1,5},{3,7},{5,1},{7,3},{9,13},{11,15},{13,9},{15,11},{17,21},{19,... | collective-permute-start | bytes 98312 | tf_op jit(solution)/shard_map/ppermute | solution.py:240
  12.7 1.4 %collective-permute-start.4 = (bf16[4,4,4096]{2,1,0:T(4,128)(2,1)S(1)}, bf16[4,4,4096]{2,1,0:T(4,128)(2,1)S(1)}, u32[]{:S(2)}, u32[]{:S(2)}) collective-permute-start(bf16[4,4,4096]{2,1,0:T(4,128)(2,1)S(1)} %shard_map.74.mine_ref), channel_id=1, source_target_pairs={{0,1},{1,0},{2,3},{3,2},{4,5},{5,4},{6,7},{7,6},{8,9},{9,8},{10,11... | collective-permute-start | bytes 393224 | tf_op jit(solution)/shard_map/ppermute | solution.py:244
  14.2 6.2 %slice-start = ((s8[16777216]{0:T(1024)(128)(4,1)}), s8[4194304]{0:T(1024)(128)(4,1)S(1)}, s32[]{:S(2)}) async-start(s8[16777216]{0:T(1024)(128)(4,1)} %bitcast), calls=%async_computation | async-start | bytes 8388608
  14.2 6.2 %slice-start.1 = ((s8[16777216]{0:T(1024)(128)(4,1)}), s8[4194304]{0:T(1024)(128)(4,1)S(1)}, s32[]{:S(2)}) async-start(s8[16777216]{0:T(1024)(128)(4,1)} %bitcast), calls=%async_computation.1 | async-start | bytes 8388608
  14.2 6.2 %slice-start.2 = ((s8[16777216]{0:T(1024)(128)(4,1)}), s8[4194304]{0:T(1024)(128)(4,1)S(1)}, s32[]{:S(2)}) async-start(s8[16777216]{0:T(1024)(128)(4,1)} %bitcast), calls=%async_computation.2 | async-start | bytes 8388608
  17.3 3.1 %slice-start.3 = ((s8[16777216]{0:T(1024)(128)(4,1)}), s8[4194304]{0:T(1024)(128)(4,1)S(1)}, s32[]{:S(2)}) async-start(s8[16777216]{0:T(1024)(128)(4,1)} %bitcast), calls=%async_computation.3 | async-start | bytes 8388608
  22.0 1.7 %collective-permute-start.5 = (bf16[32,2048]{1,0:T(8,128)(2,1)S(1)}, bf16[32,2048]{1,0:T(8,128)(2,1)S(1)}, u32[]{:S(2)}, u32[]{:S(2)}) collective-permute-start(bf16[32,2048]{1,0:T(8,128)(2,1)S(1)} %shard_map.78), channel_id=1, source_target_pairs={{0,1},{1,0},{2,3},{3,2},{4,5},{5,4},{6,7},{7,6},{8,9},{9,8},{10,11... | collective-permute-start | bytes 393224 | tf_op jit(solution)/shard_map/ppermute | solution.py:244
  23.8 5.0 %collective-permute-start.6 = (bf16[2,4,2048]{2,1,0:T(4,128)(2,1)S(1)}, bf16[2,4,2048]{2,1,0:T(4,128)(2,1)S(1)}, u32[]{:S(2)}, u32[]{:S(2)}) collective-permute-start(bf16[2,4,2048]{2,1,0:T(4,128)(2,1)S(1)} %get-tuple-element.24), channel_id=1, source_target_pairs={{0,6},{2,4},{4,2},{6,0},{8,14},{10,12},{12,10},{14,8},{1,7},{3,5},... | collective-permute-start | bytes 98312 | tf_op jit(solution)/shard_map/ppermute | solution.py:232
  24.3 4.5 %collective-permute-start.7 = (bf16[2,4,2048]{2,1,0:T(4,128)(2,1)S(1)}, bf16[2,4,2048]{2,1,0:T(4,128)(2,1)S(1)}, u32[]{:S(2)}, u32[]{:S(2)}) collective-permute-start(bf16[2,4,2048]{2,1,0:T(4,128)(2,1)S(1)} %get-tuple-element.25), channel_id=1, source_target_pairs={{0,4},{2,6},{4,0},{6,2},{8,12},{10,14},{12,8},{14,10},{1,5},{3,7},... | collective-permute-start | bytes 98312 | tf_op jit(solution)/shard_map/ppermute | solution.py:232
  25.9 3.9 %collective-permute-start.8 = (bf16[2,4,2048]{2,1,0:T(4,128)(2,1)S(1)}, bf16[2,4,2048]{2,1,0:T(4,128)(2,1)S(1)}, u32[]{:S(2)}, u32[]{:S(2)}) collective-permute-start(bf16[2,4,2048]{2,1,0:T(4,128)(2,1)S(1)} %get-tuple-element.26), channel_id=1, source_target_pairs={{0,2},{2,0},{4,6},{6,4},{8,10},{10,8},{12,14},{14,12},{1,3},{3,1},... | collective-permute-start | bytes 98312 | tf_op jit(solution)/shard_map/ppermute | solution.py:232
  29.8 4.7 %collective-permute-start.9 = (bf16[4,2048]{1,0:T(4,128)(2,1)S(1)}, bf16[4,2048]{1,0:T(4,128)(2,1)S(1)}, u32[]{:S(2)}, u32[]{:S(2)}) collective-permute-start(bf16[4,2048]{1,0:T(4,128)(2,1)S(1)} %get-tuple-element.28), channel_id=1, source_target_pairs={{0,8},{2,10},{4,12},{6,14},{8,0},{10,2},{12,4},{14,6},{1,9},{3,11}... | collective-permute-start | bytes 49160 | tf_op jit(solution)/shard_map/ppermute | solution.py:232

commit v10 on v9

--- a/solution.py
+++ b/solution.py
@@ -33,31 +33,19 @@
     return pltpu.with_memory_space_constraint(x, pltpu.VMEM)
 
 
-def pass_kernel(tokens_ref, counts_ref, out_ref, counts_out, place_ref, sems):
-    copy = pltpu.make_async_copy(tokens_ref, out_ref, sems.at[0])
-    copy.start()
-    small = pltpu.make_async_copy(counts_ref, counts_out, sems.at[1])
-    small.start()
+def first_kernel(place_ref):
     place_ref[0] = lax.axis_index("hid")
     place_ref[1] = lax.axis_index("exp")
-    copy.wait()
-    small.wait()
-
-
-def pass_on(tokens, counts):
-    return pl.pallas_call(
-        pass_kernel,
-        out_shape=(
-            jax.ShapeDtypeStruct(tokens.shape, tokens.dtype),
-            pltpu.SMEM(counts.shape, counts.dtype),
-            pltpu.SMEM((2,), jnp.int32),
-        ),
-        in_specs=[HBM, HBM],
-        out_specs=(VMEM, SMEM, SMEM),
-        scratch_shapes=[pltpu.SemaphoreType.DMA((2,))],
+
+
+def first():
+    return pl.pallas_call(
+        first_kernel,
+        out_shape=pltpu.SMEM((2,), jnp.int32),
+        out_specs=SMEM,
         compiler_params=pltpu.CompilerParams(vmem_limit_bytes=2 * MIB),
         cost_estimate=pl.CostEstimate(flops=AHEAD, bytes_accessed=0, transcendentals=0),
-    )(in_hbm(tokens), in_hbm(counts))
+    )()
 
 
 def routed_gates(own, per_expert, count, counts_ref, rows_ref, gates_ref):
@@ -67,7 +55,9 @@
     rows = jnp.sum(jnp.where(mine, rows_ref[...], 0), axis=0, keepdims=True)
     gates = jnp.sum(jnp.where(mine, gates_ref[...], 0.0), axis=0, keepdims=True)
     position = lax.broadcasted_iota(jnp.int32, (1, slots), 1)
-    rows = jnp.where(position < counts_ref[expert] * BLOCK, rows, -1)
+    here = lax.broadcasted_iota(jnp.int32, counts_ref.shape, 1) == expert
+    blocks = jnp.sum(jnp.where(here, counts_ref[...], 0), axis=1, keepdims=True)
+    rows = jnp.where(position < blocks * BLOCK, rows, -1)
     line = lax.broadcasted_iota(jnp.int32, (SOURCES * count, slots), 0)
     block = line // count
     source = jnp.zeros_like(line)
@@ -122,12 +112,12 @@
             jax.ShapeDtypeStruct((total, width), jnp.float32),
             jax.ShapeDtypeStruct((total, 128), jnp.float32),
         ),
-        in_specs=[SMEM] * 2 + [VMEM] * 5,
+        in_specs=[SMEM] + [VMEM] * 6,
         out_specs=(VMEM,) * 3,
         scratch_shapes=[pltpu.VMEM((2, total // 2, depth), jnp.float32)],
         compiler_params=pltpu.CompilerParams(vmem_limit_bytes=2 * MIB),
         cost_estimate=pl.CostEstimate(flops=GATE, bytes_accessed=0, transcendentals=total * width),
-    )(in_smem(place), in_smem(counts), mine, got, block_rows, row_gates, in_vmem(wg))
+    )(in_smem(place), counts.reshape(1, -1), mine, got, block_rows, row_gates, in_vmem(wg))
 
 
 def up_kernel(x_ref, act_ref, wu_ref, h_out):
@@ -236,7 +226,7 @@
     pairs = []
     for side, k in enumerate((first, second)):
         if k is not None:
-            pairs += [(2 * i + side, 2 * (i ^ k) + side) for i in range(SOURCES)]
+            pairs += [(2 * i + 1 - side, 2 * (i ^ k) + side) for i in range(SOURCES)]
     return lax.ppermute(x, ("exp", "hid"), pairs)
 
 
@@ -245,7 +235,8 @@
 
 
 def local(tokens, w_gate, w_up, w_down, block_counts, block_rows, row_gates):
-    tokens, counts, place = pass_on(tokens, block_counts)
+    place = first()
+    tokens, place, counts = lax.optimization_barrier((tokens, place, block_counts))
     half = SOURCES // 2
     pieces = [fetched(tokens, ORDER[b], ORDER[half + b]) for b in range(1, half)]
     pieces += [fetched(tokens, None, ORDER[half])]

time: 35.3 us -> 36.1 us (1.023)
  starting transfers between devices: 13.9 us -> 17.7 us
  waiting for transfers between devices: 10.2 us -> 7.34 us
  Pallas kernels: 10.9 us -> 10 us
  local copies, waits for them, and re-layouts: 0.05 us -> 0.79 us
    ppermute x4, waiting for transfers between devices: 4.28 us -> 1.57 us  [fetched(): return lax.ppermute(x, ('exp', 'hid'), pairs)]
    ppermute x2, starting transfers between devices: 0.23 us -> 2.03 us  [swap_cores(): return lax.ppermute(x, 'hid', [(0, 1), (1, 0)])]
    ppermute x4, starting transfers between devices: 7.47 us -> 8.55 us  [fetched(): return lax.ppermute(x, ('exp', 'hid'), pairs)]
    pallas_call x1, Pallas kernels: 0.93 us -> 0.01 us  [first(): pl.pallas_call(first_kernel, out_shape=pltpu.SMEM((2,), jnp.int32), out_s...]
    ppermute x4, starting transfers between devices: 6.2 us -> 7.11 us  [swapped(): return lax.ppermute(x, 'exp', [(i, i ^ k) for i in range(SOURCES)])]
    unnamed x16 -> x20, local copies, waits for them, and re-layouts: 0.05 us -> 0.79 us
  transfers between devices with their start and end apart: 10 -> 10, of which waited for: 6 -> 7; matrix products, arithmetic and copies ran while one was open for 0% -> 0% of each run, Pallas kernels for 4% -> 4%
where the time goes in v10:
time: 36.1 us; the launch traced here: 36 us
  starting transfers between devices  17.7 us (49%)
  Pallas kernels  10 us (28%)
  waiting for transfers between devices  7.34 us (20%)
  local copies, waits for them, and re-layouts  0.79 us (2%)
    ppermute x4, starting transfers between devices, fetched(): return lax.ppermute(x, ('exp', 'hid'), pairs)  8.55 us
    ppermute x4, starting transfers between devices, swapped(): return lax.ppermute(x, 'exp', [(i, i ^ k) for i in range(SOURCES)])  7.11 us
    ppermute x4, waiting for transfers between devices, swapped(): return lax.ppermute(x, 'exp', [(i, i ^ k) for i in range(SOURCES)])  4.78 us
    pallas_call x2, Pallas kernels, down_half(): pl.pallas_call(functools.partial(down_kernel, other), out_shape=jax.Shape...  3.12 us
    pallas_call x1, Pallas kernels, gate_rows(): pl.pallas_call(functools.partial(gate_kernel, SOURCES // block_rows.shape...  3.11 us
    pallas_call x1, Pallas kernels, hidden_rows(): pl.pallas_call(up_kernel, out_shape=jax.ShapeDtypeStruct(act.shape, jnp.b...  3.01 us
    ppermute x2, starting transfers between devices, swap_cores(): return lax.ppermute(x, 'hid', [(0, 1), (1, 0)])  2.03 us
    ppermute x4, waiting for transfers between devices, fetched(): return lax.ppermute(x, ('exp', 'hid'), pairs)  1.57 us
  transfers between devices with their start and end apart: 10, of which 7 were waited for; matrix products, arithmetic and copies ran while one was open for 0% of the time, Pallas kernels for 4%

profile of v10, /device:TPU:0, one launch (start us, length us, event | category | flops | bytes accessed | tf_op | source)
XLA Modules:
  0.0 36.0 jit_solution(4480567363055137755)
XLA Ops:
  0.0 0.0 copy-start.5
  0.0 0.0 copy-start.1
  0.0 0.0 copy-start.4
  0.0 0.0 copy-start.3
  0.0 0.0 copy-start.2
  0.0 0.7 %copy-done.1 = bf16[4,4096]{1,0:T(4,128)(2,1)S(1)} copy-done((bf16[4,4096]{1,0:T(4,128)(2,1)S(1)}, bf16[4,4096]{1,0:T(4,128)(2,1)}, u32[]{:S(2)}) %copy-start.1) | copy-done | bytes 32792
  0.8 0.0 copy-start
  0.8 4.4 %collective-permute-start.3 = (bf16[4,4096]{1,0:T(4,128)(2,1)S(1)}, bf16[4,4096]{1,0:T(4,128)(2,1)S(1)}, u32[]{:S(2)}, u32[]{:S(2)}) collective-permute-start(bf16[4,4096]{1,0:T(4,128)(2,1)S(1)} %copy-done.1), channel_id=1, source_target_pairs={{1,14},{3,12},{5,10},{7,8},{9,6},{11,4},{13,2},{15,0},{0,11},{2,9}... | collective-permute-start | bytes 98312 | tf_op jit(solution)/shard_map/ppermute | solution.py:230
  5.2 0.7 %collective-permute-start.2 = (bf16[4,4096]{1,0:T(4,128)(2,1)S(1)}, bf16[4,4096]{1,0:T(4,128)(2,1)S(1)}, u32[]{:S(2)}, u32[]{:S(2)}) collective-permute-start(bf16[4,4096]{1,0:T(4,128)(2,1)S(1)} %copy-done.1), channel_id=1, source_target_pairs={{1,12},{3,14},{5,8},{7,10},{9,4},{11,6},{13,0},{15,2},{0,9},{2,11}... | collective-permute-start | bytes 98312 | tf_op jit(solution)/shard_map/ppermute | solution.py:230
  5.9 0.1 collective-permute-start.1
  6.0 3.3 %collective-permute-start = (bf16[4,4096]{1,0:T(4,128)(2,1)S(1)}, bf16[4,4096]{1,0:T(4,128)(2,1)S(1)}, u32[]{:S(2)}, u32[]{:S(2)}) collective-permute-start(bf16[4,4096]{1,0:T(4,128)(2,1)S(1)} %copy-done.1), channel_id=1, source_target_pairs={{0,5},{2,7},{4,1},{6,3},{8,13},{10,15},{12,9},{14,11},{16,21},{18,... | collective-permute-start | bytes 98312 | tf_op jit(solution)/shard_map/ppermute | solution.py:230
  9.3 0.0 collective-permute-done.3.refs_2_
  9.4 1.4 %collective-permute-done.2.refs_1_ = bf16[4,4096]{1,0:T(4,128)(2,1)S(1)} collective-permute-done((bf16[4,4096]{1,0:T(4,128)(2,1)S(1)}, bf16[4,4096]{1,0:T(4,128)(2,1)S(1)}, u32[]{:S(2)}, u32[]{:S(2)}) %collective-permute-start.2) | collective-permute-done | bytes 32800 | tf_op jit(solution)/shard_map/ppermute | solution.py:230
  10.7 0.0 collective-permute-done.1.refs_0_
  10.7 0.2 collective-permute-done.last_ref
  10.9 1.6 %collective-permute-start.4 = (bf16[4,4,4096]{2,1,0:T(4,128)(2,1)S(1)}, bf16[4,4,4096]{2,1,0:T(4,128)(2,1)S(1)}, u32[]{:S(2)}, u32[]{:S(2)}) collective-permute-start(bf16[4,4,4096]{2,1,0:T(4,128)(2,1)S(1)} %shard_map.74.mine_ref), channel_id=1, source_target_pairs={{0,1},{1,0},{2,3},{3,2},{4,5},{5,4},{6,7},{7,6},{8,9},{9,8},{10,11... | collective-permute-start | bytes 393224 | tf_op jit(solution)/shard_map/ppermute | solution.py:234
  12.6 1.0 %collective-permute-done.4.got_ref = bf16[4,4,4096]{2,1,0:T(4,128)(2,1)S(1)} collective-permute-done((bf16[4,4,4096]{2,1,0:T(4,128)(2,1)S(1)}, bf16[4,4,4096]{2,1,0:T(4,128)(2,1)S(1)}, u32[]{:S(2)}, u32[]{:S(2)}) %collective-permute-start.4) | collective-permute-done | bytes 131104 | tf_op jit(solution)/shard_map/ppermute | solution.py:234
  13.6 0.0 copy-done.5
  13.6 0.0 copy-done.4
  13.6 0.0 copy-done.3
  13.6 0.0 copy-done.2
  13.6 0.0 slice-start
  13.6 0.0 slice-start.1
  13.6 0.0 slice-start.2
  13.6 3.1 %shard_map.75 = (bf16[32,4096]{1,0:T(8,128)(2,1)S(1)}, f32[32,2048]{1,0:T(8,128)S(1)}, f32[32,128]{1,0:T(8,128)S(1)}) custom-call(s32[2]{0:T(128)S(4)} %shard_map.73.place_ref, s32[1,4]{1,0:T(1,128)S(1)} %bitcast.3, bf16[4,4,4096]{2,1,0:T(4,128)(2,1)S(1)} %shard_map.74.mine_ref, bf16[4,4,4096]{2,1,0:T(4,128)(2,1)S(1)} %collective-permute-done.4.got_ref, ...), custom_call_target="tpu_custom_call" | custom-call | flops 5000000000 | tf_op jit(solution)/shard_map/pallas_call | solution.py:108
  16.7 0.0 copy-done
  16.7 0.0 slice-start.3
  16.7 3.0 %shard_map.76.h_ref = bf16[32,2048]{1,0:T(8,128)(2,1)S(1)} custom-call(bf16[32,4096]{1,0:T(8,128)(2,1)S(1)} %get-tuple-element.21.x_ref, f32[32,2048]{1,0:T(8,128)S(1)} %get-tuple-element.22.act_ref, bf16[4096,2048]{1,0:T(8,128)(2,1)S(1)} %copy-done), custom_call_target="tpu_custom_call" | custom-call | flops 2000000000 | tf_op jit(solution)/shard_map/pallas_call | solution.py:131
  19.8 0.0 slice-done
  19.8 0.0 slice-done.1
  19.8 0.0 slice-done.2
  19.8 0.0 slice-done.3
  19.8 1.6 %shard_map.78 = bf16[32,2048]{1,0:T(8,128)(2,1)S(1)} custom-call(s32[2]{0:T(128)S(4)} %shard_map.73.place_ref, bf16[32,2048]{1,0:T(8,128)(2,1)S(1)} %shard_map.76.h_ref, bf16[2048,4096]{1,0:T(8,128)(2,1)S(1)} %bitcast.2), custom_call_target="tpu_custom_call" | custom-call | flops 268435456 | tf_op jit(solution)/shard_map/pallas_call | solution.py:154
  21.4 0.4 %collective-permute-start.5 = (bf16[32,2048]{1,0:T(8,128)(2,1)S(1)}, bf16[32,2048]{1,0:T(8,128)(2,1)S(1)}, u32[]{:S(2)}, u32[]{:S(2)}) collective-permute-start(bf16[32,2048]{1,0:T(8,128)(2,1)S(1)} %shard_map.78), channel_id=1, source_target_pairs={{0,1},{1,0},{2,3},{3,2},{4,5},{5,4},{6,7},{7,6},{8,9},{9,8},{10,11... | collective-permute-start | bytes 393224 | tf_op jit(solution)/shard_map/ppermute | solution.py:234
  21.8 1.6 %shard_map.77.keep_ref = f32[32,2048]{1,0:T(8,128)S(1)} custom-call(s32[2]{0:T(128)S(4)} %shard_map.73.place_ref, bf16[32,2048]{1,0:T(8,128)(2,1)S(1)} %shard_map.76.h_ref, bf16[2048,4096]{1,0:T(8,128)(2,1)S(1)} %bitcast.2), custom_call_target="tpu_custom_call" | custom-call | flops 268435456 | tf_op jit(solution)/shard_map/pallas_call | solution.py:154
  23.3 0.0 collective-permute-done.5.got_ref
  23.3 0.1 shard_map.79
  23.4 2.0 %collective-permute-start.6 = (bf16[2,4,2048]{2,1,0:T(4,128)(2,1)S(1)}, bf16[2,4,2048]{2,1,0:T(4,128)(2,1)S(1)}, u32[]{:S(2)}, u32[]{:S(2)}) collective-permute-start(bf16[2,4,2048]{2,1,0:T(4,128)(2,1)S(1)} %get-tuple-element.24), channel_id=1, source_target_pairs={{0,6},{2,4},{4,2},{6,0},{8,14},{10,12},{12,10},{14,8},{1,7},{3,5},... | collective-permute-start | bytes 98312 | tf_op jit(solution)/shard_map/ppermute | solution.py:222
  25.5 0.7 %collective-permute-start.7 = (bf16[2,4,2048]{2,1,0:T(4,128)(2,1)S(1)}, bf16[2,4,2048]{2,1,0:T(4,128)(2,1)S(1)}, u32[]{:S(2)}, u32[]{:S(2)}) collective-permute-start(bf16[2,4,2048]{2,1,0:T(4,128)(2,1)S(1)} %get-tuple-element.25), channel_id=1, source_target_pairs={{0,4},{2,6},{4,0},{6,2},{8,12},{10,14},{12,8},{14,10},{1,5},{3,7},... | collective-permute-start | bytes 98312 | tf_op jit(solution)/shard_map/ppermute | solution.py:222
  26.1 0.8 %collective-permute-start.8 = (bf16[2,4,2048]{2,1,0:T(4,128)(2,1)S(1)}, bf16[2,4,2048]{2,1,0:T(4,128)(2,1)S(1)}, u32[]{:S(2)}, u32[]{:S(2)}) collective-permute-start(bf16[2,4,2048]{2,1,0:T(4,128)(2,1)S(1)} %get-tuple-element.26), channel_id=1, source_target_pairs={{0,2},{2,0},{4,6},{6,4},{8,10},{10,8},{12,14},{14,12},{1,3},{3,1},... | collective-permute-start | bytes 98312 | tf_op jit(solution)/shard_map/ppermute | solution.py:222
  27.0 1.3 %collective-permute-done.6.refs_1_ = bf16[2,4,2048]{2,1,0:T(4,128)(2,1)S(1)} collective-permute-done((bf16[2,4,2048]{2,1,0:T(4,128)(2,1)S(1)}, bf16[2,4,2048]{2,1,0:T(4,128)(2,1)S(1)}, u32[]{:S(2)}, u32[]{:S(2)}) %collective-permute-start.6) | collective-permute-done | bytes 32800 | tf_op jit(solution)/shard_map/ppermute | solution.py:222
  28.3 1.1 %collective-permute-done.7.refs_2_ = bf16[2,4,2048]{2,1,0:T(4,128)(2,1)S(1)} collective-permute-done((bf16[2,4,2048]{2,1,0:T(4,128)(2,1)S(1)}, bf16[2,4,2048]{2,1,0:T(4,128)(2,1)S(1)}, u32[]{:S(2)}, u32[]{:S(2)}) %collective-permute-start.7) | collective-permute-done | bytes 32800 | tf_op jit(solution)/shard_map/ppermute | solution.py:222
  29.4 0.7 %collective-permute-done.8.refs_3_ = bf16[2,4,2048]{2,1,0:T(4,128)(2,1)S(1)} collective-permute-done((bf16[2,4,2048]{2,1,0:T(4,128)(2,1)S(1)}, bf16[2,4,2048]{2,1,0:T(4,128)(2,1)S(1)}, u32[]{:S(2)}, u32[]{:S(2)}) %collective-permute-start.8) | collective-permute-done | bytes 32800 | tf_op jit(solution)/shard_map/ppermute | solution.py:222
  30.1 3.6 %collective-permute-start.9 = (bf16[4,2048]{1,0:T(4,128)(2,1)S(1)}, bf16[4,2048]{1,0:T(4,128)(2,1)S(1)}, u32[]{:S(2)}, u32[]{:S(2)}) collective-permute-start(bf16[4,2048]{1,0:T(4,128)(2,1)S(1)} %get-tuple-element.28), channel_id=1, source_target_pairs={{0,8},{2,10},{4,12},{6,14},{8,0},{10,2},{12,4},{14,6},{1,9},{3,11}... | collective-permute-start | bytes 49160 | tf_op jit(solution)/shard_map/ppermute | solution.py:222
  33.6 1.7 %collective-permute-done.9.got_ref = bf16[4,2048]{1,0:T(4,128)(2,1)S(1)} collective-permute-done((bf16[4,2048]{1,0:T(4,128)(2,1)S(1)}, bf16[4,2048]{1,0:T(4,128)(2,1)S(1)}, u32[]{:S(2)}, u32[]{:S(2)}) %collective-permute-start.9) | collective-permute-done | bytes 16416 | tf_op jit(solution)/shard_map/ppermute | solution.py:222
  35.4 0.6 %shard_map.81 = bf16[4,2048]{1,0:T(4,128)(2,1)} custom-call(f32[4,2048]{1,0:T(4,128)S(1)} %get-tuple-element.27.own_ref, bf16[4,2048]{1,0:T(4,128)(2,1)S(1)} %collective-permute-done.9.got_ref), custom_call_target="tpu_custom_call" | custom-call | tf_op jit(solution)/shard_map/pallas_call | solution.py:212
  (4 shorter events, 0.0 us)
Async XLA Ops:
  0.0 13.6 %copy-start.5 = (s32[4]{0:T(128)S(1)}, s32[4]{0:T(128)}, u32[]{:S(2)}) copy-start(s32[4]{0:T(128)} %param.11) | copy-start | bytes 52
  0.0 0.8 %copy-start.1 = (bf16[4,4096]{1,0:T(4,128)(2,1)S(1)}, bf16[4,4096]{1,0:T(4,128)(2,1)}, u32[]{:S(2)}) copy-start(bf16[4,4096]{1,0:T(4,128)(2,1)} %tokens_ref) | copy-start | bytes 98308
  0.0 13.6 %copy-start.4 = (f32[4,128]{1,0:T(4,128)S(1)}, f32[4,128]{1,0:T(4,128)}, u32[]{:S(2)}) copy-start(f32[4,128]{1,0:T(4,128)} %gates_ref.1) | copy-start | bytes 6148
  0.0 13.6 %copy-start.3 = (s32[4,128]{1,0:T(4,128)S(1)}, s32[4,128]{1,0:T(4,128)}, u32[]{:S(2)}) copy-start(s32[4,128]{1,0:T(4,128)} %rows_ref.1) | copy-start | bytes 6148
  0.0 13.6 %copy-start.2 = (bf16[4096,2048]{1,0:T(8,128)(2,1)S(1)}, bf16[4096,2048]{1,0:T(8,128)(2,1)}, u32[]{:S(2)}) copy-start(bf16[4096,2048]{1,0:T(8,128)(2,1)} %wg_ref.1) | copy-start | bytes 50331652
  0.8 16.0 %copy-start = (bf16[4096,2048]{1,0:T(8,128)(2,1)S(1)}, bf16[4096,2048]{1,0:T(8,128)(2,1)}, u32[]{:S(2)}) copy-start(bf16[4096,2048]{1,0:T(8,128)(2,1)} %wu_ref.1) | copy-start | bytes 50331652
  0.8 8.6 %collective-permute-start.3 = (bf16[4,4096]{1,0:T(4,128)(2,1)S(1)}, bf16[4,4096]{1,0:T(4,128)(2,1)S(1)}, u32[]{:S(2)}, u32[]{:S(2)}) collective-permute-start(bf16[4,4096]{1,0:T(4,128)(2,1)S(1)} %copy-done.1), channel_id=1, source_target_pairs={{1,14},{3,12},{5,10},{7,8},{9,6},{11,4},{13,2},{15,0},{0,11},{2,9}... | collective-permute-start | bytes 98312 | tf_op jit(solution)/shard_map/ppermute | solution.py:230
  5.2 5.5 %collective-permute-start.2 = (bf16[4,4096]{1,0:T(4,128)(2,1)S(1)}, bf16[4,4096]{1,0:T(4,128)(2,1)S(1)}, u32[]{:S(2)}, u32[]{:S(2)}) collective-permute-start(bf16[4,4096]{1,0:T(4,128)(2,1)S(1)} %copy-done.1), channel_id=1, source_target_pairs={{1,12},{3,14},{5,8},{7,10},{9,4},{11,6},{13,0},{15,2},{0,9},{2,11}... | collective-permute-start | bytes 98312 | tf_op jit(solution)/shard_map/ppermute | solution.py:230
  5.9 4.8 %collective-permute-start.1 = (bf16[4,4096]{1,0:T(4,128)(2,1)S(1)}, bf16[4,4096]{1,0:T(4,128)(2,1)S(1)}, u32[]{:S(2)}, u32[]{:S(2)}) collective-permute-start(bf16[4,4096]{1,0:T(4,128)(2,1)S(1)} %copy-done.1), channel_id=1, source_target_pairs={{1,2},{3,0},{5,6},{7,4},{9,10},{11,8},{13,14},{15,12},{0,7},{2,5},... | collective-permute-start | bytes 98312 | tf_op jit(solution)/shard_map/ppermute | solution.py:230
  6.0 4.9 %collective-permute-start = (bf16[4,4096]{1,0:T(4,128)(2,1)S(1)}, bf16[4,4096]{1,0:T(4,128)(2,1)S(1)}, u32[]{:S(2)}, u32[]{:S(2)}) collective-permute-start(bf16[4,4096]{1,0:T(4,128)(2,1)S(1)} %copy-done.1), channel_id=1, source_target_pairs={{0,5},{2,7},{4,1},{6,3},{8,13},{10,15},{12,9},{14,11},{16,21},{18,... | collective-permute-start | bytes 98312 | tf_op jit(solution)/shard_map/ppermute | solution.py:230
  10.9 2.6 %collective-permute-start.4 = (bf16[4,4,4096]{2,1,0:T(4,128)(2,1)S(1)}, bf16[4,4,4096]{2,1,0:T(4,128)(2,1)S(1)}, u32[]{:S(2)}, u32[]{:S(2)}) collective-permute-start(bf16[4,4,4096]{2,1,0:T(4,128)(2,1)S(1)} %shard_map.74.mine_ref), channel_id=1, source_target_pairs={{0,1},{1,0},{2,3},{3,2},{4,5},{5,4},{6,7},{7,6},{8,9},{9,8},{10,11... | collective-permute-start | bytes 393224 | tf_op jit(solution)/shard_map/ppermute | solution.py:234
  13.6 6.2 %slice-start = ((s8[16777216]{0:T(1024)(128)(4,1)}), s8[4194304]{0:T(1024)(128)(4,1)S(1)}, s32[]{:S(2)}) async-start(s8[16777216]{0:T(1024)(128)(4,1)} %bitcast.1), calls=%async_computation | async-start | bytes 8388608
  13.6 6.2 %slice-start.1 = ((s8[16777216]{0:T(1024)(128)(4,1)}), s8[4194304]{0:T(1024)(128)(4,1)S(1)}, s32[]{:S(2)}) async-start(s8[16777216]{0:T(1024)(128)(4,1)} %bitcast.1), calls=%async_computation.1 | async-start | bytes 8388608
  13.6 6.2 %slice-start.2 = ((s8[16777216]{0:T(1024)(128)(4,1)}), s8[4194304]{0:T(1024)(128)(4,1)S(1)}, s32[]{:S(2)}) async-start(s8[16777216]{0:T(1024)(128)(4,1)} %bitcast.1), calls=%async_computation.2 | async-start | bytes 8388608
  16.7 3.1 %slice-start.3 = ((s8[16777216]{0:T(1024)(128)(4,1)}), s8[4194304]{0:T(1024)(128)(4,1)S(1)}, s32[]{:S(2)}) async-start(s8[16777216]{0:T(1024)(128)(4,1)} %bitcast.1), calls=%async_computation.3 | async-start | bytes 8388608
  21.4 1.9 %collective-permute-start.5 = (bf16[32,2048]{1,0:T(8,128)(2,1)S(1)}, bf16[32,2048]{1,0:T(8,128)(2,1)S(1)}, u32[]{:S(2)}, u32[]{:S(2)}) collective-permute-start(bf16[32,2048]{1,0:T(8,128)(2,1)S(1)} %shard_map.78), channel_id=1, source_target_pairs={{0,1},{1,0},{2,3},{3,2},{4,5},{5,4},{6,7},{7,6},{8,9},{9,8},{10,11... | collective-permute-start | bytes 393224 | tf_op jit(solution)/shard_map/ppermute | solution.py:234
  23.4 4.9 %collective-permute-start.6 = (bf16[2,4,2048]{2,1,0:T(4,128)(2,1)S(1)}, bf16[2,4,2048]{2,1,0:T(4,128)(2,1)S(1)}, u32[]{:S(2)}, u32[]{:S(2)}) collective-permute-start(bf16[2,4,2048]{2,1,0:T(4,128)(2,1)S(1)} %get-tuple-element.24), channel_id=1, source_target_pairs={{0,6},{2,4},{4,2},{6,0},{8,14},{10,12},{12,10},{14,8},{1,7},{3,5},... | collective-permute-start | bytes 98312 | tf_op jit(solution)/shard_map/ppermute | solution.py:222
  25.5 3.9 %collective-permute-start.7 = (bf16[2,4,2048]{2,1,0:T(4,128)(2,1)S(1)}, bf16[2,4,2048]{2,1,0:T(4,128)(2,1)S(1)}, u32[]{:S(2)}, u32[]{:S(2)}) collective-permute-start(bf16[2,4,2048]{2,1,0:T(4,128)(2,1)S(1)} %get-tuple-element.25), channel_id=1, source_target_pairs={{0,4},{2,6},{4,0},{6,2},{8,12},{10,14},{12,8},{14,10},{1,5},{3,7},... | collective-permute-start | bytes 98312 | tf_op jit(solution)/shard_map/ppermute | solution.py:222
  26.1 3.9 %collective-permute-start.8 = (bf16[2,4,2048]{2,1,0:T(4,128)(2,1)S(1)}, bf16[2,4,2048]{2,1,0:T(4,128)(2,1)S(1)}, u32[]{:S(2)}, u32[]{:S(2)}) collective-permute-start(bf16[2,4,2048]{2,1,0:T(4,128)(2,1)S(1)} %get-tuple-element.26), channel_id=1, source_target_pairs={{0,2},{2,0},{4,6},{6,4},{8,10},{10,8},{12,14},{14,12},{1,3},{3,1},... | collective-permute-start | bytes 98312 | tf_op jit(solution)/shard_map/ppermute | solution.py:222
  30.1 5.3 %collective-permute-start.9 = (bf16[4,2048]{1,0:T(4,128)(2,1)S(1)}, bf16[4,2048]{1,0:T(4,128)(2,1)S(1)}, u32[]{:S(2)}, u32[]{:S(2)}) collective-permute-start(bf16[4,2048]{1,0:T(4,128)(2,1)S(1)} %get-tuple-element.28), channel_id=1, source_target_pairs={{0,8},{2,10},{4,12},{6,14},{8,0},{10,2},{12,4},{14,6},{1,9},{3,11}... | collective-permute-start | bytes 49160 | tf_op jit(solution)/shard_map/ppermute | solution.py:222

commit v11 on v10

--- a/solution.py
+++ b/solution.py
@@ -11,7 +11,7 @@
 CAP = 3
 TILE = 512
 MIB = 1 << 20
-ORDER = (0, 7, 6, 1, 2, 5, 4, 3)
+ORDER = (0, 1, 6, 7, 2, 3, 4, 5)
 SOURCES = len(ORDER)
 GATE = 5_000_000_000
 UP = 2_000_000_000
@@ -67,25 +67,35 @@
     return jnp.sum(jnp.where(rows == token, gates, 0.0), axis=1, keepdims=True)
 
 
-def pack_kernel(place_ref, tokens_ref, last_ref, *refs):
-    *pieces, out_ref = refs
-    for r, ref in enumerate(pieces[::-1]):
-        out_ref[r + 1] = ref[...]
-    out_ref[0] = jnp.where(place_ref[0] == 0, tokens_ref[...], last_ref[...])
-
-
-def pack(place, tokens, pieces):
-    return pl.pallas_call(
-        pack_kernel,
-        out_shape=jax.ShapeDtypeStruct((len(pieces), *tokens.shape), tokens.dtype),
-        in_specs=[SMEM] + [VMEM] * (1 + len(pieces)),
+def stack_kernel(*refs):
+    for at, ref in enumerate(refs[:-1]):
+        refs[-1][at] = ref[...]
+
+
+def stack(pieces):
+    return pl.pallas_call(
+        stack_kernel,
+        out_shape=jax.ShapeDtypeStruct((len(pieces), *pieces[0].shape), pieces[0].dtype),
+        in_specs=[VMEM] * len(pieces),
         out_specs=VMEM,
         compiler_params=pltpu.CompilerParams(vmem_limit_bytes=2 * MIB),
-    )(in_smem(place), tokens, *pieces)
+    )(*pieces)
 
 
 def gate_kernel(
-    per_expert, place_ref, counts_ref, mine_ref, got_ref, rows_ref, gates_ref, wg_ref, x_ref, act_ref, g_ref, wide
+    per_expert,
+    place_ref,
+    counts_ref,
+    tokens_ref,
+    mine_ref,
+    got_ref,
+    rows_ref,
+    gates_ref,
+    wg_ref,
+    x_ref,
+    act_ref,
+    g_ref,
+    wide,
 ):
     sets, count, _ = mine_ref.shape
     g = routed_gates(place_ref[1], per_expert, count, counts_ref, rows_ref, gates_ref)
@@ -94,6 +104,7 @@
         rows = pl.ds(j * count, count)
         wide[place_ref[0], rows, :] = mine_ref[j].astype(jnp.float32)
         wide[1 - place_ref[0], rows, :] = got_ref[j].astype(jnp.float32)
+    wide[0, pl.ds(0, count), :] = tokens_ref[...].astype(jnp.float32)
     x_ref[...] = wide[...].reshape(x_ref.shape).astype(jnp.bfloat16)
 
     for n in range(wg_ref.shape[1] // TILE):
@@ -102,7 +113,7 @@
         act_ref[:, cols] = gate / (1.0 + jnp.exp(-gate))
 
 
-def gate_rows(place, counts, mine, got, block_rows, row_gates, wg):
+def gate_rows(place, counts, tokens, mine, got, block_rows, row_gates, wg):
     total = 2 * mine.shape[0] * mine.shape[1]
     depth, width = wg.shape
     return pl.pallas_call(
@@ -112,12 +123,12 @@
             jax.ShapeDtypeStruct((total, width), jnp.float32),
             jax.ShapeDtypeStruct((total, 128), jnp.float32),
         ),
-        in_specs=[SMEM] + [VMEM] * 6,
+        in_specs=[SMEM] + [VMEM] * 7,
         out_specs=(VMEM,) * 3,
         scratch_shapes=[pltpu.VMEM((2, total // 2, depth), jnp.float32)],
         compiler_params=pltpu.CompilerParams(vmem_limit_bytes=2 * MIB),
         cost_estimate=pl.CostEstimate(flops=GATE, bytes_accessed=0, transcendentals=total * width),
-    )(in_smem(place), counts.reshape(1, -1), mine, got, block_rows, row_gates, in_vmem(wg))
+    )(in_smem(place), counts.reshape(1, -1), tokens, mine, got, block_rows, row_gates, in_vmem(wg))
 
 
 def up_kernel(x_ref, act_ref, wu_ref, h_out):
@@ -161,61 +172,58 @@
     )(in_smem(place), hidden, in_vmem(wd))
 
 
-def near_kernel(g_ref, keep_ref, got_ref, own_ref, *out_refs):
+def near_kernel(g_ref, keep_ref, got_ref, even_ref, odd_ref):
     both = (keep_ref[...] + got_ref[...].astype(jnp.float32)) * g_ref[:, :1]
-    pair, count, _ = own_ref.shape
-    group = SOURCES // pair
+    _, count, _ = odd_ref.shape
     for at, k in enumerate(ORDER):
-        out_ref = (own_ref, *out_refs)[k % group]
-        out_ref[k // group] = both[at * count : (at + 1) * count].astype(out_ref.dtype)
+        out_ref = (even_ref, odd_ref)[k % 2]
+        out_ref[k // 2] = both[at * count : (at + 1) * count].astype(out_ref.dtype)
 
 
 def near(g, keep, got):
     rows, width = keep.shape
-    group = SOURCES // 2
-    shape = (2, rows // SOURCES, width)
+    shape = (SOURCES // 2, rows // SOURCES, width)
     return pl.pallas_call(
         near_kernel,
-        out_shape=(jax.ShapeDtypeStruct(shape, jnp.float32),)
-        + (jax.ShapeDtypeStruct(shape, jnp.bfloat16),) * (group - 1),
+        out_shape=(jax.ShapeDtypeStruct(shape, jnp.float32), jax.ShapeDtypeStruct(shape, jnp.bfloat16)),
         in_specs=[VMEM] * 3,
-        out_specs=(VMEM,) * group,
+        out_specs=(VMEM, VMEM),
         compiler_params=pltpu.CompilerParams(vmem_limit_bytes=2 * MIB),
     )(g, keep, got)
 
 
-def far_kernel(*refs):
-    *part_refs, own_ref, next_ref = refs
-    for i, out_ref in enumerate((own_ref, next_ref)):
-        total = part_refs[0][i]
-        for part_ref in part_refs[1:]:
-            total = total + part_ref[i].astype(jnp.float32)
-        out_ref[...] = total.astype(out_ref.dtype)
-
-
-def far(parts):
-    shape = parts[0].shape[1:]
+def far_kernel(even_ref, got_ref, *out_refs):
+    for j, out_ref in enumerate(out_refs):
+        out_ref[...] = (even_ref[j] + got_ref[j].astype(jnp.float32)).astype(out_ref.dtype)
+
+
+def far(even, got):
+    sets, count, width = even.shape
     return pl.pallas_call(
         far_kernel,
-        out_shape=(jax.ShapeDtypeStruct(shape, jnp.float32), jax.ShapeDtypeStruct(shape, jnp.bfloat16)),
-        in_specs=[VMEM] * len(parts),
-        out_specs=(VMEM, VMEM),
-        compiler_params=pltpu.CompilerParams(vmem_limit_bytes=2 * MIB),
-    )(*parts)
-
-
-def sum_kernel(own_ref, got_ref, out_ref):
-    out_ref[...] = (own_ref[...] + got_ref[...].astype(jnp.float32)).astype(out_ref.dtype)
+        out_shape=(jax.ShapeDtypeStruct((count, width), jnp.float32),)
+        + (jax.ShapeDtypeStruct((count, width), jnp.bfloat16),) * (sets - 1),
+        in_specs=[VMEM, VMEM],
+        out_specs=(VMEM,) * sets,
+        compiler_params=pltpu.CompilerParams(vmem_limit_bytes=2 * MIB),
+    )(even, got)
+
+
+def sum_kernel(own_ref, *refs):
+    total = own_ref[...]
+    for ref in refs[:-1]:
+        total = total + ref[...].astype(jnp.float32)
+    refs[-1][...] = total.astype(jnp.bfloat16)
 
 
 def final_sum(own, got):
     return pl.pallas_call(
         sum_kernel,
         out_shape=jax.ShapeDtypeStruct(own.shape, jnp.bfloat16),
-        in_specs=[VMEM, VMEM],
+        in_specs=[VMEM] * (1 + len(got)),
         out_specs=VMEM,
         compiler_params=pltpu.CompilerParams(vmem_limit_bytes=2 * MIB),
-    )(own, got)
+    )(own, *got)
 
 
 def swapped(x, k):
@@ -226,7 +234,7 @@
     pairs = []
     for side, k in enumerate((first, second)):
         if k is not None:
-            pairs += [(2 * i + 1 - side, 2 * (i ^ k) + side) for i in range(SOURCES)]
+            pairs += [(2 * i + side, 2 * (i ^ k) + side) for i in range(SOURCES)]
     return lax.ppermute(x, ("exp", "hid"), pairs)
 
 
@@ -238,17 +246,17 @@
     place = first()
     tokens, place, counts = lax.optimization_barrier((tokens, place, block_counts))
     half = SOURCES // 2
-    pieces = [fetched(tokens, ORDER[b], ORDER[half + b]) for b in range(1, half)]
-    pieces += [fetched(tokens, None, ORDER[half])]
-    mine = pack(place, tokens, pieces[::-1])
-    x, act, g = gate_rows(place, counts, mine, swap_cores(mine), block_rows, row_gates, w_gate)
+    pieces = [fetched(tokens, None, ORDER[half])]
+    pieces += [fetched(tokens, ORDER[b], ORDER[half + b]) for b in range(1, half)]
+    mine = stack(pieces)
+    got = swap_cores(mine)
+    x, act, g = gate_rows(place, counts, tokens, mine, got, block_rows, row_gates, w_gate)
     hidden = hidden_rows(x, act, w_up)
     send = down_half(place, hidden, w_down, True, jnp.bfloat16)
     keep = down_half(place, hidden, w_down, False, jnp.float32)
-    own, *parts = near(g, keep, swap_cores(send))
-    returned = [swapped(parts[j - 1], j) for j in range(half - 1, 0, -1)]
-    own, other = far([own, *returned])
-    return final_sum(own, swapped(other, half))
+    even, odd = near(g, keep, swap_cores(send))
+    own, *parts = far(even, swapped(odd, 1))
+    return final_sum(own, [swapped(parts[j - 1], 2 * j) for j in range(half - 1, 0, -1)])
 
 
 def expert_block(segment, w_gate, w_up, w_down):

time: 36.1 us -> 35.5 us (0.983)
  starting transfers between devices: 17.7 us -> 12.6 us
  waiting for transfers between devices: 7.34 us -> 11.8 us
    ppermute x4, waiting for transfers between devices: 1.57 us -> 4.36 us  [fetched(): return lax.ppermute(x, ('exp', 'hid'), pairs)]
    ppermute x4, starting transfers between devices: 7.11 us -> 5.07 us  [swapped(): return lax.ppermute(x, 'exp', [(i, i ^ k) for i in range(SOURCES)])]
    ppermute x2, starting transfers between devices: 2.03 us -> 0.23 us  [swap_cores(): return lax.ppermute(x, 'hid', [(0, 1), (1, 0)])]
    ppermute x4, waiting for transfers between devices: 4.78 us -> 6.08 us  [swapped(): return lax.ppermute(x, 'exp', [(i, i ^ k) for i in range(SOURCES)])]
    ppermute x4, starting transfers between devices: 8.55 us -> 7.33 us  [fetched(): return lax.ppermute(x, ('exp', 'hid'), pairs)]
  transfers between devices with their start and end apart: 10 -> 10, of which waited for: 7 -> 6; matrix products, arithmetic and copies ran while one was open for 0% -> 0% of each run, Pallas kernels for 4% -> 4%
where the time goes in v11:
time: 35.5 us; the launch traced here: 35.4 us
  starting transfers between devices  12.6 us (35%)
  waiting for transfers between devices  11.8 us (33%)
  Pallas kernels  10 us (28%)
  local copies, waits for them, and re-layouts  0.79 us (2%)
    ppermute x4, starting transfers between devices, fetched(): return lax.ppermute(x, ('exp', 'hid'), pairs)  7.33 us
    ppermute x4, waiting for transfers between devices, swapped(): return lax.ppermute(x, 'exp', [(i, i ^ k) for i in range(SOURCES)])  6.08 us
    ppermute x4, starting transfers between devices, swapped(): return lax.ppermute(x, 'exp', [(i, i ^ k) for i in range(SOURCES)])  5.07 us
    ppermute x4, waiting for transfers between devices, fetched(): return lax.ppermute(x, ('exp', 'hid'), pairs)  4.36 us
    pallas_call x1, Pallas kernels, gate_rows(): pl.pallas_call(functools.partial(gate_kernel, SOURCES // block_rows.shape...  3.12 us
    pallas_call x2, Pallas kernels, down_half(): pl.pallas_call(functools.partial(down_kernel, other), out_shape=jax.Shape...  3.12 us
    pallas_call x1, Pallas kernels, hidden_rows(): pl.pallas_call(up_kernel, out_shape=jax.ShapeDtypeStruct(act.shape, jnp.b...  3.01 us
    ppermute x2, waiting for transfers between devices, swap_cores(): return lax.ppermute(x, 'hid', [(0, 1), (1, 0)])  1.34 us
  transfers between devices with their start and end apart: 10, of which 6 were waited for; matrix products, arithmetic and copies ran while one was open for 0% of the time, Pallas kernels for 4%

profile of v11, /device:TPU:0, one launch (start us, length us, event | category | flops | bytes accessed | tf_op | source)
XLA Modules:
  0.0 35.4 jit_solution(10109091849772566764)
XLA Ops:
  0.0 0.0 copy-start.5
  0.0 0.0 copy-start.2
  0.0 0.0 copy-start.4
  0.0 0.0 copy-start.3
  0.0 0.0 copy-start.1
  0.0 0.7 %copy-done.2 = bf16[4,4096]{1,0:T(4,128)(2,1)S(1)} copy-done((bf16[4,4096]{1,0:T(4,128)(2,1)S(1)}, bf16[4,4096]{1,0:T(4,128)(2,1)}, u32[]{:S(2)}) %copy-start.2) | copy-done | bytes 32792
  0.8 0.0 copy-start
  0.8 6.0 %collective-permute-start.3 = (bf16[4,4096]{1,0:T(4,128)(2,1)S(1)}, bf16[4,4096]{1,0:T(4,128)(2,1)S(1)}, u32[]{:S(2)}, u32[]{:S(2)}) collective-permute-start(bf16[4,4096]{1,0:T(4,128)(2,1)S(1)} %copy-done.2), channel_id=1, source_target_pairs={{0,14},{2,12},{4,10},{6,8},{8,6},{10,4},{12,2},{14,0},{1,11},{3,9}... | collective-permute-start | bytes 98312 | tf_op jit(solution)/shard_map/ppermute | solution.py:238
  6.8 0.2 collective-permute-start.2
  7.0 0.3 collective-permute-start.1
  7.3 0.8 %collective-permute-start = (bf16[4,4096]{1,0:T(4,128)(2,1)S(1)}, bf16[4,4096]{1,0:T(4,128)(2,1)S(1)}, u32[]{:S(2)}, u32[]{:S(2)}) collective-permute-start(bf16[4,4096]{1,0:T(4,128)(2,1)S(1)} %copy-done.2), channel_id=1, source_target_pairs={{1,5},{3,7},{5,1},{7,3},{9,13},{11,15},{13,9},{15,11},{17,21},{19,... | collective-permute-start | bytes 98312 | tf_op jit(solution)/shard_map/ppermute | solution.py:238
  8.1 0.5 %collective-permute-done.3.refs_3_ = bf16[4,4096]{1,0:T(4,128)(2,1)S(1)} collective-permute-done((bf16[4,4096]{1,0:T(4,128)(2,1)S(1)}, bf16[4,4096]{1,0:T(4,128)(2,1)S(1)}, u32[]{:S(2)}, u32[]{:S(2)}) %collective-permute-start.3) | collective-permute-done | bytes 32800 | tf_op jit(solution)/shard_map/ppermute | solution.py:238
  8.6 3.8 %collective-permute-done.2.refs_2_ = bf16[4,4096]{1,0:T(4,128)(2,1)S(1)} collective-permute-done((bf16[4,4096]{1,0:T(4,128)(2,1)S(1)}, bf16[4,4096]{1,0:T(4,128)(2,1)S(1)}, u32[]{:S(2)}, u32[]{:S(2)}) %collective-permute-start.2) | collective-permute-done | bytes 32800 | tf_op jit(solution)/shard_map/ppermute | solution.py:238
  12.5 0.0 collective-permute-done.1.refs_1_
  12.5 0.0 collective-permute-done.refs_0_
  12.5 0.1 collective-permute-start.4
  12.6 1.3 %collective-permute-done.4.got_ref = bf16[4,4,4096]{2,1,0:T(4,128)(2,1)S(1)} collective-permute-done((bf16[4,4,4096]{2,1,0:T(4,128)(2,1)S(1)}, bf16[4,4,4096]{2,1,0:T(4,128)(2,1)S(1)}, u32[]{:S(2)}, u32[]{:S(2)}) %collective-permute-start.4) | collective-permute-done | bytes 131104 | tf_op jit(solution)/shard_map/ppermute | solution.py:242
  13.9 0.0 copy-done.5
  13.9 0.0 copy-done.4
  13.9 0.0 copy-done.3
  13.9 0.0 copy-done.1
  13.9 0.0 slice-start
  13.9 0.0 slice-start.1
  13.9 0.0 slice-start.2
  14.0 3.1 %shard_map.75 = (bf16[32,4096]{1,0:T(8,128)(2,1)S(1)}, f32[32,2048]{1,0:T(8,128)S(1)}, f32[32,128]{1,0:T(8,128)S(1)}) custom-call(s32[2]{0:T(128)S(4)} %shard_map.73.place_ref, s32[1,4]{1,0:T(1,128)S(1)} %bitcast.3, bf16[4,4096]{1,0:T(4,128)(2,1)S(1)} %copy-done.2, bf16[4,4,4096]{2,1,0:T(4,128)(2,1)S(1)} %shard_map.74.mine_ref, ...), custom_call_target="tpu_custom_call" | custom-call | flops 5000000000 | tf_op jit(solution)/shard_map/pallas_call | solution.py:119
  17.1 0.0 copy-done
  17.1 0.0 slice-start.3
  17.1 3.0 %shard_map.76.h_ref = bf16[32,2048]{1,0:T(8,128)(2,1)S(1)} custom-call(bf16[32,4096]{1,0:T(8,128)(2,1)S(1)} %get-tuple-element.21.x_ref, f32[32,2048]{1,0:T(8,128)S(1)} %get-tuple-element.22.act_ref, bf16[4096,2048]{1,0:T(8,128)(2,1)S(1)} %copy-done), custom_call_target="tpu_custom_call" | custom-call | flops 2000000000 | tf_op jit(solution)/shard_map/pallas_call | solution.py:142
  20.1 0.0 slice-done
  20.1 0.0 slice-done.1
  20.1 0.0 slice-done.2
  20.2 0.0 slice-done.3
  20.2 1.6 %shard_map.78 = bf16[32,2048]{1,0:T(8,128)(2,1)S(1)} custom-call(s32[2]{0:T(128)S(4)} %shard_map.73.place_ref, bf16[32,2048]{1,0:T(8,128)(2,1)S(1)} %shard_map.76.h_ref, bf16[2048,4096]{1,0:T(8,128)(2,1)S(1)} %bitcast.2), custom_call_target="tpu_custom_call" | custom-call | flops 268435456 | tf_op jit(solution)/shard_map/pallas_call | solution.py:165
  21.7 0.2 collective-permute-start.5
  21.9 1.6 %shard_map.77.keep_ref = f32[32,2048]{1,0:T(8,128)S(1)} custom-call(s32[2]{0:T(128)S(4)} %shard_map.73.place_ref, bf16[32,2048]{1,0:T(8,128)(2,1)S(1)} %shard_map.76.h_ref, bf16[2048,4096]{1,0:T(8,128)(2,1)S(1)} %bitcast.2), custom_call_target="tpu_custom_call" | custom-call | flops 268435456 | tf_op jit(solution)/shard_map/pallas_call | solution.py:165
  23.5 0.0 collective-permute-done.5.got_ref
  23.5 0.1 shard_map.79
  23.6 0.6 %collective-permute-start.6 = (bf16[4,4,2048]{2,1,0:T(4,128)(2,1)S(1)}, bf16[4,4,2048]{2,1,0:T(4,128)(2,1)S(1)}, u32[]{:S(2)}, u32[]{:S(2)}) collective-permute-start(bf16[4,4,2048]{2,1,0:T(4,128)(2,1)S(1)} %get-tuple-element.24), channel_id=1, source_target_pairs={{0,2},{2,0},{4,6},{6,4},{8,10},{10,8},{12,14},{14,12},{1,3},{3,1},... | collective-permute-start | bytes 196616 | tf_op jit(solution)/shard_map/ppermute | solution.py:230
  24.2 3.8 %collective-permute-done.6.got_ref = bf16[4,4,2048]{2,1,0:T(4,128)(2,1)S(1)} collective-permute-done((bf16[4,4,2048]{2,1,0:T(4,128)(2,1)S(1)}, bf16[4,4,2048]{2,1,0:T(4,128)(2,1)S(1)}, u32[]{:S(2)}, u32[]{:S(2)}) %collective-permute-start.6) | collective-permute-done | bytes 65568 | tf_op jit(solution)/shard_map/ppermute | solution.py:230
  28.0 2.1 %collective-permute-start.7 = (bf16[4,2048]{1,0:T(4,128)(2,1)S(1)}, bf16[4,2048]{1,0:T(4,128)(2,1)S(1)}, u32[]{:S(2)}, u32[]{:S(2)}) collective-permute-start(bf16[4,2048]{1,0:T(4,128)(2,1)S(1)} %get-tuple-element.26), channel_id=1, source_target_pairs={{0,12},{2,14},{4,8},{6,10},{8,4},{10,6},{12,0},{14,2},{1,13},{3,15... | collective-permute-start | bytes 49160 | tf_op jit(solution)/shard_map/ppermute | solution.py:230
  30.1 0.0 collective-permute-start.8
  30.1 2.4 %collective-permute-start.9 = (bf16[4,2048]{1,0:T(4,128)(2,1)S(1)}, bf16[4,2048]{1,0:T(4,128)(2,1)S(1)}, u32[]{:S(2)}, u32[]{:S(2)}) collective-permute-start(bf16[4,2048]{1,0:T(4,128)(2,1)S(1)} %get-tuple-element.28), channel_id=1, source_target_pairs={{0,4},{2,6},{4,0},{6,2},{8,12},{10,14},{12,8},{14,10},{1,5},{3,7},... | collective-permute-start | bytes 49160 | tf_op jit(solution)/shard_map/ppermute | solution.py:230
  32.5 1.1 %collective-permute-done.7.refs_0_ = bf16[4,2048]{1,0:T(4,128)(2,1)S(1)} collective-permute-done((bf16[4,2048]{1,0:T(4,128)(2,1)S(1)}, bf16[4,2048]{1,0:T(4,128)(2,1)S(1)}, u32[]{:S(2)}, u32[]{:S(2)}) %collective-permute-start.7) | collective-permute-done | bytes 16416 | tf_op jit(solution)/shard_map/ppermute | solution.py:230
  33.6 1.1 %collective-permute-done.8.refs_1_ = bf16[4,2048]{1,0:T(4,128)(2,1)S(1)} collective-permute-done((bf16[4,2048]{1,0:T(4,128)(2,1)S(1)}, bf16[4,2048]{1,0:T(4,128)(2,1)S(1)}, u32[]{:S(2)}, u32[]{:S(2)}) %collective-permute-start.8) | collective-permute-done | bytes 16416 | tf_op jit(solution)/shard_map/ppermute | solution.py:230
  34.8 0.0 collective-permute-done.9.refs_2_
  34.8 0.6 %shard_map.81 = bf16[4,2048]{1,0:T(4,128)(2,1)} custom-call(f32[4,2048]{1,0:T(4,128)S(1)} %get-tuple-element.25.own_ref, bf16[4,2048]{1,0:T(4,128)(2,1)S(1)} %collective-permute-done.7.refs_0_, bf16[4,2048]{1,0:T(4,128)(2,1)S(1)} %collective-permute-done.8.refs_1_, bf16[4,2048]{1,0:T(4,128)(2,1)S(1)} %collective-permute-done.9.refs_2_), custom_call_target="tpu_custom_call" | custom-call | tf_op jit(solution)/shard_map/pallas_call | solution.py:220
  (4 shorter events, 0.0 us)
Async XLA Ops:
  0.0 13.9 %copy-start.5 = (s32[4]{0:T(128)S(1)}, s32[4]{0:T(128)}, u32[]{:S(2)}) copy-start(s32[4]{0:T(128)} %param.11) | copy-start | bytes 52
  0.0 0.8 %copy-start.2 = (bf16[4,4096]{1,0:T(4,128)(2,1)S(1)}, bf16[4,4096]{1,0:T(4,128)(2,1)}, u32[]{:S(2)}) copy-start(bf16[4,4096]{1,0:T(4,128)(2,1)} %tokens_ref) | copy-start | bytes 98308
  0.0 13.9 %copy-start.4 = (f32[4,128]{1,0:T(4,128)S(1)}, f32[4,128]{1,0:T(4,128)}, u32[]{:S(2)}) copy-start(f32[4,128]{1,0:T(4,128)} %gates_ref.1) | copy-start | bytes 6148
  0.0 13.9 %copy-start.3 = (s32[4,128]{1,0:T(4,128)S(1)}, s32[4,128]{1,0:T(4,128)}, u32[]{:S(2)}) copy-start(s32[4,128]{1,0:T(4,128)} %rows_ref.1) | copy-start | bytes 6148
  0.0 13.9 %copy-start.1 = (bf16[4096,2048]{1,0:T(8,128)(2,1)S(1)}, bf16[4096,2048]{1,0:T(8,128)(2,1)}, u32[]{:S(2)}) copy-start(bf16[4096,2048]{1,0:T(8,128)(2,1)} %wg_ref.1) | copy-start | bytes 50331652
  0.8 16.3 %copy-start = (bf16[4096,2048]{1,0:T(8,128)(2,1)S(1)}, bf16[4096,2048]{1,0:T(8,128)(2,1)}, u32[]{:S(2)}) copy-start(bf16[4096,2048]{1,0:T(8,128)(2,1)} %wu_ref.1) | copy-start | bytes 50331652
  0.8 7.9 %collective-permute-start.3 = (bf16[4,4096]{1,0:T(4,128)(2,1)S(1)}, bf16[4,4096]{1,0:T(4,128)(2,1)S(1)}, u32[]{:S(2)}, u32[]{:S(2)}) collective-permute-start(bf16[4,4096]{1,0:T(4,128)(2,1)S(1)} %copy-done.2), channel_id=1, source_target_pairs={{0,14},{2,12},{4,10},{6,8},{8,6},{10,4},{12,2},{14,0},{1,11},{3,9}... | collective-permute-start | bytes 98312 | tf_op jit(solution)/shard_map/ppermute | solution.py:238
  6.8 5.7 %collective-permute-start.2 = (bf16[4,4096]{1,0:T(4,128)(2,1)S(1)}, bf16[4,4096]{1,0:T(4,128)(2,1)S(1)}, u32[]{:S(2)}, u32[]{:S(2)}) collective-permute-start(bf16[4,4096]{1,0:T(4,128)(2,1)S(1)} %copy-done.2), channel_id=1, source_target_pairs={{0,12},{2,14},{4,8},{6,10},{8,4},{10,6},{12,0},{14,2},{1,9},{3,11}... | collective-permute-start | bytes 98312 | tf_op jit(solution)/shard_map/ppermute | solution.py:238
  7.0 5.5 %collective-permute-start.1 = (bf16[4,4096]{1,0:T(4,128)(2,1)S(1)}, bf16[4,4096]{1,0:T(4,128)(2,1)S(1)}, u32[]{:S(2)}, u32[]{:S(2)}) collective-permute-start(bf16[4,4096]{1,0:T(4,128)(2,1)S(1)} %copy-done.2), channel_id=1, source_target_pairs={{0,2},{2,0},{4,6},{6,4},{8,10},{10,8},{12,14},{14,12},{1,7},{3,5},... | collective-permute-start | bytes 98312 | tf_op jit(solution)/shard_map/ppermute | solution.py:238
  7.3 5.2 %collective-permute-start = (bf16[4,4096]{1,0:T(4,128)(2,1)S(1)}, bf16[4,4096]{1,0:T(4,128)(2,1)S(1)}, u32[]{:S(2)}, u32[]{:S(2)}) collective-permute-start(bf16[4,4096]{1,0:T(4,128)(2,1)S(1)} %copy-done.2), channel_id=1, source_target_pairs={{1,5},{3,7},{5,1},{7,3},{9,13},{11,15},{13,9},{15,11},{17,21},{19,... | collective-permute-start | bytes 98312 | tf_op jit(solution)/shard_map/ppermute | solution.py:238
  12.5 1.4 %collective-permute-start.4 = (bf16[4,4,4096]{2,1,0:T(4,128)(2,1)S(1)}, bf16[4,4,4096]{2,1,0:T(4,128)(2,1)S(1)}, u32[]{:S(2)}, u32[]{:S(2)}) collective-permute-start(bf16[4,4,4096]{2,1,0:T(4,128)(2,1)S(1)} %shard_map.74.mine_ref), channel_id=1, source_target_pairs={{0,1},{1,0},{2,3},{3,2},{4,5},{5,4},{6,7},{7,6},{8,9},{9,8},{10,11... | collective-permute-start | bytes 393224 | tf_op jit(solution)/shard_map/ppermute | solution.py:242
  13.9 6.2 %slice-start = ((s8[16777216]{0:T(1024)(128)(4,1)}), s8[4194304]{0:T(1024)(128)(4,1)S(1)}, s32[]{:S(2)}) async-start(s8[16777216]{0:T(1024)(128)(4,1)} %bitcast.1), calls=%async_computation | async-start | bytes 8388608
  13.9 6.2 %slice-start.1 = ((s8[16777216]{0:T(1024)(128)(4,1)}), s8[4194304]{0:T(1024)(128)(4,1)S(1)}, s32[]{:S(2)}) async-start(s8[16777216]{0:T(1024)(128)(4,1)} %bitcast.1), calls=%async_computation.1 | async-start | bytes 8388608
  13.9 6.2 %slice-start.2 = ((s8[16777216]{0:T(1024)(128)(4,1)}), s8[4194304]{0:T(1024)(128)(4,1)S(1)}, s32[]{:S(2)}) async-start(s8[16777216]{0:T(1024)(128)(4,1)} %bitcast.1), calls=%async_computation.2 | async-start | bytes 8388608
  17.1 3.1 %slice-start.3 = ((s8[16777216]{0:T(1024)(128)(4,1)}), s8[4194304]{0:T(1024)(128)(4,1)S(1)}, s32[]{:S(2)}) async-start(s8[16777216]{0:T(1024)(128)(4,1)} %bitcast.1), calls=%async_computation.3 | async-start | bytes 8388608
  21.7 1.7 %collective-permute-start.5 = (bf16[32,2048]{1,0:T(8,128)(2,1)S(1)}, bf16[32,2048]{1,0:T(8,128)(2,1)S(1)}, u32[]{:S(2)}, u32[]{:S(2)}) collective-permute-start(bf16[32,2048]{1,0:T(8,128)(2,1)S(1)} %shard_map.78), channel_id=1, source_target_pairs={{0,1},{1,0},{2,3},{3,2},{4,5},{5,4},{6,7},{7,6},{8,9},{9,8},{10,11... | collective-permute-start | bytes 393224 | tf_op jit(solution)/shard_map/ppermute | solution.py:242
  23.6 4.4 %collective-permute-start.6 = (bf16[4,4,2048]{2,1,0:T(4,128)(2,1)S(1)}, bf16[4,4,2048]{2,1,0:T(4,128)(2,1)S(1)}, u32[]{:S(2)}, u32[]{:S(2)}) collective-permute-start(bf16[4,4,2048]{2,1,0:T(4,128)(2,1)S(1)} %get-tuple-element.24), channel_id=1, source_target_pairs={{0,2},{2,0},{4,6},{6,4},{8,10},{10,8},{12,14},{14,12},{1,3},{3,1},... | collective-permute-start | bytes 196616 | tf_op jit(solution)/shard_map/ppermute | solution.py:230
  28.0 5.6 %collective-permute-start.7 = (bf16[4,2048]{1,0:T(4,128)(2,1)S(1)}, bf16[4,2048]{1,0:T(4,128)(2,1)S(1)}, u32[]{:S(2)}, u32[]{:S(2)}) collective-permute-start(bf16[4,2048]{1,0:T(4,128)(2,1)S(1)} %get-tuple-element.26), channel_id=1, source_target_pairs={{0,12},{2,14},{4,8},{6,10},{8,4},{10,6},{12,0},{14,2},{1,13},{3,15... | collective-permute-start | bytes 49160 | tf_op jit(solution)/shard_map/ppermute | solution.py:230
  30.1 4.6 %collective-permute-start.8 = (bf16[4,2048]{1,0:T(4,128)(2,1)S(1)}, bf16[4,2048]{1,0:T(4,128)(2,1)S(1)}, u32[]{:S(2)}, u32[]{:S(2)}) collective-permute-start(bf16[4,2048]{1,0:T(4,128)(2,1)S(1)} %get-tuple-element.27), channel_id=1, source_target_pairs={{0,8},{2,10},{4,12},{6,14},{8,0},{10,2},{12,4},{14,6},{1,9},{3,11}... | collective-permute-start | bytes 49160 | tf_op jit(solution)/shard_map/ppermute | solution.py:230
  30.1 4.6 %collective-permute-start.9 = (bf16[4,2048]{1,0:T(4,128)(2,1)S(1)}, bf16[4,2048]{1,0:T(4,128)(2,1)S(1)}, u32[]{:S(2)}, u32[]{:S(2)}) collective-permute-start(bf16[4,2048]{1,0:T(4,128)(2,1)S(1)} %get-tuple-element.28), channel_id=1, source_target_pairs={{0,4},{2,6},{4,0},{6,2},{8,12},{10,14},{12,8},{14,10},{1,5},{3,7},... | collective-permute-start | bytes 49160 | tf_op jit(solution)/shard_map/ppermute | solution.py:230

commit v12 on v10

--- a/solution.py
+++ b/solution.py
@@ -11,7 +11,7 @@
 CAP = 3
 TILE = 512
 MIB = 1 << 20
-ORDER = (0, 7, 6, 1, 2, 5, 4, 3)
+ORDER = (0, 1, 6, 7, 2, 3, 4, 5)
 SOURCES = len(ORDER)
 GATE = 5_000_000_000
 UP = 2_000_000_000
@@ -67,25 +67,35 @@
     return jnp.sum(jnp.where(rows == token, gates, 0.0), axis=1, keepdims=True)
 
 
-def pack_kernel(place_ref, tokens_ref, last_ref, *refs):
-    *pieces, out_ref = refs
-    for r, ref in enumerate(pieces[::-1]):
-        out_ref[r + 1] = ref[...]
-    out_ref[0] = jnp.where(place_ref[0] == 0, tokens_ref[...], last_ref[...])
-
-
-def pack(place, tokens, pieces):
-    return pl.pallas_call(
-        pack_kernel,
-        out_shape=jax.ShapeDtypeStruct((len(pieces), *tokens.shape), tokens.dtype),
-        in_specs=[SMEM] + [VMEM] * (1 + len(pieces)),
+def stack_kernel(*refs):
+    for at, ref in enumerate(refs[:-1]):
+        refs[-1][at] = ref[...]
+
+
+def stack(pieces):
+    return pl.pallas_call(
+        stack_kernel,
+        out_shape=jax.ShapeDtypeStruct((len(pieces), *pieces[0].shape), pieces[0].dtype),
+        in_specs=[VMEM] * len(pieces),
         out_specs=VMEM,
         compiler_params=pltpu.CompilerParams(vmem_limit_bytes=2 * MIB),
-    )(in_smem(place), tokens, *pieces)
+    )(*pieces)
 
 
 def gate_kernel(
-    per_expert, place_ref, counts_ref, mine_ref, got_ref, rows_ref, gates_ref, wg_ref, x_ref, act_ref, g_ref, wide
+    per_expert,
+    place_ref,
+    counts_ref,
+    tokens_ref,
+    mine_ref,
+    got_ref,
+    rows_ref,
+    gates_ref,
+    wg_ref,
+    x_ref,
+    act_ref,
+    g_ref,
+    wide,
 ):
     sets, count, _ = mine_ref.shape
     g = routed_gates(place_ref[1], per_expert, count, counts_ref, rows_ref, gates_ref)
@@ -94,6 +104,7 @@
         rows = pl.ds(j * count, count)
         wide[place_ref[0], rows, :] = mine_ref[j].astype(jnp.float32)
         wide[1 - place_ref[0], rows, :] = got_ref[j].astype(jnp.float32)
+    wide[0, pl.ds(0, count), :] = tokens_ref[...].astype(jnp.float32)
     x_ref[...] = wide[...].reshape(x_ref.shape).astype(jnp.bfloat16)
 
     for n in range(wg_ref.shape[1] // TILE):
@@ -102,7 +113,7 @@
         act_ref[:, cols] = gate / (1.0 + jnp.exp(-gate))
 
 
-def gate_rows(place, counts, mine, got, block_rows, row_gates, wg):
+def gate_rows(place, counts, tokens, mine, got, block_rows, row_gates, wg):
     total = 2 * mine.shape[0] * mine.shape[1]
     depth, width = wg.shape
     return pl.pallas_call(
@@ -112,12 +123,12 @@
             jax.ShapeDtypeStruct((total, width), jnp.float32),
             jax.ShapeDtypeStruct((total, 128), jnp.float32),
         ),
-        in_specs=[SMEM] + [VMEM] * 6,
+        in_specs=[SMEM] + [VMEM] * 7,
         out_specs=(VMEM,) * 3,
         scratch_shapes=[pltpu.VMEM((2, total // 2, depth), jnp.float32)],
         compiler_params=pltpu.CompilerParams(vmem_limit_bytes=2 * MIB),
         cost_estimate=pl.CostEstimate(flops=GATE, bytes_accessed=0, transcendentals=total * width),
-    )(in_smem(place), counts.reshape(1, -1), mine, got, block_rows, row_gates, in_vmem(wg))
+    )(in_smem(place), counts.reshape(1, -1), tokens, mine, got, block_rows, row_gates, in_vmem(wg))
 
 
 def up_kernel(x_ref, act_ref, wu_ref, h_out):
@@ -223,11 +234,15 @@
 
 
 def fetched(x, first, second):
-    pairs = []
-    for side, k in enumerate((first, second)):
-        if k is not None:
-            pairs += [(2 * i + 1 - side, 2 * (i ^ k) + side) for i in range(SOURCES)]
-    return lax.ppermute(x, ("exp", "hid"), pairs)
+    return lax.ppermute(
+        x,
+        ("exp", "hid"),
+        [(2 * i + 1 - side, 2 * (i ^ k) + side) for side, k in enumerate((first, second)) for i in range(SOURCES)],
+    )
+
+
+def fetched_by_one(x, k):
+    return lax.ppermute(x, ("exp", "hid"), [(2 * i + 1, 2 * (i ^ k) + 1) for i in range(SOURCES)])
 
 
 def swap_cores(x):
@@ -238,10 +253,11 @@
     place = first()
     tokens, place, counts = lax.optimization_barrier((tokens, place, block_counts))
     half = SOURCES // 2
-    pieces = [fetched(tokens, ORDER[b], ORDER[half + b]) for b in range(1, half)]
-    pieces += [fetched(tokens, None, ORDER[half])]
-    mine = pack(place, tokens, pieces[::-1])
-    x, act, g = gate_rows(place, counts, mine, swap_cores(mine), block_rows, row_gates, w_gate)
+    pieces = [fetched_by_one(tokens, ORDER[half])]
+    pieces += [fetched(tokens, ORDER[b], ORDER[half + b]) for b in range(1, half)]
+    mine = stack(pieces)
+    got = swap_cores(mine)
+    x, act, g = gate_rows(place, counts, tokens, mine, got, block_rows, row_gates, w_gate)
     hidden = hidden_rows(x, act, w_up)
     send = down_half(place, hidden, w_down, True, jnp.bfloat16)
     keep = down_half(place, hidden, w_down, False, jnp.float32)

time: 36.1 us -> 35.6 us (0.986)
  starting transfers between devices: 17.7 us -> 14.8 us
  waiting for transfers between devices: 7.34 us -> 9.66 us
    ppermute x4, starting transfers between devices: 8.55 us -> 6.03 us  [the longest x3 5.25 us: fetched(): lax.ppermute(x, ('exp', 'hid'), [(2 * i + 1 - side, 2 * (i ^ k) + side) f...]
    ppermute x4, waiting for transfers between devices: 1.57 us -> 3.89 us  [the longest x3 3.89 us: fetched(): lax.ppermute(x, ('exp', 'hid'), [(2 * i + 1 - side, 2 * (i ^ k) + side) f...]
    ppermute x2, starting transfers between devices: 2.03 us -> 1.66 us  [swap_cores(): return lax.ppermute(x, 'hid', [(0, 1), (1, 0)])]
where the time goes in v12:
time: 35.6 us; the launch traced here: 35.4 us
  starting transfers between devices  14.8 us (42%)
  Pallas kernels  10 us (28%)
  waiting for transfers between devices  9.66 us (27%)
  local copies, waits for them, and re-layouts  0.79 us (2%)
    ppermute x4, starting transfers between devices, swapped(): return lax.ppermute(x, 'exp', [(i, i ^ k) for i in range(SOURCES)])  7.1 us
    ppermute x3, starting transfers between devices, fetched(): lax.ppermute(x, ('exp', 'hid'), [(2 * i + 1 - side, 2 * (i ^ k) + side) f...  5.25 us
    ppermute x4, waiting for transfers between devices, swapped(): return lax.ppermute(x, 'exp', [(i, i ^ k) for i in range(SOURCES)])  4.78 us
    ppermute x3, waiting for transfers between devices, fetched(): lax.ppermute(x, ('exp', 'hid'), [(2 * i + 1 - side, 2 * (i ^ k) + side) f...  3.89 us
    pallas_call x1, Pallas kernels, gate_rows(): pl.pallas_call(functools.partial(gate_kernel, SOURCES // block_rows.shape...  3.12 us
    pallas_call x2, Pallas kernels, down_half(): pl.pallas_call(functools.partial(down_kernel, other), out_shape=jax.Shape...  3.12 us
    pallas_call x1, Pallas kernels, hidden_rows(): pl.pallas_call(up_kernel, out_shape=jax.ShapeDtypeStruct(act.shape, jnp.b...  3.01 us
    ppermute x2, starting transfers between devices, swap_cores(): return lax.ppermute(x, 'hid', [(0, 1), (1, 0)])  1.66 us
  transfers between devices with their start and end apart: 10, of which 7 were waited for; matrix products, arithmetic and copies ran while one was open for 0% of the time, Pallas kernels for 4%

profile of v12, /device:TPU:0, one launch (start us, length us, event | category | flops | bytes accessed | tf_op | source)
XLA Modules:
  0.0 35.4 jit_solution(17946619600412576596)
XLA Ops:
  0.0 0.0 copy-start.5
  0.0 0.0 copy-start.2
  0.0 0.0 copy-start.4
  0.0 0.0 copy-start.3
  0.0 0.0 copy-start.1
  0.0 0.7 %copy-done.2 = bf16[4,4096]{1,0:T(4,128)(2,1)S(1)} copy-done((bf16[4,4096]{1,0:T(4,128)(2,1)S(1)}, bf16[4,4096]{1,0:T(4,128)(2,1)}, u32[]{:S(2)}) %copy-start.2) | copy-done | bytes 32792
  0.8 0.0 copy-start
  0.8 4.4 %collective-permute-start.3 = (bf16[4,4096]{1,0:T(4,128)(2,1)S(1)}, bf16[4,4096]{1,0:T(4,128)(2,1)S(1)}, u32[]{:S(2)}, u32[]{:S(2)}) collective-permute-start(bf16[4,4096]{1,0:T(4,128)(2,1)S(1)} %copy-done.2), channel_id=1, source_target_pairs={{1,14},{3,12},{5,10},{7,8},{9,6},{11,4},{13,2},{15,0},{0,11},{2,9}... | collective-permute-start | bytes 98312 | tf_op jit(solution)/shard_map/ppermute | solution.py:237
  5.2 0.7 %collective-permute-start.2 = (bf16[4,4096]{1,0:T(4,128)(2,1)S(1)}, bf16[4,4096]{1,0:T(4,128)(2,1)S(1)}, u32[]{:S(2)}, u32[]{:S(2)}) collective-permute-start(bf16[4,4096]{1,0:T(4,128)(2,1)S(1)} %copy-done.2), channel_id=1, source_target_pairs={{1,12},{3,14},{5,8},{7,10},{9,4},{11,6},{13,0},{15,2},{0,9},{2,11}... | collective-permute-start | bytes 98312 | tf_op jit(solution)/shard_map/ppermute | solution.py:237
  5.9 0.1 collective-permute-start.1
  6.0 0.8 %collective-permute-start = (bf16[4,4096]{1,0:T(4,128)(2,1)S(1)}, bf16[4,4096]{1,0:T(4,128)(2,1)S(1)}, u32[]{:S(2)}, u32[]{:S(2)}) collective-permute-start(bf16[4,4096]{1,0:T(4,128)(2,1)S(1)} %copy-done.2), channel_id=1, source_target_pairs={{1,5},{3,7},{5,1},{7,3},{9,13},{11,15},{13,9},{15,11},{17,21},{19,... | collective-permute-start | bytes 98312 | tf_op jit(solution)/shard_map/ppermute | solution.py:245
  6.8 1.1 %collective-permute-done.3.refs_3_ = bf16[4,4096]{1,0:T(4,128)(2,1)S(1)} collective-permute-done((bf16[4,4096]{1,0:T(4,128)(2,1)S(1)}, bf16[4,4096]{1,0:T(4,128)(2,1)S(1)}, u32[]{:S(2)}, u32[]{:S(2)}) %collective-permute-start.3) | collective-permute-done | bytes 32800 | tf_op jit(solution)/shard_map/ppermute | solution.py:237
  7.9 2.8 %collective-permute-done.2.refs_2_ = bf16[4,4096]{1,0:T(4,128)(2,1)S(1)} collective-permute-done((bf16[4,4096]{1,0:T(4,128)(2,1)S(1)}, bf16[4,4096]{1,0:T(4,128)(2,1)S(1)}, u32[]{:S(2)}, u32[]{:S(2)}) %collective-permute-start.2) | collective-permute-done | bytes 32800 | tf_op jit(solution)/shard_map/ppermute | solution.py:237
  10.7 0.0 collective-permute-done.1.refs_1_
  10.7 0.0 collective-permute-done.refs_0_
  10.7 1.3 %collective-permute-start.4 = (bf16[4,4,4096]{2,1,0:T(4,128)(2,1)S(1)}, bf16[4,4,4096]{2,1,0:T(4,128)(2,1)S(1)}, u32[]{:S(2)}, u32[]{:S(2)}) collective-permute-start(bf16[4,4,4096]{2,1,0:T(4,128)(2,1)S(1)} %shard_map.74.mine_ref), channel_id=1, source_target_pairs={{0,1},{1,0},{2,3},{3,2},{4,5},{5,4},{6,7},{7,6},{8,9},{9,8},{10,11... | collective-permute-start | bytes 393224 | tf_op jit(solution)/shard_map/ppermute | solution.py:249
  12.0 1.0 %collective-permute-done.4.got_ref = bf16[4,4,4096]{2,1,0:T(4,128)(2,1)S(1)} collective-permute-done((bf16[4,4,4096]{2,1,0:T(4,128)(2,1)S(1)}, bf16[4,4,4096]{2,1,0:T(4,128)(2,1)S(1)}, u32[]{:S(2)}, u32[]{:S(2)}) %collective-permute-start.4) | collective-permute-done | bytes 131104 | tf_op jit(solution)/shard_map/ppermute | solution.py:249
  13.0 0.0 copy-done.5
  13.0 0.0 copy-done.4
  13.0 0.0 copy-done.3
  13.0 0.0 copy-done.1
  13.0 0.0 slice-start
  13.0 0.0 slice-start.1
  13.0 0.0 slice-start.2
  13.0 3.1 %shard_map.75 = (bf16[32,4096]{1,0:T(8,128)(2,1)S(1)}, f32[32,2048]{1,0:T(8,128)S(1)}, f32[32,128]{1,0:T(8,128)S(1)}) custom-call(s32[2]{0:T(128)S(4)} %shard_map.73.place_ref, s32[1,4]{1,0:T(1,128)S(1)} %bitcast.3, bf16[4,4096]{1,0:T(4,128)(2,1)S(1)} %copy-done.2, bf16[4,4,4096]{2,1,0:T(4,128)(2,1)S(1)} %shard_map.74.mine_ref, ...), custom_call_target="tpu_custom_call" | custom-call | flops 5000000000 | tf_op jit(solution)/shard_map/pallas_call | solution.py:119
  16.2 0.0 copy-done
  16.2 0.0 slice-start.3
  16.2 3.0 %shard_map.76.h_ref = bf16[32,2048]{1,0:T(8,128)(2,1)S(1)} custom-call(bf16[32,4096]{1,0:T(8,128)(2,1)S(1)} %get-tuple-element.21.x_ref, f32[32,2048]{1,0:T(8,128)S(1)} %get-tuple-element.22.act_ref, bf16[4096,2048]{1,0:T(8,128)(2,1)S(1)} %copy-done), custom_call_target="tpu_custom_call" | custom-call | flops 2000000000 | tf_op jit(solution)/shard_map/pallas_call | solution.py:142
  19.2 0.0 slice-done
  19.2 0.0 slice-done.1
  19.2 0.0 slice-done.2
  19.2 0.0 slice-done.3
  19.2 1.6 %shard_map.78 = bf16[32,2048]{1,0:T(8,128)(2,1)S(1)} custom-call(s32[2]{0:T(128)S(4)} %shard_map.73.place_ref, bf16[32,2048]{1,0:T(8,128)(2,1)S(1)} %shard_map.76.h_ref, bf16[2048,4096]{1,0:T(8,128)(2,1)S(1)} %bitcast.2), custom_call_target="tpu_custom_call" | custom-call | flops 268435456 | tf_op jit(solution)/shard_map/pallas_call | solution.py:165
  20.8 0.4 %collective-permute-start.5 = (bf16[32,2048]{1,0:T(8,128)(2,1)S(1)}, bf16[32,2048]{1,0:T(8,128)(2,1)S(1)}, u32[]{:S(2)}, u32[]{:S(2)}) collective-permute-start(bf16[32,2048]{1,0:T(8,128)(2,1)S(1)} %shard_map.78), channel_id=1, source_target_pairs={{0,1},{1,0},{2,3},{3,2},{4,5},{5,4},{6,7},{7,6},{8,9},{9,8},{10,11... | collective-permute-start | bytes 393224 | tf_op jit(solution)/shard_map/ppermute | solution.py:249
  21.2 1.6 %shard_map.77.keep_ref = f32[32,2048]{1,0:T(8,128)S(1)} custom-call(s32[2]{0:T(128)S(4)} %shard_map.73.place_ref, bf16[32,2048]{1,0:T(8,128)(2,1)S(1)} %shard_map.76.h_ref, bf16[2048,4096]{1,0:T(8,128)(2,1)S(1)} %bitcast.2), custom_call_target="tpu_custom_call" | custom-call | flops 268435456 | tf_op jit(solution)/shard_map/pallas_call | solution.py:165
  22.8 0.0 collective-permute-done.5.got_ref
  22.8 0.1 shard_map.79
  22.9 2.0 %collective-permute-start.6 = (bf16[2,4,2048]{2,1,0:T(4,128)(2,1)S(1)}, bf16[2,4,2048]{2,1,0:T(4,128)(2,1)S(1)}, u32[]{:S(2)}, u32[]{:S(2)}) collective-permute-start(bf16[2,4,2048]{2,1,0:T(4,128)(2,1)S(1)} %get-tuple-element.24), channel_id=1, source_target_pairs={{0,6},{2,4},{4,2},{6,0},{8,14},{10,12},{12,10},{14,8},{1,7},{3,5},... | collective-permute-start | bytes 98312 | tf_op jit(solution)/shard_map/ppermute | solution.py:233
  24.9 0.7 %collective-permute-start.7 = (bf16[2,4,2048]{2,1,0:T(4,128)(2,1)S(1)}, bf16[2,4,2048]{2,1,0:T(4,128)(2,1)S(1)}, u32[]{:S(2)}, u32[]{:S(2)}) collective-permute-start(bf16[2,4,2048]{2,1,0:T(4,128)(2,1)S(1)} %get-tuple-element.25), channel_id=1, source_target_pairs={{0,4},{2,6},{4,0},{6,2},{8,12},{10,14},{12,8},{14,10},{1,5},{3,7},... | collective-permute-start | bytes 98312 | tf_op jit(solution)/shard_map/ppermute | solution.py:233
  25.6 0.8 %collective-permute-start.8 = (bf16[2,4,2048]{2,1,0:T(4,128)(2,1)S(1)}, bf16[2,4,2048]{2,1,0:T(4,128)(2,1)S(1)}, u32[]{:S(2)}, u32[]{:S(2)}) collective-permute-start(bf16[2,4,2048]{2,1,0:T(4,128)(2,1)S(1)} %get-tuple-element.26), channel_id=1, source_target_pairs={{0,2},{2,0},{4,6},{6,4},{8,10},{10,8},{12,14},{14,12},{1,3},{3,1},... | collective-permute-start | bytes 98312 | tf_op jit(solution)/shard_map/ppermute | solution.py:233
  26.4 1.3 %collective-permute-done.6.refs_1_ = bf16[2,4,2048]{2,1,0:T(4,128)(2,1)S(1)} collective-permute-done((bf16[2,4,2048]{2,1,0:T(4,128)(2,1)S(1)}, bf16[2,4,2048]{2,1,0:T(4,128)(2,1)S(1)}, u32[]{:S(2)}, u32[]{:S(2)}) %collective-permute-start.6) | collective-permute-done | bytes 32800 | tf_op jit(solution)/shard_map/ppermute | solution.py:233
  27.8 1.1 %collective-permute-done.7.refs_2_ = bf16[2,4,2048]{2,1,0:T(4,128)(2,1)S(1)} collective-permute-done((bf16[2,4,2048]{2,1,0:T(4,128)(2,1)S(1)}, bf16[2,4,2048]{2,1,0:T(4,128)(2,1)S(1)}, u32[]{:S(2)}, u32[]{:S(2)}) %collective-permute-start.7) | collective-permute-done | bytes 32800 | tf_op jit(solution)/shard_map/ppermute | solution.py:233
  28.8 0.7 %collective-permute-done.8.refs_3_ = bf16[2,4,2048]{2,1,0:T(4,128)(2,1)S(1)} collective-permute-done((bf16[2,4,2048]{2,1,0:T(4,128)(2,1)S(1)}, bf16[2,4,2048]{2,1,0:T(4,128)(2,1)S(1)}, u32[]{:S(2)}, u32[]{:S(2)}) %collective-permute-start.8) | collective-permute-done | bytes 32800 | tf_op jit(solution)/shard_map/ppermute | solution.py:233
  29.5 3.6 %collective-permute-start.9 = (bf16[4,2048]{1,0:T(4,128)(2,1)S(1)}, bf16[4,2048]{1,0:T(4,128)(2,1)S(1)}, u32[]{:S(2)}, u32[]{:S(2)}) collective-permute-start(bf16[4,2048]{1,0:T(4,128)(2,1)S(1)} %get-tuple-element.28), channel_id=1, source_target_pairs={{0,8},{2,10},{4,12},{6,14},{8,0},{10,2},{12,4},{14,6},{1,9},{3,11}... | collective-permute-start | bytes 49160 | tf_op jit(solution)/shard_map/ppermute | solution.py:233
  33.1 1.7 %collective-permute-done.9.got_ref = bf16[4,2048]{1,0:T(4,128)(2,1)S(1)} collective-permute-done((bf16[4,2048]{1,0:T(4,128)(2,1)S(1)}, bf16[4,2048]{1,0:T(4,128)(2,1)S(1)}, u32[]{:S(2)}, u32[]{:S(2)}) %collective-permute-start.9) | collective-permute-done | bytes 16416 | tf_op jit(solution)/shard_map/ppermute | solution.py:233
  34.8 0.6 %shard_map.81 = bf16[4,2048]{1,0:T(4,128)(2,1)} custom-call(f32[4,2048]{1,0:T(4,128)S(1)} %get-tuple-element.27.own_ref, bf16[4,2048]{1,0:T(4,128)(2,1)S(1)} %collective-permute-done.9.got_ref), custom_call_target="tpu_custom_call" | custom-call | tf_op jit(solution)/shard_map/pallas_call | solution.py:223
  (4 shorter events, 0.0 us)
Async XLA Ops:
  0.0 13.0 %copy-start.5 = (s32[4]{0:T(128)S(1)}, s32[4]{0:T(128)}, u32[]{:S(2)}) copy-start(s32[4]{0:T(128)} %param.11) | copy-start | bytes 52
  0.0 0.8 %copy-start.2 = (bf16[4,4096]{1,0:T(4,128)(2,1)S(1)}, bf16[4,4096]{1,0:T(4,128)(2,1)}, u32[]{:S(2)}) copy-start(bf16[4,4096]{1,0:T(4,128)(2,1)} %tokens_ref) | copy-start | bytes 98308
  0.0 13.0 %copy-start.4 = (f32[4,128]{1,0:T(4,128)S(1)}, f32[4,128]{1,0:T(4,128)}, u32[]{:S(2)}) copy-start(f32[4,128]{1,0:T(4,128)} %gates_ref.1) | copy-start | bytes 6148
  0.0 13.0 %copy-start.3 = (s32[4,128]{1,0:T(4,128)S(1)}, s32[4,128]{1,0:T(4,128)}, u32[]{:S(2)}) copy-start(s32[4,128]{1,0:T(4,128)} %rows_ref.1) | copy-start | bytes 6148
  0.0 13.0 %copy-start.1 = (bf16[4096,2048]{1,0:T(8,128)(2,1)S(1)}, bf16[4096,2048]{1,0:T(8,128)(2,1)}, u32[]{:S(2)}) copy-start(bf16[4096,2048]{1,0:T(8,128)(2,1)} %wg_ref.1) | copy-start | bytes 50331652
  0.8 15.4 %copy-start = (bf16[4096,2048]{1,0:T(8,128)(2,1)S(1)}, bf16[4096,2048]{1,0:T(8,128)(2,1)}, u32[]{:S(2)}) copy-start(bf16[4096,2048]{1,0:T(8,128)(2,1)} %wu_ref.1) | copy-start | bytes 50331652
  0.8 7.1 %collective-permute-start.3 = (bf16[4,4096]{1,0:T(4,128)(2,1)S(1)}, bf16[4,4096]{1,0:T(4,128)(2,1)S(1)}, u32[]{:S(2)}, u32[]{:S(2)}) collective-permute-start(bf16[4,4096]{1,0:T(4,128)(2,1)S(1)} %copy-done.2), channel_id=1, source_target_pairs={{1,14},{3,12},{5,10},{7,8},{9,6},{11,4},{13,2},{15,0},{0,11},{2,9}... | collective-permute-start | bytes 98312 | tf_op jit(solution)/shard_map/ppermute | solution.py:237
  5.2 5.5 %collective-permute-start.2 = (bf16[4,4096]{1,0:T(4,128)(2,1)S(1)}, bf16[4,4096]{1,0:T(4,128)(2,1)S(1)}, u32[]{:S(2)}, u32[]{:S(2)}) collective-permute-start(bf16[4,4096]{1,0:T(4,128)(2,1)S(1)} %copy-done.2), channel_id=1, source_target_pairs={{1,12},{3,14},{5,8},{7,10},{9,4},{11,6},{13,0},{15,2},{0,9},{2,11}... | collective-permute-start | bytes 98312 | tf_op jit(solution)/shard_map/ppermute | solution.py:237
  5.9 4.8 %collective-permute-start.1 = (bf16[4,4096]{1,0:T(4,128)(2,1)S(1)}, bf16[4,4096]{1,0:T(4,128)(2,1)S(1)}, u32[]{:S(2)}, u32[]{:S(2)}) collective-permute-start(bf16[4,4096]{1,0:T(4,128)(2,1)S(1)} %copy-done.2), channel_id=1, source_target_pairs={{1,2},{3,0},{5,6},{7,4},{9,10},{11,8},{13,14},{15,12},{0,7},{2,5},... | collective-permute-start | bytes 98312 | tf_op jit(solution)/shard_map/ppermute | solution.py:237
  6.0 4.7 %collective-permute-start = (bf16[4,4096]{1,0:T(4,128)(2,1)S(1)}, bf16[4,4096]{1,0:T(4,128)(2,1)S(1)}, u32[]{:S(2)}, u32[]{:S(2)}) collective-permute-start(bf16[4,4096]{1,0:T(4,128)(2,1)S(1)} %copy-done.2), channel_id=1, source_target_pairs={{1,5},{3,7},{5,1},{7,3},{9,13},{11,15},{13,9},{15,11},{17,21},{19,... | collective-permute-start | bytes 98312 | tf_op jit(solution)/shard_map/ppermute | solution.py:245
  10.7 2.3 %collective-permute-start.4 = (bf16[4,4,4096]{2,1,0:T(4,128)(2,1)S(1)}, bf16[4,4,4096]{2,1,0:T(4,128)(2,1)S(1)}, u32[]{:S(2)}, u32[]{:S(2)}) collective-permute-start(bf16[4,4,4096]{2,1,0:T(4,128)(2,1)S(1)} %shard_map.74.mine_ref), channel_id=1, source_target_pairs={{0,1},{1,0},{2,3},{3,2},{4,5},{5,4},{6,7},{7,6},{8,9},{9,8},{10,11... | collective-permute-start | bytes 393224 | tf_op jit(solution)/shard_map/ppermute | solution.py:249
  13.0 6.2 %slice-start = ((s8[16777216]{0:T(1024)(128)(4,1)}), s8[4194304]{0:T(1024)(128)(4,1)S(1)}, s32[]{:S(2)}) async-start(s8[16777216]{0:T(1024)(128)(4,1)} %bitcast.1), calls=%async_computation | async-start | bytes 8388608
  13.0 6.2 %slice-start.1 = ((s8[16777216]{0:T(1024)(128)(4,1)}), s8[4194304]{0:T(1024)(128)(4,1)S(1)}, s32[]{:S(2)}) async-start(s8[16777216]{0:T(1024)(128)(4,1)} %bitcast.1), calls=%async_computation.1 | async-start | bytes 8388608
  13.0 6.2 %slice-start.2 = ((s8[16777216]{0:T(1024)(128)(4,1)}), s8[4194304]{0:T(1024)(128)(4,1)S(1)}, s32[]{:S(2)}) async-start(s8[16777216]{0:T(1024)(128)(4,1)} %bitcast.1), calls=%async_computation.2 | async-start | bytes 8388608
  16.2 3.1 %slice-start.3 = ((s8[16777216]{0:T(1024)(128)(4,1)}), s8[4194304]{0:T(1024)(128)(4,1)S(1)}, s32[]{:S(2)}) async-start(s8[16777216]{0:T(1024)(128)(4,1)} %bitcast.1), calls=%async_computation.3 | async-start | bytes 8388608
  20.8 2.0 %collective-permute-start.5 = (bf16[32,2048]{1,0:T(8,128)(2,1)S(1)}, bf16[32,2048]{1,0:T(8,128)(2,1)S(1)}, u32[]{:S(2)}, u32[]{:S(2)}) collective-permute-start(bf16[32,2048]{1,0:T(8,128)(2,1)S(1)} %shard_map.78), channel_id=1, source_target_pairs={{0,1},{1,0},{2,3},{3,2},{4,5},{5,4},{6,7},{7,6},{8,9},{9,8},{10,11... | collective-permute-start | bytes 393224 | tf_op jit(solution)/shard_map/ppermute | solution.py:249
  22.9 4.9 %collective-permute-start.6 = (bf16[2,4,2048]{2,1,0:T(4,128)(2,1)S(1)}, bf16[2,4,2048]{2,1,0:T(4,128)(2,1)S(1)}, u32[]{:S(2)}, u32[]{:S(2)}) collective-permute-start(bf16[2,4,2048]{2,1,0:T(4,128)(2,1)S(1)} %get-tuple-element.24), channel_id=1, source_target_pairs={{0,6},{2,4},{4,2},{6,0},{8,14},{10,12},{12,10},{14,8},{1,7},{3,5},... | collective-permute-start | bytes 98312 | tf_op jit(solution)/shard_map/ppermute | solution.py:233
  24.9 3.9 %collective-permute-start.7 = (bf16[2,4,2048]{2,1,0:T(4,128)(2,1)S(1)}, bf16[2,4,2048]{2,1,0:T(4,128)(2,1)S(1)}, u32[]{:S(2)}, u32[]{:S(2)}) collective-permute-start(bf16[2,4,2048]{2,1,0:T(4,128)(2,1)S(1)} %get-tuple-element.25), channel_id=1, source_target_pairs={{0,4},{2,6},{4,0},{6,2},{8,12},{10,14},{12,8},{14,10},{1,5},{3,7},... | collective-permute-start | bytes 98312 | tf_op jit(solution)/shard_map/ppermute | solution.py:233
  25.6 3.9 %collective-permute-start.8 = (bf16[2,4,2048]{2,1,0:T(4,128)(2,1)S(1)}, bf16[2,4,2048]{2,1,0:T(4,128)(2,1)S(1)}, u32[]{:S(2)}, u32[]{:S(2)}) collective-permute-start(bf16[2,4,2048]{2,1,0:T(4,128)(2,1)S(1)} %get-tuple-element.26), channel_id=1, source_target_pairs={{0,2},{2,0},{4,6},{6,4},{8,10},{10,8},{12,14},{14,12},{1,3},{3,1},... | collective-permute-start | bytes 98312 | tf_op jit(solution)/shard_map/ppermute | solution.py:233
  29.5 5.3 %collective-permute-start.9 = (bf16[4,2048]{1,0:T(4,128)(2,1)S(1)}, bf16[4,2048]{1,0:T(4,128)(2,1)S(1)}, u32[]{:S(2)}, u32[]{:S(2)}) collective-permute-start(bf16[4,2048]{1,0:T(4,128)(2,1)S(1)} %get-tuple-element.28), channel_id=1, source_target_pairs={{0,8},{2,10},{4,12},{6,14},{8,0},{10,2},{12,4},{14,6},{1,9},{3,11}... | collective-permute-start | bytes 49160 | tf_op jit(solution)/shard_map/ppermute | solution.py:233

commit v13 on v12

--- a/solution.py
+++ b/solution.py
@@ -241,10 +241,6 @@
     )
 
 
-def fetched_by_one(x, k):
-    return lax.ppermute(x, ("exp", "hid"), [(2 * i + 1, 2 * (i ^ k) + 1) for i in range(SOURCES)])
-
-
 def swap_cores(x):
     return lax.ppermute(x, "hid", [(0, 1), (1, 0)])
 
@@ -253,7 +249,7 @@
     place = first()
     tokens, place, counts = lax.optimization_barrier((tokens, place, block_counts))
     half = SOURCES // 2
-    pieces = [fetched_by_one(tokens, ORDER[half])]
+    pieces = [fetched(tokens, ORDER[half], ORDER[half])]
     pieces += [fetched(tokens, ORDER[b], ORDER[half + b]) for b in range(1, half)]
     mine = stack(pieces)
     got = swap_cores(mine)

time: 35.6 us -> 34.2 us (0.961)
  starting transfers between devices: 14.8 us -> 13.6 us
    ppermute x3 -> x4, starting transfers between devices: 5.25 us -> 6.27 us  [fetched(): lax.ppermute(x, ('exp', 'hid'), [(2 * i + 1 - side, 2 * (i ^ k) + side) f...]
    ppermute x4, starting transfers between devices: 7.1 us -> 6.15 us  [swapped(): return lax.ppermute(x, 'exp', [(i, i ^ k) for i in range(SOURCES)])]
    ppermute x1 -> x0, starting transfers between devices: 0.78 us -> none  [fetched_by_one(): lax.ppermute(x, ('exp', 'hid'), [(2 * i + 1, 2 * (i ^ k) + 1) for i in ra...]
    ppermute x2, starting transfers between devices: 1.66 us -> 1.15 us  [swap_cores(): return lax.ppermute(x, 'hid', [(0, 1), (1, 0)])]
    ppermute x3 -> x4, waiting for transfers between devices: 3.89 us -> 3.69 us  [fetched(): lax.ppermute(x, ('exp', 'hid'), [(2 * i + 1 - side, 2 * (i ^ k) + side) f...]
  transfers between devices with their start and end apart: 10 -> 10, of which waited for: 7 -> 7; matrix products, arithmetic and copies ran while one was open for 0% -> 0% of each run, Pallas kernels for 4% -> 5%
where the time goes in v13:
time: 34.2 us; the launch traced here: 34.1 us
  starting transfers between devices  13.6 us (40%)
  Pallas kernels  10 us (29%)
  waiting for transfers between devices  9.58 us (28%)
  local copies, waits for them, and re-layouts  0.79 us (2%)
    ppermute x4, starting transfers between devices, fetched(): lax.ppermute(x, ('exp', 'hid'), [(2 * i + 1 - side, 2 * (i ^ k) + side) f...  6.27 us
    ppermute x4, starting transfers between devices, swapped(): return lax.ppermute(x, 'exp', [(i, i ^ k) for i in range(SOURCES)])  6.15 us
    ppermute x4, waiting for transfers between devices, swapped(): return lax.ppermute(x, 'exp', [(i, i ^ k) for i in range(SOURCES)])  4.9 us
    ppermute x4, waiting for transfers between devices, fetched(): lax.ppermute(x, ('exp', 'hid'), [(2 * i + 1 - side, 2 * (i ^ k) + side) f...  3.69 us
    pallas_call x1, Pallas kernels, gate_rows(): pl.pallas_call(functools.partial(gate_kernel, SOURCES // block_rows.shape...  3.12 us
    pallas_call x2, Pallas kernels, down_half(): pl.pallas_call(functools.partial(down_kernel, other), out_shape=jax.Shape...  3.12 us
    pallas_call x1, Pallas kernels, hidden_rows(): pl.pallas_call(up_kernel, out_shape=jax.ShapeDtypeStruct(act.shape, jnp.b...  3.01 us
    ppermute x2, starting transfers between devices, swap_cores(): return lax.ppermute(x, 'hid', [(0, 1), (1, 0)])  1.15 us
  transfers between devices with their start and end apart: 10, of which 7 were waited for; matrix products, arithmetic and copies ran while one was open for 0% of the time, Pallas kernels for 5%

profile of v13, /device:TPU:0, one launch (start us, length us, event | category | flops | bytes accessed | tf_op | source)
XLA Modules:
  0.0 34.1 jit_solution(11455305685925194833)
XLA Ops:
  0.0 0.0 copy-start.5
  0.0 0.0 copy-start.2
  0.0 0.0 copy-start.4
  0.0 0.0 copy-start.3
  0.0 0.0 copy-start.1
  0.0 0.7 %copy-done.2 = bf16[4,4096]{1,0:T(4,128)(2,1)S(1)} copy-done((bf16[4,4096]{1,0:T(4,128)(2,1)S(1)}, bf16[4,4096]{1,0:T(4,128)(2,1)}, u32[]{:S(2)}) %copy-start.2) | copy-done | bytes 32792
  0.8 0.0 copy-start
  0.8 4.4 %collective-permute-start.3 = (bf16[4,4096]{1,0:T(4,128)(2,1)S(1)}, bf16[4,4096]{1,0:T(4,128)(2,1)S(1)}, u32[]{:S(2)}, u32[]{:S(2)}) collective-permute-start(bf16[4,4096]{1,0:T(4,128)(2,1)S(1)} %copy-done.2), channel_id=1, source_target_pairs={{1,14},{3,12},{5,10},{7,8},{9,6},{11,4},{13,2},{15,0},{0,11},{2,9}... | collective-permute-start | bytes 98312 | tf_op jit(solution)/shard_map/ppermute | solution.py:237
  5.2 0.7 %collective-permute-start.2 = (bf16[4,4096]{1,0:T(4,128)(2,1)S(1)}, bf16[4,4096]{1,0:T(4,128)(2,1)S(1)}, u32[]{:S(2)}, u32[]{:S(2)}) collective-permute-start(bf16[4,4096]{1,0:T(4,128)(2,1)S(1)} %copy-done.2), channel_id=1, source_target_pairs={{1,12},{3,14},{5,8},{7,10},{9,4},{11,6},{13,0},{15,2},{0,9},{2,11}... | collective-permute-start | bytes 98312 | tf_op jit(solution)/shard_map/ppermute | solution.py:237
  5.9 0.1 collective-permute-start.1
  6.0 1.0 %collective-permute-start = (bf16[4,4096]{1,0:T(4,128)(2,1)S(1)}, bf16[4,4096]{1,0:T(4,128)(2,1)S(1)}, u32[]{:S(2)}, u32[]{:S(2)}) collective-permute-start(bf16[4,4096]{1,0:T(4,128)(2,1)S(1)} %copy-done.2), channel_id=1, source_target_pairs={{1,4},{3,6},{5,0},{7,2},{9,12},{11,14},{13,8},{15,10},{0,5},{2,7},... | collective-permute-start | bytes 98312 | tf_op jit(solution)/shard_map/ppermute | solution.py:237
  7.0 0.8 %collective-permute-done.3.refs_3_ = bf16[4,4096]{1,0:T(4,128)(2,1)S(1)} collective-permute-done((bf16[4,4096]{1,0:T(4,128)(2,1)S(1)}, bf16[4,4096]{1,0:T(4,128)(2,1)S(1)}, u32[]{:S(2)}, u32[]{:S(2)}) %collective-permute-start.3) | collective-permute-done | bytes 32800 | tf_op jit(solution)/shard_map/ppermute | solution.py:237
  7.9 2.8 %collective-permute-done.2.refs_2_ = bf16[4,4096]{1,0:T(4,128)(2,1)S(1)} collective-permute-done((bf16[4,4096]{1,0:T(4,128)(2,1)S(1)}, bf16[4,4096]{1,0:T(4,128)(2,1)S(1)}, u32[]{:S(2)}, u32[]{:S(2)}) %collective-permute-start.2) | collective-permute-done | bytes 32800 | tf_op jit(solution)/shard_map/ppermute | solution.py:237
  10.7 0.0 collective-permute-done.1.refs_1_
  10.7 0.0 collective-permute-done.refs_0_
  10.7 0.8 %collective-permute-start.4 = (bf16[4,4,4096]{2,1,0:T(4,128)(2,1)S(1)}, bf16[4,4,4096]{2,1,0:T(4,128)(2,1)S(1)}, u32[]{:S(2)}, u32[]{:S(2)}) collective-permute-start(bf16[4,4,4096]{2,1,0:T(4,128)(2,1)S(1)} %shard_map.74.mine_ref), channel_id=1, source_target_pairs={{0,1},{1,0},{2,3},{3,2},{4,5},{5,4},{6,7},{7,6},{8,9},{9,8},{10,11... | collective-permute-start | bytes 393224 | tf_op jit(solution)/shard_map/ppermute | solution.py:245
  11.5 1.0 %collective-permute-done.4.got_ref = bf16[4,4,4096]{2,1,0:T(4,128)(2,1)S(1)} collective-permute-done((bf16[4,4,4096]{2,1,0:T(4,128)(2,1)S(1)}, bf16[4,4,4096]{2,1,0:T(4,128)(2,1)S(1)}, u32[]{:S(2)}, u32[]{:S(2)}) %collective-permute-start.4) | collective-permute-done | bytes 131104 | tf_op jit(solution)/shard_map/ppermute | solution.py:245
  12.5 0.0 copy-done.5
  12.5 0.0 copy-done.4
  12.5 0.0 copy-done.3
  12.5 0.0 copy-done.1
  12.5 0.0 slice-start
  12.5 0.0 slice-start.1
  12.5 0.0 slice-start.2
  12.6 3.1 %shard_map.75 = (bf16[32,4096]{1,0:T(8,128)(2,1)S(1)}, f32[32,2048]{1,0:T(8,128)S(1)}, f32[32,128]{1,0:T(8,128)S(1)}) custom-call(s32[2]{0:T(128)S(4)} %shard_map.73.place_ref, s32[1,4]{1,0:T(1,128)S(1)} %bitcast.3, bf16[4,4096]{1,0:T(4,128)(2,1)S(1)} %copy-done.2, bf16[4,4,4096]{2,1,0:T(4,128)(2,1)S(1)} %shard_map.74.mine_ref, ...), custom_call_target="tpu_custom_call" | custom-call | flops 5000000000 | tf_op jit(solution)/shard_map/pallas_call | solution.py:119
  15.7 0.0 copy-done
  15.7 0.0 slice-start.3
  15.7 3.0 %shard_map.76.h_ref = bf16[32,2048]{1,0:T(8,128)(2,1)S(1)} custom-call(bf16[32,4096]{1,0:T(8,128)(2,1)S(1)} %get-tuple-element.21.x_ref, f32[32,2048]{1,0:T(8,128)S(1)} %get-tuple-element.22.act_ref, bf16[4096,2048]{1,0:T(8,128)(2,1)S(1)} %copy-done), custom_call_target="tpu_custom_call" | custom-call | flops 2000000000 | tf_op jit(solution)/shard_map/pallas_call | solution.py:142
  18.7 0.0 slice-done
  18.7 0.0 slice-done.1
  18.7 0.0 slice-done.2
  18.7 0.0 slice-done.3
  18.8 1.6 %shard_map.78 = bf16[32,2048]{1,0:T(8,128)(2,1)S(1)} custom-call(s32[2]{0:T(128)S(4)} %shard_map.73.place_ref, bf16[32,2048]{1,0:T(8,128)(2,1)S(1)} %shard_map.76.h_ref, bf16[2048,4096]{1,0:T(8,128)(2,1)S(1)} %bitcast.2), custom_call_target="tpu_custom_call" | custom-call | flops 268435456 | tf_op jit(solution)/shard_map/pallas_call | solution.py:165
  20.3 0.4 %collective-permute-start.5 = (bf16[32,2048]{1,0:T(8,128)(2,1)S(1)}, bf16[32,2048]{1,0:T(8,128)(2,1)S(1)}, u32[]{:S(2)}, u32[]{:S(2)}) collective-permute-start(bf16[32,2048]{1,0:T(8,128)(2,1)S(1)} %shard_map.78), channel_id=1, source_target_pairs={{0,1},{1,0},{2,3},{3,2},{4,5},{5,4},{6,7},{7,6},{8,9},{9,8},{10,11... | collective-permute-start | bytes 393224 | tf_op jit(solution)/shard_map/ppermute | solution.py:245
  20.7 1.6 %shard_map.77.keep_ref = f32[32,2048]{1,0:T(8,128)S(1)} custom-call(s32[2]{0:T(128)S(4)} %shard_map.73.place_ref, bf16[32,2048]{1,0:T(8,128)(2,1)S(1)} %shard_map.76.h_ref, bf16[2048,4096]{1,0:T(8,128)(2,1)S(1)} %bitcast.2), custom_call_target="tpu_custom_call" | custom-call | flops 268435456 | tf_op jit(solution)/shard_map/pallas_call | solution.py:165
  22.3 0.0 collective-permute-done.5.got_ref
  22.3 0.1 shard_map.79
  22.4 1.5 %collective-permute-start.6 = (bf16[2,4,2048]{2,1,0:T(4,128)(2,1)S(1)}, bf16[2,4,2048]{2,1,0:T(4,128)(2,1)S(1)}, u32[]{:S(2)}, u32[]{:S(2)}) collective-permute-start(bf16[2,4,2048]{2,1,0:T(4,128)(2,1)S(1)} %get-tuple-element.24), channel_id=1, source_target_pairs={{0,6},{2,4},{4,2},{6,0},{8,14},{10,12},{12,10},{14,8},{1,7},{3,5},... | collective-permute-start | bytes 98312 | tf_op jit(solution)/shard_map/ppermute | solution.py:233
  23.9 0.9 %collective-permute-start.7 = (bf16[2,4,2048]{2,1,0:T(4,128)(2,1)S(1)}, bf16[2,4,2048]{2,1,0:T(4,128)(2,1)S(1)}, u32[]{:S(2)}, u32[]{:S(2)}) collective-permute-start(bf16[2,4,2048]{2,1,0:T(4,128)(2,1)S(1)} %get-tuple-element.25), channel_id=1, source_target_pairs={{0,4},{2,6},{4,0},{6,2},{8,12},{10,14},{12,8},{14,10},{1,5},{3,7},... | collective-permute-start | bytes 98312 | tf_op jit(solution)/shard_map/ppermute | solution.py:233
  24.8 1.1 %collective-permute-start.8 = (bf16[2,4,2048]{2,1,0:T(4,128)(2,1)S(1)}, bf16[2,4,2048]{2,1,0:T(4,128)(2,1)S(1)}, u32[]{:S(2)}, u32[]{:S(2)}) collective-permute-start(bf16[2,4,2048]{2,1,0:T(4,128)(2,1)S(1)} %get-tuple-element.26), channel_id=1, source_target_pairs={{0,2},{2,0},{4,6},{6,4},{8,10},{10,8},{12,14},{14,12},{1,3},{3,1},... | collective-permute-start | bytes 98312 | tf_op jit(solution)/shard_map/ppermute | solution.py:233
  25.9 1.4 %collective-permute-done.6.refs_1_ = bf16[2,4,2048]{2,1,0:T(4,128)(2,1)S(1)} collective-permute-done((bf16[2,4,2048]{2,1,0:T(4,128)(2,1)S(1)}, bf16[2,4,2048]{2,1,0:T(4,128)(2,1)S(1)}, u32[]{:S(2)}, u32[]{:S(2)}) %collective-permute-start.6) | collective-permute-done | bytes 32800 | tf_op jit(solution)/shard_map/ppermute | solution.py:233
  27.3 0.5 %collective-permute-done.7.refs_2_ = bf16[2,4,2048]{2,1,0:T(4,128)(2,1)S(1)} collective-permute-done((bf16[2,4,2048]{2,1,0:T(4,128)(2,1)S(1)}, bf16[2,4,2048]{2,1,0:T(4,128)(2,1)S(1)}, u32[]{:S(2)}, u32[]{:S(2)}) %collective-permute-start.7) | collective-permute-done | bytes 32800 | tf_op jit(solution)/shard_map/ppermute | solution.py:233
  27.8 0.9 %collective-permute-done.8.refs_3_ = bf16[2,4,2048]{2,1,0:T(4,128)(2,1)S(1)} collective-permute-done((bf16[2,4,2048]{2,1,0:T(4,128)(2,1)S(1)}, bf16[2,4,2048]{2,1,0:T(4,128)(2,1)S(1)}, u32[]{:S(2)}, u32[]{:S(2)}) %collective-permute-start.8) | collective-permute-done | bytes 32800 | tf_op jit(solution)/shard_map/ppermute | solution.py:233
  28.8 2.6 %collective-permute-start.9 = (bf16[4,2048]{1,0:T(4,128)(2,1)S(1)}, bf16[4,2048]{1,0:T(4,128)(2,1)S(1)}, u32[]{:S(2)}, u32[]{:S(2)}) collective-permute-start(bf16[4,2048]{1,0:T(4,128)(2,1)S(1)} %get-tuple-element.28), channel_id=1, source_target_pairs={{0,8},{2,10},{4,12},{6,14},{8,0},{10,2},{12,4},{14,6},{1,9},{3,11}... | collective-permute-start | bytes 49160 | tf_op jit(solution)/shard_map/ppermute | solution.py:233
  31.4 2.1 %collective-permute-done.9.got_ref = bf16[4,2048]{1,0:T(4,128)(2,1)S(1)} collective-permute-done((bf16[4,2048]{1,0:T(4,128)(2,1)S(1)}, bf16[4,2048]{1,0:T(4,128)(2,1)S(1)}, u32[]{:S(2)}, u32[]{:S(2)}) %collective-permute-start.9) | collective-permute-done | bytes 16416 | tf_op jit(solution)/shard_map/ppermute | solution.py:233
  33.5 0.6 %shard_map.81 = bf16[4,2048]{1,0:T(4,128)(2,1)} custom-call(f32[4,2048]{1,0:T(4,128)S(1)} %get-tuple-element.27.own_ref, bf16[4,2048]{1,0:T(4,128)(2,1)S(1)} %collective-permute-done.9.got_ref), custom_call_target="tpu_custom_call" | custom-call | tf_op jit(solution)/shard_map/pallas_call | solution.py:223
  (4 shorter events, 0.0 us)
Async XLA Ops:
  0.0 12.5 %copy-start.5 = (s32[4]{0:T(128)S(1)}, s32[4]{0:T(128)}, u32[]{:S(2)}) copy-start(s32[4]{0:T(128)} %param.11) | copy-start | bytes 52
  0.0 0.8 %copy-start.2 = (bf16[4,4096]{1,0:T(4,128)(2,1)S(1)}, bf16[4,4096]{1,0:T(4,128)(2,1)}, u32[]{:S(2)}) copy-start(bf16[4,4096]{1,0:T(4,128)(2,1)} %tokens_ref) | copy-start | bytes 98308
  0.0 12.5 %copy-start.4 = (f32[4,128]{1,0:T(4,128)S(1)}, f32[4,128]{1,0:T(4,128)}, u32[]{:S(2)}) copy-start(f32[4,128]{1,0:T(4,128)} %gates_ref.1) | copy-start | bytes 6148
  0.0 12.5 %copy-start.3 = (s32[4,128]{1,0:T(4,128)S(1)}, s32[4,128]{1,0:T(4,128)}, u32[]{:S(2)}) copy-start(s32[4,128]{1,0:T(4,128)} %rows_ref.1) | copy-start | bytes 6148
  0.0 12.5 %copy-start.1 = (bf16[4096,2048]{1,0:T(8,128)(2,1)S(1)}, bf16[4096,2048]{1,0:T(8,128)(2,1)}, u32[]{:S(2)}) copy-start(bf16[4096,2048]{1,0:T(8,128)(2,1)} %wg_ref.1) | copy-start | bytes 50331652
  0.8 14.9 %copy-start = (bf16[4096,2048]{1,0:T(8,128)(2,1)S(1)}, bf16[4096,2048]{1,0:T(8,128)(2,1)}, u32[]{:S(2)}) copy-start(bf16[4096,2048]{1,0:T(8,128)(2,1)} %wu_ref.1) | copy-start | bytes 50331652
  0.8 7.1 %collective-permute-start.3 = (bf16[4,4096]{1,0:T(4,128)(2,1)S(1)}, bf16[4,4096]{1,0:T(4,128)(2,1)S(1)}, u32[]{:S(2)}, u32[]{:S(2)}) collective-permute-start(bf16[4,4096]{1,0:T(4,128)(2,1)S(1)} %copy-done.2), channel_id=1, source_target_pairs={{1,14},{3,12},{5,10},{7,8},{9,6},{11,4},{13,2},{15,0},{0,11},{2,9}... | collective-permute-start | bytes 98312 | tf_op jit(solution)/shard_map/ppermute | solution.py:237
  5.2 5.5 %collective-permute-start.2 = (bf16[4,4096]{1,0:T(4,128)(2,1)S(1)}, bf16[4,4096]{1,0:T(4,128)(2,1)S(1)}, u32[]{:S(2)}, u32[]{:S(2)}) collective-permute-start(bf16[4,4096]{1,0:T(4,128)(2,1)S(1)} %copy-done.2), channel_id=1, source_target_pairs={{1,12},{3,14},{5,8},{7,10},{9,4},{11,6},{13,0},{15,2},{0,9},{2,11}... | collective-permute-start | bytes 98312 | tf_op jit(solution)/shard_map/ppermute | solution.py:237
  5.9 4.8 %collective-permute-start.1 = (bf16[4,4096]{1,0:T(4,128)(2,1)S(1)}, bf16[4,4096]{1,0:T(4,128)(2,1)S(1)}, u32[]{:S(2)}, u32[]{:S(2)}) collective-permute-start(bf16[4,4096]{1,0:T(4,128)(2,1)S(1)} %copy-done.2), channel_id=1, source_target_pairs={{1,2},{3,0},{5,6},{7,4},{9,10},{11,8},{13,14},{15,12},{0,7},{2,5},... | collective-permute-start | bytes 98312 | tf_op jit(solution)/shard_map/ppermute | solution.py:237
  6.0 4.7 %collective-permute-start = (bf16[4,4096]{1,0:T(4,128)(2,1)S(1)}, bf16[4,4096]{1,0:T(4,128)(2,1)S(1)}, u32[]{:S(2)}, u32[]{:S(2)}) collective-permute-start(bf16[4,4096]{1,0:T(4,128)(2,1)S(1)} %copy-done.2), channel_id=1, source_target_pairs={{1,4},{3,6},{5,0},{7,2},{9,12},{11,14},{13,8},{15,10},{0,5},{2,7},... | collective-permute-start | bytes 98312 | tf_op jit(solution)/shard_map/ppermute | solution.py:237
  10.7 1.8 %collective-permute-start.4 = (bf16[4,4,4096]{2,1,0:T(4,128)(2,1)S(1)}, bf16[4,4,4096]{2,1,0:T(4,128)(2,1)S(1)}, u32[]{:S(2)}, u32[]{:S(2)}) collective-permute-start(bf16[4,4,4096]{2,1,0:T(4,128)(2,1)S(1)} %shard_map.74.mine_ref), channel_id=1, source_target_pairs={{0,1},{1,0},{2,3},{3,2},{4,5},{5,4},{6,7},{7,6},{8,9},{9,8},{10,11... | collective-permute-start | bytes 393224 | tf_op jit(solution)/shard_map/ppermute | solution.py:245
  12.5 6.2 %slice-start = ((s8[16777216]{0:T(1024)(128)(4,1)}), s8[4194304]{0:T(1024)(128)(4,1)S(1)}, s32[]{:S(2)}) async-start(s8[16777216]{0:T(1024)(128)(4,1)} %bitcast.1), calls=%async_computation | async-start | bytes 8388608
  12.5 6.2 %slice-start.1 = ((s8[16777216]{0:T(1024)(128)(4,1)}), s8[4194304]{0:T(1024)(128)(4,1)S(1)}, s32[]{:S(2)}) async-start(s8[16777216]{0:T(1024)(128)(4,1)} %bitcast.1), calls=%async_computation.1 | async-start | bytes 8388608
  12.5 6.2 %slice-start.2 = ((s8[16777216]{0:T(1024)(128)(4,1)}), s8[4194304]{0:T(1024)(128)(4,1)S(1)}, s32[]{:S(2)}) async-start(s8[16777216]{0:T(1024)(128)(4,1)} %bitcast.1), calls=%async_computation.2 | async-start | bytes 8388608
  15.7 3.1 %slice-start.3 = ((s8[16777216]{0:T(1024)(128)(4,1)}), s8[4194304]{0:T(1024)(128)(4,1)S(1)}, s32[]{:S(2)}) async-start(s8[16777216]{0:T(1024)(128)(4,1)} %bitcast.1), calls=%async_computation.3 | async-start | bytes 8388608
  20.3 1.9 %collective-permute-start.5 = (bf16[32,2048]{1,0:T(8,128)(2,1)S(1)}, bf16[32,2048]{1,0:T(8,128)(2,1)S(1)}, u32[]{:S(2)}, u32[]{:S(2)}) collective-permute-start(bf16[32,2048]{1,0:T(8,128)(2,1)S(1)} %shard_map.78), channel_id=1, source_target_pairs={{0,1},{1,0},{2,3},{3,2},{4,5},{5,4},{6,7},{7,6},{8,9},{9,8},{10,11... | collective-permute-start | bytes 393224 | tf_op jit(solution)/shard_map/ppermute | solution.py:245
  22.4 4.9 %collective-permute-start.6 = (bf16[2,4,2048]{2,1,0:T(4,128)(2,1)S(1)}, bf16[2,4,2048]{2,1,0:T(4,128)(2,1)S(1)}, u32[]{:S(2)}, u32[]{:S(2)}) collective-permute-start(bf16[2,4,2048]{2,1,0:T(4,128)(2,1)S(1)} %get-tuple-element.24), channel_id=1, source_target_pairs={{0,6},{2,4},{4,2},{6,0},{8,14},{10,12},{12,10},{14,8},{1,7},{3,5},... | collective-permute-start | bytes 98312 | tf_op jit(solution)/shard_map/ppermute | solution.py:233
  23.9 3.9 %collective-permute-start.7 = (bf16[2,4,2048]{2,1,0:T(4,128)(2,1)S(1)}, bf16[2,4,2048]{2,1,0:T(4,128)(2,1)S(1)}, u32[]{:S(2)}, u32[]{:S(2)}) collective-permute-start(bf16[2,4,2048]{2,1,0:T(4,128)(2,1)S(1)} %get-tuple-element.25), channel_id=1, source_target_pairs={{0,4},{2,6},{4,0},{6,2},{8,12},{10,14},{12,8},{14,10},{1,5},{3,7},... | collective-permute-start | bytes 98312 | tf_op jit(solution)/shard_map/ppermute | solution.py:233
  24.8 3.9 %collective-permute-start.8 = (bf16[2,4,2048]{2,1,0:T(4,128)(2,1)S(1)}, bf16[2,4,2048]{2,1,0:T(4,128)(2,1)S(1)}, u32[]{:S(2)}, u32[]{:S(2)}) collective-permute-start(bf16[2,4,2048]{2,1,0:T(4,128)(2,1)S(1)} %get-tuple-element.26), channel_id=1, source_target_pairs={{0,2},{2,0},{4,6},{6,4},{8,10},{10,8},{12,14},{14,12},{1,3},{3,1},... | collective-permute-start | bytes 98312 | tf_op jit(solution)/shard_map/ppermute | solution.py:233
  28.8 4.7 %collective-permute-start.9 = (bf16[4,2048]{1,0:T(4,128)(2,1)S(1)}, bf16[4,2048]{1,0:T(4,128)(2,1)S(1)}, u32[]{:S(2)}, u32[]{:S(2)}) collective-permute-start(bf16[4,2048]{1,0:T(4,128)(2,1)S(1)} %get-tuple-element.28), channel_id=1, source_target_pairs={{0,8},{2,10},{4,12},{6,14},{8,0},{10,2},{12,4},{14,6},{1,9},{3,11}... | collective-permute-start | bytes 49160 | tf_op jit(solution)/shard_map/ppermute | solution.py:233

commit v14 on v13

--- a/solution.py
+++ b/solution.py
@@ -33,15 +33,22 @@
     return pltpu.with_memory_space_constraint(x, pltpu.VMEM)
 
 
+def turned(i):
+    return (1 + i + i // 2) % 2
+
+
 def first_kernel(place_ref):
-    place_ref[0] = lax.axis_index("hid")
-    place_ref[1] = lax.axis_index("exp")
+    side, own = lax.axis_index("hid"), lax.axis_index("exp")
+    place_ref[0] = side
+    place_ref[1] = own
+    place_ref[2] = turned(own)
+    place_ref[3] = lax.rem(side + turned(own), 2)
 
 
 def first():
     return pl.pallas_call(
         first_kernel,
-        out_shape=pltpu.SMEM((2,), jnp.int32),
+        out_shape=pltpu.SMEM((4,), jnp.int32),
         out_specs=SMEM,
         compiler_params=pltpu.CompilerParams(vmem_limit_bytes=2 * MIB),
         cost_estimate=pl.CostEstimate(flops=AHEAD, bytes_accessed=0, transcendentals=0),
@@ -151,8 +158,8 @@
 
 def down_kernel(other, place_ref, h_ref, wd_ref, out_ref):
     half = wd_ref.shape[1] // 2
-    side = place_ref[0]
-    base = (1 - side if other else side) * half
+    mine = place_ref[3]
+    base = (1 - mine if other else mine) * half
     for n in range(half // TILE):
         cols = pl.ds(pl.multiple_of(base + n * TILE, TILE), TILE)
         part = jnp.dot(h_ref[...], wd_ref[:, cols], preferred_element_type=jnp.float32)
@@ -215,22 +222,31 @@
     )(*parts)
 
 
-def sum_kernel(own_ref, got_ref, out_ref):
-    out_ref[...] = (own_ref[...] + got_ref[...].astype(jnp.float32)).astype(out_ref.dtype)
-
-
-def final_sum(own, got):
+def sum_kernel(place_ref, own_ref, got_ref, turned_ref, out_ref):
+    own = jnp.where(place_ref[2] == 1, turned_ref[...], own_ref[...])
+    out_ref[...] = (own + got_ref[...].astype(jnp.float32)).astype(out_ref.dtype)
+
+
+def final_sum(place, own, got, other_core):
     return pl.pallas_call(
         sum_kernel,
         out_shape=jax.ShapeDtypeStruct(own.shape, jnp.bfloat16),
-        in_specs=[VMEM, VMEM],
+        in_specs=[SMEM] + [VMEM] * 3,
         out_specs=VMEM,
         compiler_params=pltpu.CompilerParams(vmem_limit_bytes=2 * MIB),
-    )(own, got)
+    )(in_smem(place), own, got, other_core)
 
 
 def swapped(x, k):
-    return lax.ppermute(x, "exp", [(i, i ^ k) for i in range(SOURCES)])
+    pairs = [
+        (2 * i + side, 2 * (i ^ k) + (side + turned(i) + turned(i ^ k)) % 2) for i in range(SOURCES) for side in range(2)
+    ]
+    return lax.ppermute(x, ("exp", "hid"), pairs)
+
+
+def sent_home(x, k):
+    pairs = [(2 * i + side, 2 * (i ^ k) + (side + turned(i)) % 2) for i in range(SOURCES) for side in range(2)]
+    return lax.ppermute(x, ("exp", "hid"), pairs)
 
 
 def fetched(x, first, second):
@@ -260,7 +276,7 @@
     own, *parts = near(g, keep, swap_cores(send))
     returned = [swapped(parts[j - 1], j) for j in range(half - 1, 0, -1)]
     own, other = far([own, *returned])
-    return final_sum(own, swapped(other, half))
+    return final_sum(place, own, sent_home(other, half), swap_cores(own))
 
 
 def expert_block(segment, w_gate, w_up, w_down):

time: 34.2 us -> 33.2 us (0.971)
  waiting for transfers between devices: 9.58 us -> 8.66 us
    ppermute x4, waiting for transfers between devices: 4.9 us -> 3.98 us  [the longest x3 2.14 us: swapped(): return lax.ppermute(x, ('exp', 'hid'), pairs)]
    ppermute x4, starting transfers between devices: 6.15 us -> 5.49 us  [the longest x3 3.27 us: swapped(): return lax.ppermute(x, ('exp', 'hid'), pairs)]
    ppermute x2 -> x3, starting transfers between devices: 1.15 us -> 1.7 us  [swap_cores(): return lax.ppermute(x, 'hid', [(0, 1), (1, 0)])]
    ppermute x2 -> x3, waiting for transfers between devices: 0.99 us -> 0.99 us  [swap_cores(): return lax.ppermute(x, 'hid', [(0, 1), (1, 0)])]
  transfers between devices with their start and end apart: 10 -> 11, of which waited for: 7 -> 6; matrix products, arithmetic and copies ran while one was open for 0% -> 0% of each run, Pallas kernels for 5% -> 5%
where the time goes in v14:
time: 33.2 us; the launch traced here: 33.1 us
  starting transfers between devices  13.5 us (41%)
  Pallas kernels  10 us (30%)
  waiting for transfers between devices  8.66 us (26%)
  local copies, waits for them, and re-layouts  0.77 us (2%)
    ppermute x4, starting transfers between devices, fetched(): lax.ppermute(x, ('exp', 'hid'), [(2 * i + 1 - side, 2 * (i ^ k) + side) f...  6.27 us
    ppermute x4, waiting for transfers between devices, fetched(): lax.ppermute(x, ('exp', 'hid'), [(2 * i + 1 - side, 2 * (i ^ k) + side) f...  3.69 us
    ppermute x3, starting transfers between devices, swapped(): return lax.ppermute(x, ('exp', 'hid'), pairs)  3.27 us
    pallas_call x1, Pallas kernels, gate_rows(): pl.pallas_call(functools.partial(gate_kernel, SOURCES // block_rows.shape...  3.12 us
    pallas_call x2, Pallas kernels, down_half(): pl.pallas_call(functools.partial(down_kernel, other), out_shape=jax.Shape...  3.12 us
    pallas_call x1, Pallas kernels, hidden_rows(): pl.pallas_call(up_kernel, out_shape=jax.ShapeDtypeStruct(act.shape, jnp.b...  3.01 us
    ppermute x1, starting transfers between devices, sent_home(): return lax.ppermute(x, ('exp', 'hid'), pairs)  2.22 us
    ppermute x3, waiting for transfers between devices, swapped(): return lax.ppermute(x, ('exp', 'hid'), pairs)  2.14 us
  transfers between devices with their start and end apart: 11, of which 6 were waited for; matrix products, arithmetic and copies ran while one was open for 0% of the time, Pallas kernels for 5%

profile of v14, /device:TPU:0, one launch (start us, length us, event | category | flops | bytes accessed | tf_op | source)
XLA Modules:
  0.0 33.1 jit_solution(16518275841150063100)
XLA Ops:
  0.0 0.0 copy-start.5
  0.0 0.0 copy-start.2
  0.0 0.0 copy-start.4
  0.0 0.0 copy-start.3
  0.0 0.0 copy-start.1
  0.0 0.7 %copy-done.2 = bf16[4,4096]{1,0:T(4,128)(2,1)S(1)} copy-done((bf16[4,4096]{1,0:T(4,128)(2,1)S(1)}, bf16[4,4096]{1,0:T(4,128)(2,1)}, u32[]{:S(2)}) %copy-start.2) | copy-done | bytes 32792
  0.8 0.0 copy-start
  0.8 4.4 %collective-permute-start.3 = (bf16[4,4096]{1,0:T(4,128)(2,1)S(1)}, bf16[4,4096]{1,0:T(4,128)(2,1)S(1)}, u32[]{:S(2)}, u32[]{:S(2)}) collective-permute-start(bf16[4,4096]{1,0:T(4,128)(2,1)S(1)} %copy-done.2), channel_id=1, source_target_pairs={{1,14},{3,12},{5,10},{7,8},{9,6},{11,4},{13,2},{15,0},{0,11},{2,9}... | collective-permute-start | bytes 98312 | tf_op jit(solution)/shard_map/ppermute | solution.py:253
  5.2 0.7 %collective-permute-start.2 = (bf16[4,4096]{1,0:T(4,128)(2,1)S(1)}, bf16[4,4096]{1,0:T(4,128)(2,1)S(1)}, u32[]{:S(2)}, u32[]{:S(2)}) collective-permute-start(bf16[4,4096]{1,0:T(4,128)(2,1)S(1)} %copy-done.2), channel_id=1, source_target_pairs={{1,12},{3,14},{5,8},{7,10},{9,4},{11,6},{13,0},{15,2},{0,9},{2,11}... | collective-permute-start | bytes 98312 | tf_op jit(solution)/shard_map/ppermute | solution.py:253
  5.9 0.1 collective-permute-start.1
  6.0 1.0 %collective-permute-start = (bf16[4,4096]{1,0:T(4,128)(2,1)S(1)}, bf16[4,4096]{1,0:T(4,128)(2,1)S(1)}, u32[]{:S(2)}, u32[]{:S(2)}) collective-permute-start(bf16[4,4096]{1,0:T(4,128)(2,1)S(1)} %copy-done.2), channel_id=1, source_target_pairs={{1,4},{3,6},{5,0},{7,2},{9,12},{11,14},{13,8},{15,10},{0,5},{2,7},... | collective-permute-start | bytes 98312 | tf_op jit(solution)/shard_map/ppermute | solution.py:253
  7.0 0.8 %collective-permute-done.3.refs_3_ = bf16[4,4096]{1,0:T(4,128)(2,1)S(1)} collective-permute-done((bf16[4,4096]{1,0:T(4,128)(2,1)S(1)}, bf16[4,4096]{1,0:T(4,128)(2,1)S(1)}, u32[]{:S(2)}, u32[]{:S(2)}) %collective-permute-start.3) | collective-permute-done | bytes 32800 | tf_op jit(solution)/shard_map/ppermute | solution.py:253
  7.9 2.8 %collective-permute-done.2.refs_2_ = bf16[4,4096]{1,0:T(4,128)(2,1)S(1)} collective-permute-done((bf16[4,4096]{1,0:T(4,128)(2,1)S(1)}, bf16[4,4096]{1,0:T(4,128)(2,1)S(1)}, u32[]{:S(2)}, u32[]{:S(2)}) %collective-permute-start.2) | collective-permute-done | bytes 32800 | tf_op jit(solution)/shard_map/ppermute | solution.py:253
  10.7 0.0 collective-permute-done.1.refs_1_
  10.7 0.0 collective-permute-done.refs_0_
  10.7 0.8 %collective-permute-start.4 = (bf16[4,4,4096]{2,1,0:T(4,128)(2,1)S(1)}, bf16[4,4,4096]{2,1,0:T(4,128)(2,1)S(1)}, u32[]{:S(2)}, u32[]{:S(2)}) collective-permute-start(bf16[4,4,4096]{2,1,0:T(4,128)(2,1)S(1)} %shard_map.74.mine_ref), channel_id=1, source_target_pairs={{0,1},{1,0},{2,3},{3,2},{4,5},{5,4},{6,7},{7,6},{8,9},{9,8},{10,11... | collective-permute-start | bytes 393224 | tf_op jit(solution)/shard_map/ppermute | solution.py:261
  11.5 1.0 %collective-permute-done.4.got_ref = bf16[4,4,4096]{2,1,0:T(4,128)(2,1)S(1)} collective-permute-done((bf16[4,4,4096]{2,1,0:T(4,128)(2,1)S(1)}, bf16[4,4,4096]{2,1,0:T(4,128)(2,1)S(1)}, u32[]{:S(2)}, u32[]{:S(2)}) %collective-permute-start.4) | collective-permute-done | bytes 131104 | tf_op jit(solution)/shard_map/ppermute | solution.py:261
  12.5 0.0 copy-done.5
  12.5 0.0 copy-done.4
  12.5 0.0 copy-done.3
  12.5 0.0 copy-done.1
  12.5 0.0 slice-start
  12.5 0.0 slice-start.1
  12.5 0.0 slice-start.2
  12.6 3.1 %shard_map.75 = (bf16[32,4096]{1,0:T(8,128)(2,1)S(1)}, f32[32,2048]{1,0:T(8,128)S(1)}, f32[32,128]{1,0:T(8,128)S(1)}) custom-call(s32[4]{0:T(128)S(4)} %shard_map.73.place_ref, s32[1,4]{1,0:T(1,128)S(1)} %bitcast.3, bf16[4,4096]{1,0:T(4,128)(2,1)S(1)} %copy-done.2, bf16[4,4,4096]{2,1,0:T(4,128)(2,1)S(1)} %shard_map.74.mine_ref, ...), custom_call_target="tpu_custom_call" | custom-call | flops 5000000000 | tf_op jit(solution)/shard_map/pallas_call | solution.py:126
  15.7 0.0 copy-done
  15.7 0.0 slice-start.3
  15.7 3.0 %shard_map.76.h_ref = bf16[32,2048]{1,0:T(8,128)(2,1)S(1)} custom-call(bf16[32,4096]{1,0:T(8,128)(2,1)S(1)} %get-tuple-element.21.x_ref, f32[32,2048]{1,0:T(8,128)S(1)} %get-tuple-element.22.act_ref, bf16[4096,2048]{1,0:T(8,128)(2,1)S(1)} %copy-done), custom_call_target="tpu_custom_call" | custom-call | flops 2000000000 | tf_op jit(solution)/shard_map/pallas_call | solution.py:149
  18.7 0.0 slice-done
  18.7 0.0 slice-done.1
  18.7 0.0 slice-done.2
  18.7 0.0 slice-done.3
  18.8 1.6 %shard_map.78 = bf16[32,2048]{1,0:T(8,128)(2,1)S(1)} custom-call(s32[4]{0:T(128)S(4)} %shard_map.73.place_ref, bf16[32,2048]{1,0:T(8,128)(2,1)S(1)} %shard_map.76.h_ref, bf16[2048,4096]{1,0:T(8,128)(2,1)S(1)} %bitcast.2), custom_call_target="tpu_custom_call" | custom-call | flops 268435456 | tf_op jit(solution)/shard_map/pallas_call | solution.py:172
  20.3 0.4 %collective-permute-start.5 = (bf16[32,2048]{1,0:T(8,128)(2,1)S(1)}, bf16[32,2048]{1,0:T(8,128)(2,1)S(1)}, u32[]{:S(2)}, u32[]{:S(2)}) collective-permute-start(bf16[32,2048]{1,0:T(8,128)(2,1)S(1)} %shard_map.78), channel_id=1, source_target_pairs={{0,1},{1,0},{2,3},{3,2},{4,5},{5,4},{6,7},{7,6},{8,9},{9,8},{10,11... | collective-permute-start | bytes 393224 | tf_op jit(solution)/shard_map/ppermute | solution.py:261
  20.7 1.6 %shard_map.77.keep_ref = f32[32,2048]{1,0:T(8,128)S(1)} custom-call(s32[4]{0:T(128)S(4)} %shard_map.73.place_ref, bf16[32,2048]{1,0:T(8,128)(2,1)S(1)} %shard_map.76.h_ref, bf16[2048,4096]{1,0:T(8,128)(2,1)S(1)} %bitcast.2), custom_call_target="tpu_custom_call" | custom-call | flops 268435456 | tf_op jit(solution)/shard_map/pallas_call | solution.py:172
  22.3 0.0 collective-permute-done.5.got_ref
  22.3 0.1 shard_map.79
  22.4 1.5 %collective-permute-start.6 = (bf16[2,4,2048]{2,1,0:T(4,128)(2,1)S(1)}, bf16[2,4,2048]{2,1,0:T(4,128)(2,1)S(1)}, u32[]{:S(2)}, u32[]{:S(2)}) collective-permute-start(bf16[2,4,2048]{2,1,0:T(4,128)(2,1)S(1)} %get-tuple-element.24), channel_id=1, source_target_pairs={{0,6},{1,7},{2,4},{3,5},{4,2},{5,3},{6,0},{7,1},{8,14},{9,15},{10,... | collective-permute-start | bytes 98312 | tf_op jit(solution)/shard_map/ppermute | solution.py:244
  23.9 0.4 %collective-permute-start.7 = (bf16[2,4,2048]{2,1,0:T(4,128)(2,1)S(1)}, bf16[2,4,2048]{2,1,0:T(4,128)(2,1)S(1)}, u32[]{:S(2)}, u32[]{:S(2)}) collective-permute-start(bf16[2,4,2048]{2,1,0:T(4,128)(2,1)S(1)} %get-tuple-element.25), channel_id=1, source_target_pairs={{0,5},{1,4},{2,7},{3,6},{4,1},{5,0},{6,3},{7,2},{8,13},{9,12},{10,... | collective-permute-start | bytes 98312 | tf_op jit(solution)/shard_map/ppermute | solution.py:244
  24.3 1.4 %collective-permute-start.8 = (bf16[2,4,2048]{2,1,0:T(4,128)(2,1)S(1)}, bf16[2,4,2048]{2,1,0:T(4,128)(2,1)S(1)}, u32[]{:S(2)}, u32[]{:S(2)}) collective-permute-start(bf16[2,4,2048]{2,1,0:T(4,128)(2,1)S(1)} %get-tuple-element.26), channel_id=1, source_target_pairs={{0,3},{1,2},{2,1},{3,0},{4,7},{5,6},{6,5},{7,4},{8,11},{9,10},{10,... | collective-permute-start | bytes 98312 | tf_op jit(solution)/shard_map/ppermute | solution.py:244
  25.7 1.9 %collective-permute-done.6.refs_1_ = bf16[2,4,2048]{2,1,0:T(4,128)(2,1)S(1)} collective-permute-done((bf16[2,4,2048]{2,1,0:T(4,128)(2,1)S(1)}, bf16[2,4,2048]{2,1,0:T(4,128)(2,1)S(1)}, u32[]{:S(2)}, u32[]{:S(2)}) %collective-permute-start.6) | collective-permute-done | bytes 32800 | tf_op jit(solution)/shard_map/ppermute | solution.py:244
  27.6 0.0 collective-permute-done.7.refs_2_
  27.6 0.2 collective-permute-done.8.refs_3_
  27.8 0.5 %collective-permute-start.10 = (f32[4,2048]{1,0:T(4,128)S(1)}, f32[4,2048]{1,0:T(4,128)S(1)}, u32[]{:S(2)}, u32[]{:S(2)}) collective-permute-start(f32[4,2048]{1,0:T(4,128)S(1)} %get-tuple-element.27.own_ref), channel_id=1, source_target_pairs={{0,1},{1,0},{2,3},{3,2},{4,5},{5,4},{6,7},{7,6},{8,9},{9,8},{10,11... | collective-permute-start | bytes 98312 | tf_op jit(solution)/shard_map/ppermute | solution.py:261
  28.4 2.2 %collective-permute-start.9 = (bf16[4,2048]{1,0:T(4,128)(2,1)S(1)}, bf16[4,2048]{1,0:T(4,128)(2,1)S(1)}, u32[]{:S(2)}, u32[]{:S(2)}) collective-permute-start(bf16[4,2048]{1,0:T(4,128)(2,1)S(1)} %get-tuple-element.28), channel_id=1, source_target_pairs={{0,9},{1,8},{2,10},{3,11},{4,12},{5,13},{6,15},{7,14},{8,1},{9,0},... | collective-permute-start | bytes 49160 | tf_op jit(solution)/shard_map/ppermute | solution.py:249
  30.6 1.8 %collective-permute-done.9.got_ref = bf16[4,2048]{1,0:T(4,128)(2,1)S(1)} collective-permute-done((bf16[4,2048]{1,0:T(4,128)(2,1)S(1)}, bf16[4,2048]{1,0:T(4,128)(2,1)S(1)}, u32[]{:S(2)}, u32[]{:S(2)}) %collective-permute-start.9) | collective-permute-done | bytes 16416 | tf_op jit(solution)/shard_map/ppermute | solution.py:249
  32.4 0.0 collective-permute-done.10.turned_ref
  32.4 0.6 %shard_map.81 = bf16[4,2048]{1,0:T(4,128)(2,1)} custom-call(s32[4]{0:T(128)S(4)} %shard_map.73.place_ref, f32[4,2048]{1,0:T(4,128)S(1)} %get-tuple-element.27.own_ref, bf16[4,2048]{1,0:T(4,128)(2,1)S(1)} %collective-permute-done.9.got_ref, f32[4,2048]{1,0:T(4,128)S(1)} %collective-permute-done.10.turned_ref), custom_call_target="tpu_custom_call" | custom-call | tf_op jit(solution)/shard_map/pallas_call | solution.py:231
  (4 shorter events, 0.1 us)
Async XLA Ops:
  0.0 12.5 %copy-start.5 = (s32[4]{0:T(128)S(1)}, s32[4]{0:T(128)}, u32[]{:S(2)}) copy-start(s32[4]{0:T(128)} %param.11) | copy-start | bytes 52
  0.0 0.8 %copy-start.2 = (bf16[4,4096]{1,0:T(4,128)(2,1)S(1)}, bf16[4,4096]{1,0:T(4,128)(2,1)}, u32[]{:S(2)}) copy-start(bf16[4,4096]{1,0:T(4,128)(2,1)} %tokens_ref) | copy-start | bytes 98308
  0.0 12.5 %copy-start.4 = (f32[4,128]{1,0:T(4,128)S(1)}, f32[4,128]{1,0:T(4,128)}, u32[]{:S(2)}) copy-start(f32[4,128]{1,0:T(4,128)} %gates_ref.1) | copy-start | bytes 6148
  0.0 12.5 %copy-start.3 = (s32[4,128]{1,0:T(4,128)S(1)}, s32[4,128]{1,0:T(4,128)}, u32[]{:S(2)}) copy-start(s32[4,128]{1,0:T(4,128)} %rows_ref.1) | copy-start | bytes 6148
  0.0 12.5 %copy-start.1 = (bf16[4096,2048]{1,0:T(8,128)(2,1)S(1)}, bf16[4096,2048]{1,0:T(8,128)(2,1)}, u32[]{:S(2)}) copy-start(bf16[4096,2048]{1,0:T(8,128)(2,1)} %wg_ref.1) | copy-start | bytes 50331652
  0.8 14.9 %copy-start = (bf16[4096,2048]{1,0:T(8,128)(2,1)S(1)}, bf16[4096,2048]{1,0:T(8,128)(2,1)}, u32[]{:S(2)}) copy-start(bf16[4096,2048]{1,0:T(8,128)(2,1)} %wu_ref.1) | copy-start | bytes 50331652
  0.8 7.1 %collective-permute-start.3 = (bf16[4,4096]{1,0:T(4,128)(2,1)S(1)}, bf16[4,4096]{1,0:T(4,128)(2,1)S(1)}, u32[]{:S(2)}, u32[]{:S(2)}) collective-permute-start(bf16[4,4096]{1,0:T(4,128)(2,1)S(1)} %copy-done.2), channel_id=1, source_target_pairs={{1,14},{3,12},{5,10},{7,8},{9,6},{11,4},{13,2},{15,0},{0,11},{2,9}... | collective-permute-start | bytes 98312 | tf_op jit(solution)/shard_map/ppermute | solution.py:253
  5.2 5.5 %collective-permute-start.2 = (bf16[4,4096]{1,0:T(4,128)(2,1)S(1)}, bf16[4,4096]{1,0:T(4,128)(2,1)S(1)}, u32[]{:S(2)}, u32[]{:S(2)}) collective-permute-start(bf16[4,4096]{1,0:T(4,128)(2,1)S(1)} %copy-done.2), channel_id=1, source_target_pairs={{1,12},{3,14},{5,8},{7,10},{9,4},{11,6},{13,0},{15,2},{0,9},{2,11}... | collective-permute-start | bytes 98312 | tf_op jit(solution)/shard_map/ppermute | solution.py:253
  5.9 4.8 %collective-permute-start.1 = (bf16[4,4096]{1,0:T(4,128)(2,1)S(1)}, bf16[4,4096]{1,0:T(4,128)(2,1)S(1)}, u32[]{:S(2)}, u32[]{:S(2)}) collective-permute-start(bf16[4,4096]{1,0:T(4,128)(2,1)S(1)} %copy-done.2), channel_id=1, source_target_pairs={{1,2},{3,0},{5,6},{7,4},{9,10},{11,8},{13,14},{15,12},{0,7},{2,5},... | collective-permute-start | bytes 98312 | tf_op jit(solution)/shard_map/ppermute | solution.py:253
  6.0 4.7 %collective-permute-start = (bf16[4,4096]{1,0:T(4,128)(2,1)S(1)}, bf16[4,4096]{1,0:T(4,128)(2,1)S(1)}, u32[]{:S(2)}, u32[]{:S(2)}) collective-permute-start(bf16[4,4096]{1,0:T(4,128)(2,1)S(1)} %copy-done.2), channel_id=1, source_target_pairs={{1,4},{3,6},{5,0},{7,2},{9,12},{11,14},{13,8},{15,10},{0,5},{2,7},... | collective-permute-start | bytes 98312 | tf_op jit(solution)/shard_map/ppermute | solution.py:253
  10.7 1.8 %collective-permute-start.4 = (bf16[4,4,4096]{2,1,0:T(4,128)(2,1)S(1)}, bf16[4,4,4096]{2,1,0:T(4,128)(2,1)S(1)}, u32[]{:S(2)}, u32[]{:S(2)}) collective-permute-start(bf16[4,4,4096]{2,1,0:T(4,128)(2,1)S(1)} %shard_map.74.mine_ref), channel_id=1, source_target_pairs={{0,1},{1,0},{2,3},{3,2},{4,5},{5,4},{6,7},{7,6},{8,9},{9,8},{10,11... | collective-permute-start | bytes 393224 | tf_op jit(solution)/shard_map/ppermute | solution.py:261
  12.5 6.2 %slice-start = ((s8[16777216]{0:T(1024)(128)(4,1)}), s8[4194304]{0:T(1024)(128)(4,1)S(1)}, s32[]{:S(2)}) async-start(s8[16777216]{0:T(1024)(128)(4,1)} %bitcast.1), calls=%async_computation | async-start | bytes 8388608
  12.5 6.2 %slice-start.1 = ((s8[16777216]{0:T(1024)(128)(4,1)}), s8[4194304]{0:T(1024)(128)(4,1)S(1)}, s32[]{:S(2)}) async-start(s8[16777216]{0:T(1024)(128)(4,1)} %bitcast.1), calls=%async_computation.1 | async-start | bytes 8388608
  12.5 6.2 %slice-start.2 = ((s8[16777216]{0:T(1024)(128)(4,1)}), s8[4194304]{0:T(1024)(128)(4,1)S(1)}, s32[]{:S(2)}) async-start(s8[16777216]{0:T(1024)(128)(4,1)} %bitcast.1), calls=%async_computation.2 | async-start | bytes 8388608
  15.7 3.1 %slice-start.3 = ((s8[16777216]{0:T(1024)(128)(4,1)}), s8[4194304]{0:T(1024)(128)(4,1)S(1)}, s32[]{:S(2)}) async-start(s8[16777216]{0:T(1024)(128)(4,1)} %bitcast.1), calls=%async_computation.3 | async-start | bytes 8388608
  20.3 1.9 %collective-permute-start.5 = (bf16[32,2048]{1,0:T(8,128)(2,1)S(1)}, bf16[32,2048]{1,0:T(8,128)(2,1)S(1)}, u32[]{:S(2)}, u32[]{:S(2)}) collective-permute-start(bf16[32,2048]{1,0:T(8,128)(2,1)S(1)} %shard_map.78), channel_id=1, source_target_pairs={{0,1},{1,0},{2,3},{3,2},{4,5},{5,4},{6,7},{7,6},{8,9},{9,8},{10,11... | collective-permute-start | bytes 393224 | tf_op jit(solution)/shard_map/ppermute | solution.py:261
  22.4 5.2 %collective-permute-start.6 = (bf16[2,4,2048]{2,1,0:T(4,128)(2,1)S(1)}, bf16[2,4,2048]{2,1,0:T(4,128)(2,1)S(1)}, u32[]{:S(2)}, u32[]{:S(2)}) collective-permute-start(bf16[2,4,2048]{2,1,0:T(4,128)(2,1)S(1)} %get-tuple-element.24), channel_id=1, source_target_pairs={{0,6},{1,7},{2,4},{3,5},{4,2},{5,3},{6,0},{7,1},{8,14},{9,15},{10,... | collective-permute-start | bytes 98312 | tf_op jit(solution)/shard_map/ppermute | solution.py:244
  23.9 3.7 %collective-permute-start.7 = (bf16[2,4,2048]{2,1,0:T(4,128)(2,1)S(1)}, bf16[2,4,2048]{2,1,0:T(4,128)(2,1)S(1)}, u32[]{:S(2)}, u32[]{:S(2)}) collective-permute-start(bf16[2,4,2048]{2,1,0:T(4,128)(2,1)S(1)} %get-tuple-element.25), channel_id=1, source_target_pairs={{0,5},{1,4},{2,7},{3,6},{4,1},{5,0},{6,3},{7,2},{8,13},{9,12},{10,... | collective-permute-start | bytes 98312 | tf_op jit(solution)/shard_map/ppermute | solution.py:244
  24.3 3.5 %collective-permute-start.8 = (bf16[2,4,2048]{2,1,0:T(4,128)(2,1)S(1)}, bf16[2,4,2048]{2,1,0:T(4,128)(2,1)S(1)}, u32[]{:S(2)}, u32[]{:S(2)}) collective-permute-start(bf16[2,4,2048]{2,1,0:T(4,128)(2,1)S(1)} %get-tuple-element.26), channel_id=1, source_target_pairs={{0,3},{1,2},{2,1},{3,0},{4,7},{5,6},{6,5},{7,4},{8,11},{9,10},{10,... | collective-permute-start | bytes 98312 | tf_op jit(solution)/shard_map/ppermute | solution.py:244
  27.8 4.6 %collective-permute-start.10 = (f32[4,2048]{1,0:T(4,128)S(1)}, f32[4,2048]{1,0:T(4,128)S(1)}, u32[]{:S(2)}, u32[]{:S(2)}) collective-permute-start(f32[4,2048]{1,0:T(4,128)S(1)} %get-tuple-element.27.own_ref), channel_id=1, source_target_pairs={{0,1},{1,0},{2,3},{3,2},{4,5},{5,4},{6,7},{7,6},{8,9},{9,8},{10,11... | collective-permute-start | bytes 98312 | tf_op jit(solution)/shard_map/ppermute | solution.py:261
  28.4 4.1 %collective-permute-start.9 = (bf16[4,2048]{1,0:T(4,128)(2,1)S(1)}, bf16[4,2048]{1,0:T(4,128)(2,1)S(1)}, u32[]{:S(2)}, u32[]{:S(2)}) collective-permute-start(bf16[4,2048]{1,0:T(4,128)(2,1)S(1)} %get-tuple-element.28), channel_id=1, source_target_pairs={{0,9},{1,8},{2,10},{3,11},{4,12},{5,13},{6,15},{7,14},{8,1},{9,0},... | collective-permute-start | bytes 49160 | tf_op jit(solution)/shard_map/ppermute | solution.py:249

commit v15 on v14

--- a/solution.py
+++ b/solution.py
@@ -34,7 +34,7 @@
 
 
 def turned(i):
-    return (1 + i + i // 2) % 2
+    return (1 + i) % 2
 
 
 def first_kernel(place_ref):
@@ -203,27 +203,28 @@
 
 
 def far_kernel(*refs):
-    *part_refs, own_ref, next_ref = refs
-    for i, out_ref in enumerate((own_ref, next_ref)):
+    *part_refs, own_ref, turn_ref, next_ref = refs
+    for i, out_refs in enumerate(((own_ref, turn_ref), (next_ref,))):
         total = part_refs[0][i]
         for part_ref in part_refs[1:]:
             total = total + part_ref[i].astype(jnp.float32)
-        out_ref[...] = total.astype(out_ref.dtype)
+        for out_ref in out_refs:
+            out_ref[...] = total.astype(out_ref.dtype)
 
 
 def far(parts):
     shape = parts[0].shape[1:]
     return pl.pallas_call(
         far_kernel,
-        out_shape=(jax.ShapeDtypeStruct(shape, jnp.float32), jax.ShapeDtypeStruct(shape, jnp.bfloat16)),
+        out_shape=(jax.ShapeDtypeStruct(shape, jnp.float32),) + (jax.ShapeDtypeStruct(shape, jnp.bfloat16),) * 2,
         in_specs=[VMEM] * len(parts),
-        out_specs=(VMEM, VMEM),
+        out_specs=(VMEM,) * 3,
         compiler_params=pltpu.CompilerParams(vmem_limit_bytes=2 * MIB),
     )(*parts)
 
 
 def sum_kernel(place_ref, own_ref, got_ref, turned_ref, out_ref):
-    own = jnp.where(place_ref[2] == 1, turned_ref[...], own_ref[...])
+    own = jnp.where(place_ref[2] == 1, turned_ref[...].astype(jnp.float32), own_ref[...])
     out_ref[...] = (own + got_ref[...].astype(jnp.float32)).astype(out_ref.dtype)
 
 
@@ -275,8 +276,8 @@
     keep = down_half(place, hidden, w_down, False, jnp.float32)
     own, *parts = near(g, keep, swap_cores(send))
     returned = [swapped(parts[j - 1], j) for j in range(half - 1, 0, -1)]
-    own, other = far([own, *returned])
-    return final_sum(place, own, sent_home(other, half), swap_cores(own))
+    own, turn, other = far([own, *returned])
+    return final_sum(place, own, sent_home(other, half), swap_cores(turn))
 
 
 def expert_block(segment, w_gate, w_up, w_down):

time: 33.2 us -> 32.9 us (level)
  starting transfers between devices: 13.5 us -> 13.1 us
    ppermute x3, waiting for transfers between devices: 2.14 us -> 2.63 us  [swapped(): return lax.ppermute(x, ('exp', 'hid'), pairs)]
    ppermute x1, waiting for transfers between devices: 1.85 us -> 1.4 us  [sent_home(): return lax.ppermute(x, ('exp', 'hid'), pairs)]
  transfers between devices with their start and end apart: 11 -> 11, of which waited for: 6 -> 7; matrix products, arithmetic and copies ran while one was open for 0% -> 0% of each run, Pallas kernels for 5% -> 5%
where the time goes in v15:
time: 32.9 us; the launch traced here: 32.8 us
  starting transfers between devices  13.1 us (40%)
  Pallas kernels  10 us (30%)
  waiting for transfers between devices  8.71 us (26%)
  local copies, waits for them, and re-layouts  0.78 us (2%)
    ppermute x4, starting transfers between devices, fetched(): lax.ppermute(x, ('exp', 'hid'), [(2 * i + 1 - side, 2 * (i ^ k) + side) f...  6.27 us
    ppermute x4, waiting for transfers between devices, fetched(): lax.ppermute(x, ('exp', 'hid'), [(2 * i + 1 - side, 2 * (i ^ k) + side) f...  3.69 us
    pallas_call x1, Pallas kernels, gate_rows(): pl.pallas_call(functools.partial(gate_kernel, SOURCES // block_rows.shape...  3.12 us
    pallas_call x2, Pallas kernels, down_half(): pl.pallas_call(functools.partial(down_kernel, other), out_shape=jax.Shape...  3.12 us
    pallas_call x1, Pallas kernels, hidden_rows(): pl.pallas_call(up_kernel, out_shape=jax.ShapeDtypeStruct(act.shape, jnp.b...  3.01 us
    ppermute x3, starting transfers between devices, swapped(): return lax.ppermute(x, ('exp', 'hid'), pairs)  2.99 us
    ppermute x3, waiting for transfers between devices, swapped(): return lax.ppermute(x, ('exp', 'hid'), pairs)  2.63 us
    ppermute x1, starting transfers between devices, sent_home(): return lax.ppermute(x, ('exp', 'hid'), pairs)  2.33 us
  transfers between devices with their start and end apart: 11, of which 7 were waited for; matrix products, arithmetic and copies ran while one was open for 0% of the time, Pallas kernels for 5%

profile of v15, /device:TPU:0, one launch (start us, length us, event | category | flops | bytes accessed | tf_op | source)
XLA Modules:
  0.0 32.8 jit_solution(11494045358825830687)
XLA Ops:
  0.0 0.0 copy-start.5
  0.0 0.0 copy-start.2
  0.0 0.0 copy-start.4
  0.0 0.0 copy-start.3
  0.0 0.0 copy-start.1
  0.0 0.7 %copy-done.2 = bf16[4,4096]{1,0:T(4,128)(2,1)S(1)} copy-done((bf16[4,4096]{1,0:T(4,128)(2,1)S(1)}, bf16[4,4096]{1,0:T(4,128)(2,1)}, u32[]{:S(2)}) %copy-start.2) | copy-done | bytes 32792
  0.8 0.0 copy-start
  0.8 4.4 %collective-permute-start.3 = (bf16[4,4096]{1,0:T(4,128)(2,1)S(1)}, bf16[4,4096]{1,0:T(4,128)(2,1)S(1)}, u32[]{:S(2)}, u32[]{:S(2)}) collective-permute-start(bf16[4,4096]{1,0:T(4,128)(2,1)S(1)} %copy-done.2), channel_id=1, source_target_pairs={{1,14},{3,12},{5,10},{7,8},{9,6},{11,4},{13,2},{15,0},{0,11},{2,9}... | collective-permute-start | bytes 98312 | tf_op jit(solution)/shard_map/ppermute | solution.py:254
  5.2 0.7 %collective-permute-start.2 = (bf16[4,4096]{1,0:T(4,128)(2,1)S(1)}, bf16[4,4096]{1,0:T(4,128)(2,1)S(1)}, u32[]{:S(2)}, u32[]{:S(2)}) collective-permute-start(bf16[4,4096]{1,0:T(4,128)(2,1)S(1)} %copy-done.2), channel_id=1, source_target_pairs={{1,12},{3,14},{5,8},{7,10},{9,4},{11,6},{13,0},{15,2},{0,9},{2,11}... | collective-permute-start | bytes 98312 | tf_op jit(solution)/shard_map/ppermute | solution.py:254
  5.9 0.1 collective-permute-start.1
  6.0 1.0 %collective-permute-start = (bf16[4,4096]{1,0:T(4,128)(2,1)S(1)}, bf16[4,4096]{1,0:T(4,128)(2,1)S(1)}, u32[]{:S(2)}, u32[]{:S(2)}) collective-permute-start(bf16[4,4096]{1,0:T(4,128)(2,1)S(1)} %copy-done.2), channel_id=1, source_target_pairs={{1,4},{3,6},{5,0},{7,2},{9,12},{11,14},{13,8},{15,10},{0,5},{2,7},... | collective-permute-start | bytes 98312 | tf_op jit(solution)/shard_map/ppermute | solution.py:254
  7.0 0.8 %collective-permute-done.3.refs_3_ = bf16[4,4096]{1,0:T(4,128)(2,1)S(1)} collective-permute-done((bf16[4,4096]{1,0:T(4,128)(2,1)S(1)}, bf16[4,4096]{1,0:T(4,128)(2,1)S(1)}, u32[]{:S(2)}, u32[]{:S(2)}) %collective-permute-start.3) | collective-permute-done | bytes 32800 | tf_op jit(solution)/shard_map/ppermute | solution.py:254
  7.9 2.8 %collective-permute-done.2.refs_2_ = bf16[4,4096]{1,0:T(4,128)(2,1)S(1)} collective-permute-done((bf16[4,4096]{1,0:T(4,128)(2,1)S(1)}, bf16[4,4096]{1,0:T(4,128)(2,1)S(1)}, u32[]{:S(2)}, u32[]{:S(2)}) %collective-permute-start.2) | collective-permute-done | bytes 32800 | tf_op jit(solution)/shard_map/ppermute | solution.py:254
  10.7 0.0 collective-permute-done.1.refs_1_
  10.7 0.0 collective-permute-done.refs_0_
  10.7 0.8 %collective-permute-start.4 = (bf16[4,4,4096]{2,1,0:T(4,128)(2,1)S(1)}, bf16[4,4,4096]{2,1,0:T(4,128)(2,1)S(1)}, u32[]{:S(2)}, u32[]{:S(2)}) collective-permute-start(bf16[4,4,4096]{2,1,0:T(4,128)(2,1)S(1)} %shard_map.74.mine_ref), channel_id=1, source_target_pairs={{0,1},{1,0},{2,3},{3,2},{4,5},{5,4},{6,7},{7,6},{8,9},{9,8},{10,11... | collective-permute-start | bytes 393224 | tf_op jit(solution)/shard_map/ppermute | solution.py:262
  11.5 1.0 %collective-permute-done.4.got_ref = bf16[4,4,4096]{2,1,0:T(4,128)(2,1)S(1)} collective-permute-done((bf16[4,4,4096]{2,1,0:T(4,128)(2,1)S(1)}, bf16[4,4,4096]{2,1,0:T(4,128)(2,1)S(1)}, u32[]{:S(2)}, u32[]{:S(2)}) %collective-permute-start.4) | collective-permute-done | bytes 131104 | tf_op jit(solution)/shard_map/ppermute | solution.py:262
  12.5 0.0 copy-done.5
  12.5 0.0 copy-done.4
  12.5 0.0 copy-done.3
  12.5 0.0 copy-done.1
  12.5 0.0 slice-start
  12.5 0.0 slice-start.1
  12.5 0.0 slice-start.2
  12.6 3.1 %shard_map.75 = (bf16[32,4096]{1,0:T(8,128)(2,1)S(1)}, f32[32,2048]{1,0:T(8,128)S(1)}, f32[32,128]{1,0:T(8,128)S(1)}) custom-call(s32[4]{0:T(128)S(4)} %shard_map.73.place_ref, s32[1,4]{1,0:T(1,128)S(1)} %bitcast.3, bf16[4,4096]{1,0:T(4,128)(2,1)S(1)} %copy-done.2, bf16[4,4,4096]{2,1,0:T(4,128)(2,1)S(1)} %shard_map.74.mine_ref, ...), custom_call_target="tpu_custom_call" | custom-call | flops 5000000000 | tf_op jit(solution)/shard_map/pallas_call | solution.py:126
  15.7 0.0 copy-done
  15.7 0.0 slice-start.3
  15.7 3.0 %shard_map.76.h_ref = bf16[32,2048]{1,0:T(8,128)(2,1)S(1)} custom-call(bf16[32,4096]{1,0:T(8,128)(2,1)S(1)} %get-tuple-element.22.x_ref, f32[32,2048]{1,0:T(8,128)S(1)} %get-tuple-element.23.act_ref, bf16[4096,2048]{1,0:T(8,128)(2,1)S(1)} %copy-done), custom_call_target="tpu_custom_call" | custom-call | flops 2000000000 | tf_op jit(solution)/shard_map/pallas_call | solution.py:149
  18.7 0.0 slice-done
  18.7 0.0 slice-done.1
  18.7 0.0 slice-done.2
  18.7 0.0 slice-done.3
  18.8 1.6 %shard_map.78 = bf16[32,2048]{1,0:T(8,128)(2,1)S(1)} custom-call(s32[4]{0:T(128)S(4)} %shard_map.73.place_ref, bf16[32,2048]{1,0:T(8,128)(2,1)S(1)} %shard_map.76.h_ref, bf16[2048,4096]{1,0:T(8,128)(2,1)S(1)} %bitcast.2), custom_call_target="tpu_custom_call" | custom-call | flops 268435456 | tf_op jit(solution)/shard_map/pallas_call | solution.py:172
  20.3 0.4 %collective-permute-start.5 = (bf16[32,2048]{1,0:T(8,128)(2,1)S(1)}, bf16[32,2048]{1,0:T(8,128)(2,1)S(1)}, u32[]{:S(2)}, u32[]{:S(2)}) collective-permute-start(bf16[32,2048]{1,0:T(8,128)(2,1)S(1)} %shard_map.78), channel_id=1, source_target_pairs={{0,1},{1,0},{2,3},{3,2},{4,5},{5,4},{6,7},{7,6},{8,9},{9,8},{10,11... | collective-permute-start | bytes 393224 | tf_op jit(solution)/shard_map/ppermute | solution.py:262
  20.7 1.6 %shard_map.77.keep_ref = f32[32,2048]{1,0:T(8,128)S(1)} custom-call(s32[4]{0:T(128)S(4)} %shard_map.73.place_ref, bf16[32,2048]{1,0:T(8,128)(2,1)S(1)} %shard_map.76.h_ref, bf16[2048,4096]{1,0:T(8,128)(2,1)S(1)} %bitcast.2), custom_call_target="tpu_custom_call" | custom-call | flops 268435456 | tf_op jit(solution)/shard_map/pallas_call | solution.py:172
  22.3 0.0 collective-permute-done.5.got_ref
  22.3 0.1 shard_map.79
  22.4 1.5 %collective-permute-start.6 = (bf16[2,4,2048]{2,1,0:T(4,128)(2,1)S(1)}, bf16[2,4,2048]{2,1,0:T(4,128)(2,1)S(1)}, u32[]{:S(2)}, u32[]{:S(2)}) collective-permute-start(bf16[2,4,2048]{2,1,0:T(4,128)(2,1)S(1)} %get-tuple-element.25), channel_id=1, source_target_pairs={{0,7},{1,6},{2,5},{3,4},{4,3},{5,2},{6,1},{7,0},{8,15},{9,14},{10,... | collective-permute-start | bytes 98312 | tf_op jit(solution)/shard_map/ppermute | solution.py:245
  23.9 0.7 %collective-permute-start.7 = (bf16[2,4,2048]{2,1,0:T(4,128)(2,1)S(1)}, bf16[2,4,2048]{2,1,0:T(4,128)(2,1)S(1)}, u32[]{:S(2)}, u32[]{:S(2)}) collective-permute-start(bf16[2,4,2048]{2,1,0:T(4,128)(2,1)S(1)} %get-tuple-element.26), channel_id=1, source_target_pairs={{0,4},{1,5},{2,6},{3,7},{4,0},{5,1},{6,2},{7,3},{8,12},{9,13},{10,... | collective-permute-start | bytes 98312 | tf_op jit(solution)/shard_map/ppermute | solution.py:245
  24.6 0.8 %collective-permute-start.8 = (bf16[2,4,2048]{2,1,0:T(4,128)(2,1)S(1)}, bf16[2,4,2048]{2,1,0:T(4,128)(2,1)S(1)}, u32[]{:S(2)}, u32[]{:S(2)}) collective-permute-start(bf16[2,4,2048]{2,1,0:T(4,128)(2,1)S(1)} %get-tuple-element.27), channel_id=1, source_target_pairs={{0,3},{1,2},{2,1},{3,0},{4,7},{5,6},{6,5},{7,4},{8,11},{9,10},{10,... | collective-permute-start | bytes 98312 | tf_op jit(solution)/shard_map/ppermute | solution.py:245
  25.4 1.3 %collective-permute-done.6.refs_1_ = bf16[2,4,2048]{2,1,0:T(4,128)(2,1)S(1)} collective-permute-done((bf16[2,4,2048]{2,1,0:T(4,128)(2,1)S(1)}, bf16[2,4,2048]{2,1,0:T(4,128)(2,1)S(1)}, u32[]{:S(2)}, u32[]{:S(2)}) %collective-permute-start.6) | collective-permute-done | bytes 32800 | tf_op jit(solution)/shard_map/ppermute | solution.py:245
  26.7 1.1 %collective-permute-done.7.refs_2_ = bf16[2,4,2048]{2,1,0:T(4,128)(2,1)S(1)} collective-permute-done((bf16[2,4,2048]{2,1,0:T(4,128)(2,1)S(1)}, bf16[2,4,2048]{2,1,0:T(4,128)(2,1)S(1)}, u32[]{:S(2)}, u32[]{:S(2)}) %collective-permute-start.7) | collective-permute-done | bytes 32800 | tf_op jit(solution)/shard_map/ppermute | solution.py:245
  27.8 0.2 collective-permute-done.8.refs_3_
  28.0 2.3 %collective-permute-start.9 = (bf16[4,2048]{1,0:T(4,128)(2,1)S(1)}, bf16[4,2048]{1,0:T(4,128)(2,1)S(1)}, u32[]{:S(2)}, u32[]{:S(2)}) collective-permute-start(bf16[4,2048]{1,0:T(4,128)(2,1)S(1)} %get-tuple-element.29), channel_id=1, source_target_pairs={{0,9},{1,8},{2,10},{3,11},{4,13},{5,12},{6,14},{7,15},{8,1},{9,0},... | collective-permute-start | bytes 49160 | tf_op jit(solution)/shard_map/ppermute | solution.py:250
  30.4 0.4 %collective-permute-start.10 = (bf16[4,2048]{1,0:T(4,128)(2,1)S(1)}, bf16[4,2048]{1,0:T(4,128)(2,1)S(1)}, u32[]{:S(2)}, u32[]{:S(2)}) collective-permute-start(bf16[4,2048]{1,0:T(4,128)(2,1)S(1)} %get-tuple-element.30), channel_id=1, source_target_pairs={{0,1},{1,0},{2,3},{3,2},{4,5},{5,4},{6,7},{7,6},{8,9},{9,8},{10,11... | collective-permute-start | bytes 49160 | tf_op jit(solution)/shard_map/ppermute | solution.py:262
  30.8 1.4 %collective-permute-done.9.got_ref = bf16[4,2048]{1,0:T(4,128)(2,1)S(1)} collective-permute-done((bf16[4,2048]{1,0:T(4,128)(2,1)S(1)}, bf16[4,2048]{1,0:T(4,128)(2,1)S(1)}, u32[]{:S(2)}, u32[]{:S(2)}) %collective-permute-start.9) | collective-permute-done | bytes 16416 | tf_op jit(solution)/shard_map/ppermute | solution.py:250
  32.2 0.0 collective-permute-done.10.turned_ref
  32.2 0.6 %shard_map.81 = bf16[4,2048]{1,0:T(4,128)(2,1)} custom-call(s32[4]{0:T(128)S(4)} %shard_map.73.place_ref, f32[4,2048]{1,0:T(4,128)S(1)} %get-tuple-element.28.own_ref, bf16[4,2048]{1,0:T(4,128)(2,1)S(1)} %collective-permute-done.9.got_ref, bf16[4,2048]{1,0:T(4,128)(2,1)S(1)} %collective-permute-done.10.turned_ref), custom_call_target="tpu_custom_call" | custom-call | tf_op jit(solution)/shard_map/pallas_call | solution.py:232
  (4 shorter events, 0.1 us)
Async XLA Ops:
  0.0 12.5 %copy-start.5 = (s32[4]{0:T(128)S(1)}, s32[4]{0:T(128)}, u32[]{:S(2)}) copy-start(s32[4]{0:T(128)} %param.11) | copy-start | bytes 52
  0.0 0.8 %copy-start.2 = (bf16[4,4096]{1,0:T(4,128)(2,1)S(1)}, bf16[4,4096]{1,0:T(4,128)(2,1)}, u32[]{:S(2)}) copy-start(bf16[4,4096]{1,0:T(4,128)(2,1)} %tokens_ref) | copy-start | bytes 98308
  0.0 12.5 %copy-start.4 = (f32[4,128]{1,0:T(4,128)S(1)}, f32[4,128]{1,0:T(4,128)}, u32[]{:S(2)}) copy-start(f32[4,128]{1,0:T(4,128)} %gates_ref.1) | copy-start | bytes 6148
  0.0 12.5 %copy-start.3 = (s32[4,128]{1,0:T(4,128)S(1)}, s32[4,128]{1,0:T(4,128)}, u32[]{:S(2)}) copy-start(s32[4,128]{1,0:T(4,128)} %rows_ref.1) | copy-start | bytes 6148
  0.0 12.5 %copy-start.1 = (bf16[4096,2048]{1,0:T(8,128)(2,1)S(1)}, bf16[4096,2048]{1,0:T(8,128)(2,1)}, u32[]{:S(2)}) copy-start(bf16[4096,2048]{1,0:T(8,128)(2,1)} %wg_ref.1) | copy-start | bytes 50331652
  0.8 14.9 %copy-start = (bf16[4096,2048]{1,0:T(8,128)(2,1)S(1)}, bf16[4096,2048]{1,0:T(8,128)(2,1)}, u32[]{:S(2)}) copy-start(bf16[4096,2048]{1,0:T(8,128)(2,1)} %wu_ref.1) | copy-start | bytes 50331652
  0.8 7.1 %collective-permute-start.3 = (bf16[4,4096]{1,0:T(4,128)(2,1)S(1)}, bf16[4,4096]{1,0:T(4,128)(2,1)S(1)}, u32[]{:S(2)}, u32[]{:S(2)}) collective-permute-start(bf16[4,4096]{1,0:T(4,128)(2,1)S(1)} %copy-done.2), channel_id=1, source_target_pairs={{1,14},{3,12},{5,10},{7,8},{9,6},{11,4},{13,2},{15,0},{0,11},{2,9}... | collective-permute-start | bytes 98312 | tf_op jit(solution)/shard_map/ppermute | solution.py:254
  5.2 5.5 %collective-permute-start.2 = (bf16[4,4096]{1,0:T(4,128)(2,1)S(1)}, bf16[4,4096]{1,0:T(4,128)(2,1)S(1)}, u32[]{:S(2)}, u32[]{:S(2)}) collective-permute-start(bf16[4,4096]{1,0:T(4,128)(2,1)S(1)} %copy-done.2), channel_id=1, source_target_pairs={{1,12},{3,14},{5,8},{7,10},{9,4},{11,6},{13,0},{15,2},{0,9},{2,11}... | collective-permute-start | bytes 98312 | tf_op jit(solution)/shard_map/ppermute | solution.py:254
  5.9 4.8 %collective-permute-start.1 = (bf16[4,4096]{1,0:T(4,128)(2,1)S(1)}, bf16[4,4096]{1,0:T(4,128)(2,1)S(1)}, u32[]{:S(2)}, u32[]{:S(2)}) collective-permute-start(bf16[4,4096]{1,0:T(4,128)(2,1)S(1)} %copy-done.2), channel_id=1, source_target_pairs={{1,2},{3,0},{5,6},{7,4},{9,10},{11,8},{13,14},{15,12},{0,7},{2,5},... | collective-permute-start | bytes 98312 | tf_op jit(solution)/shard_map/ppermute | solution.py:254
  6.0 4.7 %collective-permute-start = (bf16[4,4096]{1,0:T(4,128)(2,1)S(1)}, bf16[4,4096]{1,0:T(4,128)(2,1)S(1)}, u32[]{:S(2)}, u32[]{:S(2)}) collective-permute-start(bf16[4,4096]{1,0:T(4,128)(2,1)S(1)} %copy-done.2), channel_id=1, source_target_pairs={{1,4},{3,6},{5,0},{7,2},{9,12},{11,14},{13,8},{15,10},{0,5},{2,7},... | collective-permute-start | bytes 98312 | tf_op jit(solution)/shard_map/ppermute | solution.py:254
  10.7 1.8 %collective-permute-start.4 = (bf16[4,4,4096]{2,1,0:T(4,128)(2,1)S(1)}, bf16[4,4,4096]{2,1,0:T(4,128)(2,1)S(1)}, u32[]{:S(2)}, u32[]{:S(2)}) collective-permute-start(bf16[4,4,4096]{2,1,0:T(4,128)(2,1)S(1)} %shard_map.74.mine_ref), channel_id=1, source_target_pairs={{0,1},{1,0},{2,3},{3,2},{4,5},{5,4},{6,7},{7,6},{8,9},{9,8},{10,11... | collective-permute-start | bytes 393224 | tf_op jit(solution)/shard_map/ppermute | solution.py:262
  12.5 6.2 %slice-start = ((s8[16777216]{0:T(1024)(128)(4,1)}), s8[4194304]{0:T(1024)(128)(4,1)S(1)}, s32[]{:S(2)}) async-start(s8[16777216]{0:T(1024)(128)(4,1)} %bitcast.1), calls=%async_computation | async-start | bytes 8388608
  12.5 6.2 %slice-start.1 = ((s8[16777216]{0:T(1024)(128)(4,1)}), s8[4194304]{0:T(1024)(128)(4,1)S(1)}, s32[]{:S(2)}) async-start(s8[16777216]{0:T(1024)(128)(4,1)} %bitcast.1), calls=%async_computation.1 | async-start | bytes 8388608
  12.5 6.2 %slice-start.2 = ((s8[16777216]{0:T(1024)(128)(4,1)}), s8[4194304]{0:T(1024)(128)(4,1)S(1)}, s32[]{:S(2)}) async-start(s8[16777216]{0:T(1024)(128)(4,1)} %bitcast.1), calls=%async_computation.2 | async-start | bytes 8388608
  15.7 3.1 %slice-start.3 = ((s8[16777216]{0:T(1024)(128)(4,1)}), s8[4194304]{0:T(1024)(128)(4,1)S(1)}, s32[]{:S(2)}) async-start(s8[16777216]{0:T(1024)(128)(4,1)} %bitcast.1), calls=%async_computation.3 | async-start | bytes 8388608
  20.3 1.9 %collective-permute-start.5 = (bf16[32,2048]{1,0:T(8,128)(2,1)S(1)}, bf16[32,2048]{1,0:T(8,128)(2,1)S(1)}, u32[]{:S(2)}, u32[]{:S(2)}) collective-permute-start(bf16[32,2048]{1,0:T(8,128)(2,1)S(1)} %shard_map.78), channel_id=1, source_target_pairs={{0,1},{1,0},{2,3},{3,2},{4,5},{5,4},{6,7},{7,6},{8,9},{9,8},{10,11... | collective-permute-start | bytes 393224 | tf_op jit(solution)/shard_map/ppermute | solution.py:262
  22.4 4.3 %collective-permute-start.6 = (bf16[2,4,2048]{2,1,0:T(4,128)(2,1)S(1)}, bf16[2,4,2048]{2,1,0:T(4,128)(2,1)S(1)}, u32[]{:S(2)}, u32[]{:S(2)}) collective-permute-start(bf16[2,4,2048]{2,1,0:T(4,128)(2,1)S(1)} %get-tuple-element.25), channel_id=1, source_target_pairs={{0,7},{1,6},{2,5},{3,4},{4,3},{5,2},{6,1},{7,0},{8,15},{9,14},{10,... | collective-permute-start | bytes 98312 | tf_op jit(solution)/shard_map/ppermute | solution.py:245
  23.9 3.9 %collective-permute-start.7 = (bf16[2,4,2048]{2,1,0:T(4,128)(2,1)S(1)}, bf16[2,4,2048]{2,1,0:T(4,128)(2,1)S(1)}, u32[]{:S(2)}, u32[]{:S(2)}) collective-permute-start(bf16[2,4,2048]{2,1,0:T(4,128)(2,1)S(1)} %get-tuple-element.26), channel_id=1, source_target_pairs={{0,4},{1,5},{2,6},{3,7},{4,0},{5,1},{6,2},{7,3},{8,12},{9,13},{10,... | collective-permute-start | bytes 98312 | tf_op jit(solution)/shard_map/ppermute | solution.py:245
  24.6 3.4 %collective-permute-start.8 = (bf16[2,4,2048]{2,1,0:T(4,128)(2,1)S(1)}, bf16[2,4,2048]{2,1,0:T(4,128)(2,1)S(1)}, u32[]{:S(2)}, u32[]{:S(2)}) collective-permute-start(bf16[2,4,2048]{2,1,0:T(4,128)(2,1)S(1)} %get-tuple-element.27), channel_id=1, source_target_pairs={{0,3},{1,2},{2,1},{3,0},{4,7},{5,6},{6,5},{7,4},{8,11},{9,10},{10,... | collective-permute-start | bytes 98312 | tf_op jit(solution)/shard_map/ppermute | solution.py:245
  28.0 4.1 %collective-permute-start.9 = (bf16[4,2048]{1,0:T(4,128)(2,1)S(1)}, bf16[4,2048]{1,0:T(4,128)(2,1)S(1)}, u32[]{:S(2)}, u32[]{:S(2)}) collective-permute-start(bf16[4,2048]{1,0:T(4,128)(2,1)S(1)} %get-tuple-element.29), channel_id=1, source_target_pairs={{0,9},{1,8},{2,10},{3,11},{4,13},{5,12},{6,14},{7,15},{8,1},{9,0},... | collective-permute-start | bytes 49160 | tf_op jit(solution)/shard_map/ppermute | solution.py:250
  30.4 1.8 %collective-permute-start.10 = (bf16[4,2048]{1,0:T(4,128)(2,1)S(1)}, bf16[4,2048]{1,0:T(4,128)(2,1)S(1)}, u32[]{:S(2)}, u32[]{:S(2)}) collective-permute-start(bf16[4,2048]{1,0:T(4,128)(2,1)S(1)} %get-tuple-element.30), channel_id=1, source_target_pairs={{0,1},{1,0},{2,3},{3,2},{4,5},{5,4},{6,7},{7,6},{8,9},{9,8},{10,11... | collective-permute-start | bytes 49160 | tf_op jit(solution)/shard_map/ppermute | solution.py:262

commit v16 on v15

--- a/solution.py
+++ b/solution.py
@@ -11,7 +11,7 @@
 CAP = 3
 TILE = 512
 MIB = 1 << 20
-ORDER = (0, 1, 6, 7, 2, 3, 4, 5)
+ORDER = (0, 6, 7, 1, 2, 4, 5, 3)
 SOURCES = len(ORDER)
 GATE = 5_000_000_000
 UP = 2_000_000_000

time: 32.9 us -> 34 us (1.033)
  waiting for transfers between devices: 8.71 us -> 11.3 us
  starting transfers between devices: 13.1 us -> 11.6 us
    ppermute x1, waiting for transfers between devices: 1.4 us -> 2.41 us  [sent_home(): return lax.ppermute(x, ('exp', 'hid'), pairs)]
    ppermute x1, starting transfers between devices: 2.33 us -> 1.33 us  [sent_home(): return lax.ppermute(x, ('exp', 'hid'), pairs)]
    ppermute x3, waiting for transfers between devices: 2.63 us -> 3.44 us  [swapped(): return lax.ppermute(x, ('exp', 'hid'), pairs)]
    ppermute x4, waiting for transfers between devices: 3.69 us -> 4.35 us  [fetched(): lax.ppermute(x, ('exp', 'hid'), [(2 * i + 1 - side, 2 * (i ^ k) + side) f...]
    ppermute x3, starting transfers between devices: 1.55 us -> 1 us  [swap_cores(): return lax.ppermute(x, 'hid', [(0, 1), (1, 0)])]
where the time goes in v16:
time: 34 us; the launch traced here: 33.8 us
  starting transfers between devices  11.6 us (34%)
  waiting for transfers between devices  11.3 us (33%)
  Pallas kernels  10 us (29%)
  local copies, waits for them, and re-layouts  0.78 us (2%)
    ppermute x4, starting transfers between devices, fetched(): lax.ppermute(x, ('exp', 'hid'), [(2 * i + 1 - side, 2 * (i ^ k) + side) f...  6.27 us
    ppermute x4, waiting for transfers between devices, fetched(): lax.ppermute(x, ('exp', 'hid'), [(2 * i + 1 - side, 2 * (i ^ k) + side) f...  4.35 us
    ppermute x3, waiting for transfers between devices, swapped(): return lax.ppermute(x, ('exp', 'hid'), pairs)  3.44 us
    pallas_call x1, Pallas kernels, gate_rows(): pl.pallas_call(functools.partial(gate_kernel, SOURCES // block_rows.shape...  3.12 us
    pallas_call x2, Pallas kernels, down_half(): pl.pallas_call(functools.partial(down_kernel, other), out_shape=jax.Shape...  3.12 us
    pallas_call x1, Pallas kernels, hidden_rows(): pl.pallas_call(up_kernel, out_shape=jax.ShapeDtypeStruct(act.shape, jnp.b...  3.01 us
    ppermute x3, starting transfers between devices, swapped(): return lax.ppermute(x, ('exp', 'hid'), pairs)  2.99 us
    ppermute x1, waiting for transfers between devices, sent_home(): return lax.ppermute(x, ('exp', 'hid'), pairs)  2.41 us
  transfers between devices with their start and end apart: 11, of which 7 were waited for; matrix products, arithmetic and copies ran while one was open for 0% of the time, Pallas kernels for 5%

profile of v16, /device:TPU:0, one launch (start us, length us, event | category | flops | bytes accessed | tf_op | source)
XLA Modules:
  0.0 33.8 jit_solution(2425226211714148482)
XLA Ops:
  0.0 0.0 copy-start.5
  0.0 0.0 copy-start.2
  0.0 0.0 copy-start.4
  0.0 0.0 copy-start.3
  0.0 0.0 copy-start.1
  0.0 0.7 %copy-done.2 = bf16[4,4096]{1,0:T(4,128)(2,1)S(1)} copy-done((bf16[4,4096]{1,0:T(4,128)(2,1)S(1)}, bf16[4,4096]{1,0:T(4,128)(2,1)}, u32[]{:S(2)}) %copy-start.2) | copy-done | bytes 32792
  0.8 0.0 copy-start
  0.8 3.4 %collective-permute-start.3 = (bf16[4,4096]{1,0:T(4,128)(2,1)S(1)}, bf16[4,4096]{1,0:T(4,128)(2,1)S(1)}, u32[]{:S(2)}, u32[]{:S(2)}) collective-permute-start(bf16[4,4096]{1,0:T(4,128)(2,1)S(1)} %copy-done.2), channel_id=1, source_target_pairs={{1,2},{3,0},{5,6},{7,4},{9,10},{11,8},{13,14},{15,12},{0,7},{2,5},... | collective-permute-start | bytes 98312 | tf_op jit(solution)/shard_map/ppermute | solution.py:254
  4.2 1.8 %collective-permute-start.2 = (bf16[4,4096]{1,0:T(4,128)(2,1)S(1)}, bf16[4,4096]{1,0:T(4,128)(2,1)S(1)}, u32[]{:S(2)}, u32[]{:S(2)}) collective-permute-start(bf16[4,4096]{1,0:T(4,128)(2,1)S(1)} %copy-done.2), channel_id=1, source_target_pairs={{1,14},{3,12},{5,10},{7,8},{9,6},{11,4},{13,2},{15,0},{0,11},{2,9}... | collective-permute-start | bytes 98312 | tf_op jit(solution)/shard_map/ppermute | solution.py:254
  6.0 0.0 collective-permute-start.1
  6.0 1.0 %collective-permute-start = (bf16[4,4096]{1,0:T(4,128)(2,1)S(1)}, bf16[4,4096]{1,0:T(4,128)(2,1)S(1)}, u32[]{:S(2)}, u32[]{:S(2)}) collective-permute-start(bf16[4,4096]{1,0:T(4,128)(2,1)S(1)} %copy-done.2), channel_id=1, source_target_pairs={{1,4},{3,6},{5,0},{7,2},{9,12},{11,14},{13,8},{15,10},{0,5},{2,7},... | collective-permute-start | bytes 98312 | tf_op jit(solution)/shard_map/ppermute | solution.py:254
  7.0 0.0 collective-permute-done.3.refs_3_
  7.0 3.5 %collective-permute-done.2.refs_2_ = bf16[4,4096]{1,0:T(4,128)(2,1)S(1)} collective-permute-done((bf16[4,4096]{1,0:T(4,128)(2,1)S(1)}, bf16[4,4096]{1,0:T(4,128)(2,1)S(1)}, u32[]{:S(2)}, u32[]{:S(2)}) %collective-permute-start.2) | collective-permute-done | bytes 32800 | tf_op jit(solution)/shard_map/ppermute | solution.py:254
  10.6 0.8 %collective-permute-done.1.refs_1_ = bf16[4,4096]{1,0:T(4,128)(2,1)S(1)} collective-permute-done((bf16[4,4096]{1,0:T(4,128)(2,1)S(1)}, bf16[4,4096]{1,0:T(4,128)(2,1)S(1)}, u32[]{:S(2)}, u32[]{:S(2)}) %collective-permute-start.1) | collective-permute-done | bytes 32800 | tf_op jit(solution)/shard_map/ppermute | solution.py:254
  11.4 0.0 collective-permute-done.refs_0_
  11.4 0.3 collective-permute-start.4
  11.7 1.1 %collective-permute-done.4.got_ref = bf16[4,4,4096]{2,1,0:T(4,128)(2,1)S(1)} collective-permute-done((bf16[4,4,4096]{2,1,0:T(4,128)(2,1)S(1)}, bf16[4,4,4096]{2,1,0:T(4,128)(2,1)S(1)}, u32[]{:S(2)}, u32[]{:S(2)}) %collective-permute-start.4) | collective-permute-done | bytes 131104 | tf_op jit(solution)/shard_map/ppermute | solution.py:262
  12.8 0.0 copy-done.5
  12.8 0.0 copy-done.4
  12.8 0.0 copy-done.3
  12.8 0.0 copy-done.1
  12.9 0.0 slice-start
  12.9 0.0 slice-start.1
  12.9 0.0 slice-start.2
  12.9 3.1 %shard_map.75 = (bf16[32,4096]{1,0:T(8,128)(2,1)S(1)}, f32[32,2048]{1,0:T(8,128)S(1)}, f32[32,128]{1,0:T(8,128)S(1)}) custom-call(s32[4]{0:T(128)S(4)} %shard_map.73.place_ref, s32[1,4]{1,0:T(1,128)S(1)} %bitcast.3, bf16[4,4096]{1,0:T(4,128)(2,1)S(1)} %copy-done.2, bf16[4,4,4096]{2,1,0:T(4,128)(2,1)S(1)} %shard_map.74.mine_ref, ...), custom_call_target="tpu_custom_call" | custom-call | flops 5000000000 | tf_op jit(solution)/shard_map/pallas_call | solution.py:126
  16.0 0.0 copy-done
  16.0 0.0 slice-start.3
  16.0 3.0 %shard_map.76.h_ref = bf16[32,2048]{1,0:T(8,128)(2,1)S(1)} custom-call(bf16[32,4096]{1,0:T(8,128)(2,1)S(1)} %get-tuple-element.22.x_ref, f32[32,2048]{1,0:T(8,128)S(1)} %get-tuple-element.23.act_ref, bf16[4096,2048]{1,0:T(8,128)(2,1)S(1)} %copy-done), custom_call_target="tpu_custom_call" | custom-call | flops 2000000000 | tf_op jit(solution)/shard_map/pallas_call | solution.py:149
  19.0 0.0 slice-done
  19.1 0.0 slice-done.1
  19.1 0.0 slice-done.2
  19.1 0.0 slice-done.3
  19.1 1.6 %shard_map.78 = bf16[32,2048]{1,0:T(8,128)(2,1)S(1)} custom-call(s32[4]{0:T(128)S(4)} %shard_map.73.place_ref, bf16[32,2048]{1,0:T(8,128)(2,1)S(1)} %shard_map.76.h_ref, bf16[2048,4096]{1,0:T(8,128)(2,1)S(1)} %bitcast.2), custom_call_target="tpu_custom_call" | custom-call | flops 268435456 | tf_op jit(solution)/shard_map/pallas_call | solution.py:172
  20.7 0.3 collective-permute-start.5
  20.9 1.6 %shard_map.77.keep_ref = f32[32,2048]{1,0:T(8,128)S(1)} custom-call(s32[4]{0:T(128)S(4)} %shard_map.73.place_ref, bf16[32,2048]{1,0:T(8,128)(2,1)S(1)} %shard_map.76.h_ref, bf16[2048,4096]{1,0:T(8,128)(2,1)S(1)} %bitcast.2), custom_call_target="tpu_custom_call" | custom-call | flops 268435456 | tf_op jit(solution)/shard_map/pallas_call | solution.py:172
  22.5 0.0 collective-permute-done.5.got_ref
  22.5 0.1 shard_map.79
  22.6 1.1 %collective-permute-start.6 = (bf16[2,4,2048]{2,1,0:T(4,128)(2,1)S(1)}, bf16[2,4,2048]{2,1,0:T(4,128)(2,1)S(1)}, u32[]{:S(2)}, u32[]{:S(2)}) collective-permute-start(bf16[2,4,2048]{2,1,0:T(4,128)(2,1)S(1)} %get-tuple-element.25), channel_id=1, source_target_pairs={{0,7},{1,6},{2,5},{3,4},{4,3},{5,2},{6,1},{7,0},{8,15},{9,14},{10,... | collective-permute-start | bytes 98312 | tf_op jit(solution)/shard_map/ppermute | solution.py:245
  23.7 1.8 %collective-permute-start.7 = (bf16[2,4,2048]{2,1,0:T(4,128)(2,1)S(1)}, bf16[2,4,2048]{2,1,0:T(4,128)(2,1)S(1)}, u32[]{:S(2)}, u32[]{:S(2)}) collective-permute-start(bf16[2,4,2048]{2,1,0:T(4,128)(2,1)S(1)} %get-tuple-element.26), channel_id=1, source_target_pairs={{0,4},{1,5},{2,6},{3,7},{4,0},{5,1},{6,2},{7,3},{8,12},{9,13},{10,... | collective-permute-start | bytes 98312 | tf_op jit(solution)/shard_map/ppermute | solution.py:245
  25.5 0.1 collective-permute-start.8
  25.6 1.3 %collective-permute-done.6.refs_1_ = bf16[2,4,2048]{2,1,0:T(4,128)(2,1)S(1)} collective-permute-done((bf16[2,4,2048]{2,1,0:T(4,128)(2,1)S(1)}, bf16[2,4,2048]{2,1,0:T(4,128)(2,1)S(1)}, u32[]{:S(2)}, u32[]{:S(2)}) %collective-permute-start.6) | collective-permute-done | bytes 32800 | tf_op jit(solution)/shard_map/ppermute | solution.py:245
  26.9 1.1 %collective-permute-done.7.refs_2_ = bf16[2,4,2048]{2,1,0:T(4,128)(2,1)S(1)} collective-permute-done((bf16[2,4,2048]{2,1,0:T(4,128)(2,1)S(1)}, bf16[2,4,2048]{2,1,0:T(4,128)(2,1)S(1)}, u32[]{:S(2)}, u32[]{:S(2)}) %collective-permute-start.7) | collective-permute-done | bytes 32800 | tf_op jit(solution)/shard_map/ppermute | solution.py:245
  28.0 1.0 %collective-permute-done.8.refs_3_ = bf16[2,4,2048]{2,1,0:T(4,128)(2,1)S(1)} collective-permute-done((bf16[2,4,2048]{2,1,0:T(4,128)(2,1)S(1)}, bf16[2,4,2048]{2,1,0:T(4,128)(2,1)S(1)}, u32[]{:S(2)}, u32[]{:S(2)}) %collective-permute-start.8) | collective-permute-done | bytes 32800 | tf_op jit(solution)/shard_map/ppermute | solution.py:245
  29.1 1.3 %collective-permute-start.9 = (bf16[4,2048]{1,0:T(4,128)(2,1)S(1)}, bf16[4,2048]{1,0:T(4,128)(2,1)S(1)}, u32[]{:S(2)}, u32[]{:S(2)}) collective-permute-start(bf16[4,2048]{1,0:T(4,128)(2,1)S(1)} %get-tuple-element.29), channel_id=1, source_target_pairs={{0,9},{1,8},{2,10},{3,11},{4,13},{5,12},{6,14},{7,15},{8,1},{9,0},... | collective-permute-start | bytes 49160 | tf_op jit(solution)/shard_map/ppermute | solution.py:250
  30.4 0.4 %collective-permute-start.10 = (bf16[4,2048]{1,0:T(4,128)(2,1)S(1)}, bf16[4,2048]{1,0:T(4,128)(2,1)S(1)}, u32[]{:S(2)}, u32[]{:S(2)}) collective-permute-start(bf16[4,2048]{1,0:T(4,128)(2,1)S(1)} %get-tuple-element.30), channel_id=1, source_target_pairs={{0,1},{1,0},{2,3},{3,2},{4,5},{5,4},{6,7},{7,6},{8,9},{9,8},{10,11... | collective-permute-start | bytes 49160 | tf_op jit(solution)/shard_map/ppermute | solution.py:262
  30.8 2.4 %collective-permute-done.9.got_ref = bf16[4,2048]{1,0:T(4,128)(2,1)S(1)} collective-permute-done((bf16[4,2048]{1,0:T(4,128)(2,1)S(1)}, bf16[4,2048]{1,0:T(4,128)(2,1)S(1)}, u32[]{:S(2)}, u32[]{:S(2)}) %collective-permute-start.9) | collective-permute-done | bytes 16416 | tf_op jit(solution)/shard_map/ppermute | solution.py:250
  33.2 0.0 collective-permute-done.10.turned_ref
  33.2 0.6 %shard_map.81 = bf16[4,2048]{1,0:T(4,128)(2,1)} custom-call(s32[4]{0:T(128)S(4)} %shard_map.73.place_ref, f32[4,2048]{1,0:T(4,128)S(1)} %get-tuple-element.28.own_ref, bf16[4,2048]{1,0:T(4,128)(2,1)S(1)} %collective-permute-done.9.got_ref, bf16[4,2048]{1,0:T(4,128)(2,1)S(1)} %collective-permute-done.10.turned_ref), custom_call_target="tpu_custom_call" | custom-call | tf_op jit(solution)/shard_map/pallas_call | solution.py:232
  (4 shorter events, 0.1 us)
Async XLA Ops:
  0.0 12.8 %copy-start.5 = (s32[4]{0:T(128)S(1)}, s32[4]{0:T(128)}, u32[]{:S(2)}) copy-start(s32[4]{0:T(128)} %param.11) | copy-start | bytes 52
  0.0 0.8 %copy-start.2 = (bf16[4,4096]{1,0:T(4,128)(2,1)S(1)}, bf16[4,4096]{1,0:T(4,128)(2,1)}, u32[]{:S(2)}) copy-start(bf16[4,4096]{1,0:T(4,128)(2,1)} %tokens_ref) | copy-start | bytes 98308
  0.0 12.8 %copy-start.4 = (f32[4,128]{1,0:T(4,128)S(1)}, f32[4,128]{1,0:T(4,128)}, u32[]{:S(2)}) copy-start(f32[4,128]{1,0:T(4,128)} %gates_ref.1) | copy-start | bytes 6148
  0.0 12.8 %copy-start.3 = (s32[4,128]{1,0:T(4,128)S(1)}, s32[4,128]{1,0:T(4,128)}, u32[]{:S(2)}) copy-start(s32[4,128]{1,0:T(4,128)} %rows_ref.1) | copy-start | bytes 6148
  0.0 12.8 %copy-start.1 = (bf16[4096,2048]{1,0:T(8,128)(2,1)S(1)}, bf16[4096,2048]{1,0:T(8,128)(2,1)}, u32[]{:S(2)}) copy-start(bf16[4096,2048]{1,0:T(8,128)(2,1)} %wg_ref.1) | copy-start | bytes 50331652
  0.8 15.2 %copy-start = (bf16[4096,2048]{1,0:T(8,128)(2,1)S(1)}, bf16[4096,2048]{1,0:T(8,128)(2,1)}, u32[]{:S(2)}) copy-start(bf16[4096,2048]{1,0:T(8,128)(2,1)} %wu_ref.1) | copy-start | bytes 50331652
  0.8 6.3 %collective-permute-start.3 = (bf16[4,4096]{1,0:T(4,128)(2,1)S(1)}, bf16[4,4096]{1,0:T(4,128)(2,1)S(1)}, u32[]{:S(2)}, u32[]{:S(2)}) collective-permute-start(bf16[4,4096]{1,0:T(4,128)(2,1)S(1)} %copy-done.2), channel_id=1, source_target_pairs={{1,2},{3,0},{5,6},{7,4},{9,10},{11,8},{13,14},{15,12},{0,7},{2,5},... | collective-permute-start | bytes 98312 | tf_op jit(solution)/shard_map/ppermute | solution.py:254
  4.2 6.4 %collective-permute-start.2 = (bf16[4,4096]{1,0:T(4,128)(2,1)S(1)}, bf16[4,4096]{1,0:T(4,128)(2,1)S(1)}, u32[]{:S(2)}, u32[]{:S(2)}) collective-permute-start(bf16[4,4096]{1,0:T(4,128)(2,1)S(1)} %copy-done.2), channel_id=1, source_target_pairs={{1,14},{3,12},{5,10},{7,8},{9,6},{11,4},{13,2},{15,0},{0,11},{2,9}... | collective-permute-start | bytes 98312 | tf_op jit(solution)/shard_map/ppermute | solution.py:254
  6.0 5.4 %collective-permute-start.1 = (bf16[4,4096]{1,0:T(4,128)(2,1)S(1)}, bf16[4,4096]{1,0:T(4,128)(2,1)S(1)}, u32[]{:S(2)}, u32[]{:S(2)}) collective-permute-start(bf16[4,4096]{1,0:T(4,128)(2,1)S(1)} %copy-done.2), channel_id=1, source_target_pairs={{1,12},{3,14},{5,8},{7,10},{9,4},{11,6},{13,0},{15,2},{0,9},{2,11}... | collective-permute-start | bytes 98312 | tf_op jit(solution)/shard_map/ppermute | solution.py:254
  6.0 5.4 %collective-permute-start = (bf16[4,4096]{1,0:T(4,128)(2,1)S(1)}, bf16[4,4096]{1,0:T(4,128)(2,1)S(1)}, u32[]{:S(2)}, u32[]{:S(2)}) collective-permute-start(bf16[4,4096]{1,0:T(4,128)(2,1)S(1)} %copy-done.2), channel_id=1, source_target_pairs={{1,4},{3,6},{5,0},{7,2},{9,12},{11,14},{13,8},{15,10},{0,5},{2,7},... | collective-permute-start | bytes 98312 | tf_op jit(solution)/shard_map/ppermute | solution.py:254
  11.4 1.4 %collective-permute-start.4 = (bf16[4,4,4096]{2,1,0:T(4,128)(2,1)S(1)}, bf16[4,4,4096]{2,1,0:T(4,128)(2,1)S(1)}, u32[]{:S(2)}, u32[]{:S(2)}) collective-permute-start(bf16[4,4,4096]{2,1,0:T(4,128)(2,1)S(1)} %shard_map.74.mine_ref), channel_id=1, source_target_pairs={{0,1},{1,0},{2,3},{3,2},{4,5},{5,4},{6,7},{7,6},{8,9},{9,8},{10,11... | collective-permute-start | bytes 393224 | tf_op jit(solution)/shard_map/ppermute | solution.py:262
  12.9 6.2 %slice-start = ((s8[16777216]{0:T(1024)(128)(4,1)}), s8[4194304]{0:T(1024)(128)(4,1)S(1)}, s32[]{:S(2)}) async-start(s8[16777216]{0:T(1024)(128)(4,1)} %bitcast.1), calls=%async_computation | async-start | bytes 8388608
  12.9 6.2 %slice-start.1 = ((s8[16777216]{0:T(1024)(128)(4,1)}), s8[4194304]{0:T(1024)(128)(4,1)S(1)}, s32[]{:S(2)}) async-start(s8[16777216]{0:T(1024)(128)(4,1)} %bitcast.1), calls=%async_computation.1 | async-start | bytes 8388608
  12.9 6.2 %slice-start.2 = ((s8[16777216]{0:T(1024)(128)(4,1)}), s8[4194304]{0:T(1024)(128)(4,1)S(1)}, s32[]{:S(2)}) async-start(s8[16777216]{0:T(1024)(128)(4,1)} %bitcast.1), calls=%async_computation.2 | async-start | bytes 8388608
  16.0 3.1 %slice-start.3 = ((s8[16777216]{0:T(1024)(128)(4,1)}), s8[4194304]{0:T(1024)(128)(4,1)S(1)}, s32[]{:S(2)}) async-start(s8[16777216]{0:T(1024)(128)(4,1)} %bitcast.1), calls=%async_computation.3 | async-start | bytes 8388608
  20.7 1.8 %collective-permute-start.5 = (bf16[32,2048]{1,0:T(8,128)(2,1)S(1)}, bf16[32,2048]{1,0:T(8,128)(2,1)S(1)}, u32[]{:S(2)}, u32[]{:S(2)}) collective-permute-start(bf16[32,2048]{1,0:T(8,128)(2,1)S(1)} %shard_map.78), channel_id=1, source_target_pairs={{0,1},{1,0},{2,3},{3,2},{4,5},{5,4},{6,7},{7,6},{8,9},{9,8},{10,11... | collective-permute-start | bytes 393224 | tf_op jit(solution)/shard_map/ppermute | solution.py:262
  22.6 4.3 %collective-permute-start.6 = (bf16[2,4,2048]{2,1,0:T(4,128)(2,1)S(1)}, bf16[2,4,2048]{2,1,0:T(4,128)(2,1)S(1)}, u32[]{:S(2)}, u32[]{:S(2)}) collective-permute-start(bf16[2,4,2048]{2,1,0:T(4,128)(2,1)S(1)} %get-tuple-element.25), channel_id=1, source_target_pairs={{0,7},{1,6},{2,5},{3,4},{4,3},{5,2},{6,1},{7,0},{8,15},{9,14},{10,... | collective-permute-start | bytes 98312 | tf_op jit(solution)/shard_map/ppermute | solution.py:245
  23.7 4.3 %collective-permute-start.7 = (bf16[2,4,2048]{2,1,0:T(4,128)(2,1)S(1)}, bf16[2,4,2048]{2,1,0:T(4,128)(2,1)S(1)}, u32[]{:S(2)}, u32[]{:S(2)}) collective-permute-start(bf16[2,4,2048]{2,1,0:T(4,128)(2,1)S(1)} %get-tuple-element.26), channel_id=1, source_target_pairs={{0,4},{1,5},{2,6},{3,7},{4,0},{5,1},{6,2},{7,3},{8,12},{9,13},{10,... | collective-permute-start | bytes 98312 | tf_op jit(solution)/shard_map/ppermute | solution.py:245
  25.5 3.5 %collective-permute-start.8 = (bf16[2,4,2048]{2,1,0:T(4,128)(2,1)S(1)}, bf16[2,4,2048]{2,1,0:T(4,128)(2,1)S(1)}, u32[]{:S(2)}, u32[]{:S(2)}) collective-permute-start(bf16[2,4,2048]{2,1,0:T(4,128)(2,1)S(1)} %get-tuple-element.27), channel_id=1, source_target_pairs={{0,3},{1,2},{2,1},{3,0},{4,7},{5,6},{6,5},{7,4},{8,11},{9,10},{10,... | collective-permute-start | bytes 98312 | tf_op jit(solution)/shard_map/ppermute | solution.py:245
  29.1 4.1 %collective-permute-start.9 = (bf16[4,2048]{1,0:T(4,128)(2,1)S(1)}, bf16[4,2048]{1,0:T(4,128)(2,1)S(1)}, u32[]{:S(2)}, u32[]{:S(2)}) collective-permute-start(bf16[4,2048]{1,0:T(4,128)(2,1)S(1)} %get-tuple-element.29), channel_id=1, source_target_pairs={{0,9},{1,8},{2,10},{3,11},{4,13},{5,12},{6,14},{7,15},{8,1},{9,0},... | collective-permute-start | bytes 49160 | tf_op jit(solution)/shard_map/ppermute | solution.py:250
  30.4 2.8 %collective-permute-start.10 = (bf16[4,2048]{1,0:T(4,128)(2,1)S(1)}, bf16[4,2048]{1,0:T(4,128)(2,1)S(1)}, u32[]{:S(2)}, u32[]{:S(2)}) collective-permute-start(bf16[4,2048]{1,0:T(4,128)(2,1)S(1)} %get-tuple-element.30), channel_id=1, source_target_pairs={{0,1},{1,0},{2,3},{3,2},{4,5},{5,4},{6,7},{7,6},{8,9},{9,8},{10,11... | collective-permute-start | bytes 49160 | tf_op jit(solution)/shard_map/ppermute | solution.py:262

commit v17 on v16

--- a/solution.py
+++ b/solution.py
@@ -11,7 +11,7 @@
 CAP = 3
 TILE = 512
 MIB = 1 << 20
-ORDER = (0, 6, 7, 1, 2, 4, 5, 3)
+ORDER = (0, 3, 7, 5, 2, 1, 6, 4)
 SOURCES = len(ORDER)
 GATE = 5_000_000_000
 UP = 2_000_000_000

time: 34 us -> 33.7 us (level)
  waiting for transfers between devices: 11.3 us -> 9.7 us
  starting transfers between devices: 11.6 us -> 12.9 us
    ppermute x4, starting transfers between devices: 6.27 us -> 7.75 us  [fetched(): lax.ppermute(x, ('exp', 'hid'), [(2 * i + 1 - side, 2 * (i ^ k) + side) f...]
    ppermute x4, waiting for transfers between devices: 4.35 us -> 3.07 us  [fetched(): lax.ppermute(x, ('exp', 'hid'), [(2 * i + 1 - side, 2 * (i ^ k) + side) f...]
    ppermute x3, waiting for transfers between devices: 3.44 us -> 3.03 us  [swapped(): return lax.ppermute(x, ('exp', 'hid'), pairs)]
    ppermute x3, starting transfers between devices: 1 us -> 0.63 us  [swap_cores(): return lax.ppermute(x, 'hid', [(0, 1), (1, 0)])]
where the time goes in v17:
time: 33.7 us; the launch traced here: 33.5 us
  starting transfers between devices  12.9 us (38%)
  Pallas kernels  10 us (30%)
  waiting for transfers between devices  9.7 us (29%)
  local copies, waits for them, and re-layouts  0.78 us (2%)
    ppermute x4, starting transfers between devices, fetched(): lax.ppermute(x, ('exp', 'hid'), [(2 * i + 1 - side, 2 * (i ^ k) + side) f...  7.75 us
    pallas_call x1, Pallas kernels, gate_rows(): pl.pallas_call(functools.partial(gate_kernel, SOURCES // block_rows.shape...  3.12 us
    pallas_call x2, Pallas kernels, down_half(): pl.pallas_call(functools.partial(down_kernel, other), out_shape=jax.Shape...  3.12 us
    ppermute x4, waiting for transfers between devices, fetched(): lax.ppermute(x, ('exp', 'hid'), [(2 * i + 1 - side, 2 * (i ^ k) + side) f...  3.07 us
    ppermute x3, waiting for transfers between devices, swapped(): return lax.ppermute(x, ('exp', 'hid'), pairs)  3.03 us
    ppermute x3, starting transfers between devices, swapped(): return lax.ppermute(x, ('exp', 'hid'), pairs)  3.01 us
    pallas_call x1, Pallas kernels, hidden_rows(): pl.pallas_call(up_kernel, out_shape=jax.ShapeDtypeStruct(act.shape, jnp.b...  3.01 us
    ppermute x1, waiting for transfers between devices, sent_home(): return lax.ppermute(x, ('exp', 'hid'), pairs)  2.26 us
  transfers between devices with their start and end apart: 11, of which 7 were waited for; matrix products, arithmetic and copies ran while one was open for 0% of the time, Pallas kernels for 5%

profile of v17, /device:TPU:0, one launch (start us, length us, event | category | flops | bytes accessed | tf_op | source)
XLA Modules:
  0.0 33.5 jit_solution(1567103945768118097)
XLA Ops:
  0.0 0.0 copy-start.5
  0.0 0.0 copy-start.2
  0.0 0.0 copy-start.4
  0.0 0.0 copy-start.3
  0.0 0.0 copy-start.1
  0.0 0.7 %copy-done.2 = bf16[4,4096]{1,0:T(4,128)(2,1)S(1)} copy-done((bf16[4,4096]{1,0:T(4,128)(2,1)S(1)}, bf16[4,4096]{1,0:T(4,128)(2,1)}, u32[]{:S(2)}) %copy-start.2) | copy-done | bytes 32792
  0.8 0.0 copy-start
  0.8 3.5 %collective-permute-start.3 = (bf16[4,4096]{1,0:T(4,128)(2,1)S(1)}, bf16[4,4096]{1,0:T(4,128)(2,1)S(1)}, u32[]{:S(2)}, u32[]{:S(2)}) collective-permute-start(bf16[4,4096]{1,0:T(4,128)(2,1)S(1)} %copy-done.2), channel_id=1, source_target_pairs={{1,10},{3,8},{5,14},{7,12},{9,2},{11,0},{13,6},{15,4},{0,9},{2,11}... | collective-permute-start | bytes 98312 | tf_op jit(solution)/shard_map/ppermute | solution.py:254
  4.3 2.6 %collective-permute-start.2 = (bf16[4,4096]{1,0:T(4,128)(2,1)S(1)}, bf16[4,4096]{1,0:T(4,128)(2,1)S(1)}, u32[]{:S(2)}, u32[]{:S(2)}) collective-permute-start(bf16[4,4096]{1,0:T(4,128)(2,1)S(1)} %copy-done.2), channel_id=1, source_target_pairs={{1,14},{3,12},{5,10},{7,8},{9,6},{11,4},{13,2},{15,0},{0,13},{2,15... | collective-permute-start | bytes 98312 | tf_op jit(solution)/shard_map/ppermute | solution.py:254
  6.8 0.2 collective-permute-start.1
  7.0 1.5 %collective-permute-start = (bf16[4,4096]{1,0:T(4,128)(2,1)S(1)}, bf16[4,4096]{1,0:T(4,128)(2,1)S(1)}, u32[]{:S(2)}, u32[]{:S(2)}) collective-permute-start(bf16[4,4096]{1,0:T(4,128)(2,1)S(1)} %copy-done.2), channel_id=1, source_target_pairs={{1,4},{3,6},{5,0},{7,2},{9,12},{11,14},{13,8},{15,10},{0,5},{2,7},... | collective-permute-start | bytes 98312 | tf_op jit(solution)/shard_map/ppermute | solution.py:254
  8.5 0.0 collective-permute-done.3.refs_3_
  8.5 1.8 %collective-permute-done.2.refs_2_ = bf16[4,4096]{1,0:T(4,128)(2,1)S(1)} collective-permute-done((bf16[4,4096]{1,0:T(4,128)(2,1)S(1)}, bf16[4,4096]{1,0:T(4,128)(2,1)S(1)}, u32[]{:S(2)}, u32[]{:S(2)}) %collective-permute-start.2) | collective-permute-done | bytes 32800 | tf_op jit(solution)/shard_map/ppermute | solution.py:254
  10.3 1.3 %collective-permute-done.1.refs_1_ = bf16[4,4096]{1,0:T(4,128)(2,1)S(1)} collective-permute-done((bf16[4,4096]{1,0:T(4,128)(2,1)S(1)}, bf16[4,4096]{1,0:T(4,128)(2,1)S(1)}, u32[]{:S(2)}, u32[]{:S(2)}) %collective-permute-start.1) | collective-permute-done | bytes 32800 | tf_op jit(solution)/shard_map/ppermute | solution.py:254
  11.6 0.0 collective-permute-done.refs_0_
  11.6 0.1 collective-permute-start.4
  11.7 1.3 %collective-permute-done.4.got_ref = bf16[4,4,4096]{2,1,0:T(4,128)(2,1)S(1)} collective-permute-done((bf16[4,4,4096]{2,1,0:T(4,128)(2,1)S(1)}, bf16[4,4,4096]{2,1,0:T(4,128)(2,1)S(1)}, u32[]{:S(2)}, u32[]{:S(2)}) %collective-permute-start.4) | collective-permute-done | bytes 131104 | tf_op jit(solution)/shard_map/ppermute | solution.py:262
  13.0 0.0 copy-done.5
  13.0 0.0 copy-done.4
  13.0 0.0 copy-done.3
  13.0 0.0 copy-done.1
  13.1 0.0 slice-start
  13.1 0.0 slice-start.1
  13.1 0.0 slice-start.2
  13.1 3.1 %shard_map.75 = (bf16[32,4096]{1,0:T(8,128)(2,1)S(1)}, f32[32,2048]{1,0:T(8,128)S(1)}, f32[32,128]{1,0:T(8,128)S(1)}) custom-call(s32[4]{0:T(128)S(4)} %shard_map.73.place_ref, s32[1,4]{1,0:T(1,128)S(1)} %bitcast.3, bf16[4,4096]{1,0:T(4,128)(2,1)S(1)} %copy-done.2, bf16[4,4,4096]{2,1,0:T(4,128)(2,1)S(1)} %shard_map.74.mine_ref, ...), custom_call_target="tpu_custom_call" | custom-call | flops 5000000000 | tf_op jit(solution)/shard_map/pallas_call | solution.py:126
  16.2 0.0 copy-done
  16.2 0.0 slice-start.3
  16.2 3.0 %shard_map.76.h_ref = bf16[32,2048]{1,0:T(8,128)(2,1)S(1)} custom-call(bf16[32,4096]{1,0:T(8,128)(2,1)S(1)} %get-tuple-element.22.x_ref, f32[32,2048]{1,0:T(8,128)S(1)} %get-tuple-element.23.act_ref, bf16[4096,2048]{1,0:T(8,128)(2,1)S(1)} %copy-done), custom_call_target="tpu_custom_call" | custom-call | flops 2000000000 | tf_op jit(solution)/shard_map/pallas_call | solution.py:149
  19.2 0.0 slice-done
  19.3 0.0 slice-done.1
  19.3 0.0 slice-done.2
  19.3 0.0 slice-done.3
  19.3 1.6 %shard_map.78 = bf16[32,2048]{1,0:T(8,128)(2,1)S(1)} custom-call(s32[4]{0:T(128)S(4)} %shard_map.73.place_ref, bf16[32,2048]{1,0:T(8,128)(2,1)S(1)} %shard_map.76.h_ref, bf16[2048,4096]{1,0:T(8,128)(2,1)S(1)} %bitcast.2), custom_call_target="tpu_custom_call" | custom-call | flops 268435456 | tf_op jit(solution)/shard_map/pallas_call | solution.py:172
  20.9 0.2 collective-permute-start.5
  21.0 1.6 %shard_map.77.keep_ref = f32[32,2048]{1,0:T(8,128)S(1)} custom-call(s32[4]{0:T(128)S(4)} %shard_map.73.place_ref, bf16[32,2048]{1,0:T(8,128)(2,1)S(1)} %shard_map.76.h_ref, bf16[2048,4096]{1,0:T(8,128)(2,1)S(1)} %bitcast.2), custom_call_target="tpu_custom_call" | custom-call | flops 268435456 | tf_op jit(solution)/shard_map/pallas_call | solution.py:172
  22.6 0.0 collective-permute-done.5.got_ref
  22.6 0.1 shard_map.79
  22.7 1.3 %collective-permute-start.6 = (bf16[2,4,2048]{2,1,0:T(4,128)(2,1)S(1)}, bf16[2,4,2048]{2,1,0:T(4,128)(2,1)S(1)}, u32[]{:S(2)}, u32[]{:S(2)}) collective-permute-start(bf16[2,4,2048]{2,1,0:T(4,128)(2,1)S(1)} %get-tuple-element.25), channel_id=1, source_target_pairs={{0,7},{1,6},{2,5},{3,4},{4,3},{5,2},{6,1},{7,0},{8,15},{9,14},{10,... | collective-permute-start | bytes 98312 | tf_op jit(solution)/shard_map/ppermute | solution.py:245
  24.0 1.2 %collective-permute-start.7 = (bf16[2,4,2048]{2,1,0:T(4,128)(2,1)S(1)}, bf16[2,4,2048]{2,1,0:T(4,128)(2,1)S(1)}, u32[]{:S(2)}, u32[]{:S(2)}) collective-permute-start(bf16[2,4,2048]{2,1,0:T(4,128)(2,1)S(1)} %get-tuple-element.26), channel_id=1, source_target_pairs={{0,4},{1,5},{2,6},{3,7},{4,0},{5,1},{6,2},{7,3},{8,12},{9,13},{10,... | collective-permute-start | bytes 98312 | tf_op jit(solution)/shard_map/ppermute | solution.py:245
  25.1 0.6 %collective-permute-start.8 = (bf16[2,4,2048]{2,1,0:T(4,128)(2,1)S(1)}, bf16[2,4,2048]{2,1,0:T(4,128)(2,1)S(1)}, u32[]{:S(2)}, u32[]{:S(2)}) collective-permute-start(bf16[2,4,2048]{2,1,0:T(4,128)(2,1)S(1)} %get-tuple-element.27), channel_id=1, source_target_pairs={{0,3},{1,2},{2,1},{3,0},{4,7},{5,6},{6,5},{7,4},{8,11},{9,10},{10,... | collective-permute-start | bytes 98312 | tf_op jit(solution)/shard_map/ppermute | solution.py:245
  25.7 1.3 %collective-permute-done.6.refs_1_ = bf16[2,4,2048]{2,1,0:T(4,128)(2,1)S(1)} collective-permute-done((bf16[2,4,2048]{2,1,0:T(4,128)(2,1)S(1)}, bf16[2,4,2048]{2,1,0:T(4,128)(2,1)S(1)}, u32[]{:S(2)}, u32[]{:S(2)}) %collective-permute-start.6) | collective-permute-done | bytes 32800 | tf_op jit(solution)/shard_map/ppermute | solution.py:245
  27.0 0.9 %collective-permute-done.7.refs_2_ = bf16[2,4,2048]{2,1,0:T(4,128)(2,1)S(1)} collective-permute-done((bf16[2,4,2048]{2,1,0:T(4,128)(2,1)S(1)}, bf16[2,4,2048]{2,1,0:T(4,128)(2,1)S(1)}, u32[]{:S(2)}, u32[]{:S(2)}) %collective-permute-start.7) | collective-permute-done | bytes 32800 | tf_op jit(solution)/shard_map/ppermute | solution.py:245
  27.9 0.9 %collective-permute-done.8.refs_3_ = bf16[2,4,2048]{2,1,0:T(4,128)(2,1)S(1)} collective-permute-done((bf16[2,4,2048]{2,1,0:T(4,128)(2,1)S(1)}, bf16[2,4,2048]{2,1,0:T(4,128)(2,1)S(1)}, u32[]{:S(2)}, u32[]{:S(2)}) %collective-permute-start.8) | collective-permute-done | bytes 32800 | tf_op jit(solution)/shard_map/ppermute | solution.py:245
  28.8 1.5 %collective-permute-start.9 = (bf16[4,2048]{1,0:T(4,128)(2,1)S(1)}, bf16[4,2048]{1,0:T(4,128)(2,1)S(1)}, u32[]{:S(2)}, u32[]{:S(2)}) collective-permute-start(bf16[4,2048]{1,0:T(4,128)(2,1)S(1)} %get-tuple-element.29), channel_id=1, source_target_pairs={{0,9},{1,8},{2,10},{3,11},{4,13},{5,12},{6,14},{7,15},{8,1},{9,0},... | collective-permute-start | bytes 49160 | tf_op jit(solution)/shard_map/ppermute | solution.py:250
  30.3 0.4 %collective-permute-start.10 = (bf16[4,2048]{1,0:T(4,128)(2,1)S(1)}, bf16[4,2048]{1,0:T(4,128)(2,1)S(1)}, u32[]{:S(2)}, u32[]{:S(2)}) collective-permute-start(bf16[4,2048]{1,0:T(4,128)(2,1)S(1)} %get-tuple-element.30), channel_id=1, source_target_pairs={{0,1},{1,0},{2,3},{3,2},{4,5},{5,4},{6,7},{7,6},{8,9},{9,8},{10,11... | collective-permute-start | bytes 49160 | tf_op jit(solution)/shard_map/ppermute | solution.py:262
  30.7 2.3 %collective-permute-done.9.got_ref = bf16[4,2048]{1,0:T(4,128)(2,1)S(1)} collective-permute-done((bf16[4,2048]{1,0:T(4,128)(2,1)S(1)}, bf16[4,2048]{1,0:T(4,128)(2,1)S(1)}, u32[]{:S(2)}, u32[]{:S(2)}) %collective-permute-start.9) | collective-permute-done | bytes 16416 | tf_op jit(solution)/shard_map/ppermute | solution.py:250
  32.9 0.0 collective-permute-done.10.turned_ref
  32.9 0.6 %shard_map.81 = bf16[4,2048]{1,0:T(4,128)(2,1)} custom-call(s32[4]{0:T(128)S(4)} %shard_map.73.place_ref, f32[4,2048]{1,0:T(4,128)S(1)} %get-tuple-element.28.own_ref, bf16[4,2048]{1,0:T(4,128)(2,1)S(1)} %collective-permute-done.9.got_ref, bf16[4,2048]{1,0:T(4,128)(2,1)S(1)} %collective-permute-done.10.turned_ref), custom_call_target="tpu_custom_call" | custom-call | tf_op jit(solution)/shard_map/pallas_call | solution.py:232
  (4 shorter events, 0.1 us)
Async XLA Ops:
  0.0 13.0 %copy-start.5 = (s32[4]{0:T(128)S(1)}, s32[4]{0:T(128)}, u32[]{:S(2)}) copy-start(s32[4]{0:T(128)} %param.11) | copy-start | bytes 52
  0.0 0.8 %copy-start.2 = (bf16[4,4096]{1,0:T(4,128)(2,1)S(1)}, bf16[4,4096]{1,0:T(4,128)(2,1)}, u32[]{:S(2)}) copy-start(bf16[4,4096]{1,0:T(4,128)(2,1)} %tokens_ref) | copy-start | bytes 98308
  0.0 13.0 %copy-start.4 = (f32[4,128]{1,0:T(4,128)S(1)}, f32[4,128]{1,0:T(4,128)}, u32[]{:S(2)}) copy-start(f32[4,128]{1,0:T(4,128)} %gates_ref.1) | copy-start | bytes 6148
  0.0 13.0 %copy-start.3 = (s32[4,128]{1,0:T(4,128)S(1)}, s32[4,128]{1,0:T(4,128)}, u32[]{:S(2)}) copy-start(s32[4,128]{1,0:T(4,128)} %rows_ref.1) | copy-start | bytes 6148
  0.0 13.0 %copy-start.1 = (bf16[4096,2048]{1,0:T(8,128)(2,1)S(1)}, bf16[4096,2048]{1,0:T(8,128)(2,1)}, u32[]{:S(2)}) copy-start(bf16[4096,2048]{1,0:T(8,128)(2,1)} %wg_ref.1) | copy-start | bytes 50331652
  0.8 15.4 %copy-start = (bf16[4096,2048]{1,0:T(8,128)(2,1)S(1)}, bf16[4096,2048]{1,0:T(8,128)(2,1)}, u32[]{:S(2)}) copy-start(bf16[4096,2048]{1,0:T(8,128)(2,1)} %wu_ref.1) | copy-start | bytes 50331652
  0.8 7.8 %collective-permute-start.3 = (bf16[4,4096]{1,0:T(4,128)(2,1)S(1)}, bf16[4,4096]{1,0:T(4,128)(2,1)S(1)}, u32[]{:S(2)}, u32[]{:S(2)}) collective-permute-start(bf16[4,4096]{1,0:T(4,128)(2,1)S(1)} %copy-done.2), channel_id=1, source_target_pairs={{1,10},{3,8},{5,14},{7,12},{9,2},{11,0},{13,6},{15,4},{0,9},{2,11}... | collective-permute-start | bytes 98312 | tf_op jit(solution)/shard_map/ppermute | solution.py:254
  4.3 6.1 %collective-permute-start.2 = (bf16[4,4096]{1,0:T(4,128)(2,1)S(1)}, bf16[4,4096]{1,0:T(4,128)(2,1)S(1)}, u32[]{:S(2)}, u32[]{:S(2)}) collective-permute-start(bf16[4,4096]{1,0:T(4,128)(2,1)S(1)} %copy-done.2), channel_id=1, source_target_pairs={{1,14},{3,12},{5,10},{7,8},{9,6},{11,4},{13,2},{15,0},{0,13},{2,15... | collective-permute-start | bytes 98312 | tf_op jit(solution)/shard_map/ppermute | solution.py:254
  6.8 4.8 %collective-permute-start.1 = (bf16[4,4096]{1,0:T(4,128)(2,1)S(1)}, bf16[4,4096]{1,0:T(4,128)(2,1)S(1)}, u32[]{:S(2)}, u32[]{:S(2)}) collective-permute-start(bf16[4,4096]{1,0:T(4,128)(2,1)S(1)} %copy-done.2), channel_id=1, source_target_pairs={{1,6},{3,4},{5,2},{7,0},{9,14},{11,12},{13,10},{15,8},{0,3},{2,1},... | collective-permute-start | bytes 98312 | tf_op jit(solution)/shard_map/ppermute | solution.py:254
  7.0 4.6 %collective-permute-start = (bf16[4,4096]{1,0:T(4,128)(2,1)S(1)}, bf16[4,4096]{1,0:T(4,128)(2,1)S(1)}, u32[]{:S(2)}, u32[]{:S(2)}) collective-permute-start(bf16[4,4096]{1,0:T(4,128)(2,1)S(1)} %copy-done.2), channel_id=1, source_target_pairs={{1,4},{3,6},{5,0},{7,2},{9,12},{11,14},{13,8},{15,10},{0,5},{2,7},... | collective-permute-start | bytes 98312 | tf_op jit(solution)/shard_map/ppermute | solution.py:254
  11.6 1.4 %collective-permute-start.4 = (bf16[4,4,4096]{2,1,0:T(4,128)(2,1)S(1)}, bf16[4,4,4096]{2,1,0:T(4,128)(2,1)S(1)}, u32[]{:S(2)}, u32[]{:S(2)}) collective-permute-start(bf16[4,4,4096]{2,1,0:T(4,128)(2,1)S(1)} %shard_map.74.mine_ref), channel_id=1, source_target_pairs={{0,1},{1,0},{2,3},{3,2},{4,5},{5,4},{6,7},{7,6},{8,9},{9,8},{10,11... | collective-permute-start | bytes 393224 | tf_op jit(solution)/shard_map/ppermute | solution.py:262
  13.1 6.2 %slice-start = ((s8[16777216]{0:T(1024)(128)(4,1)}), s8[4194304]{0:T(1024)(128)(4,1)S(1)}, s32[]{:S(2)}) async-start(s8[16777216]{0:T(1024)(128)(4,1)} %bitcast.1), calls=%async_computation | async-start | bytes 8388608
  13.1 6.2 %slice-start.1 = ((s8[16777216]{0:T(1024)(128)(4,1)}), s8[4194304]{0:T(1024)(128)(4,1)S(1)}, s32[]{:S(2)}) async-start(s8[16777216]{0:T(1024)(128)(4,1)} %bitcast.1), calls=%async_computation.1 | async-start | bytes 8388608
  13.1 6.2 %slice-start.2 = ((s8[16777216]{0:T(1024)(128)(4,1)}), s8[4194304]{0:T(1024)(128)(4,1)S(1)}, s32[]{:S(2)}) async-start(s8[16777216]{0:T(1024)(128)(4,1)} %bitcast.1), calls=%async_computation.2 | async-start | bytes 8388608
  16.2 3.1 %slice-start.3 = ((s8[16777216]{0:T(1024)(128)(4,1)}), s8[4194304]{0:T(1024)(128)(4,1)S(1)}, s32[]{:S(2)}) async-start(s8[16777216]{0:T(1024)(128)(4,1)} %bitcast.1), calls=%async_computation.3 | async-start | bytes 8388608
  20.9 1.7 %collective-permute-start.5 = (bf16[32,2048]{1,0:T(8,128)(2,1)S(1)}, bf16[32,2048]{1,0:T(8,128)(2,1)S(1)}, u32[]{:S(2)}, u32[]{:S(2)}) collective-permute-start(bf16[32,2048]{1,0:T(8,128)(2,1)S(1)} %shard_map.78), channel_id=1, source_target_pairs={{0,1},{1,0},{2,3},{3,2},{4,5},{5,4},{6,7},{7,6},{8,9},{9,8},{10,11... | collective-permute-start | bytes 393224 | tf_op jit(solution)/shard_map/ppermute | solution.py:262
  22.7 4.3 %collective-permute-start.6 = (bf16[2,4,2048]{2,1,0:T(4,128)(2,1)S(1)}, bf16[2,4,2048]{2,1,0:T(4,128)(2,1)S(1)}, u32[]{:S(2)}, u32[]{:S(2)}) collective-permute-start(bf16[2,4,2048]{2,1,0:T(4,128)(2,1)S(1)} %get-tuple-element.25), channel_id=1, source_target_pairs={{0,7},{1,6},{2,5},{3,4},{4,3},{5,2},{6,1},{7,0},{8,15},{9,14},{10,... | collective-permute-start | bytes 98312 | tf_op jit(solution)/shard_map/ppermute | solution.py:245
  24.0 3.9 %collective-permute-start.7 = (bf16[2,4,2048]{2,1,0:T(4,128)(2,1)S(1)}, bf16[2,4,2048]{2,1,0:T(4,128)(2,1)S(1)}, u32[]{:S(2)}, u32[]{:S(2)}) collective-permute-start(bf16[2,4,2048]{2,1,0:T(4,128)(2,1)S(1)} %get-tuple-element.26), channel_id=1, source_target_pairs={{0,4},{1,5},{2,6},{3,7},{4,0},{5,1},{6,2},{7,3},{8,12},{9,13},{10,... | collective-permute-start | bytes 98312 | tf_op jit(solution)/shard_map/ppermute | solution.py:245
  25.1 3.6 %collective-permute-start.8 = (bf16[2,4,2048]{2,1,0:T(4,128)(2,1)S(1)}, bf16[2,4,2048]{2,1,0:T(4,128)(2,1)S(1)}, u32[]{:S(2)}, u32[]{:S(2)}) collective-permute-start(bf16[2,4,2048]{2,1,0:T(4,128)(2,1)S(1)} %get-tuple-element.27), channel_id=1, source_target_pairs={{0,3},{1,2},{2,1},{3,0},{4,7},{5,6},{6,5},{7,4},{8,11},{9,10},{10,... | collective-permute-start | bytes 98312 | tf_op jit(solution)/shard_map/ppermute | solution.py:245
  28.8 4.1 %collective-permute-start.9 = (bf16[4,2048]{1,0:T(4,128)(2,1)S(1)}, bf16[4,2048]{1,0:T(4,128)(2,1)S(1)}, u32[]{:S(2)}, u32[]{:S(2)}) collective-permute-start(bf16[4,2048]{1,0:T(4,128)(2,1)S(1)} %get-tuple-element.29), channel_id=1, source_target_pairs={{0,9},{1,8},{2,10},{3,11},{4,13},{5,12},{6,14},{7,15},{8,1},{9,0},... | collective-permute-start | bytes 49160 | tf_op jit(solution)/shard_map/ppermute | solution.py:250
  30.3 2.7 %collective-permute-start.10 = (bf16[4,2048]{1,0:T(4,128)(2,1)S(1)}, bf16[4,2048]{1,0:T(4,128)(2,1)S(1)}, u32[]{:S(2)}, u32[]{:S(2)}) collective-permute-start(bf16[4,2048]{1,0:T(4,128)(2,1)S(1)} %get-tuple-element.30), channel_id=1, source_target_pairs={{0,1},{1,0},{2,3},{3,2},{4,5},{5,4},{6,7},{7,6},{8,9},{9,8},{10,11... | collective-permute-start | bytes 49160 | tf_op jit(solution)/shard_map/ppermute | solution.py:262

commit v18 on v15

--- a/solution.py
+++ b/solution.py
@@ -34,7 +34,7 @@
 
 
 def turned(i):
-    return (1 + i) % 2
+    return (1 + i + i // 2) % 2
 
 
 def first_kernel(place_ref):

time: 32.9 us -> 32.9 us (level)
  waiting for transfers between devices: 8.71 us -> 8.25 us
    ppermute x3, waiting for transfers between devices: 2.63 us -> 2.14 us  [swapped(): return lax.ppermute(x, ('exp', 'hid'), pairs)]
    ppermute x3, starting transfers between devices: 1.55 us -> 1.15 us  [swap_cores(): return lax.ppermute(x, 'hid', [(0, 1), (1, 0)])]
    ppermute x1, starting transfers between devices: 2.33 us -> 2.69 us  [sent_home(): return lax.ppermute(x, ('exp', 'hid'), pairs)]
  transfers between devices with their start and end apart: 11 -> 11, of which waited for: 7 -> 6; matrix products, arithmetic and copies ran while one was open for 0% -> 0% of each run, Pallas kernels for 5% -> 5%
where the time goes in v18:
time: 32.9 us; the launch traced here: 32.6 us
  starting transfers between devices  13.4 us (41%)
  Pallas kernels  10 us (30%)
  waiting for transfers between devices  8.25 us (25%)
  local copies, waits for them, and re-layouts  0.77 us (2%)
    ppermute x4, starting transfers between devices, fetched(): lax.ppermute(x, ('exp', 'hid'), [(2 * i + 1 - side, 2 * (i ^ k) + side) f...  6.27 us
    ppermute x4, waiting for transfers between devices, fetched(): lax.ppermute(x, ('exp', 'hid'), [(2 * i + 1 - side, 2 * (i ^ k) + side) f...  3.69 us
    ppermute x3, starting transfers between devices, swapped(): return lax.ppermute(x, ('exp', 'hid'), pairs)  3.27 us
    pallas_call x1, Pallas kernels, gate_rows(): pl.pallas_call(functools.partial(gate_kernel, SOURCES // block_rows.shape...  3.12 us
    pallas_call x2, Pallas kernels, down_half(): pl.pallas_call(functools.partial(down_kernel, other), out_shape=jax.Shape...  3.12 us
    pallas_call x1, Pallas kernels, hidden_rows(): pl.pallas_call(up_kernel, out_shape=jax.ShapeDtypeStruct(act.shape, jnp.b...  3.01 us
    ppermute x1, starting transfers between devices, sent_home(): return lax.ppermute(x, ('exp', 'hid'), pairs)  2.69 us
    ppermute x3, waiting for transfers between devices, swapped(): return lax.ppermute(x, ('exp', 'hid'), pairs)  2.14 us
  transfers between devices with their start and end apart: 11, of which 6 were waited for; matrix products, arithmetic and copies ran while one was open for 0% of the time, Pallas kernels for 5%

profile of v18, /device:TPU:0, one launch (start us, length us, event | category | flops | bytes accessed | tf_op | source)
XLA Modules:
  0.0 32.6 jit_solution(1535277896430685850)
XLA Ops:
  0.0 0.0 copy-start.5
  0.0 0.0 copy-start.2
  0.0 0.0 copy-start.4
  0.0 0.0 copy-start.3
  0.0 0.0 copy-start.1
  0.0 0.7 %copy-done.2 = bf16[4,4096]{1,0:T(4,128)(2,1)S(1)} copy-done((bf16[4,4096]{1,0:T(4,128)(2,1)S(1)}, bf16[4,4096]{1,0:T(4,128)(2,1)}, u32[]{:S(2)}) %copy-start.2) | copy-done | bytes 32792
  0.8 0.0 copy-start
  0.8 4.4 %collective-permute-start.3 = (bf16[4,4096]{1,0:T(4,128)(2,1)S(1)}, bf16[4,4096]{1,0:T(4,128)(2,1)S(1)}, u32[]{:S(2)}, u32[]{:S(2)}) collective-permute-start(bf16[4,4096]{1,0:T(4,128)(2,1)S(1)} %copy-done.2), channel_id=1, source_target_pairs={{1,14},{3,12},{5,10},{7,8},{9,6},{11,4},{13,2},{15,0},{0,11},{2,9}... | collective-permute-start | bytes 98312 | tf_op jit(solution)/shard_map/ppermute | solution.py:254
  5.2 0.7 %collective-permute-start.2 = (bf16[4,4096]{1,0:T(4,128)(2,1)S(1)}, bf16[4,4096]{1,0:T(4,128)(2,1)S(1)}, u32[]{:S(2)}, u32[]{:S(2)}) collective-permute-start(bf16[4,4096]{1,0:T(4,128)(2,1)S(1)} %copy-done.2), channel_id=1, source_target_pairs={{1,12},{3,14},{5,8},{7,10},{9,4},{11,6},{13,0},{15,2},{0,9},{2,11}... | collective-permute-start | bytes 98312 | tf_op jit(solution)/shard_map/ppermute | solution.py:254
  5.9 0.1 collective-permute-start.1
  6.0 1.0 %collective-permute-start = (bf16[4,4096]{1,0:T(4,128)(2,1)S(1)}, bf16[4,4096]{1,0:T(4,128)(2,1)S(1)}, u32[]{:S(2)}, u32[]{:S(2)}) collective-permute-start(bf16[4,4096]{1,0:T(4,128)(2,1)S(1)} %copy-done.2), channel_id=1, source_target_pairs={{1,4},{3,6},{5,0},{7,2},{9,12},{11,14},{13,8},{15,10},{0,5},{2,7},... | collective-permute-start | bytes 98312 | tf_op jit(solution)/shard_map/ppermute | solution.py:254
  7.0 0.8 %collective-permute-done.3.refs_3_ = bf16[4,4096]{1,0:T(4,128)(2,1)S(1)} collective-permute-done((bf16[4,4096]{1,0:T(4,128)(2,1)S(1)}, bf16[4,4096]{1,0:T(4,128)(2,1)S(1)}, u32[]{:S(2)}, u32[]{:S(2)}) %collective-permute-start.3) | collective-permute-done | bytes 32800 | tf_op jit(solution)/shard_map/ppermute | solution.py:254
  7.9 2.8 %collective-permute-done.2.refs_2_ = bf16[4,4096]{1,0:T(4,128)(2,1)S(1)} collective-permute-done((bf16[4,4096]{1,0:T(4,128)(2,1)S(1)}, bf16[4,4096]{1,0:T(4,128)(2,1)S(1)}, u32[]{:S(2)}, u32[]{:S(2)}) %collective-permute-start.2) | collective-permute-done | bytes 32800 | tf_op jit(solution)/shard_map/ppermute | solution.py:254
  10.7 0.0 collective-permute-done.1.refs_1_
  10.7 0.0 collective-permute-done.refs_0_
  10.7 0.8 %collective-permute-start.4 = (bf16[4,4,4096]{2,1,0:T(4,128)(2,1)S(1)}, bf16[4,4,4096]{2,1,0:T(4,128)(2,1)S(1)}, u32[]{:S(2)}, u32[]{:S(2)}) collective-permute-start(bf16[4,4,4096]{2,1,0:T(4,128)(2,1)S(1)} %shard_map.74.mine_ref), channel_id=1, source_target_pairs={{0,1},{1,0},{2,3},{3,2},{4,5},{5,4},{6,7},{7,6},{8,9},{9,8},{10,11... | collective-permute-start | bytes 393224 | tf_op jit(solution)/shard_map/ppermute | solution.py:262
  11.5 1.0 %collective-permute-done.4.got_ref = bf16[4,4,4096]{2,1,0:T(4,128)(2,1)S(1)} collective-permute-done((bf16[4,4,4096]{2,1,0:T(4,128)(2,1)S(1)}, bf16[4,4,4096]{2,1,0:T(4,128)(2,1)S(1)}, u32[]{:S(2)}, u32[]{:S(2)}) %collective-permute-start.4) | collective-permute-done | bytes 131104 | tf_op jit(solution)/shard_map/ppermute | solution.py:262
  12.5 0.0 copy-done.5
  12.5 0.0 copy-done.4
  12.5 0.0 copy-done.3
  12.5 0.0 copy-done.1
  12.5 0.0 slice-start
  12.5 0.0 slice-start.1
  12.5 0.0 slice-start.2
  12.6 3.1 %shard_map.75 = (bf16[32,4096]{1,0:T(8,128)(2,1)S(1)}, f32[32,2048]{1,0:T(8,128)S(1)}, f32[32,128]{1,0:T(8,128)S(1)}) custom-call(s32[4]{0:T(128)S(4)} %shard_map.73.place_ref, s32[1,4]{1,0:T(1,128)S(1)} %bitcast.3, bf16[4,4096]{1,0:T(4,128)(2,1)S(1)} %copy-done.2, bf16[4,4,4096]{2,1,0:T(4,128)(2,1)S(1)} %shard_map.74.mine_ref, ...), custom_call_target="tpu_custom_call" | custom-call | flops 5000000000 | tf_op jit(solution)/shard_map/pallas_call | solution.py:126
  15.7 0.0 copy-done
  15.7 0.0 slice-start.3
  15.7 3.0 %shard_map.76.h_ref = bf16[32,2048]{1,0:T(8,128)(2,1)S(1)} custom-call(bf16[32,4096]{1,0:T(8,128)(2,1)S(1)} %get-tuple-element.22.x_ref, f32[32,2048]{1,0:T(8,128)S(1)} %get-tuple-element.23.act_ref, bf16[4096,2048]{1,0:T(8,128)(2,1)S(1)} %copy-done), custom_call_target="tpu_custom_call" | custom-call | flops 2000000000 | tf_op jit(solution)/shard_map/pallas_call | solution.py:149
  18.7 0.0 slice-done
  18.7 0.0 slice-done.1
  18.7 0.0 slice-done.2
  18.7 0.0 slice-done.3
  18.8 1.6 %shard_map.78 = bf16[32,2048]{1,0:T(8,128)(2,1)S(1)} custom-call(s32[4]{0:T(128)S(4)} %shard_map.73.place_ref, bf16[32,2048]{1,0:T(8,128)(2,1)S(1)} %shard_map.76.h_ref, bf16[2048,4096]{1,0:T(8,128)(2,1)S(1)} %bitcast.2), custom_call_target="tpu_custom_call" | custom-call | flops 268435456 | tf_op jit(solution)/shard_map/pallas_call | solution.py:172
  20.3 0.4 %collective-permute-start.5 = (bf16[32,2048]{1,0:T(8,128)(2,1)S(1)}, bf16[32,2048]{1,0:T(8,128)(2,1)S(1)}, u32[]{:S(2)}, u32[]{:S(2)}) collective-permute-start(bf16[32,2048]{1,0:T(8,128)(2,1)S(1)} %shard_map.78), channel_id=1, source_target_pairs={{0,1},{1,0},{2,3},{3,2},{4,5},{5,4},{6,7},{7,6},{8,9},{9,8},{10,11... | collective-permute-start | bytes 393224 | tf_op jit(solution)/shard_map/ppermute | solution.py:262
  20.7 1.6 %shard_map.77.keep_ref = f32[32,2048]{1,0:T(8,128)S(1)} custom-call(s32[4]{0:T(128)S(4)} %shard_map.73.place_ref, bf16[32,2048]{1,0:T(8,128)(2,1)S(1)} %shard_map.76.h_ref, bf16[2048,4096]{1,0:T(8,128)(2,1)S(1)} %bitcast.2), custom_call_target="tpu_custom_call" | custom-call | flops 268435456 | tf_op jit(solution)/shard_map/pallas_call | solution.py:172
  22.3 0.0 collective-permute-done.5.got_ref
  22.3 0.1 shard_map.79
  22.4 1.5 %collective-permute-start.6 = (bf16[2,4,2048]{2,1,0:T(4,128)(2,1)S(1)}, bf16[2,4,2048]{2,1,0:T(4,128)(2,1)S(1)}, u32[]{:S(2)}, u32[]{:S(2)}) collective-permute-start(bf16[2,4,2048]{2,1,0:T(4,128)(2,1)S(1)} %get-tuple-element.25), channel_id=1, source_target_pairs={{0,6},{1,7},{2,4},{3,5},{4,2},{5,3},{6,0},{7,1},{8,14},{9,15},{10,... | collective-permute-start | bytes 98312 | tf_op jit(solution)/shard_map/ppermute | solution.py:245
  23.9 0.4 %collective-permute-start.7 = (bf16[2,4,2048]{2,1,0:T(4,128)(2,1)S(1)}, bf16[2,4,2048]{2,1,0:T(4,128)(2,1)S(1)}, u32[]{:S(2)}, u32[]{:S(2)}) collective-permute-start(bf16[2,4,2048]{2,1,0:T(4,128)(2,1)S(1)} %get-tuple-element.26), channel_id=1, source_target_pairs={{0,5},{1,4},{2,7},{3,6},{4,1},{5,0},{6,3},{7,2},{8,13},{9,12},{10,... | collective-permute-start | bytes 98312 | tf_op jit(solution)/shard_map/ppermute | solution.py:245
  24.3 1.4 %collective-permute-start.8 = (bf16[2,4,2048]{2,1,0:T(4,128)(2,1)S(1)}, bf16[2,4,2048]{2,1,0:T(4,128)(2,1)S(1)}, u32[]{:S(2)}, u32[]{:S(2)}) collective-permute-start(bf16[2,4,2048]{2,1,0:T(4,128)(2,1)S(1)} %get-tuple-element.27), channel_id=1, source_target_pairs={{0,3},{1,2},{2,1},{3,0},{4,7},{5,6},{6,5},{7,4},{8,11},{9,10},{10,... | collective-permute-start | bytes 98312 | tf_op jit(solution)/shard_map/ppermute | solution.py:245
  25.7 1.9 %collective-permute-done.6.refs_1_ = bf16[2,4,2048]{2,1,0:T(4,128)(2,1)S(1)} collective-permute-done((bf16[2,4,2048]{2,1,0:T(4,128)(2,1)S(1)}, bf16[2,4,2048]{2,1,0:T(4,128)(2,1)S(1)}, u32[]{:S(2)}, u32[]{:S(2)}) %collective-permute-start.6) | collective-permute-done | bytes 32800 | tf_op jit(solution)/shard_map/ppermute | solution.py:245
  27.6 0.0 collective-permute-done.7.refs_2_
  27.6 0.2 collective-permute-done.8.refs_3_
  27.8 2.7 %collective-permute-start.9 = (bf16[4,2048]{1,0:T(4,128)(2,1)S(1)}, bf16[4,2048]{1,0:T(4,128)(2,1)S(1)}, u32[]{:S(2)}, u32[]{:S(2)}) collective-permute-start(bf16[4,2048]{1,0:T(4,128)(2,1)S(1)} %get-tuple-element.29), channel_id=1, source_target_pairs={{0,9},{1,8},{2,10},{3,11},{4,12},{5,13},{6,15},{7,14},{8,1},{9,0},... | collective-permute-start | bytes 49160 | tf_op jit(solution)/shard_map/ppermute | solution.py:250
  30.5 0.0 collective-permute-start.10
  30.5 1.4 %collective-permute-done.9.got_ref = bf16[4,2048]{1,0:T(4,128)(2,1)S(1)} collective-permute-done((bf16[4,2048]{1,0:T(4,128)(2,1)S(1)}, bf16[4,2048]{1,0:T(4,128)(2,1)S(1)}, u32[]{:S(2)}, u32[]{:S(2)}) %collective-permute-start.9) | collective-permute-done | bytes 16416 | tf_op jit(solution)/shard_map/ppermute | solution.py:250
  32.0 0.0 collective-permute-done.10.turned_ref
  32.0 0.6 %shard_map.81 = bf16[4,2048]{1,0:T(4,128)(2,1)} custom-call(s32[4]{0:T(128)S(4)} %shard_map.73.place_ref, f32[4,2048]{1,0:T(4,128)S(1)} %get-tuple-element.28.own_ref, bf16[4,2048]{1,0:T(4,128)(2,1)S(1)} %collective-permute-done.9.got_ref, bf16[4,2048]{1,0:T(4,128)(2,1)S(1)} %collective-permute-done.10.turned_ref), custom_call_target="tpu_custom_call" | custom-call | tf_op jit(solution)/shard_map/pallas_call | solution.py:232
  (4 shorter events, 0.1 us)
Async XLA Ops:
  0.0 12.5 %copy-start.5 = (s32[4]{0:T(128)S(1)}, s32[4]{0:T(128)}, u32[]{:S(2)}) copy-start(s32[4]{0:T(128)} %param.11) | copy-start | bytes 52
  0.0 0.8 %copy-start.2 = (bf16[4,4096]{1,0:T(4,128)(2,1)S(1)}, bf16[4,4096]{1,0:T(4,128)(2,1)}, u32[]{:S(2)}) copy-start(bf16[4,4096]{1,0:T(4,128)(2,1)} %tokens_ref) | copy-start | bytes 98308
  0.0 12.5 %copy-start.4 = (f32[4,128]{1,0:T(4,128)S(1)}, f32[4,128]{1,0:T(4,128)}, u32[]{:S(2)}) copy-start(f32[4,128]{1,0:T(4,128)} %gates_ref.1) | copy-start | bytes 6148
  0.0 12.5 %copy-start.3 = (s32[4,128]{1,0:T(4,128)S(1)}, s32[4,128]{1,0:T(4,128)}, u32[]{:S(2)}) copy-start(s32[4,128]{1,0:T(4,128)} %rows_ref.1) | copy-start | bytes 6148
  0.0 12.5 %copy-start.1 = (bf16[4096,2048]{1,0:T(8,128)(2,1)S(1)}, bf16[4096,2048]{1,0:T(8,128)(2,1)}, u32[]{:S(2)}) copy-start(bf16[4096,2048]{1,0:T(8,128)(2,1)} %wg_ref.1) | copy-start | bytes 50331652
  0.8 14.9 %copy-start = (bf16[4096,2048]{1,0:T(8,128)(2,1)S(1)}, bf16[4096,2048]{1,0:T(8,128)(2,1)}, u32[]{:S(2)}) copy-start(bf16[4096,2048]{1,0:T(8,128)(2,1)} %wu_ref.1) | copy-start | bytes 50331652
  0.8 7.1 %collective-permute-start.3 = (bf16[4,4096]{1,0:T(4,128)(2,1)S(1)}, bf16[4,4096]{1,0:T(4,128)(2,1)S(1)}, u32[]{:S(2)}, u32[]{:S(2)}) collective-permute-start(bf16[4,4096]{1,0:T(4,128)(2,1)S(1)} %copy-done.2), channel_id=1, source_target_pairs={{1,14},{3,12},{5,10},{7,8},{9,6},{11,4},{13,2},{15,0},{0,11},{2,9}... | collective-permute-start | bytes 98312 | tf_op jit(solution)/shard_map/ppermute | solution.py:254
  5.2 5.5 %collective-permute-start.2 = (bf16[4,4096]{1,0:T(4,128)(2,1)S(1)}, bf16[4,4096]{1,0:T(4,128)(2,1)S(1)}, u32[]{:S(2)}, u32[]{:S(2)}) collective-permute-start(bf16[4,4096]{1,0:T(4,128)(2,1)S(1)} %copy-done.2), channel_id=1, source_target_pairs={{1,12},{3,14},{5,8},{7,10},{9,4},{11,6},{13,0},{15,2},{0,9},{2,11}... | collective-permute-start | bytes 98312 | tf_op jit(solution)/shard_map/ppermute | solution.py:254
  5.9 4.8 %collective-permute-start.1 = (bf16[4,4096]{1,0:T(4,128)(2,1)S(1)}, bf16[4,4096]{1,0:T(4,128)(2,1)S(1)}, u32[]{:S(2)}, u32[]{:S(2)}) collective-permute-start(bf16[4,4096]{1,0:T(4,128)(2,1)S(1)} %copy-done.2), channel_id=1, source_target_pairs={{1,2},{3,0},{5,6},{7,4},{9,10},{11,8},{13,14},{15,12},{0,7},{2,5},... | collective-permute-start | bytes 98312 | tf_op jit(solution)/shard_map/ppermute | solution.py:254
  6.0 4.7 %collective-permute-start = (bf16[4,4096]{1,0:T(4,128)(2,1)S(1)}, bf16[4,4096]{1,0:T(4,128)(2,1)S(1)}, u32[]{:S(2)}, u32[]{:S(2)}) collective-permute-start(bf16[4,4096]{1,0:T(4,128)(2,1)S(1)} %copy-done.2), channel_id=1, source_target_pairs={{1,4},{3,6},{5,0},{7,2},{9,12},{11,14},{13,8},{15,10},{0,5},{2,7},... | collective-permute-start | bytes 98312 | tf_op jit(solution)/shard_map/ppermute | solution.py:254
  10.7 1.8 %collective-permute-start.4 = (bf16[4,4,4096]{2,1,0:T(4,128)(2,1)S(1)}, bf16[4,4,4096]{2,1,0:T(4,128)(2,1)S(1)}, u32[]{:S(2)}, u32[]{:S(2)}) collective-permute-start(bf16[4,4,4096]{2,1,0:T(4,128)(2,1)S(1)} %shard_map.74.mine_ref), channel_id=1, source_target_pairs={{0,1},{1,0},{2,3},{3,2},{4,5},{5,4},{6,7},{7,6},{8,9},{9,8},{10,11... | collective-permute-start | bytes 393224 | tf_op jit(solution)/shard_map/ppermute | solution.py:262
  12.5 6.2 %slice-start = ((s8[16777216]{0:T(1024)(128)(4,1)}), s8[4194304]{0:T(1024)(128)(4,1)S(1)}, s32[]{:S(2)}) async-start(s8[16777216]{0:T(1024)(128)(4,1)} %bitcast.1), calls=%async_computation | async-start | bytes 8388608
  12.5 6.2 %slice-start.1 = ((s8[16777216]{0:T(1024)(128)(4,1)}), s8[4194304]{0:T(1024)(128)(4,1)S(1)}, s32[]{:S(2)}) async-start(s8[16777216]{0:T(1024)(128)(4,1)} %bitcast.1), calls=%async_computation.1 | async-start | bytes 8388608
  12.5 6.2 %slice-start.2 = ((s8[16777216]{0:T(1024)(128)(4,1)}), s8[4194304]{0:T(1024)(128)(4,1)S(1)}, s32[]{:S(2)}) async-start(s8[16777216]{0:T(1024)(128)(4,1)} %bitcast.1), calls=%async_computation.2 | async-start | bytes 8388608
  15.7 3.1 %slice-start.3 = ((s8[16777216]{0:T(1024)(128)(4,1)}), s8[4194304]{0:T(1024)(128)(4,1)S(1)}, s32[]{:S(2)}) async-start(s8[16777216]{0:T(1024)(128)(4,1)} %bitcast.1), calls=%async_computation.3 | async-start | bytes 8388608
  20.3 1.9 %collective-permute-start.5 = (bf16[32,2048]{1,0:T(8,128)(2,1)S(1)}, bf16[32,2048]{1,0:T(8,128)(2,1)S(1)}, u32[]{:S(2)}, u32[]{:S(2)}) collective-permute-start(bf16[32,2048]{1,0:T(8,128)(2,1)S(1)} %shard_map.78), channel_id=1, source_target_pairs={{0,1},{1,0},{2,3},{3,2},{4,5},{5,4},{6,7},{7,6},{8,9},{9,8},{10,11... | collective-permute-start | bytes 393224 | tf_op jit(solution)/shard_map/ppermute | solution.py:262
  22.4 5.2 %collective-permute-start.6 = (bf16[2,4,2048]{2,1,0:T(4,128)(2,1)S(1)}, bf16[2,4,2048]{2,1,0:T(4,128)(2,1)S(1)}, u32[]{:S(2)}, u32[]{:S(2)}) collective-permute-start(bf16[2,4,2048]{2,1,0:T(4,128)(2,1)S(1)} %get-tuple-element.25), channel_id=1, source_target_pairs={{0,6},{1,7},{2,4},{3,5},{4,2},{5,3},{6,0},{7,1},{8,14},{9,15},{10,... | collective-permute-start | bytes 98312 | tf_op jit(solution)/shard_map/ppermute | solution.py:245
  23.9 3.7 %collective-permute-start.7 = (bf16[2,4,2048]{2,1,0:T(4,128)(2,1)S(1)}, bf16[2,4,2048]{2,1,0:T(4,128)(2,1)S(1)}, u32[]{:S(2)}, u32[]{:S(2)}) collective-permute-start(bf16[2,4,2048]{2,1,0:T(4,128)(2,1)S(1)} %get-tuple-element.26), channel_id=1, source_target_pairs={{0,5},{1,4},{2,7},{3,6},{4,1},{5,0},{6,3},{7,2},{8,13},{9,12},{10,... | collective-permute-start | bytes 98312 | tf_op jit(solution)/shard_map/ppermute | solution.py:245
  24.3 3.5 %collective-permute-start.8 = (bf16[2,4,2048]{2,1,0:T(4,128)(2,1)S(1)}, bf16[2,4,2048]{2,1,0:T(4,128)(2,1)S(1)}, u32[]{:S(2)}, u32[]{:S(2)}) collective-permute-start(bf16[2,4,2048]{2,1,0:T(4,128)(2,1)S(1)} %get-tuple-element.27), channel_id=1, source_target_pairs={{0,3},{1,2},{2,1},{3,0},{4,7},{5,6},{6,5},{7,4},{8,11},{9,10},{10,... | collective-permute-start | bytes 98312 | tf_op jit(solution)/shard_map/ppermute | solution.py:245
  27.8 4.1 %collective-permute-start.9 = (bf16[4,2048]{1,0:T(4,128)(2,1)S(1)}, bf16[4,2048]{1,0:T(4,128)(2,1)S(1)}, u32[]{:S(2)}, u32[]{:S(2)}) collective-permute-start(bf16[4,2048]{1,0:T(4,128)(2,1)S(1)} %get-tuple-element.29), channel_id=1, source_target_pairs={{0,9},{1,8},{2,10},{3,11},{4,12},{5,13},{6,15},{7,14},{8,1},{9,0},... | collective-permute-start | bytes 49160 | tf_op jit(solution)/shard_map/ppermute | solution.py:250
  30.5 1.4 %collective-permute-start.10 = (bf16[4,2048]{1,0:T(4,128)(2,1)S(1)}, bf16[4,2048]{1,0:T(4,128)(2,1)S(1)}, u32[]{:S(2)}, u32[]{:S(2)}) collective-permute-start(bf16[4,2048]{1,0:T(4,128)(2,1)S(1)} %get-tuple-element.30), channel_id=1, source_target_pairs={{0,1},{1,0},{2,3},{3,2},{4,5},{5,4},{6,7},{7,6},{8,9},{9,8},{10,11... | collective-permute-start | bytes 49160 | tf_op jit(solution)/shard_map/ppermute | solution.py:262

commit v19 on v18

--- a/solution.py
+++ b/solution.py
@@ -11,7 +11,7 @@
 CAP = 3
 TILE = 512
 MIB = 1 << 20
-ORDER = (0, 1, 6, 7, 2, 3, 4, 5)
+ORDER = (0, 3, 6, 7, 2, 1, 4, 5)
 SOURCES = len(ORDER)
 GATE = 5_000_000_000
 UP = 2_000_000_000

time: 32.9 us -> 32.9 us (level)
  waiting for transfers between devices: 8.25 us -> 8.67 us
    ppermute x3, starting transfers between devices: 1.15 us -> 0.49 us  [swap_cores(): return lax.ppermute(x, 'hid', [(0, 1), (1, 0)])]
    ppermute x4, starting transfers between devices: 6.27 us -> 6.85 us  [fetched(): lax.ppermute(x, ('exp', 'hid'), [(2 * i + 1 - side, 2 * (i ^ k) + side) f...]
  transfers between devices with their start and end apart: 11 -> 11, of which waited for: 6 -> 7; matrix products, arithmetic and copies ran while one was open for 0% -> 0% of each run, Pallas kernels for 5% -> 5%
where the time goes in v19:
time: 32.9 us; the launch traced here: 32.8 us
  starting transfers between devices  13.1 us (40%)
  Pallas kernels  10 us (30%)
  waiting for transfers between devices  8.67 us (26%)
  local copies, waits for them, and re-layouts  0.78 us (2%)
    ppermute x4, starting transfers between devices, fetched(): lax.ppermute(x, ('exp', 'hid'), [(2 * i + 1 - side, 2 * (i ^ k) + side) f...  6.85 us
    ppermute x4, waiting for transfers between devices, fetched(): lax.ppermute(x, ('exp', 'hid'), [(2 * i + 1 - side, 2 * (i ^ k) + side) f...  3.76 us
    ppermute x3, starting transfers between devices, swapped(): return lax.ppermute(x, ('exp', 'hid'), pairs)  3.29 us
    pallas_call x1, Pallas kernels, gate_rows(): pl.pallas_call(functools.partial(gate_kernel, SOURCES // block_rows.shape...  3.12 us
    pallas_call x2, Pallas kernels, down_half(): pl.pallas_call(functools.partial(down_kernel, other), out_shape=jax.Shape...  3.12 us
    pallas_call x1, Pallas kernels, hidden_rows(): pl.pallas_call(up_kernel, out_shape=jax.ShapeDtypeStruct(act.shape, jnp.b...  3.01 us
    ppermute x1, starting transfers between devices, sent_home(): return lax.ppermute(x, ('exp', 'hid'), pairs)  2.52 us
    ppermute x3, waiting for transfers between devices, swapped(): return lax.ppermute(x, ('exp', 'hid'), pairs)  2.21 us
  transfers between devices with their start and end apart: 11, of which 7 were waited for; matrix products, arithmetic and copies ran while one was open for 0% of the time, Pallas kernels for 5%

profile of v19, /device:TPU:0, one launch (start us, length us, event | category | flops | bytes accessed | tf_op | source)
XLA Modules:
  0.0 32.8 jit_solution(12540145103810469365)
XLA Ops:
  0.0 0.0 copy-start.5
  0.0 0.0 copy-start.2
  0.0 0.0 copy-start.4
  0.0 0.0 copy-start.3
  0.0 0.0 copy-start.1
  0.0 0.7 %copy-done.2 = bf16[4,4096]{1,0:T(4,128)(2,1)S(1)} copy-done((bf16[4,4096]{1,0:T(4,128)(2,1)S(1)}, bf16[4,4096]{1,0:T(4,128)(2,1)}, u32[]{:S(2)}) %copy-start.2) | copy-done | bytes 32792
  0.8 0.0 copy-start
  0.8 4.4 %collective-permute-start.3 = (bf16[4,4096]{1,0:T(4,128)(2,1)S(1)}, bf16[4,4096]{1,0:T(4,128)(2,1)S(1)}, u32[]{:S(2)}, u32[]{:S(2)}) collective-permute-start(bf16[4,4096]{1,0:T(4,128)(2,1)S(1)} %copy-done.2), channel_id=1, source_target_pairs={{1,14},{3,12},{5,10},{7,8},{9,6},{11,4},{13,2},{15,0},{0,11},{2,9}... | collective-permute-start | bytes 98312 | tf_op jit(solution)/shard_map/ppermute | solution.py:254
  5.2 0.7 %collective-permute-start.2 = (bf16[4,4096]{1,0:T(4,128)(2,1)S(1)}, bf16[4,4096]{1,0:T(4,128)(2,1)S(1)}, u32[]{:S(2)}, u32[]{:S(2)}) collective-permute-start(bf16[4,4096]{1,0:T(4,128)(2,1)S(1)} %copy-done.2), channel_id=1, source_target_pairs={{1,12},{3,14},{5,8},{7,10},{9,4},{11,6},{13,0},{15,2},{0,9},{2,11}... | collective-permute-start | bytes 98312 | tf_op jit(solution)/shard_map/ppermute | solution.py:254
  5.9 1.1 %collective-permute-start.1 = (bf16[4,4096]{1,0:T(4,128)(2,1)S(1)}, bf16[4,4096]{1,0:T(4,128)(2,1)S(1)}, u32[]{:S(2)}, u32[]{:S(2)}) collective-permute-start(bf16[4,4096]{1,0:T(4,128)(2,1)S(1)} %copy-done.2), channel_id=1, source_target_pairs={{1,6},{3,4},{5,2},{7,0},{9,14},{11,12},{13,10},{15,8},{0,3},{2,1},... | collective-permute-start | bytes 98312 | tf_op jit(solution)/shard_map/ppermute | solution.py:254
  7.0 0.6 %collective-permute-start = (bf16[4,4096]{1,0:T(4,128)(2,1)S(1)}, bf16[4,4096]{1,0:T(4,128)(2,1)S(1)}, u32[]{:S(2)}, u32[]{:S(2)}) collective-permute-start(bf16[4,4096]{1,0:T(4,128)(2,1)S(1)} %copy-done.2), channel_id=1, source_target_pairs={{1,4},{3,6},{5,0},{7,2},{9,12},{11,14},{13,8},{15,10},{0,5},{2,7},... | collective-permute-start | bytes 98312 | tf_op jit(solution)/shard_map/ppermute | solution.py:254
  7.6 0.3 collective-permute-done.3.refs_3_
  7.9 2.8 %collective-permute-done.2.refs_2_ = bf16[4,4096]{1,0:T(4,128)(2,1)S(1)} collective-permute-done((bf16[4,4096]{1,0:T(4,128)(2,1)S(1)}, bf16[4,4096]{1,0:T(4,128)(2,1)S(1)}, u32[]{:S(2)}, u32[]{:S(2)}) %collective-permute-start.2) | collective-permute-done | bytes 32800 | tf_op jit(solution)/shard_map/ppermute | solution.py:254
  10.7 0.0 collective-permute-done.1.refs_1_
  10.7 0.7 %collective-permute-done.refs_0_ = bf16[4,4096]{1,0:T(4,128)(2,1)S(1)} collective-permute-done((bf16[4,4096]{1,0:T(4,128)(2,1)S(1)}, bf16[4,4096]{1,0:T(4,128)(2,1)S(1)}, u32[]{:S(2)}, u32[]{:S(2)}) %collective-permute-start) | collective-permute-done | bytes 32800 | tf_op jit(solution)/shard_map/ppermute | solution.py:254
  11.4 0.2 collective-permute-start.4
  11.6 1.2 %collective-permute-done.4.got_ref = bf16[4,4,4096]{2,1,0:T(4,128)(2,1)S(1)} collective-permute-done((bf16[4,4,4096]{2,1,0:T(4,128)(2,1)S(1)}, bf16[4,4,4096]{2,1,0:T(4,128)(2,1)S(1)}, u32[]{:S(2)}, u32[]{:S(2)}) %collective-permute-start.4) | collective-permute-done | bytes 131104 | tf_op jit(solution)/shard_map/ppermute | solution.py:262
  12.8 0.0 copy-done.5
  12.8 0.0 copy-done.4
  12.8 0.0 copy-done.3
  12.8 0.0 copy-done.1
  12.8 0.0 slice-start
  12.9 0.0 slice-start.1
  12.9 0.0 slice-start.2
  12.9 3.1 %shard_map.75 = (bf16[32,4096]{1,0:T(8,128)(2,1)S(1)}, f32[32,2048]{1,0:T(8,128)S(1)}, f32[32,128]{1,0:T(8,128)S(1)}) custom-call(s32[4]{0:T(128)S(4)} %shard_map.73.place_ref, s32[1,4]{1,0:T(1,128)S(1)} %bitcast.3, bf16[4,4096]{1,0:T(4,128)(2,1)S(1)} %copy-done.2, bf16[4,4,4096]{2,1,0:T(4,128)(2,1)S(1)} %shard_map.74.mine_ref, ...), custom_call_target="tpu_custom_call" | custom-call | flops 5000000000 | tf_op jit(solution)/shard_map/pallas_call | solution.py:126
  16.0 0.0 copy-done
  16.0 0.0 slice-start.3
  16.0 3.0 %shard_map.76.h_ref = bf16[32,2048]{1,0:T(8,128)(2,1)S(1)} custom-call(bf16[32,4096]{1,0:T(8,128)(2,1)S(1)} %get-tuple-element.22.x_ref, f32[32,2048]{1,0:T(8,128)S(1)} %get-tuple-element.23.act_ref, bf16[4096,2048]{1,0:T(8,128)(2,1)S(1)} %copy-done), custom_call_target="tpu_custom_call" | custom-call | flops 2000000000 | tf_op jit(solution)/shard_map/pallas_call | solution.py:149
  19.0 0.0 slice-done
  19.0 0.0 slice-done.1
  19.1 0.0 slice-done.2
  19.1 0.0 slice-done.3
  19.1 1.6 %shard_map.78 = bf16[32,2048]{1,0:T(8,128)(2,1)S(1)} custom-call(s32[4]{0:T(128)S(4)} %shard_map.73.place_ref, bf16[32,2048]{1,0:T(8,128)(2,1)S(1)} %shard_map.76.h_ref, bf16[2048,4096]{1,0:T(8,128)(2,1)S(1)} %bitcast.2), custom_call_target="tpu_custom_call" | custom-call | flops 268435456 | tf_op jit(solution)/shard_map/pallas_call | solution.py:172
  20.7 0.2 collective-permute-start.5
  20.8 1.6 %shard_map.77.keep_ref = f32[32,2048]{1,0:T(8,128)S(1)} custom-call(s32[4]{0:T(128)S(4)} %shard_map.73.place_ref, bf16[32,2048]{1,0:T(8,128)(2,1)S(1)} %shard_map.76.h_ref, bf16[2048,4096]{1,0:T(8,128)(2,1)S(1)} %bitcast.2), custom_call_target="tpu_custom_call" | custom-call | flops 268435456 | tf_op jit(solution)/shard_map/pallas_call | solution.py:172
  22.4 0.0 collective-permute-done.5.got_ref
  22.4 0.1 shard_map.79
  22.5 0.8 %collective-permute-start.6 = (bf16[2,4,2048]{2,1,0:T(4,128)(2,1)S(1)}, bf16[2,4,2048]{2,1,0:T(4,128)(2,1)S(1)}, u32[]{:S(2)}, u32[]{:S(2)}) collective-permute-start(bf16[2,4,2048]{2,1,0:T(4,128)(2,1)S(1)} %get-tuple-element.25), channel_id=1, source_target_pairs={{0,6},{1,7},{2,4},{3,5},{4,2},{5,3},{6,0},{7,1},{8,14},{9,15},{10,... | collective-permute-start | bytes 98312 | tf_op jit(solution)/shard_map/ppermute | solution.py:245
  23.3 1.3 %collective-permute-start.7 = (bf16[2,4,2048]{2,1,0:T(4,128)(2,1)S(1)}, bf16[2,4,2048]{2,1,0:T(4,128)(2,1)S(1)}, u32[]{:S(2)}, u32[]{:S(2)}) collective-permute-start(bf16[2,4,2048]{2,1,0:T(4,128)(2,1)S(1)} %get-tuple-element.26), channel_id=1, source_target_pairs={{0,5},{1,4},{2,7},{3,6},{4,1},{5,0},{6,3},{7,2},{8,13},{9,12},{10,... | collective-permute-start | bytes 98312 | tf_op jit(solution)/shard_map/ppermute | solution.py:245
  24.7 1.1 %collective-permute-start.8 = (bf16[2,4,2048]{2,1,0:T(4,128)(2,1)S(1)}, bf16[2,4,2048]{2,1,0:T(4,128)(2,1)S(1)}, u32[]{:S(2)}, u32[]{:S(2)}) collective-permute-start(bf16[2,4,2048]{2,1,0:T(4,128)(2,1)S(1)} %get-tuple-element.27), channel_id=1, source_target_pairs={{0,3},{1,2},{2,1},{3,0},{4,7},{5,6},{6,5},{7,4},{8,11},{9,10},{10,... | collective-permute-start | bytes 98312 | tf_op jit(solution)/shard_map/ppermute | solution.py:245
  25.8 1.7 %collective-permute-done.6.refs_1_ = bf16[2,4,2048]{2,1,0:T(4,128)(2,1)S(1)} collective-permute-done((bf16[2,4,2048]{2,1,0:T(4,128)(2,1)S(1)}, bf16[2,4,2048]{2,1,0:T(4,128)(2,1)S(1)}, u32[]{:S(2)}, u32[]{:S(2)}) %collective-permute-start.6) | collective-permute-done | bytes 32800 | tf_op jit(solution)/shard_map/ppermute | solution.py:245
  27.5 0.0 collective-permute-done.7.refs_2_
  27.5 0.5 %collective-permute-done.8.refs_3_ = bf16[2,4,2048]{2,1,0:T(4,128)(2,1)S(1)} collective-permute-done((bf16[2,4,2048]{2,1,0:T(4,128)(2,1)S(1)}, bf16[2,4,2048]{2,1,0:T(4,128)(2,1)S(1)}, u32[]{:S(2)}, u32[]{:S(2)}) %collective-permute-start.8) | collective-permute-done | bytes 32800 | tf_op jit(solution)/shard_map/ppermute | solution.py:245
  28.0 2.5 %collective-permute-start.9 = (bf16[4,2048]{1,0:T(4,128)(2,1)S(1)}, bf16[4,2048]{1,0:T(4,128)(2,1)S(1)}, u32[]{:S(2)}, u32[]{:S(2)}) collective-permute-start(bf16[4,2048]{1,0:T(4,128)(2,1)S(1)} %get-tuple-element.29), channel_id=1, source_target_pairs={{0,9},{1,8},{2,10},{3,11},{4,12},{5,13},{6,15},{7,14},{8,1},{9,0},... | collective-permute-start | bytes 49160 | tf_op jit(solution)/shard_map/ppermute | solution.py:250
  30.5 0.1 collective-permute-start.10
  30.7 1.5 %collective-permute-done.9.got_ref = bf16[4,2048]{1,0:T(4,128)(2,1)S(1)} collective-permute-done((bf16[4,2048]{1,0:T(4,128)(2,1)S(1)}, bf16[4,2048]{1,0:T(4,128)(2,1)S(1)}, u32[]{:S(2)}, u32[]{:S(2)}) %collective-permute-start.9) | collective-permute-done | bytes 16416 | tf_op jit(solution)/shard_map/ppermute | solution.py:250
  32.2 0.0 collective-permute-done.10.turned_ref
  32.2 0.6 %shard_map.81 = bf16[4,2048]{1,0:T(4,128)(2,1)} custom-call(s32[4]{0:T(128)S(4)} %shard_map.73.place_ref, f32[4,2048]{1,0:T(4,128)S(1)} %get-tuple-element.28.own_ref, bf16[4,2048]{1,0:T(4,128)(2,1)S(1)} %collective-permute-done.9.got_ref, bf16[4,2048]{1,0:T(4,128)(2,1)S(1)} %collective-permute-done.10.turned_ref), custom_call_target="tpu_custom_call" | custom-call | tf_op jit(solution)/shard_map/pallas_call | solution.py:232
  (4 shorter events, 0.1 us)
Async XLA Ops:
  0.0 12.8 %copy-start.5 = (s32[4]{0:T(128)S(1)}, s32[4]{0:T(128)}, u32[]{:S(2)}) copy-start(s32[4]{0:T(128)} %param.11) | copy-start | bytes 52
  0.0 0.8 %copy-start.2 = (bf16[4,4096]{1,0:T(4,128)(2,1)S(1)}, bf16[4,4096]{1,0:T(4,128)(2,1)}, u32[]{:S(2)}) copy-start(bf16[4,4096]{1,0:T(4,128)(2,1)} %tokens_ref) | copy-start | bytes 98308
  0.0 12.8 %copy-start.4 = (f32[4,128]{1,0:T(4,128)S(1)}, f32[4,128]{1,0:T(4,128)}, u32[]{:S(2)}) copy-start(f32[4,128]{1,0:T(4,128)} %gates_ref.1) | copy-start | bytes 6148
  0.0 12.8 %copy-start.3 = (s32[4,128]{1,0:T(4,128)S(1)}, s32[4,128]{1,0:T(4,128)}, u32[]{:S(2)}) copy-start(s32[4,128]{1,0:T(4,128)} %rows_ref.1) | copy-start | bytes 6148
  0.0 12.8 %copy-start.1 = (bf16[4096,2048]{1,0:T(8,128)(2,1)S(1)}, bf16[4096,2048]{1,0:T(8,128)(2,1)}, u32[]{:S(2)}) copy-start(bf16[4096,2048]{1,0:T(8,128)(2,1)} %wg_ref.1) | copy-start | bytes 50331652
  0.8 15.2 %copy-start = (bf16[4096,2048]{1,0:T(8,128)(2,1)S(1)}, bf16[4096,2048]{1,0:T(8,128)(2,1)}, u32[]{:S(2)}) copy-start(bf16[4096,2048]{1,0:T(8,128)(2,1)} %wu_ref.1) | copy-start | bytes 50331652
  0.8 7.1 %collective-permute-start.3 = (bf16[4,4096]{1,0:T(4,128)(2,1)S(1)}, bf16[4,4096]{1,0:T(4,128)(2,1)S(1)}, u32[]{:S(2)}, u32[]{:S(2)}) collective-permute-start(bf16[4,4096]{1,0:T(4,128)(2,1)S(1)} %copy-done.2), channel_id=1, source_target_pairs={{1,14},{3,12},{5,10},{7,8},{9,6},{11,4},{13,2},{15,0},{0,11},{2,9}... | collective-permute-start | bytes 98312 | tf_op jit(solution)/shard_map/ppermute | solution.py:254
  5.2 5.5 %collective-permute-start.2 = (bf16[4,4096]{1,0:T(4,128)(2,1)S(1)}, bf16[4,4096]{1,0:T(4,128)(2,1)S(1)}, u32[]{:S(2)}, u32[]{:S(2)}) collective-permute-start(bf16[4,4096]{1,0:T(4,128)(2,1)S(1)} %copy-done.2), channel_id=1, source_target_pairs={{1,12},{3,14},{5,8},{7,10},{9,4},{11,6},{13,0},{15,2},{0,9},{2,11}... | collective-permute-start | bytes 98312 | tf_op jit(solution)/shard_map/ppermute | solution.py:254
  5.9 4.8 %collective-permute-start.1 = (bf16[4,4096]{1,0:T(4,128)(2,1)S(1)}, bf16[4,4096]{1,0:T(4,128)(2,1)S(1)}, u32[]{:S(2)}, u32[]{:S(2)}) collective-permute-start(bf16[4,4096]{1,0:T(4,128)(2,1)S(1)} %copy-done.2), channel_id=1, source_target_pairs={{1,6},{3,4},{5,2},{7,0},{9,14},{11,12},{13,10},{15,8},{0,3},{2,1},... | collective-permute-start | bytes 98312 | tf_op jit(solution)/shard_map/ppermute | solution.py:254
  7.0 4.3 %collective-permute-start = (bf16[4,4096]{1,0:T(4,128)(2,1)S(1)}, bf16[4,4096]{1,0:T(4,128)(2,1)S(1)}, u32[]{:S(2)}, u32[]{:S(2)}) collective-permute-start(bf16[4,4096]{1,0:T(4,128)(2,1)S(1)} %copy-done.2), channel_id=1, source_target_pairs={{1,4},{3,6},{5,0},{7,2},{9,12},{11,14},{13,8},{15,10},{0,5},{2,7},... | collective-permute-start | bytes 98312 | tf_op jit(solution)/shard_map/ppermute | solution.py:254
  11.4 1.4 %collective-permute-start.4 = (bf16[4,4,4096]{2,1,0:T(4,128)(2,1)S(1)}, bf16[4,4,4096]{2,1,0:T(4,128)(2,1)S(1)}, u32[]{:S(2)}, u32[]{:S(2)}) collective-permute-start(bf16[4,4,4096]{2,1,0:T(4,128)(2,1)S(1)} %shard_map.74.mine_ref), channel_id=1, source_target_pairs={{0,1},{1,0},{2,3},{3,2},{4,5},{5,4},{6,7},{7,6},{8,9},{9,8},{10,11... | collective-permute-start | bytes 393224 | tf_op jit(solution)/shard_map/ppermute | solution.py:262
  12.8 6.2 %slice-start = ((s8[16777216]{0:T(1024)(128)(4,1)}), s8[4194304]{0:T(1024)(128)(4,1)S(1)}, s32[]{:S(2)}) async-start(s8[16777216]{0:T(1024)(128)(4,1)} %bitcast.1), calls=%async_computation | async-start | bytes 8388608
  12.9 6.2 %slice-start.1 = ((s8[16777216]{0:T(1024)(128)(4,1)}), s8[4194304]{0:T(1024)(128)(4,1)S(1)}, s32[]{:S(2)}) async-start(s8[16777216]{0:T(1024)(128)(4,1)} %bitcast.1), calls=%async_computation.1 | async-start | bytes 8388608
  12.9 6.2 %slice-start.2 = ((s8[16777216]{0:T(1024)(128)(4,1)}), s8[4194304]{0:T(1024)(128)(4,1)S(1)}, s32[]{:S(2)}) async-start(s8[16777216]{0:T(1024)(128)(4,1)} %bitcast.1), calls=%async_computation.2 | async-start | bytes 8388608
  16.0 3.1 %slice-start.3 = ((s8[16777216]{0:T(1024)(128)(4,1)}), s8[4194304]{0:T(1024)(128)(4,1)S(1)}, s32[]{:S(2)}) async-start(s8[16777216]{0:T(1024)(128)(4,1)} %bitcast.1), calls=%async_computation.3 | async-start | bytes 8388608
  20.7 1.7 %collective-permute-start.5 = (bf16[32,2048]{1,0:T(8,128)(2,1)S(1)}, bf16[32,2048]{1,0:T(8,128)(2,1)S(1)}, u32[]{:S(2)}, u32[]{:S(2)}) collective-permute-start(bf16[32,2048]{1,0:T(8,128)(2,1)S(1)} %shard_map.78), channel_id=1, source_target_pairs={{0,1},{1,0},{2,3},{3,2},{4,5},{5,4},{6,7},{7,6},{8,9},{9,8},{10,11... | collective-permute-start | bytes 393224 | tf_op jit(solution)/shard_map/ppermute | solution.py:262
  22.5 5.0 %collective-permute-start.6 = (bf16[2,4,2048]{2,1,0:T(4,128)(2,1)S(1)}, bf16[2,4,2048]{2,1,0:T(4,128)(2,1)S(1)}, u32[]{:S(2)}, u32[]{:S(2)}) collective-permute-start(bf16[2,4,2048]{2,1,0:T(4,128)(2,1)S(1)} %get-tuple-element.25), channel_id=1, source_target_pairs={{0,6},{1,7},{2,4},{3,5},{4,2},{5,3},{6,0},{7,1},{8,14},{9,15},{10,... | collective-permute-start | bytes 98312 | tf_op jit(solution)/shard_map/ppermute | solution.py:245
  23.3 4.2 %collective-permute-start.7 = (bf16[2,4,2048]{2,1,0:T(4,128)(2,1)S(1)}, bf16[2,4,2048]{2,1,0:T(4,128)(2,1)S(1)}, u32[]{:S(2)}, u32[]{:S(2)}) collective-permute-start(bf16[2,4,2048]{2,1,0:T(4,128)(2,1)S(1)} %get-tuple-element.26), channel_id=1, source_target_pairs={{0,5},{1,4},{2,7},{3,6},{4,1},{5,0},{6,3},{7,2},{8,13},{9,12},{10,... | collective-permute-start | bytes 98312 | tf_op jit(solution)/shard_map/ppermute | solution.py:245
  24.7 3.3 %collective-permute-start.8 = (bf16[2,4,2048]{2,1,0:T(4,128)(2,1)S(1)}, bf16[2,4,2048]{2,1,0:T(4,128)(2,1)S(1)}, u32[]{:S(2)}, u32[]{:S(2)}) collective-permute-start(bf16[2,4,2048]{2,1,0:T(4,128)(2,1)S(1)} %get-tuple-element.27), channel_id=1, source_target_pairs={{0,3},{1,2},{2,1},{3,0},{4,7},{5,6},{6,5},{7,4},{8,11},{9,10},{10,... | collective-permute-start | bytes 98312 | tf_op jit(solution)/shard_map/ppermute | solution.py:245
  28.0 4.1 %collective-permute-start.9 = (bf16[4,2048]{1,0:T(4,128)(2,1)S(1)}, bf16[4,2048]{1,0:T(4,128)(2,1)S(1)}, u32[]{:S(2)}, u32[]{:S(2)}) collective-permute-start(bf16[4,2048]{1,0:T(4,128)(2,1)S(1)} %get-tuple-element.29), channel_id=1, source_target_pairs={{0,9},{1,8},{2,10},{3,11},{4,12},{5,13},{6,15},{7,14},{8,1},{9,0},... | collective-permute-start | bytes 49160 | tf_op jit(solution)/shard_map/ppermute | solution.py:250
  30.5 1.6 %collective-permute-start.10 = (bf16[4,2048]{1,0:T(4,128)(2,1)S(1)}, bf16[4,2048]{1,0:T(4,128)(2,1)S(1)}, u32[]{:S(2)}, u32[]{:S(2)}) collective-permute-start(bf16[4,2048]{1,0:T(4,128)(2,1)S(1)} %get-tuple-element.30), channel_id=1, source_target_pairs={{0,1},{1,0},{2,3},{3,2},{4,5},{5,4},{6,7},{7,6},{8,9},{9,8},{10,11... | collective-permute-start | bytes 49160 | tf_op jit(solution)/shard_map/ppermute | solution.py:262
